TPU v7x, 32 devices: a whole 2x2x4 slice. The times are simulated.
32 devices in a mesh: ep: 8 (over y, x, core), tp: 4 (over z).
Axes of the slice: x: 2, y: 2, z: 4, core: 2. Of those that a mesh axis runs over, the one named last changes fastest.
Arguments:
- inputs: bfloat16 [4096, 2048], P('ep'), may hold values from -6 to 6
- gain_attn: float32 [2048], replicated, may hold values from 0.5 to 1.5
- w_query: bfloat16 [2048, 3072], P(None, 'tp'), may hold values from -0.125 to 0.125
- w_latent: bfloat16 [2048, 576], replicated, may hold values from -0.125 to 0.125
- gain_latent: float32 [512], replicated, may hold values from 0.5 to 1.5
- w_latent_up: bfloat16 [512, 4096], P(None, 'tp'), may hold values from -0.25 to 0.25
- w_output: bfloat16 [2048, 2048], P('tp'), may hold values from -0.5 to 0.5
- gain_ffn: float32 [2048], replicated, may hold values from 0.5 to 1.5
- w_router: float32 [2048, 8], replicated, may hold values from -0.0625 to 0.0625
- w_shared_in: bfloat16 [2, 2048, 2816], P(None, None, 'tp'), may hold values from -0.125 to 0.125
- w_shared_out: bfloat16 [2816, 2048], P('tp'), may hold values from -0.109375 to 0.109375
- w_expert_in: bfloat16 [8, 2, 2048, 1408], P('ep', None, None, 'tp'), may hold values from -0.125 to 0.125
- w_expert_out: bfloat16 [8, 1408, 2048], P('ep', 'tp'), may hold values from -0.21875 to 0.21875
- expert_ids: int32 [4096, 6], P('ep'), may hold values from 0 to 7, as said below
- slot_ids: int32 [4096, 6], P('ep'), may hold values from 0 to 432, as said below
- cotangent: bfloat16 [4096, 2048], P('ep'), may hold values from -6 to 6
Outputs:
- block_out: bfloat16 [4096, 2048], P('ep')
- grad_inputs: bfloat16 [4096, 2048], P('ep')
- grad_gain_attn: float32 [2048], P(('ep', 'tp'))
- grad_query: float32 [2048, 3072], P('ep', 'tp')
- grad_latent: float32 [2048, 576], P(('ep', 'tp'))
- grad_gain_latent: float32 [512], P(('ep', 'tp'))
- grad_latent_up: float32 [512, 4096], P('ep', 'tp')
- grad_output: float32 [2048, 2048], P('tp', 'ep')
- grad_gain_ffn: float32 [2048], P(('ep', 'tp'))
- grad_router: float32 [2048, 8], P(('ep', 'tp'))
- grad_shared_in: float32 [2, 2048, 2816], P(None, 'ep', 'tp')
- grad_shared_out: float32 [2816, 2048], P('tp', 'ep')
- grad_expert_in: float32 [8, 2, 2048, 1408], P('ep', None, None, 'tp')
- grad_expert_out: float32 [8, 1408, 2048], P('ep', 'tp')
Inputs may be any that keep to these rules, and one draw needn't show every extreme that they name: `expert_ids`: each row names 6 different experts; in the 512 rows of each index of ep, some expert is named by more than 432 rows. `slot_ids`: within the 512 rows of one index of ep, the pairs naming one expert are numbered 0, 1, 2, ... in the order of rows and then k; numbers 432 and beyond are replaced by 432, which marks a dropped pair.
All inputs are finite; a program needn't handle non-finite values.
Results may differ from a plain program's by a relative error of at most 0.02.
Values may be sent and summed in bfloat16 or wider, within the bound.
A program may use at most 320 MiB of HBM per device.

v0:
```python
import math

import jax
import jax.numpy as jnp
from jax import lax
from jax.sharding import PartitionSpec as P

NOPE = 128
ROPE = 64
VDIM = 128
KV_RANK = 512
TOPK = 6
BLOCK = 256


EPSILON = 1e-06
HIGHEST = lax.Precision.HIGHEST


def angles(length, rope_width):
    half_width = rope_width // 2
    position = jnp.arange(length, dtype=jnp.float32)
    inverse = jnp.exp(jnp.arange(half_width, dtype=jnp.float32) * (-math.log(10000.0) / half_width))
    angle_table = position[:, None] * inverse[None, :]
    return (jnp.cos(angle_table), jnp.sin(angle_table))


def rotate(values, cosine, sine_table):
    half_width = values.shape[-1] // 2
    front_part = values[..., :half_width]
    second = values[..., half_width:]
    return jnp.concatenate(
        [front_part * cosine - second * sine_table, second * cosine + front_part * sine_table],
        axis=-1,
    )


def silu_parts(gate_val):
    sigmoid_val = jax.nn.sigmoid(gate_val)
    return (gate_val * sigmoid_val, sigmoid_val * (1.0 + gate_val * (1.0 - sigmoid_val)))


def norm_back(grad_norm, gain_vec, normed, inverse):
    scaled = grad_norm * gain_vec
    return inverse * (scaled - normed * jnp.mean(scaled * normed, axis=-1, keepdims=True))


def attention_scores(query_rot, key_nope, key_rope, score_scale, allowed):
    nope_scores = jnp.einsum(
        "qhd,khd->hqk", query_rot[..., :NOPE], key_nope, preferred_element_type=jnp.float32
    )
    rope_scores = jnp.einsum(
        "qhr,kr->hqk", query_rot[..., NOPE:], key_rope, preferred_element_type=jnp.float32
    )
    return jnp.where(allowed[None], (nope_scores + rope_scores) * score_scale, -1e30)


def expert_forward(received, w_expert_in, w_expert_out, sources):
    sectioned = received.reshape(sources, -1, received.shape[1], received.shape[2])
    gate_up = jnp.einsum(
        "secd,egdh->secgh", sectioned, w_expert_in, preferred_element_type=jnp.float32
    )
    gate_val, gate_slope = silu_parts(gate_up[..., 0, :])
    activated = (gate_val * gate_up[..., 1, :]).astype(jnp.bfloat16)
    produced = jnp.einsum(
        "sech,ehd->secd", activated, w_expert_out, preferred_element_type=jnp.float32
    )
    return (sectioned, gate_up, activated, produced.reshape(received.shape))


def body(
    inputs,
    gain_attn,
    w_query,
    w_latent,
    gain_latent,
    w_latent_up,
    w_output,
    gain_ffn,
    w_router,
    w_shared_in,
    w_shared_out,
    w_expert_in,
    w_expert_out,
    expert_ids,
    slot_ids,
    cotangent,
):
    tokens, model_width = inputs.shape
    tp_count = lax.axis_size("tp")
    tp_index = lax.axis_index("tp")
    heads_here = w_output.shape[0] // VDIM
    experts = w_router.shape[1]
    local_experts = w_expert_in.shape[0]
    sources = experts // local_experts
    capacity = (9 * tokens * TOPK + 64 * experts - 1) // (64 * experts) * 8
    qk_width = NOPE + ROPE
    score_scale = qk_width ** (-0.5)
    rows_part = tokens // tp_count
    row_start = tp_index * rows_part
    resid = inputs.astype(jnp.float32)
    inv_first = lax.rsqrt(jnp.mean(resid * resid, axis=-1, keepdims=True) + EPSILON)
    normed_first = resid * inv_first
    hidden_attn = (normed_first * gain_attn).astype(jnp.bfloat16)
    cosine, sine_table = angles(tokens, ROPE)
    query_raw = jnp.dot(hidden_attn, w_query, preferred_element_type=jnp.float32).reshape(
        tokens, heads_here, qk_width
    )
    query_rot = jnp.concatenate(
        [
            query_raw[..., :NOPE],
            rotate(query_raw[..., NOPE:], cosine[:, None], sine_table[:, None]),
        ],
        axis=-1,
    ).astype(jnp.bfloat16)
    latent = jnp.dot(hidden_attn, w_latent, preferred_element_type=jnp.float32)
    compressed = latent[:, :KV_RANK]
    inv_latent = lax.rsqrt(jnp.mean(compressed * compressed, axis=-1, keepdims=True) + EPSILON)
    normed_latent = compressed * inv_latent
    latent_in = (normed_latent * gain_latent).astype(jnp.bfloat16)
    key_rope = rotate(latent[:, KV_RANK:], cosine, sine_table).astype(jnp.bfloat16)
    key_value = (
        jnp.dot(latent_in, w_latent_up, preferred_element_type=jnp.float32)
        .astype(jnp.bfloat16)
        .reshape(tokens, heads_here, NOPE + VDIM)
    )
    key_nope = key_value[..., :NOPE]
    values = key_value[..., NOPE:]
    block_ids = jnp.arange(tokens) // BLOCK
    allowed = block_ids[None, :] <= block_ids[:, None]
    scores = attention_scores(query_rot, key_nope, key_rope, score_scale, allowed)
    row_peak = jnp.max(scores, axis=-1, keepdims=True)
    exp_scores = jnp.exp(scores - row_peak)
    totals = jnp.sum(exp_scores, axis=-1, keepdims=True)
    attn_probs = exp_scores / totals
    log_total = row_peak + jnp.log(totals)
    attended = (
        jnp.einsum(
            "hqk,khd->qhd",
            attn_probs.astype(jnp.bfloat16),
            values,
            preferred_element_type=jnp.float32,
        )
        .astype(jnp.bfloat16)
        .reshape(tokens, heads_here * VDIM)
    )
    attn_full = lax.psum(
        jnp.dot(attended, w_output, preferred_element_type=jnp.float32).astype(jnp.bfloat16), "tp"
    ).astype(jnp.float32)
    middle = resid + attn_full
    inv_second = lax.rsqrt(jnp.mean(middle * middle, axis=-1, keepdims=True) + EPSILON)
    normed_second = middle * inv_second
    hidden_ffn = (normed_second * gain_ffn).astype(jnp.bfloat16)
    hidden_wide = hidden_ffn.astype(jnp.float32)
    logits = jnp.dot(hidden_wide, w_router, precision=HIGHEST, preferred_element_type=jnp.float32)
    logit_peak = jnp.max(logits, axis=-1, keepdims=True)
    exp_logits = jnp.exp(logits - logit_peak)
    router_probs = exp_logits / jnp.sum(exp_logits, axis=-1, keepdims=True)
    route_onehot = (
        expert_ids[:, :, None] == jnp.arange(experts, dtype=jnp.int32)[None, None, :]
    ).astype(jnp.float32)
    pair_gate = jnp.sum(route_onehot * router_probs[:, None, :], axis=-1)
    kept_pair = slot_ids < capacity
    flat_index = jnp.where(kept_pair, expert_ids * capacity + slot_ids, experts * capacity)
    row_numbers = jnp.broadcast_to(jnp.arange(tokens, dtype=jnp.int32)[:, None], (tokens, TOPK))
    owner_row = (
        jnp.full((experts * capacity,), tokens, jnp.int32)
        .at[flat_index.reshape(-1)]
        .set(row_numbers.reshape(-1), mode="drop")
    )
    outgoing = jnp.take(hidden_ffn, owner_row, axis=0, mode="fill", fill_value=0).reshape(
        experts, capacity, model_width
    )
    received = lax.all_to_all(outgoing, "ep", split_axis=0, concat_axis=0, tiled=True)
    sectioned, gate_up, activated, produced = expert_forward(
        received, w_expert_in, w_expert_out, sources
    )
    returned = lax.all_to_all(
        produced.astype(jnp.bfloat16), "ep", split_axis=0, concat_axis=0, tiled=True
    ).astype(produced.dtype)
    out_grad = cotangent.astype(jnp.float32)
    back_rows = returned.reshape(-1, model_width)
    combined = jnp.zeros((tokens, model_width), jnp.float32)
    gate_cols = []
    for pick_index in range(TOPK):
        taken_rows = jnp.take(
            back_rows, flat_index[:, pick_index], axis=0, mode="fill", fill_value=0.0
        )
        combined = combined + pair_gate[:, pick_index : pick_index + 1] * taken_rows
        gate_cols.append(jnp.sum(out_grad * taken_rows, axis=-1))
    gate_grad = jnp.stack(gate_cols, axis=1)
    shared_gate = jnp.dot(hidden_ffn, w_shared_in[0], preferred_element_type=jnp.float32)
    shared_up = jnp.dot(hidden_ffn, w_shared_in[1], preferred_element_type=jnp.float32)
    shared_val, shared_slope = silu_parts(shared_gate)
    shared_act = (shared_val * shared_up).astype(jnp.bfloat16)
    branch_part = jnp.dot(shared_act, w_shared_out, preferred_element_type=jnp.float32) + combined
    ffn_full = lax.psum(branch_part.astype(jnp.bfloat16), "tp").astype(jnp.float32)
    block_out = (middle + ffn_full).astype(jnp.bfloat16)
    slot_gate = (
        jnp.zeros((experts * capacity,), jnp.float32)
        .at[flat_index.reshape(-1)]
        .set(pair_gate.reshape(-1), mode="drop")
    )
    gathered_grad = jnp.take(cotangent, owner_row, axis=0, mode="fill", fill_value=0)
    slot_grad = (
        (slot_gate[:, None] * gathered_grad.astype(jnp.float32))
        .astype(jnp.bfloat16)
        .reshape(experts, capacity, model_width)
    )
    grad_arrived = lax.all_to_all(slot_grad, "ep", split_axis=0, concat_axis=0, tiled=True).reshape(
        sectioned.shape
    )
    act_grad = jnp.einsum(
        "secd,ehd->sech", grad_arrived, w_expert_out, preferred_element_type=jnp.float32
    )
    gate_val, gate_slope = silu_parts(gate_up[..., 0, :])
    up_val = gate_up[..., 1, :]
    gu_grad = jnp.stack([act_grad * up_val * gate_slope, act_grad * gate_val], axis=-2).astype(
        jnp.bfloat16
    )
    grad_expert_out = jnp.einsum(
        "sech,secd->ehd", activated, grad_arrived, preferred_element_type=jnp.float32
    )
    grad_expert_in = jnp.einsum(
        "secd,secgh->egdh", sectioned, gu_grad, preferred_element_type=jnp.float32
    )
    rows_grad = jnp.einsum(
        "secgh,egdh->secd", gu_grad, w_expert_in, preferred_element_type=jnp.float32
    ).reshape(received.shape)
    returned_grad = (
        lax.all_to_all(
            rows_grad.astype(jnp.bfloat16), "ep", split_axis=0, concat_axis=0, tiled=True
        )
        .astype(rows_grad.dtype)
        .reshape(-1, model_width)
    )
    routed_grad = jnp.zeros((tokens, model_width), jnp.float32)
    for pick_index in range(TOPK):
        routed_grad = routed_grad + jnp.take(
            returned_grad, flat_index[:, pick_index], axis=0, mode="fill", fill_value=0.0
        )
    shared_act_grad = jnp.einsum(
        "td,fd->tf", cotangent, w_shared_out, preferred_element_type=jnp.float32
    )
    shared_gate_grad = (shared_act_grad * shared_up * shared_slope).astype(jnp.bfloat16)
    shared_up_grad = (shared_act_grad * shared_val).astype(jnp.bfloat16)
    shared_out_grad = jnp.einsum(
        "tf,td->fd", shared_act, cotangent, preferred_element_type=jnp.float32
    )
    shared_in_grad = jnp.stack(
        [
            jnp.einsum(
                "td,tf->df", hidden_ffn, shared_gate_grad, preferred_element_type=jnp.float32
            ),
            jnp.einsum("td,tf->df", hidden_ffn, shared_up_grad, preferred_element_type=jnp.float32),
        ],
        axis=0,
    )
    shared_back = jnp.einsum(
        "tf,df->td", shared_gate_grad, w_shared_in[0], preferred_element_type=jnp.float32
    ) + jnp.einsum("tf,df->td", shared_up_grad, w_shared_in[1], preferred_element_type=jnp.float32)
    prob_grad = jnp.sum(route_onehot * gate_grad[:, :, None], axis=1)
    logit_grad = router_probs * (
        prob_grad - jnp.sum(router_probs * prob_grad, axis=-1, keepdims=True)
    )
    router_back = jnp.einsum(
        "te,de->td", logit_grad, w_router, precision=HIGHEST, preferred_element_type=jnp.float32
    )
    router_grad = jnp.einsum(
        "td,te->de", hidden_wide, logit_grad, precision=HIGHEST, preferred_element_type=jnp.float32
    )
    ffn_grad = lax.psum(
        (shared_back + routed_grad + router_back).astype(jnp.bfloat16), "tp"
    ).astype(jnp.float32)
    middle_grad = out_grad + norm_back(ffn_grad, gain_ffn, normed_second, inv_second)
    gain_ffn_grad = jnp.sum(
        lax.dynamic_slice_in_dim(ffn_grad * normed_second, row_start, rows_part, 0), axis=0
    )
    branch_grad = middle_grad.astype(jnp.bfloat16)
    output_w_grad = jnp.einsum(
        "tf,td->fd", attended, branch_grad, preferred_element_type=jnp.float32
    )
    attended_grad = (
        jnp.einsum("td,fd->tf", branch_grad, w_output, preferred_element_type=jnp.float32)
        .astype(jnp.bfloat16)
        .reshape(tokens, heads_here, VDIM)
    )
    scores_again = attention_scores(query_rot, key_nope, key_rope, score_scale, allowed)
    probs_again = jnp.exp(scores_again - log_total)
    values_grad = jnp.einsum(
        "hqk,qhd->khd",
        probs_again.astype(jnp.bfloat16),
        attended_grad,
        preferred_element_type=jnp.float32,
    )
    prob_part = jnp.einsum(
        "qhd,khd->hqk", attended_grad, values, preferred_element_type=jnp.float32
    )
    score_grad = (
        probs_again * (prob_part - jnp.sum(probs_again * prob_part, axis=-1, keepdims=True))
    ).astype(jnp.bfloat16)
    query_nope_grad = (
        jnp.einsum("hqk,khd->qhd", score_grad, key_nope, preferred_element_type=jnp.float32)
        * score_scale
    )
    query_rope_grad = (
        jnp.einsum("hqk,kr->qhr", score_grad, key_rope, preferred_element_type=jnp.float32)
        * score_scale
    )
    key_nope_grad = (
        jnp.einsum(
            "hqk,qhd->khd", score_grad, query_rot[..., :NOPE], preferred_element_type=jnp.float32
        )
        * score_scale
    )
    key_rope_grad = (
        jnp.einsum(
            "hqk,qhr->kr", score_grad, query_rot[..., NOPE:], preferred_element_type=jnp.float32
        )
        * score_scale
    )
    kv_grad = (
        jnp.concatenate([key_nope_grad, values_grad], axis=-1)
        .astype(jnp.bfloat16)
        .reshape(tokens, heads_here * (NOPE + VDIM))
    )
    latent_up_grad = jnp.einsum("tr,tf->rf", latent_in, kv_grad, preferred_element_type=jnp.float32)
    latent_in_grad = jnp.einsum(
        "tf,rf->tr", kv_grad, w_latent_up, preferred_element_type=jnp.float32
    )
    gain_latent_grad = jnp.sum(latent_in_grad * normed_latent, axis=0)
    latent_grad_part = jnp.concatenate(
        [
            norm_back(latent_in_grad, gain_latent, normed_latent, inv_latent),
            rotate(key_rope_grad, cosine, -sine_table),
        ],
        axis=-1,
    )
    query_grad = (
        jnp.concatenate(
            [query_nope_grad, rotate(query_rope_grad, cosine[:, None], -sine_table[:, None])],
            axis=-1,
        )
        .astype(jnp.bfloat16)
        .reshape(tokens, heads_here * qk_width)
    )
    query_w_grad = jnp.einsum(
        "td,tf->df", hidden_attn, query_grad, preferred_element_type=jnp.float32
    )
    hidden_part = jnp.einsum("tf,df->td", query_grad, w_query, preferred_element_type=jnp.float32)
    hidden_sum, latent_sum = (
        lax.psum(hidden_part.astype(jnp.bfloat16), "tp").astype(jnp.float32),
        lax.psum(latent_grad_part.astype(jnp.bfloat16), "tp").astype(jnp.float32),
    )
    latent_low = latent_sum.astype(jnp.bfloat16)
    attn_in_grad = hidden_sum + jnp.einsum(
        "tf,df->td", latent_low, w_latent, preferred_element_type=jnp.float32
    )
    latent_w_grad = jnp.einsum(
        "td,tf->df",
        lax.dynamic_slice_in_dim(hidden_attn, row_start, rows_part, 0),
        lax.dynamic_slice_in_dim(latent_low, row_start, rows_part, 0),
        preferred_element_type=jnp.float32,
    )
    gain_attn_grad = jnp.sum(
        lax.dynamic_slice_in_dim(attn_in_grad * normed_first, row_start, rows_part, 0), axis=0
    )
    grad_inputs = (
        middle_grad + norm_back(attn_in_grad, gain_attn, normed_first, inv_first)
    ).astype(jnp.bfloat16)
    grad_query, grad_latent_up, grad_output, grad_shared_in, grad_shared_out = (
        lax.psum_scatter(
            query_w_grad.astype(jnp.bfloat16), "ep", scatter_dimension=0, tiled=True
        ).astype(jnp.float32),
        lax.psum_scatter(
            latent_up_grad.astype(jnp.bfloat16), "ep", scatter_dimension=0, tiled=True
        ).astype(jnp.float32),
        lax.psum_scatter(
            output_w_grad.astype(jnp.bfloat16), "ep", scatter_dimension=1, tiled=True
        ).astype(jnp.float32),
        lax.psum_scatter(
            shared_in_grad.astype(jnp.bfloat16), "ep", scatter_dimension=1, tiled=True
        ).astype(jnp.float32),
        lax.psum_scatter(
            shared_out_grad.astype(jnp.bfloat16), "ep", scatter_dimension=1, tiled=True
        ).astype(jnp.float32),
    )
    grad_latent, grad_gain_latent, grad_gain_attn, grad_gain_ffn, grad_router = (
        lax.psum_scatter(latent_w_grad, ("ep", "tp"), scatter_dimension=0, tiled=True),
        lax.psum_scatter(gain_latent_grad, ("ep", "tp"), scatter_dimension=0, tiled=True),
        lax.psum_scatter(gain_attn_grad, ("ep", "tp"), scatter_dimension=0, tiled=True),
        lax.psum_scatter(gain_ffn_grad, ("ep", "tp"), scatter_dimension=0, tiled=True),
        lax.psum_scatter(router_grad, ("ep", "tp"), scatter_dimension=0, tiled=True),
    )
    return (
        block_out,
        grad_inputs,
        grad_gain_attn,
        grad_query,
        grad_latent,
        grad_gain_latent,
        grad_latent_up,
        grad_output,
        grad_gain_ffn,
        grad_router,
        grad_shared_in,
        grad_shared_out,
        grad_expert_in,
        grad_expert_out,
    )


def solution(mesh):
    placed = (
        P("ep", None),
        P(),
        P(None, "tp"),
        P(),
        P(),
        P(None, "tp"),
        P("tp", None),
        P(),
        P(),
        P(None, None, "tp"),
        P("tp", None),
        P("ep", None, None, "tp"),
        P("ep", "tp", None),
        P("ep", None),
        P("ep", None),
        P("ep", None),
    )
    return jax.shard_map(
        body,
        mesh=mesh,
        in_specs=placed,
        out_specs=(
            P("ep", None),
            P("ep", None),
            P(("ep", "tp")),
            P("ep", "tp"),
            P(("ep", "tp"), None),
            P(("ep", "tp")),
            P("ep", "tp"),
            P("tp", "ep"),
            P(("ep", "tp")),
            P(("ep", "tp"), None),
            P(None, "ep", "tp"),
            P("tp", "ep"),
            P("ep", None, None, "tp"),
            P("ep", "tp", None),
        ),
        check_vma=False,
    )
```

profile of v0, /device:TPU:0, one launch (start us, length us, event | category | flops | bytes accessed | tf_op | source)
XLA Modules:
  0.0 1965.0 jit_solution(2642623008473623605)
XLA Ops:
  9.8 4.3 convert_multiply_fusion.6
  25.9 3.5 fusion.127
  38.8 11.8 scatter_custom_fusion
  50.7 76.3 %all-reduce.9.cloned.1.call-done = bf16[512,2048]{1,0:T(8,128)(2,1)} async-done(((bf16[512,2048]{1,0:T(8,128)(2,1)}), bf16[512,2048]{1,0:T(8,128)(2,1)}) %all-reduce.9.cloned.1.call-update) | async-done | bytes 2097168 | tf_op jit(solution)/shard_map/psum | solution.py:147
  130.5 3.9 multiply_convert_fusion.2
  134.4 29.3 %gather_fusion = bf16[3456,2048]{1,0:T(8,128)(2,1)} fusion(bf16[512,2048]{1,0:T(8,128)(2,1)} %get-tuple-element.32, s32[4096]{0:T(1024)S(1)} %pad_clamp_fusion), kind=kCustom, calls=%fused_computation.clone | custom fusion | bytes 28325376 | tf_op jit(solution)/shard_map/jit(_take)/gather | solution.py:171
  163.8 8.0 broadcast_select_fusion
  171.8 159.9 %all_to_all.20 = bf16[8,432,2048]{2,1,0:T(8,128)(2,1)S(1)} all-to-all(bf16[8,432,2048]{2,1,0:T(8,128)(2,1)S(1)} %bitcast.268), channel_id=1, replica_groups=mesh['ep'=8,'tp'=4] {'ep'}, dimensions={0} | all-to-all | bytes 28311552 | tf_op jit(solution)/shard_map/all_to_all | solution.py:174
  331.7 5.0 copy-done.12
  336.8 18.9 fusion.35
  355.7 14.7 convolution_convert_fusion
  370.4 5.7 all-to-all-start.1
  376.1 29.4 %gather_fusion.7 = bf16[3456,2048]{1,0:T(8,128)(2,1)} fusion(bf16[512,2048]{1,0:T(8,128)(2,1)} %param.35, s32[4096]{0:T(1024)S(1)} %pad_clamp_fusion), kind=kCustom, calls=%fused_computation.2.clone | custom fusion | bytes 28325376 | tf_op jit(solution)/shard_map/jit(_take)/gather | solution.py:204
  405.8 3.3 fusion.123
  410.3 121.7 %all-to-all-done.1 = bf16[8,432,2048]{2,1,0:T(8,128)(2,1)} async-done(((bf16[8,432,2048]{2,1,0:T(8,128)(2,1)}), bf16[8,432,2048]{2,1,0:T(8,128)(2,1)}, u32[]{:S(2)}, u32[]{:S(2)}) %all-to-all-start.1) | async-done | bytes 14155808 | tf_op jit(solution)/shard_map/all_to_all | solution.py:178
  532.0 16.1 bitcast_convert_fusion.2
  548.0 14.5 gather_fusion.6
  562.5 14.5 gather_fusion.5
  577.0 14.5 gather_fusion.4
  591.5 14.4 gather_fusion.3
  605.9 14.7 gather_fusion.2
  620.6 14.5 gather_fusion.1
  635.2 10.5 fusion.29
  646.1 11.9 scatter_custom_fusion.1
  658.1 8.9 multiply_convert_fusion
  666.9 158.8 %all_to_all.21 = bf16[8,432,2048]{2,1,0:T(8,128)(2,1)S(1)} all-to-all(bf16[8,432,2048]{2,1,0:T(8,128)(2,1)S(1)} %bitcast.267), channel_id=1, replica_groups=mesh['ep'=8,'tp'=4] {'ep'}, dimensions={0} | all-to-all | bytes 28311552 | tf_op jit(solution)/shard_map/all_to_all | solution.py:210
  825.7 16.9 fusion.61
  842.6 17.2 bitcast_convert_fusion
  859.8 5.5 all-to-all-start.3
  865.9 4.3 fusion.50
  870.2 3.6 fusion.54
  877.0 3.8 fusion.52
  880.8 3.8 fusion.48
  884.7 136.5 %all-to-all-done.3 = bf16[8,432,2048]{2,1,0:T(8,128)(2,1)} async-done(((bf16[8,432,2048]{2,1,0:T(8,128)(2,1)}), bf16[8,432,2048]{2,1,0:T(8,128)(2,1)}, u32[]{:S(2)}, u32[]{:S(2)}) %all-to-all-start.3) | async-done | bytes 14155808 | tf_op jit(solution)/shard_map/all_to_all | solution.py:231
  1021.2 16.2 bitcast_convert_fusion.1
  1037.5 14.5 gather_fusion.13
  1051.9 14.5 gather_fusion.12
  1066.4 14.5 gather_fusion.11
  1080.9 14.5 gather_fusion.10
  1095.4 14.5 gather_fusion.9
  1110.0 14.5 gather_fusion.8
  1124.6 15.0 fusion.34
  1139.8 13.7 add_convert_fusion.2
  1153.5 69.9 %all-reduce.11.cloned.1.call-done = bf16[512,2048]{1,0:T(8,128)(2,1)} async-done(((bf16[512,2048]{1,0:T(8,128)(2,1)}), bf16[512,2048]{1,0:T(8,128)(2,1)}) %all-reduce.11.cloned.1.call-update) | async-done | bytes 2097168 | tf_op jit(solution)/shard_map/psum | solution.py:272
  1223.5 3.7 multiply_reduce_fusion.2
  1247.5 5.3 convolution_convert_fusion.4
  1253.1 3.6 fusion.45
  1261.5 4.9 fusion.106
  1266.4 3.3 convolution_convert_fusion.8
  1269.8 4.9 convolution_convert_fusion.5
  1274.8 5.4 convolution_convert_fusion.1
  1280.4 140.9 %all-reduce.13.cloned.1.call-done = (bf16[512,2048]{1,0:T(8,128)(2,1)}, bf16[512,2048]{1,0:T(8,128)(2,1)}, bf16[512,576]{0,1:T(8,128)(2,1)}) async-done(((bf16[512,2048]{1,0:T(8,128)(2,1)}, bf16[512,2048]{1,0:T(8,128)(2,1)}, bf16[512,576]{0,1:T(8,128)(2,1)}), (bf16[512,2048]{1,0:T(8,128)(2,1)}, bf16[512,2048]{1,0:T(8,128)(2,1)}, bf16[512,576]{0,1:T(8,128)(2,1)})) %all-reduce.13.cloned.1.call-update) | async-done | bytes 4784144 | tf_op jit(solution)/shard_map/psum | solution.py:197
  1421.4 4.2 fusion.91
  1425.6 43.9 %reduce-scatter.20.cloned.1.call-done = bf16[704,256]{1,0:T(8,128)(2,1)} async-done(((bf16[704,2048]{1,0:T(8,128)(2,1)}), bf16[704,256]{1,0:T(8,128)(2,1)}) %reduce-scatter.20.cloned.1.call-update) | async-done | bytes 360464 | tf_op jit(solution)/shard_map/reduce_scatter | solution.py:384
  1471.4 61.0 %reduce-scatter.18.cloned.1.call-done = bf16[2,256,704]{1,2,0:T(8,128)(2,1)} async-done(((bf16[2,2048,704]{1,2,0:T(8,128)(2,1)}), bf16[2,256,704]{1,2,0:T(8,128)(2,1)}) %reduce-scatter.18.cloned.1.call-update) | async-done | bytes 720912 | tf_op jit(solution)/shard_map/reduce_scatter | solution.py:381
  1534.7 135.2 %reduce-scatter.22.cloned.1.call-done = f32[64,8]{1,0:T(8,128)} async-done(((f32[2048,8]{1,0:T(8,128)}), f32[64,8]{1,0:T(8,128)}) %reduce-scatter.22.cloned.1.call-update) | async-done | bytes 2064
  1671.3 17.1 fusion.40
  1688.5 13.3 convolution_bitcast_fusion
  1707.4 43.5 %reduce-scatter.16.cloned.1.call-done = bf16[512,256]{1,0:T(8,128)(2,1)} async-done(((bf16[512,2048]{1,0:T(8,128)(2,1)}), bf16[512,256]{1,0:T(8,128)(2,1)}) %reduce-scatter.16.cloned.1.call-update) | async-done | bytes 262160 | tf_op jit(solution)/shard_map/reduce_scatter | solution.py:378
  1752.7 48.3 %reduce-scatter.10.cloned.1.call-done = bf16[256,768]{1,0:T(8,128)(2,1)} async-done(((bf16[2048,768]{1,0:T(8,128)(2,1)}), bf16[256,768]{1,0:T(8,128)(2,1)}) %reduce-scatter.10.cloned.1.call-update) | async-done | bytes 393232 | tf_op jit(solution)/shard_map/reduce_scatter | solution.py:372
  1802.9 5.7 multiply_reduce_fusion
  1812.0 40.9 %all-reduce.3 = (f32[2048]{0:T(1024)S(1)}, f32[512]{0:T(512)S(1)}, f32[2048]{0:T(1024)S(1)}) all-reduce(f32[2048]{0:T(1024)S(1)} %fusion.88, f32[512]{0:T(512)S(1)} %get-tuple-element.16, f32[2048]{0:T(1024)S(1)} %fusion.87), channel_id=2, replica_groups=mesh['ep'=8,'tp'=4] {'ep','tp'}, use_global_device_ids=true, to_apply=%region_28.31.clone | all-reduce | flops 4608 | bytes 36864
  1854.6 7.9 add_convert_fusion
  1862.5 95.4 %reduce-scatter.12.cloned.1.call-done = f32[64,576]{1,0:T(8,128)} async-done(((f32[2048,576]{1,0:T(8,128)}), f32[64,576]{1,0:T(8,128)}) %reduce-scatter.12.cloned.1.call-update) | async-done | bytes 147472 | tf_op jit(solution)/shard_map/reduce_scatter | solution.py:389
  (328 shorter events, 78.2 us)
Async XLA Ops:
  7.2 18.8 copy-start
  7.2 119.8 %all-reduce.9.cloned.1.call-start = ((), (), s32[]{:S(2)}) async-start(), calls=%async_computation.11 | async-start | bytes 4194304 | tf_op jit(solution)/shard_map/psum | solution.py:147
  7.3 8.4 copy-start.97
  16.7 13.5 copy-start.33
  16.7 13.8 copy-start.35
  16.7 13.8 copy-start.37
  37.6 92.5 %copy-start.48 = (f32[2048]{0:T(1024)S(1)}, f32[2048]{0:T(1024)}, u32[]{:S(2)}) copy-start(f32[2048]{0:T(1024)} %param.27) | copy-start | bytes 24580
  50.7 113.1 %copy-start.54 = (pred[3456]{0:T(1024)(128)(4,1)}, pred[3456]{0:T(1024)(128)(4,1)S(1)}, u32[]{:S(2)}) copy-start(pred[3456]{0:T(1024)(128)(4,1)S(1)} %compare_and_fusion) | copy-start | bytes 10372
  171.8 165.0 %copy-start.99 = (bf16[1,2,2048,352]{2,3,1,0:T(8,128)(2,1)S(1)}, bf16[1,2,2048,352]{2,3,1,0:T(8,128)(2,1)}, u32[]{:S(2)}) copy-start(bf16[1,2,2048,352]{2,3,1,0:T(8,128)(2,1)} %param.31) | copy-start | bytes 8650756
  336.8 18.9 copy-start.104
  370.4 161.6 %all-to-all-start.1 = ((bf16[8,432,2048]{2,1,0:T(8,128)(2,1)}), bf16[8,432,2048]{2,1,0:T(8,128)(2,1)}, u32[]{:S(2)}, u32[]{:S(2)}) async-start(bf16[8,432,2048]{2,1,0:T(8,128)(2,1)} %convolution_convert_fusion), calls=%async_computation.1 | async-start | bytes 28311552 | tf_op jit(solution)/shard_map/all_to_all | solution.py:178
  376.1 29.7 %copy-start.39 = (f32[2048,8]{0,1:T(8,128)S(1)}, f32[2048,8]{0,1:T(8,128)}, u32[]{:S(2)}) copy-start(f32[2048,8]{0,1:T(8,128)} %param.28) | copy-start | bytes 196612
  405.5 171.5 %copy-start.69 = (s32[1024]{0:T(1024)}, s32[1024]{0:T(1024)S(1)}, u32[]{:S(2)}) copy-start(s32[1024]{0:T(1024)S(1)} %pad_clamp_fusion.3) | copy-start | bytes 12292
  405.6 200.4 %copy-start.71 = (s32[1024]{0:T(1024)}, s32[1024]{0:T(1024)S(1)}, u32[]{:S(2)}) copy-start(s32[1024]{0:T(1024)S(1)} %pad_clamp_fusion.5) | copy-start | bytes 12292
  405.6 142.4 %copy-start.77 = (s32[1024]{0:T(1024)}, s32[1024]{0:T(1024)S(1)}, u32[]{:S(2)}) copy-start(s32[1024]{0:T(1024)S(1)} %pad_clamp_fusion.1) | copy-start | bytes 12292
  405.6 185.9 %copy-start.75 = (s32[1024]{0:T(1024)}, s32[1024]{0:T(1024)S(1)}, u32[]{:S(2)}) copy-start(s32[1024]{0:T(1024)S(1)} %pad_clamp_fusion.4) | copy-start | bytes 12292
  405.6 215.0 %copy-start.73 = (s32[1024]{0:T(1024)}, s32[1024]{0:T(1024)S(1)}, u32[]{:S(2)}) copy-start(s32[1024]{0:T(1024)S(1)} %pad_clamp_fusion.6) | copy-start | bytes 12292
  405.7 156.8 %copy-start.79 = (s32[1024]{0:T(1024)}, s32[1024]{0:T(1024)S(1)}, u32[]{:S(2)}) copy-start(s32[1024]{0:T(1024)S(1)} %pad_clamp_fusion.2) | copy-start | bytes 12292
  405.7 229.4 %copy-start.85 = (pred[512]{0:T(512)(128)(4,1)}, pred[512]{0:T(512)(128)(4,1)S(1)}, u32[]{:S(2)}) copy-start(pred[512]{0:T(512)(128)(4,1)S(1)} %get-tuple-element.83) | copy-start | bytes 1540
  405.7 229.4 %copy-start.87 = (pred[512]{0:T(512)(128)(4,1)}, pred[512]{0:T(512)(128)(4,1)S(1)}, u32[]{:S(2)}) copy-start(pred[512]{0:T(512)(128)(4,1)S(1)} %get-tuple-element.84) | copy-start | bytes 1540
  405.7 229.4 %copy-start.89 = (pred[512]{0:T(512)(128)(4,1)}, pred[512]{0:T(512)(128)(4,1)S(1)}, u32[]{:S(2)}) copy-start(pred[512]{0:T(512)(128)(4,1)S(1)} %get-tuple-element.87) | copy-start | bytes 1540
  405.7 229.4 %copy-start.91 = (pred[512]{0:T(512)(128)(4,1)}, pred[512]{0:T(512)(128)(4,1)S(1)}, u32[]{:S(2)}) copy-start(pred[512]{0:T(512)(128)(4,1)S(1)} %get-tuple-element.88) | copy-start | bytes 1540
  405.8 229.4 %copy-start.93 = (pred[512]{0:T(512)(128)(4,1)}, pred[512]{0:T(512)(128)(4,1)S(1)}, u32[]{:S(2)}) copy-start(pred[512]{0:T(512)(128)(4,1)S(1)} %get-tuple-element.85) | copy-start | bytes 1540
  405.8 229.4 %copy-start.95 = (pred[512]{0:T(512)(128)(4,1)}, pred[512]{0:T(512)(128)(4,1)S(1)}, u32[]{:S(2)}) copy-start(pred[512]{0:T(512)(128)(4,1)S(1)} %get-tuple-element.86) | copy-start | bytes 1540
  410.3 235.4 %copy-start.41 = (f32[512,8]{0,1:T(8,128)}, f32[512,8]{0,1:T(8,128)S(1)}, u32[]{:S(2)}) copy-start(f32[512,8]{0,1:T(8,128)S(1)} %fusion.100) | copy-start | bytes 49156
  635.2 10.6 copy-start.53
  635.2 22.9 %copy-start.55 = (pred[3456]{0:T(1024)(128)(4,1)S(1)}, pred[3456]{0:T(1024)(128)(4,1)}, u32[]{:S(2)}) copy-start(pred[3456]{0:T(1024)(128)(4,1)} %copy-done.54) | copy-start | bytes 10372
  645.8 21.2 %copy-start.46 = (f32[512,6]{0,1:T(8,128)}, f32[512,6]{0,1:T(8,128)S(1)}, u32[]{:S(2)}) copy-start(f32[512,6]{0,1:T(8,128)S(1)} %get-tuple-element.25) | copy-start | bytes 36868
  825.7 16.9 copy-start.13
  859.8 161.4 %all-to-all-start.3 = ((bf16[8,432,2048]{2,1,0:T(8,128)(2,1)}), bf16[8,432,2048]{2,1,0:T(8,128)(2,1)}, u32[]{:S(2)}, u32[]{:S(2)}) async-start(bf16[8,432,2048]{2,1,0:T(8,128)(2,1)} %bitcast_convert_fusion), calls=%async_computation.3 | async-start | bytes 28311552 | tf_op jit(solution)/shard_map/all_to_all | solution.py:231
  865.4 358.1 %all-reduce.11.cloned.1.call-start = ((), (), s32[]{:S(2)}) async-start(), calls=%async_computation.12 | async-start | bytes 4194304 | tf_op jit(solution)/shard_map/psum | solution.py:272
  870.2 6.8 slice-start
  877.0 7.7 copy-start.30
  877.0 7.7 copy-start.32
  884.7 152.8 %copy-start.78 = (s32[1024]{0:T(1024)S(1)}, s32[1024]{0:T(1024)}, u32[]{:S(2)}) copy-start(s32[1024]{0:T(1024)} %copy-done.77) | copy-start | bytes 12292
  1037.5 14.5 copy-start.80
  1051.9 14.5 copy-start.70
  1066.4 14.5 copy-start.76
  1080.9 14.5 copy-start.72
  1095.4 14.5 copy-start.74
  1109.9 14.6 copy-start.40
  1109.9 14.6 copy-start.42
  1109.9 14.6 copy-start.86
  1110.0 14.6 copy-start.88
  1110.0 14.6 copy-start.90
  1110.0 14.6 copy-start.92
  1110.0 14.6 copy-start.94
  1110.0 14.6 copy-start.96
  1124.6 15.1 copy-start.51
  1124.6 15.1 copy-start.57
  1124.6 15.1 copy-start.47
  1139.6 281.7 %all-reduce.13.cloned.1.call-start = ((), (), s32[]{:S(2)}) async-start(), calls=%async_computation.20 | async-start | bytes 9568256 | tf_op jit(solution)/shard_map/psum | solution.py:197
  1139.8 83.7 %copy-start.49 = (f32[2048]{0:T(1024)S(1)}, f32[2048]{0:T(1024)}, u32[]{:S(2)}) copy-start(f32[2048]{0:T(1024)} %param.27) | copy-start | bytes 24580
  1153.5 73.6 %copy-start.62 = (f32[512]{0:T(512)S(1)}, f32[512]{0:T(512)}, u32[]{:S(2)}) copy-start(f32[512]{0:T(512)} %copy-done.61) | copy-start | bytes 6148
  1247.5 222.0 %reduce-scatter.20.cloned.1.call-start = ((), (), s32[]{:S(2)}) async-start(), calls=%async_computation.18 | async-start | bytes 3244032 | tf_op jit(solution)/shard_map/reduce_scatter | solution.py:384
  1252.8 279.6 %reduce-scatter.18.cloned.1.call-start = ((), (), s32[]{:S(2)}) async-start(), calls=%async_computation.17 | async-start | bytes 6488064 | tf_op jit(solution)/shard_map/reduce_scatter | solution.py:381
  1261.4 408.5 %reduce-scatter.22.cloned.1.call-start = ((), (), s32[]{:S(2)}) async-start(), calls=%async_computation.19 | async-start | bytes 1081344
  1266.4 439.4 %reduce-scatter.14.cloned.1.call-start = ((), (), s32[]{:S(2)}) async-start(), calls=%async_computation.15 | async-start | bytes 1179648 | tf_op jit(solution)/shard_map/reduce_scatter | solution.py:375
  1269.7 481.2 %reduce-scatter.16.cloned.1.call-start = ((), (), s32[]{:S(2)}) async-start(), calls=%async_computation.16 | async-start | bytes 2359296 | tf_op jit(solution)/shard_map/reduce_scatter | solution.py:378
  1274.7 526.2 %reduce-scatter.10.cloned.1.call-start = ((), (), s32[]{:S(2)}) async-start(), calls=%async_computation.13 | async-start | bytes 3538944 | tf_op jit(solution)/shard_map/reduce_scatter | solution.py:372
  1280.2 677.7 %reduce-scatter.12.cloned.1.call-start = ((), (), s32[]{:S(2)}) async-start(), calls=%async_computation.14 | async-start | bytes 5406720 | tf_op jit(solution)/shard_map/reduce_scatter | solution.py:389
  1688.4 13.3 copy-start.9
  1701.7 101.2 %copy-start.60 = (f32[2048]{0:T(1024)S(1)}, f32[2048]{0:T(1024)}, u32[]{:S(2)}) copy-start(f32[2048]{0:T(1024)} %param.21) | copy-start | bytes 24580
  1701.7 101.2 %copy-start.68 = (f32[512]{0:T(512)S(1)}, f32[512]{0:T(512)}, u32[]{:S(2)}) copy-start(f32[512]{0:T(512)} %copy-done.67) | copy-start | bytes 6148
  (58 other events, 149.9 us)
Sparse Core Ops, SparseCore 0:
  37.8 89.2 all-reduce.8
  1139.8 83.6 all-reduce.10
  1247.6 173.7 all-reduce.12
  1425.5 43.8 reduce-scatter.19
  1473.3 59.0 reduce-scatter.17
  1534.6 135.2 reduce-scatter.21
  1673.1 32.6 reduce-scatter.13
  1709.7 41.1 reduce-scatter.15
  1754.7 46.2 reduce-scatter.9
  1803.7 154.2 reduce-scatter.11
where the time goes:
time: 1970 us; the launch traced here: 1960 us
  waiting for transfers between devices  975 us (49%)
  blocking collectives  360 us (18%)
  local copies, waits for them, and re-layouts  284 us (14%)
  matrix products  210 us (11%)
  other arithmetic  108 us (5%)
    all_to_all x1, blocking collectives, body(): lax.all_to_all(outgoing, 'ep', split_axis=0, concat_axis=0, tiled=True)  160 us
    all_to_all x1, blocking collectives, body(): lax.all_to_all(slot_grad, 'ep', split_axis=0, concat_axis=0, tiled=True)  159 us
    psum x1, waiting for transfers between devices, body(): lax.psum(branch_part.astype(jnp.bfloat16), 'tp').astype(jnp.float32)  141 us
    all_to_all x1, waiting for transfers between devices, body(): lax.all_to_all(rows_grad.astype(jnp.bfloat16), 'ep', split_axis=0, concat...  137 us
    unnamed x11, waiting for transfers between devices  135 us
    all_to_all x1, waiting for transfers between devices, body(): lax.all_to_all(produced.astype(jnp.bfloat16), 'ep', split_axis=0, concat_...  122 us
    reduce_scatter x1, waiting for transfers between devices, body(): lax.psum_scatter(latent_w_grad, ('ep', 'tp'), scatter_dimension=0, tiled=...  95.4 us
    gather x6, local copies, waits for them, and re-layouts, body(): jnp.take(back_rows, flat_index[:, pick_index], axis=0, mode='fill', fill_...  87.1 us
  transfers between devices with their start and end apart: 12, of which 12 were waited for; matrix products, arithmetic and copies ran while one was open for 9% of the time, Pallas kernels for 0%

commit v1 on v0

--- a/solution.py
+++ b/solution.py
@@ -68,7 +68,7 @@
     return (sectioned, gate_up, activated, produced.reshape(received.shape))
 
 
-def body(
+def body_slots(
     inputs,
     gain_attn,
     w_query,
@@ -410,7 +410,308 @@
     )
 
 
+def padded_hidden(routed, shared):
+    return -(-(routed + shared + 24) // 128) * 128
+
+
+def split_wide(values):
+    high = values.astype(jnp.bfloat16)
+    rest = values - high.astype(jnp.float32)
+    mid = rest.astype(jnp.bfloat16)
+    low = (rest - mid.astype(jnp.float32)).astype(jnp.bfloat16)
+    return (high, mid, low)
+
+
+def body_dense(
+    inputs,
+    gain_attn,
+    w_query,
+    w_latent,
+    gain_latent,
+    w_latent_up,
+    w_output,
+    gain_ffn,
+    w_router,
+    w_shared_in,
+    w_shared_out,
+    w_expert_in,
+    w_expert_out,
+    expert_ids,
+    slot_ids,
+    cotangent,
+):
+    f32, bf16 = jnp.float32, jnp.bfloat16
+    tokens, model_width = inputs.shape
+    ep_count, tp_count = lax.axis_size("ep"), lax.axis_size("tp")
+    ep_index, tp_index = lax.axis_index("ep"), lax.axis_index("tp")
+    heads_here = w_output.shape[0] // VDIM
+    experts = w_router.shape[1]
+    capacity = (9 * tokens * TOPK + 64 * experts - 1) // (64 * experts) * 8
+    qk_width = NOPE + ROPE
+    score_scale = qk_width ** (-0.5)
+    rows_part = tokens // tp_count
+    row_start = tp_index * rows_part
+    every = ("ep", "tp")
+
+    expert_range = jnp.arange(experts, dtype=jnp.int32)
+    kept = jnp.any(
+        (expert_ids[:, :, None] == expert_range) & (slot_ids < capacity)[:, :, None], axis=1
+    ).astype(f32)
+    kept_here = lax.all_to_all(kept, "ep", split_axis=1, concat_axis=0, tiled=True)
+    cot_all = lax.all_gather(cotangent, "ep", tiled=True)
+
+    routed = w_expert_in.shape[3]
+    shared = w_shared_in.shape[2] // ep_count
+    hidden = padded_hidden(routed, shared)
+    shared_start = ep_index * shared
+    shared_in = lax.dynamic_slice_in_dim(w_shared_in, shared_start, shared, 2)
+    shared_out = lax.dynamic_slice_in_dim(w_shared_out, shared_start, shared, 0)
+    router_parts = jnp.concatenate(split_wide(w_router), axis=1)
+    fill = hidden - routed - shared
+    w_in = jnp.concatenate(
+        [
+            w_expert_in[0, 0],
+            shared_in[0],
+            jnp.pad(router_parts, ((0, 0), (0, fill - router_parts.shape[1]))),
+            w_expert_in[0, 1],
+            shared_in[1],
+            jnp.zeros((model_width, fill), bf16),
+        ],
+        axis=1,
+    )
+    w_out = jnp.concatenate(
+        [w_expert_out[0], shared_out, jnp.zeros((fill, model_width), bf16)], axis=0
+    )
+
+    resid = inputs.astype(f32)
+    inv_first = lax.rsqrt(jnp.mean(resid * resid, axis=-1, keepdims=True) + EPSILON)
+    normed_first = resid * inv_first
+    hidden_attn = (normed_first * gain_attn).astype(bf16)
+    cosine, sine_table = angles(tokens, ROPE)
+    query_raw = jnp.dot(hidden_attn, w_query, preferred_element_type=f32).reshape(
+        tokens, heads_here, qk_width
+    )
+    query_rot = jnp.concatenate(
+        [
+            query_raw[..., :NOPE],
+            rotate(query_raw[..., NOPE:], cosine[:, None], sine_table[:, None]),
+        ],
+        axis=-1,
+    ).astype(bf16)
+    latent = jnp.dot(hidden_attn, w_latent, preferred_element_type=f32)
+    compressed = latent[:, :KV_RANK]
+    inv_latent = lax.rsqrt(jnp.mean(compressed * compressed, axis=-1, keepdims=True) + EPSILON)
+    normed_latent = compressed * inv_latent
+    latent_in = (normed_latent * gain_latent).astype(bf16)
+    key_rope = rotate(latent[:, KV_RANK:], cosine, sine_table).astype(bf16)
+    key_value = (
+        jnp.dot(latent_in, w_latent_up, preferred_element_type=f32)
+        .astype(bf16)
+        .reshape(tokens, heads_here, NOPE + VDIM)
+    )
+    key_nope = key_value[..., :NOPE]
+    values = key_value[..., NOPE:]
+    block_ids = jnp.arange(tokens) // BLOCK
+    allowed = block_ids[None, :] <= block_ids[:, None]
+    scores = attention_scores(query_rot, key_nope, key_rope, score_scale, allowed)
+    row_peak = jnp.max(scores, axis=-1, keepdims=True)
+    exp_scores = jnp.exp(scores - row_peak)
+    totals = jnp.sum(exp_scores, axis=-1, keepdims=True)
+    attn_probs = exp_scores / totals
+    log_total = row_peak + jnp.log(totals)
+    attended = (
+        jnp.einsum("hqk,khd->qhd", attn_probs.astype(bf16), values, preferred_element_type=f32)
+        .astype(bf16)
+        .reshape(tokens, heads_here * VDIM)
+    )
+    attn_part = jnp.dot(attended, w_output, preferred_element_type=f32).astype(bf16)
+
+    attn_rows = lax.psum_scatter(attn_part, "tp", scatter_dimension=0, tiled=True).astype(f32)
+    resid_rows = lax.dynamic_slice_in_dim(resid, row_start, rows_part, 0)
+    cot_rows = lax.dynamic_slice_in_dim(cotangent, row_start, rows_part, 0).astype(f32)
+    middle = resid_rows + attn_rows
+    inv_second = lax.rsqrt(jnp.mean(middle * middle, axis=-1, keepdims=True) + EPSILON)
+    normed_second = middle * inv_second
+    hidden_rows = (normed_second * gain_ffn).astype(bf16)
+    hidden_all = lax.all_gather(hidden_rows, every, tiled=True)
+
+    gate_up = jnp.dot(hidden_all, w_in, preferred_element_type=f32)
+    gate_val, up_val = gate_up[:, :hidden], gate_up[:, hidden:]
+    base = routed + shared
+    logits = (
+        gate_val[:, base : base + experts]
+        + gate_val[:, base + experts : base + 2 * experts]
+        + gate_val[:, base + 2 * experts : base + 3 * experts]
+    )
+    exp_logits = jnp.exp(logits - jnp.max(logits, axis=-1, keepdims=True))
+    router_probs = exp_logits / jnp.sum(exp_logits, axis=-1, keepdims=True)
+    here = (expert_range == ep_index).astype(f32)[None]
+    prob_here = jnp.sum(router_probs * here, axis=-1, keepdims=True)
+    unit_index = jnp.arange(hidden)[None]
+    is_routed = unit_index < routed
+    unit_gate = jnp.where(is_routed, prob_here * kept_here, 1.0)
+    silu_val, silu_slope = silu_parts(gate_val)
+    activated = silu_val * up_val
+    gated = (activated * unit_gate).astype(bf16)
+    out_part = jnp.dot(gated, w_out, preferred_element_type=f32).astype(bf16)
+    act_grad = jnp.einsum("td,fd->tf", cot_all, w_out, preferred_element_type=f32)
+    pair_grad = (
+        jnp.sum(jnp.where(is_routed, activated * act_grad, 0.0), axis=-1, keepdims=True) * kept_here
+    )
+    logit_grad = pair_grad * prob_here * (here - router_probs)
+    act_grad = act_grad * unit_gate
+    gate_grad = (act_grad * up_val * silu_slope).astype(bf16)
+    up_grad = (act_grad * silu_val).astype(bf16)
+    rows_grad = (
+        jnp.einsum("tf,df->td", gate_grad, w_in[:, :hidden], preferred_element_type=f32)
+        + jnp.einsum("tf,df->td", up_grad, w_in[:, hidden:], preferred_element_type=f32)
+        + jnp.einsum(
+            "te,de->td", logit_grad, w_router, precision=HIGHEST, preferred_element_type=f32
+        )
+    ).astype(bf16)
+    out_grad_w = jnp.einsum("tf,td->fd", gated, cot_all, preferred_element_type=f32)
+    in_grad_gate = jnp.einsum("td,tf->df", hidden_all, gate_grad, preferred_element_type=f32)
+    in_grad_up = jnp.einsum("td,tf->df", hidden_all, up_grad, preferred_element_type=f32)
+    router_grad = jnp.einsum(
+        "td,te->de",
+        hidden_all.astype(f32),
+        logit_grad,
+        precision=HIGHEST,
+        preferred_element_type=f32,
+    )
+    grad_expert_in = jnp.stack([in_grad_gate[:, :routed], in_grad_up[:, :routed]])[None]
+    grad_expert_out = out_grad_w[None, :routed]
+    shared_in_part = jnp.stack([in_grad_gate[:, routed:base], in_grad_up[:, routed:base]])
+    grad_shared_in = lax.all_to_all(
+        shared_in_part.astype(bf16), "ep", split_axis=1, concat_axis=2, tiled=True
+    ).astype(f32)
+    grad_shared_out = lax.all_to_all(
+        out_grad_w[routed:base].astype(bf16), "ep", split_axis=1, concat_axis=0, tiled=True
+    ).astype(f32)
+
+    def sum_rows(part):
+        plane = lax.psum_scatter(part, "ep", scatter_dimension=0, tiled=True)
+        return lax.psum_scatter(plane, "tp", scatter_dimension=0, tiled=True).astype(f32)
+
+    ffn_grad = sum_rows(rows_grad)
+    ffn_rows = sum_rows(out_part)
+    block_out = lax.all_gather((middle + ffn_rows).astype(bf16), "tp", tiled=True)
+    middle_grad = cot_rows + norm_back(ffn_grad, gain_ffn, normed_second, inv_second)
+    gain_ffn_grad = jnp.sum(ffn_grad * normed_second, axis=0)
+    branch_grad = lax.all_gather(middle_grad.astype(bf16), "tp", tiled=True)
+
+    output_w_grad = jnp.einsum("tf,td->fd", attended, branch_grad, preferred_element_type=f32)
+    attended_grad = (
+        jnp.einsum("td,fd->tf", branch_grad, w_output, preferred_element_type=f32)
+        .astype(bf16)
+        .reshape(tokens, heads_here, VDIM)
+    )
+    scores_again = attention_scores(query_rot, key_nope, key_rope, score_scale, allowed)
+    probs_again = jnp.exp(scores_again - log_total)
+    values_grad = jnp.einsum(
+        "hqk,qhd->khd", probs_again.astype(bf16), attended_grad, preferred_element_type=f32
+    )
+    prob_part = jnp.einsum("qhd,khd->hqk", attended_grad, values, preferred_element_type=f32)
+    score_grad = (
+        probs_again * (prob_part - jnp.sum(probs_again * prob_part, axis=-1, keepdims=True))
+    ).astype(bf16)
+    query_nope_grad = (
+        jnp.einsum("hqk,khd->qhd", score_grad, key_nope, preferred_element_type=f32) * score_scale
+    )
+    query_rope_grad = (
+        jnp.einsum("hqk,kr->qhr", score_grad, key_rope, preferred_element_type=f32) * score_scale
+    )
+    key_nope_grad = (
+        jnp.einsum("hqk,qhd->khd", score_grad, query_rot[..., :NOPE], preferred_element_type=f32)
+        * score_scale
+    )
+    key_rope_grad = (
+        jnp.einsum("hqk,qhr->kr", score_grad, query_rot[..., NOPE:], preferred_element_type=f32)
+        * score_scale
+    )
+    kv_grad = (
+        jnp.concatenate([key_nope_grad, values_grad], axis=-1)
+        .astype(bf16)
+        .reshape(tokens, heads_here * (NOPE + VDIM))
+    )
+    latent_up_grad = jnp.einsum("tr,tf->rf", latent_in, kv_grad, preferred_element_type=f32)
+    latent_in_grad = jnp.einsum("tf,rf->tr", kv_grad, w_latent_up, preferred_element_type=f32)
+    gain_latent_grad = jnp.sum(latent_in_grad * normed_latent, axis=0)
+    latent_grad_part = jnp.concatenate(
+        [
+            norm_back(latent_in_grad, gain_latent, normed_latent, inv_latent),
+            rotate(key_rope_grad, cosine, -sine_table),
+        ],
+        axis=-1,
+    ).astype(bf16)
+    query_grad = (
+        jnp.concatenate(
+            [query_nope_grad, rotate(query_rope_grad, cosine[:, None], -sine_table[:, None])],
+            axis=-1,
+        )
+        .astype(bf16)
+        .reshape(tokens, heads_here * qk_width)
+    )
+    query_w_grad = jnp.einsum("td,tf->df", hidden_attn, query_grad, preferred_element_type=f32)
+    hidden_part = (
+        jnp.einsum("tf,df->td", query_grad, w_query, preferred_element_type=f32)
+        + jnp.einsum("tf,df->td", latent_grad_part, w_latent, preferred_element_type=f32)
+    ).astype(bf16)
+    attn_in_grad = lax.psum_scatter(hidden_part, "tp", scatter_dimension=0, tiled=True).astype(f32)
+    latent_w_grad = jnp.einsum(
+        "td,tf->df", hidden_attn, latent_grad_part, preferred_element_type=f32
+    )
+    normed_rows = lax.dynamic_slice_in_dim(normed_first, row_start, rows_part, 0)
+    inv_rows = lax.dynamic_slice_in_dim(inv_first, row_start, rows_part, 0)
+    gain_attn_grad = jnp.sum(attn_in_grad * normed_rows, axis=0)
+    grad_inputs = lax.all_gather(
+        (middle_grad + norm_back(attn_in_grad, gain_attn, normed_rows, inv_rows)).astype(bf16),
+        "tp",
+        tiled=True,
+    )
+    grad_query, grad_latent_up, grad_output = (
+        lax.psum_scatter(
+            query_w_grad.astype(bf16), "ep", scatter_dimension=0, tiled=True
+        ).astype(f32),
+        lax.psum_scatter(
+            latent_up_grad.astype(bf16), "ep", scatter_dimension=0, tiled=True
+        ).astype(f32),
+        lax.psum_scatter(
+            output_w_grad.astype(bf16), "ep", scatter_dimension=1, tiled=True
+        ).astype(f32),
+    )
+
+    def sum_all(part):
+        plane = lax.psum_scatter(part, "ep", scatter_dimension=0, tiled=True)
+        return lax.psum_scatter(plane, "tp", scatter_dimension=0, tiled=True)
+
+    grad_latent, grad_gain_latent, grad_gain_attn, grad_gain_ffn, grad_router = (
+        sum_all(latent_w_grad),
+        sum_all(gain_latent_grad),
+        sum_all(gain_attn_grad),
+        sum_all(gain_ffn_grad),
+        sum_all(router_grad),
+    )
+    return (
+        block_out,
+        grad_inputs,
+        grad_gain_attn,
+        grad_query,
+        grad_latent,
+        grad_gain_latent,
+        grad_latent_up,
+        grad_output,
+        grad_gain_ffn,
+        grad_router,
+        grad_shared_in,
+        grad_shared_out,
+        grad_expert_in,
+        grad_expert_out,
+    )
+
+
 def solution(mesh):
+    body = body_dense if mesh.shape["ep"] == 8 else body_slots
     placed = (
         P("ep", None),
         P(),

time: 1970 us -> 1200 us (0.61)
  blocking collectives: 360 us -> 34.7 us
  local copies, waits for them, and re-layouts: 284 us -> 60.6 us
  waiting for transfers between devices: 975 us -> 784 us
  other arithmetic: 108 us -> 44.8 us
  matrix products: 210 us -> 236 us
    all_to_all x2 -> x0, blocking collectives: 319 us -> none  [the longest x1 160 us: body(): lax.all_to_all(outgoing, 'ep', split_axis=0, concat_axis=0, tiled=True)]
    psum x3 -> x0, waiting for transfers between devices: 287 us -> none  [the longest x1 141 us: body(): lax.psum(branch_part.astype(jnp.bfloat16), 'tp').astype(jnp.float32)]
    all_gather x0 -> x5, waiting for transfers between devices: none -> 268 us  [the longest x1 95.6 us: body_dense(): hidden_all = lax.all_gather(hidden_rows, every, tiled=True)]
    all_to_all x2 -> x3, waiting for transfers between devices: 258 us -> 0.01 us  [the longest x1 0.01 us: body_dense(): lax.all_to_all(kept, 'ep', split_axis=1, concat_axis=0, tiled=True)]
    gather x14 -> x0, local copies, waits for them, and re-layouts: 233 us -> none  [the longest x6 87.1 us: body(): jnp.take(back_rows, flat_index[:, pick_index], axis=0, mode='fill', fill_...]
    reduce_scatter x6 -> x11, waiting for transfers between devices: 294 us -> 483 us  [the longest x2 216 us: sum_rows(): plane = lax.psum_scatter(part, 'ep', scatter_dimension=0, tiled=True)]
    unnamed x11 -> x20, waiting for transfers between devices: 135 us -> 32.2 us
    reshape x2 -> x0, other arithmetic: 32.3 us -> none  [the longest x1 16.2 us: body(): returned_grad = lax.all_to_all(rows_grad.astype(jnp.bfloat16), 'ep', spli...]
  transfers between devices with their start and end apart: 12 -> 21, of which waited for: 12 -> 18; matrix products, arithmetic and copies ran while one was open for 9% -> 16% of each run, Pallas kernels for 0% -> 0%
where the time goes in v1:
time: 1200 us; the launch traced here: 1190 us
  waiting for transfers between devices  784 us (65%)
  matrix products  236 us (20%)
  local copies, waits for them, and re-layouts  60.6 us (5%)
  other arithmetic  44.8 us (4%)
  blocking collectives  34.7 us (3%)
  between operations  18.1 us (2%)
  starting transfers between devices  13.4 us (1%)
    reduce_scatter x2, waiting for transfers between devices, sum_rows(): plane = lax.psum_scatter(part, 'ep', scatter_dimension=0, tiled=True)  216 us
    all_gather x1, waiting for transfers between devices, body_dense(): hidden_all = lax.all_gather(hidden_rows, every, tiled=True)  95.6 us
    reduce_scatter x2, waiting for transfers between devices, sum_rows(): lax.psum_scatter(plane, 'tp', scatter_dimension=0, tiled=True).astype(f32)  89.2 us
    all_gather x1, waiting for transfers between devices, body_dense(): cot_all = lax.all_gather(cotangent, 'ep', tiled=True)  62.6 us
    reduce_scatter x2, waiting for transfers between devices, sum_all(): plane = lax.psum_scatter(part, 'ep', scatter_dimension=0, tiled=True)  48.2 us
    all_gather x1, waiting for transfers between devices, body_dense(): lax.all_gather((middle + ffn_rows).astype(bf16), 'tp', tiled=True)  46.2 us
    all_gather x1, waiting for transfers between devices, body_dense(): lax.all_gather((middle_grad + norm_back(attn_in_grad, gain_attn, normed_r...  45.5 us
    reduce_scatter x1, waiting for transfers between devices, body_dense(): lax.psum_scatter(output_w_grad.astype(bf16), 'ep', scatter_dimension=1, t...  43.7 us
  transfers between devices with their start and end apart: 21, of which 18 were waited for; matrix products, arithmetic and copies ran while one was open for 16% of the time, Pallas kernels for 0%

profile of v1, /device:TPU:0, one launch (start us, length us, event | category | flops | bytes accessed | tf_op | source)
XLA Modules:
  0.0 1191.6 jit_solution(17020822397317504142)
XLA Ops:
  7.3 2.2 multiply_reduce_fusion.1
  9.8 3.9 fusion.93
  16.7 2.6 reshape.277
  19.3 2.5 fusion.95
  21.8 2.1 copy.141
  23.9 3.6 fusion.92
  33.1 2.6 convolution_convert_fusion.3
  35.8 4.1 convert_element_type.170
  39.9 42.6 %reduce-scatter.18.cloned.1.call-done = bf16[128,2048]{1,0:T(8,128)(2,1)} async-done(((bf16[512,2048]{1,0:T(8,128)(2,1)}), bf16[128,2048]{1,0:T(8,128)(2,1)}) %reduce-scatter.18.cloned.1.call-update) | async-done | bytes 524304 | tf_op jit(solution)/shard_map/reduce_scatter | solution.py:529
  87.5 3.7 all-to-all-start
  91.8 2.8 constant_dynamic-update-slice_fusion.4
  94.6 2.0 constant_dynamic-update-slice_fusion.3
  98.8 1.9 constant_dynamic-update-slice_fusion
  103.2 1.9 slice_bitcast_fusion.3
  105.1 95.6 %all-gather.6.cloned.1.call-done = bf16[4096,2048]{1,0:T(8,128)(2,1)} async-done(((bf16[128,2048]{1,0:T(8,128)(2,1)}), bf16[4096,2048]{1,0:T(8,128)(2,1)}) %all-gather.6.cloned.1.call-update) | async-done | bytes 16777232 | tf_op jit(solution)/shard_map/all_gather | solution.py:536
  200.7 21.6 %fusion.98 = f32[4096,1024]{0,1:T(8,128)S(1)} fusion(bf16[4096,2048]{1,0:T(8,128)(2,1)} %all-gather.6.cloned.1.call-done, bf16[2048,1024]{0,1:T(8,128)(2,1)} %broadcast_dynamic-update-slice_fusion), kind=kOutput, calls=%fused_computation.198 | convolution fusion | flops 17179869184 | bytes 37748736 | tf_op jit(solution)/shard_map/dot_general | solution.py:538
  222.4 5.6 copy-done.46
  228.2 62.6 %all-gather.10.cloned.1.call-done = bf16[4096,2048]{1,0:T(8,128)(2,1)} async-done(((bf16[512,2048]{1,0:T(8,128)(2,1)}), bf16[4096,2048]{1,0:T(8,128)(2,1)}) %all-gather.10.cloned.1.call-update) | async-done | bytes 16777232 | tf_op jit(solution)/shard_map/all_gather | solution.py:461
  290.8 22.3 %multiply_convert_fusion = (bf16[4096,512]{0,1:T(8,128)(2,1)}, bf16[4096,512]{0,1:T(8,128)(2,1)}, f32[4096]{0:T(1024)S(1)}, bf16[4096,512]{0,1:T(8,128)(2,1)}) fusion(f32[4096]{0:T(1024)S(1)} %mul.530, pred[512]{0:T(512)(128)(4,1)S(1)} %iota_compare_fusion.2, f32[4096,1024]{0,1:T(8,128)} %copy-done.46, bf16[4096,2048]{1,0:T(8,128)(2,1)} %all-gather.10.cloned.1.call-done, ...), kind=kOutput, calls=%fused_computation.8 | convolution fusion | flops 8640262144 | bytes 47973888 | tf_op jit(solution)/shard_map/td,fd->tf/dot_general | solution.py:557
  313.1 30.7 %fusion.66 = f32[4096,2048]{1,0:T(8,128)} fusion(f32[2048,8]{0,1:T(8,128)S(1)} %copy-done.33, f32[4096]{0:T(1024)S(1)} %multiply_multiply_fusion, f32[8]{0:T(128)S(1)} %compare_convert_fusion, f32[4096,8]{0,1:T(8,128)S(1)} %get-tuple-element.97, f32[4096]{0:T(1024)S(1)} %fusion.64, f32[4096]{0:T(1024)S(1)} %get-tuple-element.96), kind=kOutput, calls=%fused_computation.136 | convolution fusion | flops 805437440 | bytes 33800224 | tf_op jit(solution)/shard_map/te,de->td/dot_general | solution.py:568
  343.9 15.5 %fusion.10 = f32[4096,2048]{1,0:T(8,128)} fusion(bf16[4096,512]{0,1:T(8,128)(2,1)S(1)} %copy-done.60, bf16[2048,72]{0,1:T(8,128)(2,1)S(1)} %copy-done.32, bf16[2048,88]{0,1:T(8,128)(2,1)S(1)} %copy-done.27, bf16[2048,352]{0,1:T(8,128)(2,1)S(1)} %copy-done.18), kind=kOutput, calls=%fused_computation.35 | convolution fusion | flops 8596226048 | bytes 39845888 | tf_op jit(solution)/shard_map/tf,df->td/dot_general | solution.py:566
  360.1 31.4 %add_convert_fusion = bf16[4096,2048]{1,0:T(8,128)(2,1)} fusion(f32[4096,2048]{1,0:T(8,128)} %fusion.66, f32[4096,2048]{1,0:T(8,128)} %fusion.10, bf16[4096,512]{0,1:T(8,128)(2,1)} %get-tuple-element.104, bf16[2048,72]{0,1:T(8,128)(2,1)} %broadcast.219, bf16[2048,88]{0,1:T(8,128)(2,1)} %get-tuple-element.99, bf16[2048,352]{0,1:T(8,128)(2,1)} %get-tuple-element.108), kind=kOutput, calls=%fused_computation | convolution fusion | flops 8621391872 | bytes 90177536 | tf_op jit(solution)/shard_map/tf,df->td/dot_general | solution.py:567
  391.6 116.1 %reduce-scatter.24.cloned.1.call-done = bf16[512,2048]{1,0:T(8,128)(2,1)} async-done(((bf16[4096,2048]{1,0:T(8,128)(2,1)}), bf16[512,2048]{1,0:T(8,128)(2,1)}) %reduce-scatter.24.cloned.1.call-update) | async-done | bytes 2097168 | tf_op jit(solution)/shard_map/reduce_scatter | solution.py:593
  507.8 46.1 %reduce-scatter.26.cloned.1.call-done = bf16[128,2048]{1,0:T(8,128)(2,1)} async-done(((bf16[512,2048]{1,0:T(8,128)(2,1)}), bf16[128,2048]{1,0:T(8,128)(2,1)}) %reduce-scatter.26.cloned.1.call-update) | async-done | bytes 524304 | tf_op jit(solution)/shard_map/reduce_scatter | solution.py:594
  555.6 2.7 fusion.91
  558.3 15.1 %convolution_convert_fusion = bf16[4096,2048]{1,0:T(8,128)(2,1)} fusion(bf16[4096,512]{0,1:T(8,128)(2,1)} %get-tuple-element.107, bf16[88,2048]{1,0:T(8,128)(2,1)} %constant_dynamic-slice_fusion, bf16[352,2048]{1,0:T(8,128)(2,1)} %bitcast.144, bf16[512]{0:T(512)(128)(2,1)S(1)} %pad.25.clone), kind=kOutput, calls=%fused_computation.1 | convolution fusion | flops 8604614656 | bytes 22774784 | tf_op jit(solution)/shard_map/dot_general | solution.py:556
  574.2 10.8 fusion.65
  585.5 18.2 %all-gather.12.cloned.1.call-done = bf16[512,2048]{1,0:T(8,128)(2,1)} async-done(((bf16[128,2048]{1,0:T(8,128)(2,1)}), bf16[512,2048]{1,0:T(8,128)(2,1)}) %all-gather.12.cloned.1.call-update) | async-done | bytes 2097168 | tf_op jit(solution)/shard_map/all_gather | solution.py:601
  603.7 3.6 convolution_convert_fusion.6
  618.8 3.3 add_convert_fusion.1
  622.2 99.8 %reduce-scatter.20.cloned.1.call-done = bf16[512,2048]{1,0:T(8,128)(2,1)} async-done(((bf16[4096,2048]{1,0:T(8,128)(2,1)}), bf16[512,2048]{1,0:T(8,128)(2,1)}) %reduce-scatter.20.cloned.1.call-update) | async-done | bytes 2097168 | tf_op jit(solution)/shard_map/reduce_scatter | solution.py:593
  722.1 5.5 fusion.62
  727.6 30.6 %reduce-scatter.38.cloned.1.call-done = f32[256,8]{0,1:T(8,128)} async-done(((f32[2048,8]{0,1:T(8,128)}), f32[256,8]{0,1:T(8,128)}) %reduce-scatter.38.cloned.1.call-update) | async-done | bytes 8208 | tf_op jit(solution)/shard_map/reduce_scatter | solution.py:685
  760.0 3.3 convolution_convert_fusion.4
  763.3 4.3 convolution_convert_fusion.2
  767.8 5.5 convolution_convert_fusion.1
  773.3 4.0 broadcast_multiply_fusion
  781.1 12.9 %fusion.100 = f32[512,2048]{1,0:T(8,128)S(1)} fusion(bf16[4096,512]{0,1:T(8,128)(2,1)} %get-tuple-element.107, bf16[4096,2048]{1,0:T(8,128)(2,1)} %all-gather.10.cloned.1.call-done), kind=kOutput, calls=%fused_computation.200 | convolution fusion | flops 8589934592 | bytes 25165824 | tf_op jit(solution)/shard_map/tf,td->fd/dot_general | solution.py:572
  794.0 2.0 copy-done.12
  796.8 3.4 all-to-all-start.2
  800.3 4.8 reduce-scatter.28.cloned.1.call-done
  807.3 43.1 %reduce-scatter.22.cloned.1.call-done = bf16[128,2048]{1,0:T(8,128)(2,1)} async-done(((bf16[512,2048]{1,0:T(8,128)(2,1)}), bf16[128,2048]{1,0:T(8,128)(2,1)}) %reduce-scatter.22.cloned.1.call-update) | async-done | bytes 524304 | tf_op jit(solution)/shard_map/reduce_scatter | solution.py:594
  850.5 3.6 fusion.44
  854.2 15.0 %fusion.102 = f32[2048,512]{0,1:T(8,128)} fusion(bf16[4096,512]{0,1:T(8,128)(2,1)} %get-tuple-element.104, bf16[4096,2048]{1,0:T(8,128)(2,1)} %all-gather.6.cloned.1.call-done), kind=kOutput, calls=%fused_computation.202 | convolution fusion | flops 8589934592 | bytes 25165824 | tf_op jit(solution)/shard_map/td,tf->df/dot_general | solution.py:574
  869.5 13.6 %fusion.101 = f32[2048,512]{0,1:T(8,128)S(1)} fusion(bf16[4096,512]{0,1:T(8,128)(2,1)} %get-tuple-element.105, bf16[4096,2048]{1,0:T(8,128)(2,1)} %all-gather.6.cloned.1.call-done), kind=kOutput, calls=%fused_computation.201 | convolution fusion | flops 8589934592 | bytes 25165824 | tf_op jit(solution)/shard_map/td,tf->df/dot_general | solution.py:573
  883.1 2.9 slice_bitcast_fusion.1
  887.0 3.6 copy.122
  890.6 17.6 %reduce-scatter.32.cloned.1.call-done = f32[256,576]{0,1:T(8,128)} async-done(((f32[2048,576]{0,1:T(8,128)}), f32[256,576]{0,1:T(8,128)}) %reduce-scatter.32.cloned.1.call-update) | async-done | bytes 589840 | tf_op jit(solution)/shard_map/reduce_scatter | solution.py:685
  908.1 2.2 copy.137
  910.3 4.3 all-to-all-start.1
  914.6 6.1 maximum_bitcast_fusion
  922.5 7.5 reduce-scatter.42.cloned.1.call-done
  932.3 3.3 convert_bitcast_fusion
  935.6 4.0 copy.123
  939.6 28.1 %reduce-scatter.34.cloned.1.call-done = bf16[64,1024]{1,0:T(8,128)(2,1)} async-done(((bf16[512,1024]{1,0:T(8,128)(2,1)}), bf16[64,1024]{1,0:T(8,128)(2,1)}) %reduce-scatter.34.cloned.1.call-update) | async-done | bytes 131088 | tf_op jit(solution)/shard_map/reduce_scatter | solution.py:676
  969.3 43.7 %reduce-scatter.36.cloned.1.call-done = bf16[512,256]{1,0:T(8,128)(2,1)} async-done(((bf16[512,2048]{1,0:T(8,128)(2,1)}), bf16[512,256]{1,0:T(8,128)(2,1)}) %reduce-scatter.36.cloned.1.call-update) | async-done | bytes 262160 | tf_op jit(solution)/shard_map/reduce_scatter | solution.py:679
  1014.8 23.1 %all-reduce.7 = (f32[2048]{0:T(1024)S(1)}, f32[512]{0:T(512)S(1)}, f32[2048]{0:T(1024)S(1)}) all-reduce(f32[2048]{0:T(1024)S(1)} %get-tuple-element.84, f32[512]{0:T(512)S(1)} %get-tuple-element.86, f32[2048]{0:T(1024)S(1)} %get-tuple-element.88), channel_id=8, replica_groups=mesh['ep'=8,'tp'=4] {'ep'}, use_global_device_ids=true, to_apply=%region_21.22.clone | all-reduce | flops 4608 | bytes 36864
  1038.1 11.7 all-reduce.8
  1051.5 11.0 reduce-scatter.30.cloned.1.call-done
  1062.5 1.9 convert_element_type.207
  1064.4 45.5 %all-gather.14.cloned.1.call-done = bf16[512,2048]{1,0:T(8,128)(2,1)} async-done(((bf16[128,2048]{1,0:T(8,128)(2,1)}), bf16[512,2048]{1,0:T(8,128)(2,1)}) %all-gather.14.cloned.1.call-update) | async-done | bytes 2097168 | tf_op jit(solution)/shard_map/all_gather | solution.py:667
  1110.0 46.2 %all-gather.8.cloned.1.call-done = bf16[512,2048]{1,0:T(8,128)(2,1)} async-done(((bf16[128,2048]{1,0:T(8,128)(2,1)}), bf16[512,2048]{1,0:T(8,128)(2,1)}) %all-gather.8.cloned.1.call-update) | async-done | bytes 2097168 | tf_op jit(solution)/shard_map/all_gather | solution.py:598
  1156.2 23.7 %reduce-scatter.40.cloned.1.call-done = f32[64,576]{1,0:T(8,128)} async-done(((f32[256,576]{1,0:T(8,128)}), f32[64,576]{1,0:T(8,128)}) %reduce-scatter.40.cloned.1.call-update) | async-done | bytes 147472
  1179.9 3.3 copy.157
  (234 shorter events, 52.7 us)
Async XLA Ops:
  7.2 16.7 %copy-start = (bf16[2048,768]{1,0:T(8,128)(2,1)S(1)}, bf16[2048,768]{1,0:T(8,128)(2,1)}, u32[]{:S(2)}) copy-start(bf16[2048,768]{1,0:T(8,128)(2,1)} %param.18) | copy-start | bytes 9437188
  7.2 75.3 %reduce-scatter.18.cloned.1.call-start = ((), (), s32[]{:S(2)}) async-start(), calls=%async_computation.16 | async-start | bytes 2621440 | tf_op jit(solution)/shard_map/reduce_scatter | solution.py:529
  7.3 6.5 copy-start.51
  9.5 14.4 %copy-start.47 = (f32[512]{0:T(512)}, f32[512]{0:T(512)S(1)}, u32[]{:S(2)}) copy-start(f32[512]{0:T(512)S(1)} %add_rsqrt_fusion.1) | copy-start | bytes 6148
  9.7 5.0 copy-start.49
  9.8 5.0 copy-start.55
  14.8 13.5 %copy-start.24 = (f32[512,32]{0,1:T(8,128)}, f32[512,32]{0,1:T(8,128)S(1)}, u32[]{:S(2)}) copy-start(f32[512,32]{0,1:T(8,128)S(1)} %get-tuple-element.129) | copy-start | bytes 196612
  14.8 13.7 %copy-start.28 = (bf16[512,32]{0,1:T(8,128)(2,1)}, bf16[512,32]{0,1:T(8,128)(2,1)S(1)}, u32[]{:S(2)}) copy-start(bf16[512,32]{0,1:T(8,128)(2,1)S(1)} %get-tuple-element.112) | copy-start | bytes 98308
  14.8 13.7 %copy-start.30 = (bf16[512,32]{0,1:T(8,128)(2,1)}, bf16[512,32]{0,1:T(8,128)(2,1)S(1)}, u32[]{:S(2)}) copy-start(bf16[512,32]{0,1:T(8,128)(2,1)S(1)} %get-tuple-element.113) | copy-start | bytes 98308
  14.8 9.1 copy-start.38
  23.9 3.6 copy-start.7
  27.5 2.3 copy-start.9
  29.8 2.4 copy-start.1
  29.8 2.4 copy-start.36
  35.7 165.0 %all-gather.6.cloned.1.call-start = ((), (), s32[]{:S(2)}) async-start(), calls=%async_computation.17 | async-start | bytes 17301504 | tf_op jit(solution)/shard_map/all_gather | solution.py:536
  35.8 49.3 %copy-start.35 = (f32[2048]{0:T(1024)S(1)}, f32[2048]{0:T(1024)}, u32[]{:S(2)}) copy-start(f32[2048]{0:T(1024)} %param.23) | copy-start | bytes 24580
  39.9 46.9 %copy-start.44 = (s32[512,6]{0,1:T(8,128)S(1)}, s32[512,6]{0,1:T(8,128)}, u32[]{:S(2)}) copy-start(s32[512,6]{0,1:T(8,128)} %param.30) | copy-start | bytes 36868
  39.9 46.9 %copy-start.45 = (s32[512,6]{0,1:T(8,128)S(1)}, s32[512,6]{0,1:T(8,128)}, u32[]{:S(2)}) copy-start(s32[512,6]{0,1:T(8,128)} %param.29) | copy-start | bytes 36868
  84.1 12.6 %copy-start.33 = (f32[2048,8]{0,1:T(8,128)S(1)}, f32[2048,8]{0,1:T(8,128)}, u32[]{:S(2)}) copy-start(f32[2048,8]{0,1:T(8,128)} %param.24) | copy-start | bytes 196612
  86.0 204.8 %all-gather.10.cloned.1.call-start = ((), (), s32[]{:S(2)}) async-start(), calls=%async_computation.21 | async-start | bytes 18874368 | tf_op jit(solution)/shard_map/all_gather | solution.py:461
  87.5 140.7 %all-to-all-start = ((f32[512,8,1]{0,2,1:T(1,128)}), f32[512,8,1]{0,2,1:T(1,128)S(1)}, u32[]{:S(2)}, u32[]{:S(2)}) async-start(f32[512,8,1]{0,2,1:T(1,128)} %copy.113), calls=%async_computation.1 | async-start | bytes 32768 | tf_op jit(solution)/shard_map/all_to_all | solution.py:460
  91.1 416.6 %reduce-scatter.24.cloned.1.call-start = ((), (), s32[]{:S(2)}) async-start(), calls=%async_computation.22 | async-start | bytes 18874368 | tf_op jit(solution)/shard_map/reduce_scatter | solution.py:593
  91.7 5.8 copy-start.4
  222.3 5.8 copy-start.46
  313.1 30.8 %copy-start.18 = (bf16[2048,352]{0,1:T(8,128)(2,1)S(1)}, bf16[2048,352]{0,1:T(8,128)(2,1)}, u32[]{:S(2)}) copy-start(bf16[2048,352]{0,1:T(8,128)(2,1)} %get-tuple-element.109) | copy-start | bytes 4325380
  313.1 30.8 %copy-start.27 = (bf16[2048,88]{0,1:T(8,128)(2,1)S(1)}, bf16[2048,88]{0,1:T(8,128)(2,1)}, u32[]{:S(2)}) copy-start(bf16[2048,88]{0,1:T(8,128)(2,1)} %get-tuple-element.101) | copy-start | bytes 1081348
  313.1 30.7 %copy-start.32 = (bf16[2048,72]{0,1:T(8,128)(2,1)S(1)}, bf16[2048,72]{0,1:T(8,128)(2,1)}, u32[]{:S(2)}) copy-start(bf16[2048,72]{0,1:T(8,128)(2,1)} %get-tuple-element.122) | copy-start | bytes 884740
  313.1 30.7 %copy-start.60 = (bf16[4096,512]{0,1:T(8,128)(2,1)S(1)}, bf16[4096,512]{0,1:T(8,128)(2,1)}, u32[]{:S(2)}) copy-start(bf16[4096,512]{0,1:T(8,128)(2,1)} %get-tuple-element.105) | copy-start | bytes 12582916
  391.6 162.2 %reduce-scatter.26.cloned.1.call-start = ((), (), s32[]{:S(2)}) async-start(), calls=%async_computation.23 | async-start | bytes 2621440 | tf_op jit(solution)/shard_map/reduce_scatter | solution.py:594
  507.7 96.0 %all-gather.12.cloned.1.call-start = ((), (), s32[]{:S(2)}) async-start(), calls=%async_computation.24 | async-start | bytes 2621440 | tf_op jit(solution)/shard_map/all_gather | solution.py:601
  558.3 163.7 %reduce-scatter.20.cloned.1.call-start = ((), (), s32[]{:S(2)}) async-start(), calls=%async_computation.18 | async-start | bytes 18874368 | tf_op jit(solution)/shard_map/reduce_scatter | solution.py:593
  573.5 184.7 %reduce-scatter.38.cloned.1.call-start = ((), (), s32[]{:S(2)}) async-start(), calls=%async_computation.31 | async-start | bytes 73728 | tf_op jit(solution)/shard_map/reduce_scatter | solution.py:685
  585.1 220.1 %reduce-scatter.28.cloned.1.call-start = ((), (), s32[]{:S(2)}) async-start(), calls=%async_computation.25 | async-start | bytes 2621440 | tf_op jit(solution)/shard_map/reduce_scatter | solution.py:660
  603.7 3.7 copy-start.2
  609.4 2.2 copy-start.20
  609.4 2.2 copy-start.22
  610.8 2.2 copy-start.29
  610.8 2.2 copy-start.31
  612.4 2.5 copy-start.6
  612.4 2.5 copy-start.43
  612.4 2.4 copy-start.50
  612.4 2.4 copy-start.56
  613.5 2.3 copy-start.25
  615.9 1.9 copy-start.23
  615.9 2.9 copy-start.53
  622.1 99.9 %copy-start.39 = (f32[2048]{0:T(1024)S(1)}, f32[2048]{0:T(1024)}, u32[]{:S(2)}) copy-start(f32[2048]{0:T(1024)} %param.17) | copy-start | bytes 24580
  622.1 99.9 %copy-start.48 = (f32[512]{0:T(512)S(1)}, f32[512]{0:T(512)}, u32[]{:S(2)}) copy-start(f32[512]{0:T(512)} %copy-done.47) | copy-start | bytes 6148
  622.2 228.3 %reduce-scatter.22.cloned.1.call-start = ((), (), s32[]{:S(2)}) async-start(), calls=%async_computation.19 | async-start | bytes 2621440 | tf_op jit(solution)/shard_map/reduce_scatter | solution.py:594
  722.0 186.1 %reduce-scatter.32.cloned.1.call-start = ((), (), s32[]{:S(2)}) async-start(), calls=%async_computation.28 | async-start | bytes 5308416 | tf_op jit(solution)/shard_map/reduce_scatter | solution.py:685
  727.6 202.4 %reduce-scatter.42.cloned.1.call-start = ((), (), s32[]{:S(2)}) async-start(), calls=%async_computation.33 | async-start | bytes 163840
  759.7 207.9 %reduce-scatter.34.cloned.1.call-start = ((), (), s32[]{:S(2)}) async-start(), calls=%async_computation.29 | async-start | bytes 1179648 | tf_op jit(solution)/shard_map/reduce_scatter | solution.py:676
  763.3 249.8 %reduce-scatter.36.cloned.1.call-start = ((), (), s32[]{:S(2)}) async-start(), calls=%async_computation.30 | async-start | bytes 2359296 | tf_op jit(solution)/shard_map/reduce_scatter | solution.py:679
  767.7 294.8 %reduce-scatter.30.cloned.1.call-start = ((), (), s32[]{:S(2)}) async-start(), calls=%async_computation.27 | async-start | bytes 3538944 | tf_op jit(solution)/shard_map/reduce_scatter | solution.py:673
  773.3 4.1 copy-start.59
  773.3 5.9 copy-start.58
  794.0 2.0 copy-start.12
  796.8 113.5 %all-to-all-start.2 = ((bf16[88,8,256]{2,0,1:T(8,128)(2,1)}), bf16[88,8,256]{2,0,1:T(8,128)(2,1)S(1)}, u32[]{:S(2)}, u32[]{:S(2)}) async-start(bf16[88,8,256]{2,0,1:T(8,128)(2,1)} %bitcast.136), calls=%async_computation.13 | async-start | bytes 720896 | tf_op jit(solution)/shard_map/all_to_all | solution.py:588
  800.3 309.7 %all-gather.14.cloned.1.call-start = ((), (), s32[]{:S(2)}) async-start(), calls=%async_computation.26 | async-start | bytes 2621440 | tf_op jit(solution)/shard_map/all_gather | solution.py:667
  854.1 302.0 %all-gather.8.cloned.1.call-start = ((), (), s32[]{:S(2)}) async-start(), calls=%async_computation.20 | async-start | bytes 2621440 | tf_op jit(solution)/shard_map/all_gather | solution.py:598
  869.2 310.7 %reduce-scatter.40.cloned.1.call-start = ((), (), s32[]{:S(2)}) async-start(), calls=%async_computation.32 | async-start | bytes 819200
  869.4 13.6 %copy-start.14 = (f32[2048,512]{0,1:T(8,128)S(1)}, f32[2048,512]{0,1:T(8,128)}, u32[]{:S(2)}) copy-start(f32[2048,512]{0,1:T(8,128)} %fusion.102) | copy-start | bytes 12582916
  910.3 22.0 %all-to-all-start.1 = ((bf16[2,2048,88]{2,0,1:T(2,128)(2,1)}), bf16[2,2048,88]{2,0,1:T(2,128)(2,1)}, u32[]{:S(2)}, u32[]{:S(2)}) async-start(bf16[2,2048,88]{2,0,1:T(2,128)(2,1)} %copy.122), calls=%async_computation.12 | async-start | bytes 2097152 | tf_op jit(solution)/shard_map/all_to_all | solution.py:585
  914.6 6.1 copy-start.13
  1179.9 3.3 copy-start.17
  (18 other events, 20.7 us)
Sparse Core Ops, SparseCore 0:
  35.8 46.5 reduce-scatter.17
  86.5 114.1 all-gather.5
  202.7 88.0 all-gather.9
  391.7 115.9 reduce-scatter.23
  509.9 43.8 reduce-scatter.25
  558.4 45.2 all-gather.11
  607.3 114.6 reduce-scatter.19
  725.0 33.2 reduce-scatter.37
  761.2 43.8 reduce-scatter.27
  807.3 43.1 reduce-scatter.21
  854.9 53.2 reduce-scatter.31
  910.8 19.1 reduce-scatter.41
  933.5 34.1 reduce-scatter.33
  971.7 41.2 reduce-scatter.35
  1016.3 46.1 reduce-scatter.29
  1064.0 45.9 all-gather.13
  1111.5 44.6 all-gather.7
  1159.0 20.8 reduce-scatter.39

commit v2 on v1

--- a/solution.py
+++ b/solution.py
@@ -1,8 +1,11 @@
+import functools
 import math
 
 import jax
 import jax.numpy as jnp
 from jax import lax
+from jax.experimental import pallas as pl
+from jax.experimental.pallas import tpu as pltpu
 from jax.sharding import PartitionSpec as P
 
 NOPE = 128
@@ -410,6 +413,272 @@
     )
 
 
+MESH = pl.DeviceIdType.MESH
+
+
+def plane_partners(ep):
+    flip = lambda bit: ep + bit - 2 * bit * (lax.rem(lax.div(ep, bit), 2))
+    return flip(1), flip(2), flip(4), flip
+
+
+def greet(devices):
+    barrier = pltpu.get_barrier_semaphore()
+    for ep, tp in devices:
+        pl.semaphore_signal(barrier, inc=1, device_id=(ep, tp), device_id_type=MESH)
+    pl.semaphore_wait(barrier, len(devices))
+
+
+def remote(src, dst, send, recv, device):
+    return pltpu.make_async_remote_copy(
+        src_ref=src, dst_ref=dst, send_sem=send, recv_sem=recv, device_id=device, device_id_type=MESH
+    )
+
+
+def line_order(tp):
+    pick = lambda a, b, c, d: jnp.where(tp == 0, a, jnp.where(tp == 1, b, jnp.where(tp == 2, c, d)))
+    return (tp, pick(1, 0, 3, 2), pick(2, 2, 1, 1), pick(3, 3, 0, 0))
+
+
+def gather_kernel(rows, depth, own_ref, all_ref, local_sem, zsend, zrecv, psend, precv):
+    ep, tp = lax.axis_index("ep"), lax.axis_index("tp")
+    pair, xn, yn, flip = plane_partners(ep)
+    parity = lax.rem(ep, 2)
+    passed = jnp.where(parity == 0, xn, yn)
+    onward = jnp.where(parity == 0, yn, xn)
+    diag = xn + yn - ep
+    twin = lambda b: b + pair - ep
+    up, down = jnp.minimum(tp + 1, depth - 1), jnp.maximum(tp - 1, 0)
+    barrier = pltpu.get_barrier_semaphore()
+    for to in (pair, xn, yn):
+        pl.semaphore_signal(barrier, inc=1, device_id=(to, tp), device_id_type=MESH)
+
+    @pl.when(tp > 0)
+    def _():
+        pl.semaphore_signal(barrier, inc=1, device_id=(ep, down), device_id_type=MESH)
+
+    @pl.when(tp < depth - 1)
+    def _():
+        pl.semaphore_signal(barrier, inc=1, device_id=(ep, up), device_id_type=MESH)
+
+    pl.semaphore_wait(barrier, jnp.where((tp > 0) & (tp < depth - 1), 5, 4))
+    local = pltpu.make_async_copy(own_ref, all_ref.at[ep, tp], local_sem)
+    local.start()
+    order = line_order(tp)
+
+    def unit(block, chunk):
+        return all_ref.at[block, chunk]
+
+    def along(src, chunk, way, to):
+        return remote(src, unit(ep, chunk), zsend.at[chunk, way], zrecv.at[chunk], (ep, to))
+
+    def plane(src, block, chunk, slot, to):
+        return remote(src, unit(block, chunk), psend.at[chunk, slot], precv.at[chunk, slot], (to, tp))
+
+    def goes_up(chunk):
+        return (chunk <= tp) & (tp < depth - 1)
+
+    def goes_down(chunk):
+        return (chunk >= tp) & (tp > 0)
+
+    for k in range(depth + 1):
+        if k < depth:
+            chunk = order[k]
+            src = own_ref if k == 0 else unit(ep, chunk)
+            if k > 0:
+                along(src, chunk, 0, up).wait_recv()
+
+            @pl.when(goes_up(chunk))
+            def _():
+                along(src, chunk, 0, up).start()
+
+            @pl.when(goes_down(chunk))
+            def _():
+                along(src, chunk, 1, down).start()
+
+            plane(src, ep, chunk, 1, xn).start()
+            plane(src, ep, chunk, 2, yn).start()
+            plane(src, ep, chunk, 0, pair).start()
+        if k > 0:
+            chunk = order[k - 1]
+            plane(unit(xn, chunk), xn, chunk, 1, xn).wait_recv()
+            plane(unit(yn, chunk), yn, chunk, 2, yn).wait_recv()
+            plane(unit(passed, chunk), passed, chunk, 3, onward).start()
+            plane(unit(xn, chunk), xn, chunk, 4, pair).start()
+            plane(unit(yn, chunk), yn, chunk, 5, pair).start()
+        if k > 1:
+            chunk = order[k - 2]
+            plane(unit(diag, chunk), diag, chunk, 3, onward).wait_recv()
+            plane(unit(diag, chunk), diag, chunk, 6, pair).start()
+    chunk = order[depth - 1]
+    plane(unit(diag, chunk), diag, chunk, 3, onward).wait_recv()
+    plane(unit(diag, chunk), diag, chunk, 6, pair).start()
+    for k in range(depth):
+        chunk = order[k]
+        for slot, block in ((0, pair), (4, twin(xn)), (5, twin(yn)), (6, twin(diag))):
+            plane(unit(block, chunk), block, chunk, slot, pair).wait_recv()
+    local.wait()
+    for k in range(depth):
+        chunk = order[k]
+
+        @pl.when(goes_up(chunk))
+        def _():
+            along(own_ref, chunk, 0, up).wait_send()
+
+        @pl.when(goes_down(chunk))
+        def _():
+            along(own_ref, chunk, 1, down).wait_send()
+
+        for slot in range(7):
+            plane(own_ref, ep, chunk, slot, pair).wait_send()
+
+
+def gather_all(own, blocks, depth, cid):
+    rows, width = own.shape
+    out = pl.pallas_call(
+        functools.partial(gather_kernel, rows, depth),
+        out_shape=jax.ShapeDtypeStruct((blocks, depth, rows, width), own.dtype),
+        in_specs=[pl.BlockSpec(memory_space=pltpu.VMEM)],
+        out_specs=pl.BlockSpec(memory_space=pl.ANY),
+        scratch_shapes=[
+            pltpu.SemaphoreType.DMA,
+            pltpu.SemaphoreType.DMA((depth, 2)),
+            pltpu.SemaphoreType.DMA((depth,)),
+            pltpu.SemaphoreType.DMA((depth, 7)),
+            pltpu.SemaphoreType.DMA((depth, 7)),
+        ],
+        compiler_params=pltpu.CompilerParams(collective_id=cid, has_side_effects=True, vmem_limit_bytes=56 << 20),
+    )(own)
+    return out.reshape(blocks * depth * rows, width)
+
+
+def sum_kernel(rows, depth, part_ref, out_ref, mine, got_pair, got_first, got_second, got_z, keep,
+               mine_sem, ps, pr, fs, fr, ss, sr, zs, zr):
+    f32 = jnp.float32
+    ep, tp = lax.axis_index("ep"), lax.axis_index("tp")
+    pair, xn, yn, flip = plane_partners(ep)
+    parity = lax.rem(ep, 2)
+    first = jnp.where(parity == 0, xn, yn)
+    second = jnp.where(parity == 0, yn, xn)
+    diag = xn + yn - ep
+    other = lambda b: b + pair - ep
+    blocks = (first, diag, ep, second)
+    greet([(pair, tp), (xn, tp), (yn, tp)] + [(ep, lax.rem(tp + k, depth)) for k in range(1, depth)])
+    steps = [(k + 1) % depth for k in range(depth)]
+
+    def chunk_of(i):
+        return lax.rem(tp + steps[i], depth)
+
+    def pair_copy(i, slot):
+        return remote(part_ref.at[other(blocks[slot]), chunk_of(i)], got_pair.at[i, pslot(slot)], ps.at[i, slot], pr.at[i, pslot(slot)], (pair, tp))
+
+    def pslot(slot):
+        return {0: 3, 1: 1, 2: 2, 3: 0}[slot]
+
+    def pair_wait(i, slot):
+        return remote(part_ref.at[ep, chunk_of(i)], got_pair.at[i, slot], ps.at[i, slot], pr.at[i, slot], (pair, tp))
+
+    def mine_copy(i, slot):
+        return pltpu.make_async_copy(part_ref.at[blocks[slot], chunk_of(i)], mine.at[i, slot], mine_sem.at[i, slot])
+
+    def first_copy(i, slot):
+        return remote(mine.at[i, slot], got_first.at[i, slot], fs.at[i, slot], fr.at[i, slot], (first, tp))
+
+    def second_copy(i):
+        return remote(mine.at[i, 3], got_second.at[i], ss.at[i], sr.at[i], (second, tp))
+
+    def z_copy(i):
+        k = steps[i]
+        return remote(mine.at[i, 2], got_z.at[k - 1], zs.at[k - 1], zr.at[k - 1], (ep, lax.rem(tp + k, depth)))
+
+    def add(dst, a, b):
+        def body(r, _):
+            sl = pl.ds(pl.multiple_of(r * 16, 16), 16)
+            dst[sl, :] = (a[sl, :].astype(f32) + b[sl, :].astype(f32)).astype(dst.dtype)
+            return 0
+        lax.fori_loop(0, rows // 16, body, 0)
+
+    for i in range(depth):
+        for slot in (3, 1, 2, 0):
+            pair_copy(i, slot).start()
+        for slot in range(4):
+            mine_copy(i, slot).start()
+
+    def stage_a(i):
+        for slot in range(4):
+            mine_copy(i, slot).wait()
+            pair_wait(i, slot).wait_recv()
+            add(mine.at[i, slot], mine.at[i, slot], got_pair.at[i, slot])
+            if slot < 2:
+                first_copy(i, slot).start()
+
+    def stage_b(i):
+        first_copy(i, 1).wait_recv()
+        add(mine.at[i, 3], mine.at[i, 3], got_first.at[i, 1])
+        second_copy(i).start()
+        first_copy(i, 0).wait_recv()
+        add(mine.at[i, 2], mine.at[i, 2], got_first.at[i, 0])
+
+    def stage_c(i):
+        second_copy(i).wait_recv()
+        if i < depth - 1:
+            add(mine.at[i, 2], mine.at[i, 2], got_second.at[i])
+            z_copy(i).start()
+        else:
+            add(keep, mine.at[i, 2], got_second.at[i])
+
+    for t in range(depth + 2):
+        if t < depth:
+            stage_a(t)
+        if 0 <= t - 1 < depth:
+            stage_b(t - 1)
+        if 0 <= t - 2 < depth:
+            stage_c(t - 2)
+    for i in range(depth - 1):
+        z_copy(i).wait_recv()
+
+    def total(r, _):
+        sl = pl.ds(pl.multiple_of(r * 16, 16), 16)
+        v = keep[sl, :]
+        for k in range(depth - 1):
+            v = v + got_z[k, sl, :].astype(f32)
+        out_ref[sl, :] = v
+        return 0
+
+    lax.fori_loop(0, rows // 16, total, 0)
+    for i in range(depth):
+        for slot in range(4):
+            pair_copy(i, slot).wait_send()
+        for slot in range(2):
+            first_copy(i, slot).wait_send()
+        second_copy(i).wait_send()
+        if i < depth - 1:
+            z_copy(i).wait_send()
+
+
+def sum_all_rows(part, blocks, depth, cid):
+    width = part.shape[-1]
+    rows = part.shape[0] // (blocks * depth)
+    bf, f32 = part.dtype, jnp.float32
+    D = pltpu.SemaphoreType.DMA
+    return pl.pallas_call(
+        functools.partial(sum_kernel, rows, depth),
+        out_shape=jax.ShapeDtypeStruct((rows, width), f32),
+        in_specs=[pl.BlockSpec(memory_space=pl.ANY)],
+        out_specs=pl.BlockSpec(memory_space=pltpu.VMEM),
+        scratch_shapes=[
+            pltpu.VMEM((depth, 4, rows, width), bf),
+            pltpu.VMEM((depth, 4, rows, width), bf),
+            pltpu.VMEM((depth, 2, rows, width), bf),
+            pltpu.VMEM((depth, rows, width), bf),
+            pltpu.VMEM((depth - 1, rows, width), bf),
+            pltpu.VMEM((rows, width), f32),
+            D((depth, 4)), D((depth, 4)), D((depth, 4)), D((depth, 2)), D((depth, 2)), D((depth,)), D((depth,)),
+            D((depth - 1,)), D((depth - 1,)),
+        ],
+        compiler_params=pltpu.CompilerParams(collective_id=cid, has_side_effects=True, vmem_limit_bytes=56 << 20),
+    )(part.reshape(blocks, depth, rows, width))
+
+
 def padded_hidden(routed, shared):
     return -(-(routed + shared + 24) // 128) * 128
 
@@ -451,7 +720,6 @@
     score_scale = qk_width ** (-0.5)
     rows_part = tokens // tp_count
     row_start = tp_index * rows_part
-    every = ("ep", "tp")
 
     expert_range = jnp.arange(experts, dtype=jnp.int32)
     kept = jnp.any(
@@ -533,7 +801,7 @@
     inv_second = lax.rsqrt(jnp.mean(middle * middle, axis=-1, keepdims=True) + EPSILON)
     normed_second = middle * inv_second
     hidden_rows = (normed_second * gain_ffn).astype(bf16)
-    hidden_all = lax.all_gather(hidden_rows, every, tiled=True)
+    hidden_all = gather_all(hidden_rows, ep_count, tp_count, 0)
 
     gate_up = jnp.dot(hidden_all, w_in, preferred_element_type=f32)
     gate_val, up_val = gate_up[:, :hidden], gate_up[:, hidden:]
@@ -593,7 +861,7 @@
         plane = lax.psum_scatter(part, "ep", scatter_dimension=0, tiled=True)
         return lax.psum_scatter(plane, "tp", scatter_dimension=0, tiled=True).astype(f32)
 
-    ffn_grad = sum_rows(rows_grad)
+    ffn_grad = sum_all_rows(rows_grad, ep_count, tp_count, 1)
     ffn_rows = sum_rows(out_part)
     block_out = lax.all_gather((middle + ffn_rows).astype(bf16), "tp", tiled=True)
     middle_grad = cot_rows + norm_back(ffn_grad, gain_ffn, normed_second, inv_second)
@@ -711,7 +979,8 @@
 
 
 def solution(mesh):
-    body = body_dense if mesh.shape["ep"] == 8 else body_slots
+    near = mesh.shape["ep"] == 8 and mesh.shape["tp"] == 4
+    body = body_dense if near else body_slots
     placed = (
         P("ep", None),
         P(),

time: 1200 us -> 958 us (0.80)
  waiting for transfers between devices: 784 us -> 330 us
  Pallas kernels: 0 us -> 202 us
    pallas_call x0 -> x2, Pallas kernels: none -> 202 us  [the longest x1 112 us: gather_all(): pl.pallas_call(functools.partial(gather_kernel, rows, depth), out_shape=j...]
    reduce_scatter x2 -> x1, waiting for transfers between devices: 216 us -> 66.5 us  [sum_rows(): plane = lax.psum_scatter(part, 'ep', scatter_dimension=0, tiled=True)]
    all_gather x1 -> x0, waiting for transfers between devices: 95.6 us -> none  [body_dense(): hidden_all = lax.all_gather(hidden_rows, every, tiled=True)]
    all_gather x1, waiting for transfers between devices: 62.6 us -> 0.03 us  [body_dense(): cot_all = lax.all_gather(cotangent, 'ep', tiled=True)]
    all_gather x1, waiting for transfers between devices: 46.2 us -> 0.01 us  [body_dense(): lax.all_gather((middle + ffn_rows).astype(bf16), 'tp', tiled=True)]
    reduce_scatter x2 -> x1, waiting for transfers between devices: 89.2 us -> 43.5 us  [sum_rows(): lax.psum_scatter(plane, 'tp', scatter_dimension=0, tiled=True).astype(f32)]
    all_gather x1, waiting for transfers between devices: 45.5 us -> 0.01 us  [body_dense(): lax.all_gather((middle_grad + norm_back(attn_in_grad, gain_attn, normed_r...]
    reduce_scatter x1, waiting for transfers between devices: 42.6 us -> 22.2 us  [body_dense(): lax.psum_scatter(attn_part, 'tp', scatter_dimension=0, tiled=True)]
  transfers between devices with their start and end apart: 21 -> 18, of which waited for: 18 -> 12; matrix products, arithmetic and copies ran while one was open for 16% -> 21% of each run, Pallas kernels for 0% -> 12%
where the time goes in v2:
time: 958 us; the launch traced here: 949 us
  waiting for transfers between devices  330 us (34%)
  matrix products  238 us (25%)
  Pallas kernels  202 us (21%)
  local copies, waits for them, and re-layouts  65.3 us (7%)
  other arithmetic  44.6 us (5%)
  blocking collectives  34.6 us (4%)
  between operations  19.6 us (2%)
  starting transfers between devices  14.4 us (2%)
    pallas_call x1, Pallas kernels, gather_all(): pl.pallas_call(functools.partial(gather_kernel, rows, depth), out_shape=j...  112 us
    pallas_call x1, Pallas kernels, sum_all_rows(): pl.pallas_call(functools.partial(sum_kernel, rows, depth), out_shape=jax....  90.1 us
    reduce_scatter x1, waiting for transfers between devices, sum_rows(): plane = lax.psum_scatter(part, 'ep', scatter_dimension=0, tiled=True)  66.5 us
    unnamed x17, waiting for transfers between devices  49.8 us
    reduce_scatter x1, waiting for transfers between devices, sum_rows(): lax.psum_scatter(plane, 'tp', scatter_dimension=0, tiled=True).astype(f32)  43.5 us
    reduce_scatter x1, waiting for transfers between devices, body_dense(): lax.psum_scatter(output_w_grad.astype(bf16), 'ep', scatter_dimension=1, t...  43.3 us
    reduce_scatter x2, waiting for transfers between devices, sum_all(): plane = lax.psum_scatter(part, 'ep', scatter_dimension=0, tiled=True)  38.7 us
    unnamed x140, local copies, waits for them, and re-layouts  36.6 us
  transfers between devices with their start and end apart: 18, of which 12 were waited for; matrix products, arithmetic and copies ran while one was open for 21% of the time, Pallas kernels for 12%

profile of v2, /device:TPU:0, one launch (start us, length us, event | category | flops | bytes accessed | tf_op | source)
XLA Modules:
  0.0 948.8 jit_solution(4467448257030455421)
XLA Ops:
  8.1 2.2 multiply_reduce_fusion.1
  10.6 3.9 fusion.87
  15.7 1.8 convolution_convert_fusion.5
  17.5 2.6 reshape.283
  20.1 2.5 fusion.89
  22.6 2.1 copy.141
  24.8 3.6 fusion.86
  33.9 2.6 convolution_convert_fusion.3
  37.8 5.2 all-to-all-start
  43.2 4.1 convert_element_type.167
  47.4 3.1 constant_dynamic-update-slice_fusion.4
  50.5 2.0 constant_dynamic-update-slice_fusion.3
  54.7 2.0 constant_dynamic-update-slice_fusion
  59.2 1.9 slice_bitcast_fusion.3
  61.1 22.2 %reduce-scatter.16.cloned.1.call-done = bf16[128,2048]{1,0:T(8,128)(2,1)} async-done(((bf16[512,2048]{1,0:T(8,128)(2,1)}), bf16[128,2048]{1,0:T(8,128)(2,1)}) %reduce-scatter.16.cloned.1.call-update) | async-done | bytes 524304 | tf_op jit(solution)/shard_map/reduce_scatter | solution.py:797
  83.3 2.1 multiply_reduce_fusion.6
  87.3 111.9 %shard_map.263 = bf16[8,4,128,2048]{3,2,1,0:T(8,128)(2,1)} custom-call(bf16[128,2048]{1,0:T(8,128)(2,1)} %multiply_convert_fusion.5.own_ref), custom_call_target="tpu_custom_call" | custom-call | tf_op jit(solution)/shard_map/pallas_call | solution.py:537
  199.2 21.6 %fusion.92 = f32[4096,1024]{0,1:T(8,128)S(1)} fusion(bf16[4096,2048]{1,0:T(8,128)(2,1)} %bitcast.130, bf16[2048,1024]{0,1:T(8,128)(2,1)} %broadcast_dynamic-update-slice_fusion), kind=kOutput, calls=%fused_computation.193 | convolution fusion | flops 17179869184 | bytes 37748736 | tf_op jit(solution)/shard_map/dot_general | solution.py:806
  221.0 5.6 copy-done.46
  226.8 22.3 %multiply_convert_fusion = (bf16[4096,512]{0,1:T(8,128)(2,1)}, bf16[4096,512]{0,1:T(8,128)(2,1)}, f32[4096]{0:T(1024)S(1)}, bf16[4096,512]{0,1:T(8,128)(2,1)}) fusion(f32[4096]{0:T(1024)S(1)} %mul.530, pred[512]{0:T(512)(128)(4,1)S(1)} %iota_compare_fusion.2, f32[4096,1024]{0,1:T(8,128)} %copy-done.46, bf16[4096,2048]{1,0:T(8,128)(2,1)} %all-gather.7.cloned.1.call-done, ...), kind=kOutput, calls=%fused_computation.8 | convolution fusion | flops 8640262144 | bytes 47973888 | tf_op jit(solution)/shard_map/td,fd->tf/dot_general | solution.py:825
  249.1 30.6 %fusion.60 = f32[4096,2048]{1,0:T(8,128)} fusion(f32[2048,8]{0,1:T(8,128)S(1)} %copy-done.33, f32[4096]{0:T(1024)S(1)} %multiply_multiply_fusion, f32[8]{0:T(128)S(1)} %compare_convert_fusion, f32[4096,8]{0,1:T(8,128)S(1)} %get-tuple-element.97, f32[4096]{0:T(1024)S(1)} %fusion.58, f32[4096]{0:T(1024)S(1)} %get-tuple-element.96), kind=kOutput, calls=%fused_computation.131 | convolution fusion | flops 805437440 | bytes 33800224 | tf_op jit(solution)/shard_map/te,de->td/dot_general | solution.py:836
  279.7 15.4 %fusion.10 = f32[4096,2048]{1,0:T(8,128)} fusion(bf16[4096,512]{0,1:T(8,128)(2,1)S(1)} %copy-done.60, bf16[2048,72]{0,1:T(8,128)(2,1)S(1)} %copy-done.32, bf16[2048,88]{0,1:T(8,128)(2,1)S(1)} %copy-done.27, bf16[2048,352]{0,1:T(8,128)(2,1)S(1)} %copy-done.18), kind=kOutput, calls=%fused_computation.35 | convolution fusion | flops 8596226048 | bytes 39845888 | tf_op jit(solution)/shard_map/tf,df->td/dot_general | solution.py:834
  295.9 31.6 %add_convert_fusion = bf16[4096,2048]{1,0:T(8,128)(2,1)} fusion(f32[4096,2048]{1,0:T(8,128)} %fusion.60, f32[4096,2048]{1,0:T(8,128)} %fusion.10, bf16[4096,512]{0,1:T(8,128)(2,1)} %get-tuple-element.104, bf16[2048,72]{0,1:T(8,128)(2,1)} %broadcast.219, bf16[2048,88]{0,1:T(8,128)(2,1)} %get-tuple-element.99, bf16[2048,352]{0,1:T(8,128)(2,1)} %get-tuple-element.108), kind=kOutput, calls=%fused_computation | convolution fusion | flops 8621391872 | bytes 90177536 | tf_op jit(solution)/shard_map/tf,df->td/dot_general | solution.py:835
  327.5 90.1 %shard_map.264 = f32[128,2048]{1,0:T(8,128)} custom-call(bf16[8,4,128,2048]{3,2,1,0:T(8,128)(2,1)} %bitcast.134), custom_call_target="tpu_custom_call" | custom-call | tf_op jit(solution)/shard_map/pallas_call | solution.py:663
  419.1 2.5 fusion.85
  421.7 15.1 %convolution_convert_fusion = bf16[4096,2048]{1,0:T(8,128)(2,1)} fusion(bf16[4096,512]{0,1:T(8,128)(2,1)} %get-tuple-element.107, bf16[88,2048]{1,0:T(8,128)(2,1)} %constant_dynamic-slice_fusion, bf16[352,2048]{1,0:T(8,128)(2,1)} %bitcast.151, bf16[512]{0:T(512)(128)(2,1)S(1)} %pad.25.clone), kind=kOutput, calls=%fused_computation.1 | convolution fusion | flops 8604614656 | bytes 22774784 | tf_op jit(solution)/shard_map/dot_general | solution.py:824
  437.5 10.8 %fusion.59 = f32[2048,8]{0,1:T(8,128)} fusion(bf16[4096,2048]{1,0:T(8,128)(2,1)} %bitcast.131, f32[4096]{0:T(1024)S(1)} %multiply_multiply_fusion, f32[8]{0:T(128)S(1)} %compare_convert_fusion, f32[4096,8]{0,1:T(8,128)S(1)} %get-tuple-element.97, f32[4096]{0:T(1024)S(1)} %fusion.58, f32[4096]{0:T(1024)S(1)} %get-tuple-element.96), kind=kOutput, calls=%fused_computation.130 | convolution fusion | flops 805437440 | bytes 17023008 | tf_op jit(solution)/shard_map/td,te->de/dot_general | solution.py:843
  448.6 18.4 %all-gather.9.cloned.1.call-done = bf16[512,2048]{1,0:T(8,128)(2,1)} async-done(((bf16[128,2048]{1,0:T(8,128)(2,1)}), bf16[512,2048]{1,0:T(8,128)(2,1)}) %all-gather.9.cloned.1.call-update) | async-done | bytes 2097168 | tf_op jit(solution)/shard_map/all_gather | solution.py:869
  467.0 3.6 convolution_convert_fusion.6
  479.2 1.8 fusion.93
  482.1 3.3 add_convert_fusion.1
  485.5 66.5 %reduce-scatter.18.cloned.1.call-done = bf16[512,2048]{1,0:T(8,128)(2,1)} async-done(((bf16[4096,2048]{1,0:T(8,128)(2,1)}), bf16[512,2048]{1,0:T(8,128)(2,1)}) %reduce-scatter.18.cloned.1.call-update) | async-done | bytes 2097168 | tf_op jit(solution)/shard_map/reduce_scatter | solution.py:861
  552.2 5.5 fusion.56
  557.7 31.3 %reduce-scatter.32.cloned.1.call-done = f32[256,8]{0,1:T(8,128)} async-done(((f32[2048,8]{0,1:T(8,128)}), f32[256,8]{0,1:T(8,128)}) %reduce-scatter.32.cloned.1.call-update) | async-done | bytes 8208 | tf_op jit(solution)/shard_map/reduce_scatter | solution.py:953
  590.8 3.3 convolution_convert_fusion.4
  594.2 4.3 convolution_convert_fusion.2
  598.6 5.4 convolution_convert_fusion.1
  604.1 4.0 broadcast_multiply_fusion
  612.0 15.0 %fusion.96 = f32[2048,512]{0,1:T(8,128)} fusion(bf16[4096,512]{0,1:T(8,128)(2,1)} %get-tuple-element.104, bf16[4096,2048]{1,0:T(8,128)(2,1)} %bitcast.132), kind=kOutput, calls=%fused_computation.197 | convolution fusion | flops 8589934592 | bytes 25165824 | tf_op jit(solution)/shard_map/td,tf->df/dot_general | solution.py:842
  627.0 8.5 reduce-scatter.22.cloned.1.call-done
  637.1 43.5 %reduce-scatter.20.cloned.1.call-done = bf16[128,2048]{1,0:T(8,128)(2,1)} async-done(((bf16[512,2048]{1,0:T(8,128)(2,1)}), bf16[128,2048]{1,0:T(8,128)(2,1)}) %reduce-scatter.20.cloned.1.call-update) | async-done | bytes 524304 | tf_op jit(solution)/shard_map/reduce_scatter | solution.py:862
  680.6 3.7 fusion.42
  684.6 14.9 %fusion.95 = f32[2048,512]{0,1:T(8,128)} fusion(bf16[4096,512]{0,1:T(8,128)(2,1)} %get-tuple-element.105, bf16[4096,2048]{1,0:T(8,128)(2,1)} %bitcast.133), kind=kOutput, calls=%fused_computation.196 | convolution fusion | flops 8589934592 | bytes 25165824 | tf_op jit(solution)/shard_map/td,tf->df/dot_general | solution.py:841
  699.6 13.5 %fusion.94 = f32[512,2048]{1,0:T(8,128)S(1)} fusion(bf16[4096,512]{0,1:T(8,128)(2,1)} %get-tuple-element.107, bf16[4096,2048]{1,0:T(8,128)(2,1)} %all-gather.7.cloned.1.call-done), kind=kOutput, calls=%fused_computation.195 | convolution fusion | flops 8589934592 | bytes 25165824 | tf_op jit(solution)/shard_map/tf,td->fd/dot_general | solution.py:840
  713.1 2.0 copy-done.13
  715.9 3.6 all-to-all-start.2
  719.5 6.0 slice_bitcast_fusion.1
  727.8 3.6 copy.122
  731.4 7.4 reduce-scatter.26.cloned.1.call-done
  738.8 2.2 copy.137
  741.1 4.3 all-to-all-start.1
  745.4 6.1 maximum_bitcast_fusion
  753.3 25.9 %reduce-scatter.36.cloned.1.call-done = f32[64,8]{1,0:T(8,128)} async-done(((f32[256,8]{1,0:T(8,128)}), f32[64,8]{1,0:T(8,128)}) %reduce-scatter.36.cloned.1.call-update) | async-done | bytes 2064
  781.5 3.3 convert_bitcast_fusion
  784.7 4.0 copy.123
  788.7 27.7 %reduce-scatter.28.cloned.1.call-done = bf16[64,1024]{1,0:T(8,128)(2,1)} async-done(((bf16[512,1024]{1,0:T(8,128)(2,1)}), bf16[64,1024]{1,0:T(8,128)(2,1)}) %reduce-scatter.28.cloned.1.call-update) | async-done | bytes 131088 | tf_op jit(solution)/shard_map/reduce_scatter | solution.py:944
  818.1 43.3 %reduce-scatter.30.cloned.1.call-done = bf16[512,256]{1,0:T(8,128)(2,1)} async-done(((bf16[512,2048]{1,0:T(8,128)(2,1)}), bf16[512,256]{1,0:T(8,128)(2,1)}) %reduce-scatter.30.cloned.1.call-update) | async-done | bytes 262160 | tf_op jit(solution)/shard_map/reduce_scatter | solution.py:947
  861.4 1.8 convert_element_type.207
  863.1 23.0 %all-reduce.7 = (f32[2048]{0:T(1024)S(1)}, f32[512]{0:T(512)S(1)}, f32[2048]{0:T(1024)S(1)}) all-reduce(f32[2048]{0:T(1024)S(1)} %get-tuple-element.84, f32[512]{0:T(512)S(1)} %get-tuple-element.86, f32[2048]{0:T(1024)S(1)} %get-tuple-element.88), channel_id=6, replica_groups=mesh['ep'=8,'tp'=4] {'ep'}, use_global_device_ids=true, to_apply=%region_19.20.clone | all-reduce | flops 4608 | bytes 36864
  886.3 11.7 %all-reduce.8 = (f32[256]{0:T(256)S(1)}, f32[64]{0:T(128)S(1)}, f32[256]{0:T(256)S(1)}) all-reduce(f32[256]{0:T(256)S(1)} %dynamic-slice.5, f32[64]{0:T(128)S(1)} %dynamic-slice.9, f32[256]{0:T(256)S(1)} %dynamic-slice.13), channel_id=7, replica_groups=mesh['ep'=8,'tp'=4] {'tp'}, use_global_device_ids=true, to_apply=%region_20.21.clone | all-reduce | flops 576 | bytes 4608
  899.7 11.5 %reduce-scatter.24.cloned.1.call-done = bf16[256,768]{1,0:T(8,128)(2,1)} async-done(((bf16[2048,768]{1,0:T(8,128)(2,1)}), bf16[256,768]{1,0:T(8,128)(2,1)}) %reduce-scatter.24.cloned.1.call-update) | async-done | bytes 393232 | tf_op jit(solution)/shard_map/reduce_scatter | solution.py:941
  911.3 1.9 convert_element_type.203
  913.2 23.2 %reduce-scatter.34.cloned.1.call-done = f32[64,576]{1,0:T(8,128)} async-done(((f32[256,576]{1,0:T(8,128)}), f32[64,576]{1,0:T(8,128)}) %reduce-scatter.34.cloned.1.call-update) | async-done | bytes 147472
  936.4 3.3 copy.157
  (227 shorter events, 45.5 us)
Async XLA Ops:
  8.0 16.7 %copy-start = (bf16[2048,768]{1,0:T(8,128)(2,1)S(1)}, bf16[2048,768]{1,0:T(8,128)(2,1)}, u32[]{:S(2)}) copy-start(bf16[2048,768]{1,0:T(8,128)(2,1)} %param.18) | copy-start | bytes 9437188
  8.0 75.2 %reduce-scatter.16.cloned.1.call-start = ((), (), s32[]{:S(2)}) async-start(), calls=%async_computation.14 | async-start | bytes 2621440 | tf_op jit(solution)/shard_map/reduce_scatter | solution.py:797
  8.1 6.5 copy-start.51
  10.3 14.4 %copy-start.47 = (f32[512]{0:T(512)}, f32[512]{0:T(512)S(1)}, u32[]{:S(2)}) copy-start(f32[512]{0:T(512)S(1)} %add_rsqrt_fusion.1) | copy-start | bytes 6148
  10.6 5.0 copy-start.49
  10.6 5.0 copy-start.55
  15.6 13.5 %copy-start.24 = (f32[512,32]{0,1:T(8,128)}, f32[512,32]{0,1:T(8,128)S(1)}, u32[]{:S(2)}) copy-start(f32[512,32]{0,1:T(8,128)S(1)} %get-tuple-element.129) | copy-start | bytes 196612
  15.6 13.7 %copy-start.28 = (bf16[512,32]{0,1:T(8,128)(2,1)}, bf16[512,32]{0,1:T(8,128)(2,1)S(1)}, u32[]{:S(2)}) copy-start(bf16[512,32]{0,1:T(8,128)(2,1)S(1)} %get-tuple-element.112) | copy-start | bytes 98308
  15.6 13.7 %copy-start.30 = (bf16[512,32]{0,1:T(8,128)(2,1)}, bf16[512,32]{0,1:T(8,128)(2,1)S(1)}, u32[]{:S(2)}) copy-start(bf16[512,32]{0,1:T(8,128)(2,1)S(1)} %get-tuple-element.113) | copy-start | bytes 98308
  15.7 9.1 copy-start.38
  24.8 3.6 copy-start.8
  28.3 2.3 copy-start.10
  30.7 2.4 copy-start.1
  30.7 2.4 copy-start.36
  32.1 1.8 copy-start.54
  33.9 3.2 copy-start.44
  33.9 3.2 copy-start.45
  36.5 190.2 %all-gather.7.cloned.1.call-start = ((), (), s32[]{:S(2)}) async-start(), calls=%async_computation.18 | async-start | bytes 18874368 | tf_op jit(solution)/shard_map/all_gather | solution.py:729
  37.8 188.9 %all-to-all-start = ((f32[512,8,1]{0,2,1:T(1,128)}), f32[512,8,1]{0,2,1:T(1,128)S(1)}, u32[]{:S(2)}, u32[]{:S(2)}) async-start(f32[512,8,1]{0,2,1:T(1,128)} %copy.113), calls=%async_computation.1 | async-start | bytes 32768 | tf_op jit(solution)/shard_map/all_to_all | solution.py:728
  43.0 424.0 %all-gather.9.cloned.1.call-start = ((), (), s32[]{:S(2)}) async-start(), calls=%async_computation.19 | async-start | bytes 2621440 | tf_op jit(solution)/shard_map/all_gather | solution.py:869
  43.2 9.3 copy-start.33
  47.3 6.0 copy-start.5
  59.2 27.1 %copy-start.35 = (f32[2048]{0:T(1024)S(1)}, f32[2048]{0:T(1024)}, u32[]{:S(2)}) copy-start(f32[2048]{0:T(1024)} %param.23) | copy-start | bytes 24580
  220.8 5.8 copy-start.46
  249.0 30.7 %copy-start.18 = (bf16[2048,352]{0,1:T(8,128)(2,1)S(1)}, bf16[2048,352]{0,1:T(8,128)(2,1)}, u32[]{:S(2)}) copy-start(bf16[2048,352]{0,1:T(8,128)(2,1)} %get-tuple-element.109) | copy-start | bytes 4325380
  249.0 30.6 %copy-start.27 = (bf16[2048,88]{0,1:T(8,128)(2,1)S(1)}, bf16[2048,88]{0,1:T(8,128)(2,1)}, u32[]{:S(2)}) copy-start(bf16[2048,88]{0,1:T(8,128)(2,1)} %get-tuple-element.101) | copy-start | bytes 1081348
  249.1 30.6 %copy-start.32 = (bf16[2048,72]{0,1:T(8,128)(2,1)S(1)}, bf16[2048,72]{0,1:T(8,128)(2,1)}, u32[]{:S(2)}) copy-start(bf16[2048,72]{0,1:T(8,128)(2,1)} %get-tuple-element.122) | copy-start | bytes 884740
  249.1 30.6 %copy-start.60 = (bf16[4096,512]{0,1:T(8,128)(2,1)S(1)}, bf16[4096,512]{0,1:T(8,128)(2,1)}, u32[]{:S(2)}) copy-start(bf16[4096,512]{0,1:T(8,128)(2,1)} %get-tuple-element.105) | copy-start | bytes 12582916
  327.5 90.1 %copy-start.4 = (f32[128,2048]{1,0:T(8,128)S(1)}, f32[128,2048]{1,0:T(8,128)}, u32[]{:S(2)}) copy-start(f32[128,2048]{1,0:T(8,128)} %copy-done.3) | copy-start | bytes 3145732
  421.6 130.4 %reduce-scatter.18.cloned.1.call-start = ((), (), s32[]{:S(2)}) async-start(), calls=%async_computation.15 | async-start | bytes 18874368 | tf_op jit(solution)/shard_map/reduce_scatter | solution.py:861
  436.8 152.2 %reduce-scatter.32.cloned.1.call-start = ((), (), s32[]{:S(2)}) async-start(), calls=%async_computation.26 | async-start | bytes 73728 | tf_op jit(solution)/shard_map/reduce_scatter | solution.py:953
  448.4 187.1 %reduce-scatter.22.cloned.1.call-start = ((), (), s32[]{:S(2)}) async-start(), calls=%async_computation.20 | async-start | bytes 2621440 | tf_op jit(solution)/shard_map/reduce_scatter | solution.py:928
  467.0 3.7 copy-start.2
  472.7 2.2 copy-start.20
  472.7 2.2 copy-start.22
  474.1 1.6 copy-start.9
  474.1 2.2 copy-start.29
  474.1 2.2 copy-start.31
  474.9 1.8 copy-start.52
  475.7 2.5 copy-start.7
  475.7 2.5 copy-start.43
  475.7 2.4 copy-start.50
  475.7 2.4 copy-start.56
  476.8 2.3 copy-start.25
  479.2 1.9 copy-start.23
  479.2 2.9 copy-start.53
  485.5 66.7 %copy-start.39 = (f32[2048]{0:T(1024)S(1)}, f32[2048]{0:T(1024)}, u32[]{:S(2)}) copy-start(f32[2048]{0:T(1024)} %param.17) | copy-start | bytes 24580
  485.5 66.7 %copy-start.48 = (f32[512]{0:T(512)S(1)}, f32[512]{0:T(512)}, u32[]{:S(2)}) copy-start(f32[512]{0:T(512)} %copy-done.47) | copy-start | bytes 6148
  485.5 195.1 %reduce-scatter.20.cloned.1.call-start = ((), (), s32[]{:S(2)}) async-start(), calls=%async_computation.16 | async-start | bytes 2621440 | tf_op jit(solution)/shard_map/reduce_scatter | solution.py:862
  552.1 186.8 %reduce-scatter.26.cloned.1.call-start = ((), (), s32[]{:S(2)}) async-start(), calls=%async_computation.23 | async-start | bytes 5308416 | tf_op jit(solution)/shard_map/reduce_scatter | solution.py:953
  557.6 221.5 %reduce-scatter.36.cloned.1.call-start = ((), (), s32[]{:S(2)}) async-start(), calls=%async_computation.28 | async-start | bytes 163840
  590.5 225.9 %reduce-scatter.28.cloned.1.call-start = ((), (), s32[]{:S(2)}) async-start(), calls=%async_computation.24 | async-start | bytes 1179648 | tf_op jit(solution)/shard_map/reduce_scatter | solution.py:944
  594.1 267.2 %reduce-scatter.30.cloned.1.call-start = ((), (), s32[]{:S(2)}) async-start(), calls=%async_computation.25 | async-start | bytes 2359296 | tf_op jit(solution)/shard_map/reduce_scatter | solution.py:947
  598.5 312.7 %reduce-scatter.24.cloned.1.call-start = ((), (), s32[]{:S(2)}) async-start(), calls=%async_computation.22 | async-start | bytes 3538944 | tf_op jit(solution)/shard_map/reduce_scatter | solution.py:941
  604.0 4.2 copy-start.59
  604.0 6.1 copy-start.58
  604.1 309.2 %all-gather.11.cloned.1.call-start = ((), (), s32[]{:S(2)}) async-start(), calls=%async_computation.21 | async-start | bytes 2621440 | tf_op jit(solution)/shard_map/all_gather | solution.py:935
  684.3 228.9 %all-gather.5.cloned.1.call-start = ((), (), s32[]{:S(2)}) async-start(), calls=%async_computation.17 | async-start | bytes 2621440 | tf_op jit(solution)/shard_map/all_gather | solution.py:866
  713.1 2.0 copy-start.13
  715.9 25.2 %all-to-all-start.2 = ((bf16[88,8,256]{2,0,1:T(8,128)(2,1)}), bf16[88,8,256]{2,0,1:T(8,128)(2,1)S(1)}, u32[]{:S(2)}, u32[]{:S(2)}) async-start(bf16[88,8,256]{2,0,1:T(8,128)(2,1)} %bitcast.143), calls=%async_computation.11 | async-start | bytes 720896 | tf_op jit(solution)/shard_map/all_to_all | solution.py:856
  719.5 216.9 %reduce-scatter.34.cloned.1.call-start = ((), (), s32[]{:S(2)}) async-start(), calls=%async_computation.27 | async-start | bytes 819200
  741.1 40.4 %all-to-all-start.1 = ((bf16[2,2048,88]{2,0,1:T(2,128)(2,1)}), bf16[2,2048,88]{2,0,1:T(2,128)(2,1)}, u32[]{:S(2)}, u32[]{:S(2)}) async-start(bf16[2,2048,88]{2,0,1:T(2,128)(2,1)} %copy.122), calls=%async_computation.10 | async-start | bytes 2097152 | tf_op jit(solution)/shard_map/all_to_all | solution.py:853
  745.3 6.2 copy-start.14
  936.4 3.3 copy-start.17
  (15 other events, 15.4 us)
Sparse Core Ops, SparseCore 0:
  36.7 46.5 reduce-scatter.15
  421.8 45.2 all-gather.8
  684.5 45.1 all-gather.10
  731.1 46.1 all-gather.4
Sparse Core Ops, SparseCore 1:
  39.1 127.7 all-gather.6
  436.9 115.1 reduce-scatter.17
  555.8 33.2 reduce-scatter.31
  591.9 43.5 reduce-scatter.21
  637.9 42.7 reduce-scatter.19
  684.6 54.2 reduce-scatter.25
  741.6 37.5 reduce-scatter.35
  782.2 34.2 reduce-scatter.27
  820.2 41.1 reduce-scatter.29
  865.1 46.1 reduce-scatter.23
  914.0 22.3 reduce-scatter.33

commit v3 on v2

--- a/solution.py
+++ b/solution.py
@@ -417,8 +417,17 @@
 
 
 def plane_partners(ep):
-    flip = lambda bit: ep + bit - 2 * bit * (lax.rem(lax.div(ep, bit), 2))
-    return flip(1), flip(2), flip(4), flip
+    def flip(bit):
+        return ep + bit - 2 * bit * lax.rem(lax.div(ep, bit), 2)
+
+    return flip(1), flip(2), flip(4)
+
+
+def line_order(tp):
+    def pick(a, b, c, d):
+        return jnp.where(tp == 0, a, jnp.where(tp == 1, b, jnp.where(tp == 2, c, d)))
+
+    return (tp, pick(1, 0, 3, 2), pick(2, 2, 1, 1), pick(3, 3, 0, 0))
 
 
 def greet(devices):
@@ -434,45 +443,92 @@
     )
 
 
-def line_order(tp):
-    pick = lambda a, b, c, d: jnp.where(tp == 0, a, jnp.where(tp == 1, b, jnp.where(tp == 2, c, d)))
-    return (tp, pick(1, 0, 3, 2), pick(2, 2, 1, 1), pick(3, 3, 0, 0))
-
-
-def gather_kernel(rows, depth, own_ref, all_ref, local_sem, zsend, zrecv, psend, precv):
+def experts_kernel(
+    depth, blocks, routed, shared, experts,
+    part_ref, resid_ref, gain_ref, cot_ref, kept_ref, w_in_ref, w_out_ref,
+    middle_ref, h_out, cot_all, grads_out, gated_out, out_out, rows_out,
+    h_all, got_z, resid_own, cot_tile, gu, act_grad, prob_lanes, diff_lanes, pair_lanes,
+    grads_tile, gated_tile, out_tile, rows_tile,
+    local_sem, z_send, z_recv, line_send, line_recv, h_send, h_recv, c_send, c_recv, tile_sem, store_sem,
+):
+    f32, bf16 = jnp.float32, jnp.bfloat16
     ep, tp = lax.axis_index("ep"), lax.axis_index("tp")
-    pair, xn, yn, flip = plane_partners(ep)
+    pair, xn, yn = plane_partners(ep)
     parity = lax.rem(ep, 2)
     passed = jnp.where(parity == 0, xn, yn)
     onward = jnp.where(parity == 0, yn, xn)
     diag = xn + yn - ep
-    twin = lambda b: b + pair - ep
+    rows = h_all.shape[2]
+    width = h_all.shape[3]
+    hidden = w_out_ref.shape[0]
+    half = blocks // 2
+    tile = half * rows
     up, down = jnp.minimum(tp + 1, depth - 1), jnp.maximum(tp - 1, 0)
-    barrier = pltpu.get_barrier_semaphore()
-    for to in (pair, xn, yn):
-        pl.semaphore_signal(barrier, inc=1, device_id=(to, tp), device_id_type=MESH)
-
-    @pl.when(tp > 0)
-    def _():
-        pl.semaphore_signal(barrier, inc=1, device_id=(ep, down), device_id_type=MESH)
-
-    @pl.when(tp < depth - 1)
-    def _():
-        pl.semaphore_signal(barrier, inc=1, device_id=(ep, up), device_id_type=MESH)
-
-    pl.semaphore_wait(barrier, jnp.where((tp > 0) & (tp < depth - 1), 5, 4))
-    local = pltpu.make_async_copy(own_ref, all_ref.at[ep, tp], local_sem)
-    local.start()
+
+    def twin(block):
+        return block + pair - ep
+
+    greet([(pair, tp), (xn, tp), (yn, tp)] + [(ep, lax.rem(tp + k, depth)) for k in range(1, depth)])
+
+    def z_copy(k):
+        to = lax.rem(tp + k, depth)
+        start = pl.multiple_of(to * rows, rows)
+        return remote(part_ref.at[pl.ds(start, rows)], got_z.at[k - 1], z_send.at[k - 1], z_recv.at[k - 1], (ep, to))
+
+    for k in range(1, depth):
+        z_copy(k).start()
+
+    def h_copy(block, chunk, slot, to):
+        ref = h_all.at[chunk, block]
+        return remote(ref, ref, h_send.at[chunk, slot], h_recv.at[chunk, slot], (to, tp))
+
+    def c_copy(block, chunk, slot, to):
+        ref = cot_all.at[chunk, block]
+        return remote(ref, ref, c_send.at[chunk, slot], c_recv.at[chunk, slot], (to, tp))
+
+    def c_first(chunk, slot, to):
+        src = cot_ref.at[pl.ds(pl.multiple_of(chunk * rows, rows), rows)]
+        return remote(src, cot_all.at[chunk, ep], c_send.at[chunk, slot], c_recv.at[chunk, slot], (to, tp))
+
+    def own_cot(chunk):
+        src = cot_ref.at[pl.ds(pl.multiple_of(chunk * rows, rows), rows)]
+        return pltpu.make_async_copy(src, cot_all.at[chunk, ep], local_sem.at[chunk])
+
     order = line_order(tp)
 
-    def unit(block, chunk):
-        return all_ref.at[block, chunk]
-
-    def along(src, chunk, way, to):
-        return remote(src, unit(ep, chunk), zsend.at[chunk, way], zrecv.at[chunk], (ep, to))
-
-    def plane(src, block, chunk, slot, to):
-        return remote(src, unit(block, chunk), psend.at[chunk, slot], precv.at[chunk, slot], (to, tp))
+    def order_at(k):
+        return jnp.where(k == 0, order[0], jnp.where(k == 1, order[1], jnp.where(k == 2, order[2], order[3])))
+
+    resid_copy = pltpu.make_async_copy(
+        resid_ref.at[pl.ds(pl.multiple_of(tp * rows, rows), rows)], resid_own, local_sem.at[depth]
+    )
+    resid_copy.start()
+    for k in range(depth):
+        c_first(order[k], 1, xn).start()
+        c_first(order[k], 2, yn).start()
+        c_first(order[k], 0, pair).start()
+        own_cot(order[k]).start()
+    resid_copy.wait()
+    for k in range(1, depth):
+        z_copy(k).wait_recv()
+
+    def norm_rows(r, _):
+        here = pl.ds(pl.multiple_of(r * 16, 16), 16)
+        own = pl.ds(pl.multiple_of(tp * rows + r * 16, 16), 16)
+        total = part_ref[own, :].astype(f32)
+        for k in range(depth - 1):
+            total = total + got_z[k, here, :].astype(f32)
+        middle = resid_own[here, :].astype(f32) + total
+        inverse = lax.rsqrt(jnp.mean(middle * middle, axis=-1, keepdims=True) + EPSILON)
+        middle_ref[here, :] = middle
+        h_all[tp, ep, here, :] = (middle * inverse * gain_ref[...]).astype(bf16)
+        return 0
+
+    lax.fori_loop(0, rows // 16, norm_rows, 0)
+
+    def along(chunk, way, to):
+        ref = h_all.at[chunk, ep]
+        return remote(ref, ref, line_send.at[chunk, way], line_recv.at[chunk], (ep, to))
 
     def goes_up(chunk):
         return (chunk <= tp) & (tp < depth - 1)
@@ -480,88 +536,270 @@
     def goes_down(chunk):
         return (chunk >= tp) & (tp > 0)
 
-    for k in range(depth + 1):
-        if k < depth:
-            chunk = order[k]
-            src = own_ref if k == 0 else unit(ep, chunk)
-            if k > 0:
-                along(src, chunk, 0, up).wait_recv()
-
-            @pl.when(goes_up(chunk))
-            def _():
-                along(src, chunk, 0, up).start()
-
-            @pl.when(goes_down(chunk))
-            def _():
-                along(src, chunk, 1, down).start()
-
-            plane(src, ep, chunk, 1, xn).start()
-            plane(src, ep, chunk, 2, yn).start()
-            plane(src, ep, chunk, 0, pair).start()
+    def send_chunk(k):
+        chunk = order[k]
         if k > 0:
-            chunk = order[k - 1]
-            plane(unit(xn, chunk), xn, chunk, 1, xn).wait_recv()
-            plane(unit(yn, chunk), yn, chunk, 2, yn).wait_recv()
-            plane(unit(passed, chunk), passed, chunk, 3, onward).start()
-            plane(unit(xn, chunk), xn, chunk, 4, pair).start()
-            plane(unit(yn, chunk), yn, chunk, 5, pair).start()
-        if k > 1:
-            chunk = order[k - 2]
-            plane(unit(diag, chunk), diag, chunk, 3, onward).wait_recv()
-            plane(unit(diag, chunk), diag, chunk, 6, pair).start()
-    chunk = order[depth - 1]
-    plane(unit(diag, chunk), diag, chunk, 3, onward).wait_recv()
-    plane(unit(diag, chunk), diag, chunk, 6, pair).start()
-    for k in range(depth):
-        chunk = order[k]
-        for slot, block in ((0, pair), (4, twin(xn)), (5, twin(yn)), (6, twin(diag))):
-            plane(unit(block, chunk), block, chunk, slot, pair).wait_recv()
-    local.wait()
-    for k in range(depth):
-        chunk = order[k]
+            along(chunk, 0, up).wait_recv()
 
         @pl.when(goes_up(chunk))
         def _():
-            along(own_ref, chunk, 0, up).wait_send()
+            along(chunk, 0, up).start()
 
         @pl.when(goes_down(chunk))
         def _():
-            along(own_ref, chunk, 1, down).wait_send()
+            along(chunk, 1, down).start()
+
+        h_copy(ep, chunk, 1, xn).start()
+        h_copy(ep, chunk, 2, yn).start()
+        h_copy(ep, chunk, 0, pair).start()
+
+    def forward_chunk(chunk):
+        for copy in (h_copy, c_copy):
+            copy(xn, chunk, 1, xn).wait_recv()
+            copy(yn, chunk, 2, yn).wait_recv()
+            copy(passed, chunk, 3, onward).start()
+            copy(xn, chunk, 4, pair).start()
+            copy(yn, chunk, 5, pair).start()
+
+    def forward_diag(chunk):
+        for copy in (h_copy, c_copy):
+            copy(diag, chunk, 3, onward).wait_recv()
+            copy(diag, chunk, 6, pair).start()
+
+    def await_pair(chunk, slots):
+        for copy in (h_copy, c_copy):
+            for slot, block in slots:
+                copy(block, chunk, slot, pair).wait_recv()
+
+    send_chunk(0)
+    send_chunk(1)
+
+    lanes = lax.broadcasted_iota(jnp.int32, (1, 128), 1)
+    base = routed + shared
+    slab = base // 128 * 128
+    lane0 = base - slab
+    near_half = lax.div(ep, half)
+
+    def tile_copies(i):
+        k, side = lax.div(i, 2), lax.rem(i, 2)
+        chunk = order_at(k)
+        start = jnp.where(side == 0, near_half, 1 - near_half) * half
+        group = pl.ds(start, half)
+        slot = lax.rem(i, 2)
+        stores = [
+            pltpu.make_async_copy(h_all.at[chunk, group], h_out.at[chunk, group], store_sem.at[slot, 0]),
+            pltpu.make_async_copy(grads_tile.at[slot], grads_out.at[chunk, group], store_sem.at[slot, 1]),
+            pltpu.make_async_copy(gated_tile.at[slot], gated_out.at[chunk, group], store_sem.at[slot, 2]),
+            pltpu.make_async_copy(out_tile.at[slot], out_out.at[group, chunk], store_sem.at[slot, 3]),
+            pltpu.make_async_copy(rows_tile.at[slot], rows_out.at[chunk, group], store_sem.at[slot, 4]),
+        ]
+        load = pltpu.make_async_copy(cot_all.at[chunk, group], cot_tile, tile_sem)
+        return chunk, start, slot, load, stores
+
+    def step(i, _):
+        k, side = lax.div(i, 2), lax.rem(i, 2)
+        chunk, start, slot, load, stores = tile_copies(i)
+
+        @pl.when(side == 0)
+        def _():
+            own_cot(chunk).wait()
+            forward_chunk(chunk)
+
+        @pl.when(i == 0)
+        def _():
+            send_chunk(2)
+
+        @pl.when(side == 0)
+        def _():
+            await_pair(chunk, ((0, pair), (4, twin(xn))))
+
+        @pl.when(side == 1)
+        def _():
+            forward_diag(chunk)
+
+        @pl.when(i == 1)
+        def _():
+            send_chunk(3)
+
+        @pl.when(side == 1)
+        def _():
+            await_pair(chunk, ((5, twin(yn)), (6, twin(diag))))
+
+        load.start()
+
+        @pl.when(i >= 2)
+        def _():
+            for copy in tile_copies(i - 2)[4]:
+                copy.wait()
+
+        group = pl.ds(start, half)
+        stores[0].start()
+        for n in range(0, 2 * hidden, 512):
+            gu[:, n : n + 512] = jnp.dot(
+                h_all[chunk, group].reshape(tile, width), w_in_ref[:, n : n + 512], preferred_element_type=f32
+            )
+        piece = gu[:, slab : slab + 128]
+        logits = piece + pltpu.roll(piece, 128 - experts, 1) + pltpu.roll(piece, 128 - 2 * experts, 1)
+        is_logit = (lanes >= lane0) & (lanes < lane0 + experts)
+        logits = jnp.where(is_logit, logits, -1e30)
+        exps = jnp.exp(logits - jnp.max(logits, axis=-1, keepdims=True))
+        probs = exps / jnp.sum(exps, axis=-1, keepdims=True)
+        here = (lanes == lane0 + ep).astype(f32)
+        kept = kept_ref[chunk, group].reshape(tile, 128).astype(f32)
+        prob_here = jnp.sum(probs * here * kept, axis=-1, keepdims=True)
+        prob_lanes[...] = jnp.broadcast_to(prob_here, (tile, 128))
+        diff_lanes[...] = here - probs
+        load.wait()
+        act_grad[...] = lax.dot_general(
+            cot_tile[...].reshape(tile, width), w_out_ref[...], (((1,), (1,)), ((), ())), preferred_element_type=f32
+        )
+        strip = 64
+
+        def strips(r, _):
+            at = pl.ds(pl.multiple_of(r * strip, strip), strip)
+            gate_here = prob_lanes[at, :]
+            pair_sum = jnp.zeros((strip, 128), f32)
+            per = rows // strip
+            block, inner = lax.div(r, per), pl.ds(pl.multiple_of(lax.rem(r, per) * strip, strip), strip)
+            for n in range(0, hidden, 128):
+                gate = gu[at, n : n + 128]
+                up_val = gu[at, hidden + n : hidden + n + 128]
+                grad = act_grad[at, n : n + 128]
+                if n + 128 <= routed:
+                    scale = gate_here
+                elif n >= routed:
+                    scale = None
+                else:
+                    scale = jnp.where(lanes < routed - n, gate_here, 1.0)
+                sig = jax.nn.sigmoid(gate)
+                silu = gate * sig
+                act = silu * up_val
+                if n < routed:
+                    both = act * grad
+                    if n + 128 > routed:
+                        both = jnp.where(lanes < routed - n, both, 0.0)
+                    pair_sum = pair_sum + both
+                    act = act * scale
+                    grad = grad * scale
+                gated_tile[slot, block, inner, n : n + 128] = act.astype(bf16)
+                grads_tile[slot, block, inner, n : n + 128] = (
+                    grad * up_val * (sig * (1.0 + gate * (1.0 - sig)))
+                ).astype(bf16)
+                grads_tile[slot, block, inner, hidden + n : hidden + n + 128] = (grad * silu).astype(bf16)
+            pair_lanes[at, :] = pair_sum
+            return 0
+
+        lax.fori_loop(0, tile // strip, strips, 0)
+        pair_grad = jnp.sum(pair_lanes[...], axis=-1, keepdims=True)
+        logit_grad = pair_grad * prob_lanes[...] * diff_lanes[...]
+        logit_grad = logit_grad + pltpu.roll(logit_grad, experts, 1) + pltpu.roll(logit_grad, 2 * experts, 1)
+        old = grads_tile[slot, :, :, slab : slab + 128].reshape(tile, 128)
+        grads_tile[slot, :, :, slab : slab + 128] = (
+            jnp.where(lanes >= lane0, logit_grad.astype(bf16), old).reshape(half, rows, 128)
+        )
+        for n in range(0, width, 512):
+            rows_tile[slot, :, :, n : n + 512] = (
+                lax.dot_general(
+                    grads_tile[slot].reshape(tile, 2 * hidden), w_in_ref[n : n + 512, :], (((1,), (1,)), ((), ())),
+                    preferred_element_type=f32,
+                ).astype(bf16).reshape(half, rows, 512)
+            )
+            out_tile[slot, :, :, n : n + 512] = (
+                jnp.dot(gated_tile[slot].reshape(tile, hidden), w_out_ref[:, n : n + 512], preferred_element_type=f32)
+                .astype(bf16).reshape(half, rows, 512)
+            )
+        for copy in stores[1:]:
+            copy.start()
+        return 0
+
+    lax.fori_loop(0, 2 * depth, step, 0)
+    for i in (2 * depth - 2, 2 * depth - 1):
+        for copy in tile_copies(i)[4]:
+            copy.wait()
+    for k in range(1, depth):
+        z_copy(k).wait_send()
+
+    def drain(k, _):
+        chunk = order_at(k)
+
+        @pl.when(goes_up(chunk))
+        def _():
+            along(chunk, 0, up).wait_send()
+
+        @pl.when(goes_down(chunk))
+        def _():
+            along(chunk, 1, down).wait_send()
 
         for slot in range(7):
-            plane(own_ref, ep, chunk, slot, pair).wait_send()
-
-
-def gather_all(own, blocks, depth, cid):
-    rows, width = own.shape
-    out = pl.pallas_call(
-        functools.partial(gather_kernel, rows, depth),
-        out_shape=jax.ShapeDtypeStruct((blocks, depth, rows, width), own.dtype),
-        in_specs=[pl.BlockSpec(memory_space=pltpu.VMEM)],
-        out_specs=pl.BlockSpec(memory_space=pl.ANY),
+            h_copy(ep, chunk, slot, pair).wait_send()
+            c_copy(ep, chunk, slot, pair).wait_send()
+        return 0
+
+    lax.fori_loop(0, depth, drain, 0)
+
+
+def experts_call(attn_part, inputs, gain, cotangent, kept, w_in, w_out, blocks, depth, routed, shared, experts, cid):
+    f32, bf16 = jnp.float32, jnp.bfloat16
+    tokens, width = inputs.shape
+    rows = tokens // depth
+    hidden = w_out.shape[0]
+    half = blocks // 2
+    tile = half * rows
+    dma = pltpu.SemaphoreType.DMA
+    vmem, anywhere = pl.BlockSpec(memory_space=pltpu.VMEM), pl.BlockSpec(memory_space=pl.ANY)
+
+    def units(size):
+        return jax.ShapeDtypeStruct((depth, blocks, rows, size), bf16)
+
+    return pl.pallas_call(
+        functools.partial(experts_kernel, depth, blocks, routed, shared, experts),
+        out_shape=(
+            jax.ShapeDtypeStruct((rows, width), f32),
+            units(width), units(width), units(2 * hidden), units(hidden),
+            jax.ShapeDtypeStruct((blocks, depth, rows, width), bf16), units(width),
+        ),
+        in_specs=[vmem, anywhere, vmem, anywhere, vmem, vmem, vmem],
+        out_specs=(vmem,) + (anywhere,) * 6,
         scratch_shapes=[
-            pltpu.SemaphoreType.DMA,
-            pltpu.SemaphoreType.DMA((depth, 2)),
-            pltpu.SemaphoreType.DMA((depth,)),
-            pltpu.SemaphoreType.DMA((depth, 7)),
-            pltpu.SemaphoreType.DMA((depth, 7)),
+            pltpu.VMEM((depth, blocks, rows, width), bf16),
+            pltpu.VMEM((depth - 1, rows, width), bf16),
+            pltpu.VMEM((rows, width), bf16),
+            pltpu.VMEM((half, rows, width), bf16),
+            pltpu.VMEM((tile, 2 * hidden), f32),
+            pltpu.VMEM((tile, hidden), f32),
+            pltpu.VMEM((tile, 128), f32),
+            pltpu.VMEM((tile, 128), f32),
+            pltpu.VMEM((tile, 128), f32),
+            pltpu.VMEM((2, half, rows, 2 * hidden), bf16),
+            pltpu.VMEM((2, half, rows, hidden), bf16),
+            pltpu.VMEM((2, half, rows, width), bf16),
+            pltpu.VMEM((2, half, rows, width), bf16),
+            dma((depth + 1,)),
+            dma((depth - 1,)), dma((depth - 1,)),
+            dma((depth, 2)), dma((depth,)),
+            dma((depth, 7)), dma((depth, 7)),
+            dma((depth, 7)), dma((depth, 7)),
+            dma, dma((2, 5)),
         ],
-        compiler_params=pltpu.CompilerParams(collective_id=cid, has_side_effects=True, vmem_limit_bytes=56 << 20),
-    )(own)
-    return out.reshape(blocks * depth * rows, width)
-
-
-def sum_kernel(rows, depth, part_ref, out_ref, mine, got_pair, got_first, got_second, got_z, keep,
-               mine_sem, ps, pr, fs, fr, ss, sr, zs, zr):
+        compiler_params=pltpu.CompilerParams(collective_id=cid, has_side_effects=True, vmem_limit_bytes=60 << 20),
+    )(attn_part, inputs, gain.reshape(1, width), cotangent, kept, w_in, w_out)
+
+
+def sum_kernel(
+    depth, part_ref, h_ref, grads_ref, gated_ref, cot_ref, out_ref, in_grad, out_grad,
+    mine, got_pair, got_first, got_second, got_z, keep, h_tile, grads_tile, gated_tile, cot_tile,
+    mine_sem, ps, pr, fs, fr, ss, sr, zs, zr, tile_sem,
+):
     f32 = jnp.float32
+    rows = part_ref.shape[2]
     ep, tp = lax.axis_index("ep"), lax.axis_index("tp")
-    pair, xn, yn, flip = plane_partners(ep)
+    pair, xn, yn = plane_partners(ep)
     parity = lax.rem(ep, 2)
     first = jnp.where(parity == 0, xn, yn)
     second = jnp.where(parity == 0, yn, xn)
     diag = xn + yn - ep
-    other = lambda b: b + pair - ep
     blocks = (first, diag, ep, second)
+    pair_slot = (3, 1, 2, 0)
     greet([(pair, tp), (xn, tp), (yn, tp)] + [(ep, lax.rem(tp + k, depth)) for k in range(1, depth)])
     steps = [(k + 1) % depth for k in range(depth)]
 
@@ -569,16 +807,15 @@
         return lax.rem(tp + steps[i], depth)
 
     def pair_copy(i, slot):
-        return remote(part_ref.at[other(blocks[slot]), chunk_of(i)], got_pair.at[i, pslot(slot)], ps.at[i, slot], pr.at[i, pslot(slot)], (pair, tp))
-
-    def pslot(slot):
-        return {0: 3, 1: 1, 2: 2, 3: 0}[slot]
+        src = part_ref.at[chunk_of(i), blocks[slot] + pair - ep]
+        to = pair_slot[slot]
+        return remote(src, got_pair.at[i, to], ps.at[i, slot], pr.at[i, to], (pair, tp))
 
     def pair_wait(i, slot):
-        return remote(part_ref.at[ep, chunk_of(i)], got_pair.at[i, slot], ps.at[i, slot], pr.at[i, slot], (pair, tp))
+        return remote(part_ref.at[0, 0], got_pair.at[i, slot], ps.at[i, slot], pr.at[i, slot], (pair, tp))
 
     def mine_copy(i, slot):
-        return pltpu.make_async_copy(part_ref.at[blocks[slot], chunk_of(i)], mine.at[i, slot], mine_sem.at[i, slot])
+        return pltpu.make_async_copy(part_ref.at[chunk_of(i), blocks[slot]], mine.at[i, slot], mine_sem.at[i, slot])
 
     def first_copy(i, slot):
         return remote(mine.at[i, slot], got_first.at[i, slot], fs.at[i, slot], fr.at[i, slot], (first, tp))
@@ -592,9 +829,10 @@
 
     def add(dst, a, b):
         def body(r, _):
-            sl = pl.ds(pl.multiple_of(r * 16, 16), 16)
-            dst[sl, :] = (a[sl, :].astype(f32) + b[sl, :].astype(f32)).astype(dst.dtype)
+            at = pl.ds(pl.multiple_of(r * 16, 16), 16)
+            dst[at, :] = (a[at, :].astype(f32) + b[at, :].astype(f32)).astype(dst.dtype)
             return 0
+
         lax.fori_loop(0, rows // 16, body, 0)
 
     for i in range(depth):
@@ -602,6 +840,14 @@
             pair_copy(i, slot).start()
         for slot in range(4):
             mine_copy(i, slot).start()
+
+    def tile_loads(c):
+        return [
+            pltpu.make_async_copy(src.at[c], dst, tile_sem.at[n])
+            for n, (src, dst) in enumerate(
+                ((h_ref, h_tile), (grads_ref, grads_tile), (gated_ref, gated_tile), (cot_ref, cot_tile))
+            )
+        ]
 
     def stage_a(i):
         for slot in range(4):
@@ -626,6 +872,42 @@
         else:
             add(keep, mine.at[i, 2], got_second.at[i])
 
+    count = h_tile.shape[0] * rows
+    width = h_tile.shape[2]
+    hidden = gated_tile.shape[2]
+
+    def weights(c):
+        for load in tile_loads(c):
+            load.wait()
+        turned = (((0,), (0,)), ((), ()))
+
+        def in_part(m, _):
+            at = pl.ds(pl.multiple_of(m * 512, 512), 512)
+            found = lax.dot_general(
+                h_tile[:, :, at].reshape(count, 512), grads_tile[...].reshape(count, 2 * hidden), turned,
+                preferred_element_type=f32,
+            )
+            in_grad[at, :] = found if c == 0 else in_grad[at, :] + found
+            return 0
+
+        lax.fori_loop(0, width // 512, in_part, 0)
+
+        def out_part(m, _):
+            at = pl.ds(pl.multiple_of(m * 512, 512), 512)
+            found = lax.dot_general(
+                gated_tile[...].reshape(count, hidden), cot_tile[:, :, at].reshape(count, 512), turned,
+                preferred_element_type=f32,
+            )
+            out_grad[:, at] = found if c == 0 else out_grad[:, at] + found
+            return 0
+
+        lax.fori_loop(0, width // 512, out_part, 0)
+        if c + 1 < depth:
+            for load in tile_loads(c + 1):
+                load.start()
+
+    for load in tile_loads(0):
+        load.start()
     for t in range(depth + 2):
         if t < depth:
             stage_a(t)
@@ -633,15 +915,17 @@
             stage_b(t - 1)
         if 0 <= t - 2 < depth:
             stage_c(t - 2)
+        if t < depth:
+            weights(t)
     for i in range(depth - 1):
         z_copy(i).wait_recv()
 
     def total(r, _):
-        sl = pl.ds(pl.multiple_of(r * 16, 16), 16)
-        v = keep[sl, :]
+        at = pl.ds(pl.multiple_of(r * 16, 16), 16)
+        value = keep[at, :]
         for k in range(depth - 1):
-            v = v + got_z[k, sl, :].astype(f32)
-        out_ref[sl, :] = v
+            value = value + got_z[k, at, :].astype(f32)
+        out_ref[at, :] = value
         return 0
 
     lax.fori_loop(0, rows // 16, total, 0)
@@ -655,28 +939,37 @@
             z_copy(i).wait_send()
 
 
-def sum_all_rows(part, blocks, depth, cid):
-    width = part.shape[-1]
-    rows = part.shape[0] // (blocks * depth)
-    bf, f32 = part.dtype, jnp.float32
-    D = pltpu.SemaphoreType.DMA
+def sum_call(part, h_all, grads, gated, cot_all, cid):
+    f32, bf16 = jnp.float32, jnp.bfloat16
+    depth, blocks, rows, width = part.shape
+    hidden = gated.shape[3]
+    dma = pltpu.SemaphoreType.DMA
+    vmem, anywhere = pl.BlockSpec(memory_space=pltpu.VMEM), pl.BlockSpec(memory_space=pl.ANY)
     return pl.pallas_call(
-        functools.partial(sum_kernel, rows, depth),
-        out_shape=jax.ShapeDtypeStruct((rows, width), f32),
-        in_specs=[pl.BlockSpec(memory_space=pl.ANY)],
-        out_specs=pl.BlockSpec(memory_space=pltpu.VMEM),
+        functools.partial(sum_kernel, depth),
+        out_shape=(
+            jax.ShapeDtypeStruct((rows, width), f32),
+            jax.ShapeDtypeStruct((width, 2 * hidden), f32),
+            jax.ShapeDtypeStruct((hidden, width), f32),
+        ),
+        in_specs=[anywhere] * 5,
+        out_specs=(vmem, vmem, vmem),
         scratch_shapes=[
-            pltpu.VMEM((depth, 4, rows, width), bf),
-            pltpu.VMEM((depth, 4, rows, width), bf),
-            pltpu.VMEM((depth, 2, rows, width), bf),
-            pltpu.VMEM((depth, rows, width), bf),
-            pltpu.VMEM((depth - 1, rows, width), bf),
+            pltpu.VMEM((depth, 4, rows, width), bf16),
+            pltpu.VMEM((depth, 4, rows, width), bf16),
+            pltpu.VMEM((depth, 2, rows, width), bf16),
+            pltpu.VMEM((depth, rows, width), bf16),
+            pltpu.VMEM((depth - 1, rows, width), bf16),
             pltpu.VMEM((rows, width), f32),
-            D((depth, 4)), D((depth, 4)), D((depth, 4)), D((depth, 2)), D((depth, 2)), D((depth,)), D((depth,)),
-            D((depth - 1,)), D((depth - 1,)),
+            pltpu.VMEM((blocks, rows, width), bf16),
+            pltpu.VMEM((blocks, rows, 2 * hidden), bf16),
+            pltpu.VMEM((blocks, rows, hidden), bf16),
+            pltpu.VMEM((blocks, rows, width), bf16),
+            dma((depth, 4)), dma((depth, 4)), dma((depth, 4)), dma((depth, 2)), dma((depth, 2)),
+            dma((depth,)), dma((depth,)), dma((depth - 1,)), dma((depth - 1,)), dma((4,)),
         ],
-        compiler_params=pltpu.CompilerParams(collective_id=cid, has_side_effects=True, vmem_limit_bytes=56 << 20),
-    )(part.reshape(blocks, depth, rows, width))
+        compiler_params=pltpu.CompilerParams(collective_id=cid, has_side_effects=True, vmem_limit_bytes=62 << 20),
+    )(part, h_all, grads, gated, cot_all)
 
 
 def padded_hidden(routed, shared):
@@ -726,7 +1019,11 @@
         (expert_ids[:, :, None] == expert_range) & (slot_ids < capacity)[:, :, None], axis=1
     ).astype(f32)
     kept_here = lax.all_to_all(kept, "ep", split_axis=1, concat_axis=0, tiled=True)
-    cot_all = lax.all_gather(cotangent, "ep", tiled=True)
+    rows_part = tokens // tp_count
+    kept_lanes = jnp.broadcast_to(
+        kept_here.reshape(ep_count, tp_count, rows_part, 1).swapaxes(0, 1),
+        (tp_count, ep_count, rows_part, 128),
+    ).astype(bf16)
 
     routed = w_expert_in.shape[3]
     shared = w_shared_in.shape[2] // ep_count
@@ -794,59 +1091,19 @@
     )
     attn_part = jnp.dot(attended, w_output, preferred_element_type=f32).astype(bf16)
 
-    attn_rows = lax.psum_scatter(attn_part, "tp", scatter_dimension=0, tiled=True).astype(f32)
-    resid_rows = lax.dynamic_slice_in_dim(resid, row_start, rows_part, 0)
+    middle, hidden_all, cot_all, hidden_grads, gated, out_part, rows_grad = experts_call(
+        attn_part, inputs, gain_ffn, cotangent, kept_lanes, w_in, w_out,
+        ep_count, tp_count, routed, shared, experts, 0,
+    )
+    ffn_grad, in_grad_w, out_grad_w = sum_call(
+        rows_grad, hidden_all, hidden_grads, gated, cot_all, 1
+    )
     cot_rows = lax.dynamic_slice_in_dim(cotangent, row_start, rows_part, 0).astype(f32)
-    middle = resid_rows + attn_rows
     inv_second = lax.rsqrt(jnp.mean(middle * middle, axis=-1, keepdims=True) + EPSILON)
     normed_second = middle * inv_second
-    hidden_rows = (normed_second * gain_ffn).astype(bf16)
-    hidden_all = gather_all(hidden_rows, ep_count, tp_count, 0)
-
-    gate_up = jnp.dot(hidden_all, w_in, preferred_element_type=f32)
-    gate_val, up_val = gate_up[:, :hidden], gate_up[:, hidden:]
     base = routed + shared
-    logits = (
-        gate_val[:, base : base + experts]
-        + gate_val[:, base + experts : base + 2 * experts]
-        + gate_val[:, base + 2 * experts : base + 3 * experts]
-    )
-    exp_logits = jnp.exp(logits - jnp.max(logits, axis=-1, keepdims=True))
-    router_probs = exp_logits / jnp.sum(exp_logits, axis=-1, keepdims=True)
-    here = (expert_range == ep_index).astype(f32)[None]
-    prob_here = jnp.sum(router_probs * here, axis=-1, keepdims=True)
-    unit_index = jnp.arange(hidden)[None]
-    is_routed = unit_index < routed
-    unit_gate = jnp.where(is_routed, prob_here * kept_here, 1.0)
-    silu_val, silu_slope = silu_parts(gate_val)
-    activated = silu_val * up_val
-    gated = (activated * unit_gate).astype(bf16)
-    out_part = jnp.dot(gated, w_out, preferred_element_type=f32).astype(bf16)
-    act_grad = jnp.einsum("td,fd->tf", cot_all, w_out, preferred_element_type=f32)
-    pair_grad = (
-        jnp.sum(jnp.where(is_routed, activated * act_grad, 0.0), axis=-1, keepdims=True) * kept_here
-    )
-    logit_grad = pair_grad * prob_here * (here - router_probs)
-    act_grad = act_grad * unit_gate
-    gate_grad = (act_grad * up_val * silu_slope).astype(bf16)
-    up_grad = (act_grad * silu_val).astype(bf16)
-    rows_grad = (
-        jnp.einsum("tf,df->td", gate_grad, w_in[:, :hidden], preferred_element_type=f32)
-        + jnp.einsum("tf,df->td", up_grad, w_in[:, hidden:], preferred_element_type=f32)
-        + jnp.einsum(
-            "te,de->td", logit_grad, w_router, precision=HIGHEST, preferred_element_type=f32
-        )
-    ).astype(bf16)
-    out_grad_w = jnp.einsum("tf,td->fd", gated, cot_all, preferred_element_type=f32)
-    in_grad_gate = jnp.einsum("td,tf->df", hidden_all, gate_grad, preferred_element_type=f32)
-    in_grad_up = jnp.einsum("td,tf->df", hidden_all, up_grad, preferred_element_type=f32)
-    router_grad = jnp.einsum(
-        "td,te->de",
-        hidden_all.astype(f32),
-        logit_grad,
-        precision=HIGHEST,
-        preferred_element_type=f32,
-    )
+    in_grad_gate, in_grad_up = in_grad_w[:, :hidden], in_grad_w[:, hidden:]
+    router_grad = in_grad_gate[:, base : base + experts]
     grad_expert_in = jnp.stack([in_grad_gate[:, :routed], in_grad_up[:, :routed]])[None]
     grad_expert_out = out_grad_w[None, :routed]
     shared_in_part = jnp.stack([in_grad_gate[:, routed:base], in_grad_up[:, routed:base]])
@@ -857,12 +1114,13 @@
         out_grad_w[routed:base].astype(bf16), "ep", split_axis=1, concat_axis=0, tiled=True
     ).astype(f32)
 
-    def sum_rows(part):
-        plane = lax.psum_scatter(part, "ep", scatter_dimension=0, tiled=True)
-        return lax.psum_scatter(plane, "tp", scatter_dimension=0, tiled=True).astype(f32)
-
-    ffn_grad = sum_all_rows(rows_grad, ep_count, tp_count, 1)
-    ffn_rows = sum_rows(out_part)
+    ffn_plane = lax.psum_scatter(
+        out_part.reshape(ep_count * tokens, model_width),
+        "ep",
+        scatter_dimension=0,
+        tiled=True,
+    )
+    ffn_rows = lax.psum_scatter(ffn_plane, "tp", scatter_dimension=0, tiled=True).astype(f32)
     block_out = lax.all_gather((middle + ffn_rows).astype(bf16), "tp", tiled=True)
     middle_grad = cot_rows + norm_back(ffn_grad, gain_ffn, normed_second, inv_second)
     gain_ffn_grad = jnp.sum(ffn_grad * normed_second, axis=0)

time: 958 us -> 903 us (0.943)
  matrix products: 238 us -> 47.7 us
  Pallas kernels: 202 us -> 292 us
  local copies, waits for them, and re-layouts: 65.3 us -> 91 us
  waiting for transfers between devices: 330 us -> 352 us
    dot_general x10 -> x0, matrix products: 191 us -> none  [the longest x1 31.6 us: body_dense(): jnp.einsum('tf,df->td', up_grad, w_in[:, hidden:], preferred_element_type...]
    pallas_call x2, Pallas kernels: 202 us -> 292 us  [the longest x1 196 us: experts_call(): pl.pallas_call(functools.partial(experts_kernel, depth, blocks, routed, s...]
    unnamed x17 -> x14, waiting for transfers between devices: 49.8 us -> 24.7 us
    all_gather x1, waiting for transfers between devices: 18.4 us -> 42 us  [body_dense(): branch_grad = lax.all_gather(middle_grad.astype(bf16), 'tp', tiled=True)]
    reduce_scatter x1, waiting for transfers between devices: 8.48 us -> 30.8 us  [body_dense(): lax.psum_scatter(hidden_part, 'tp', scatter_dimension=0, tiled=True)]
    reduce_scatter x3, waiting for transfers between devices: 132 us -> 118 us  [the longest x1 54.5 us: body_dense(): lax.psum_scatter(out_part.reshape(ep_count * tokens, model_width), 'ep',...]
    reduce_scatter x2, waiting for transfers between devices: 38.7 us -> 52.2 us  [sum_all(): plane = lax.psum_scatter(part, 'ep', scatter_dimension=0, tiled=True)]
    unnamed x140 -> x117, local copies, waits for them, and re-layouts: 36.6 us -> 35.7 us
  transfers between devices with their start and end apart: 18 -> 16, of which waited for: 12 -> 11; matrix products, arithmetic and copies ran while one was open for 21% -> 18% of each run, Pallas kernels for 12% -> 0%
where the time goes in v3:
time: 903 us; the launch traced here: 898 us
  waiting for transfers between devices  352 us (39%)
  Pallas kernels  292 us (32%)
  local copies, waits for them, and re-layouts  91 us (10%)
  other arithmetic  48.6 us (5%)
  matrix products  47.7 us (5%)
  blocking collectives  34.6 us (4%)
  between operations  18.8 us (2%)
  starting transfers between devices  13.8 us (2%)
    pallas_call x1, Pallas kernels, experts_call(): pl.pallas_call(functools.partial(experts_kernel, depth, blocks, routed, s...  196 us
    pallas_call x1, Pallas kernels, sum_call(): pl.pallas_call(functools.partial(sum_kernel, depth), out_shape=(jax.Shape...  96.1 us
    reduce_scatter x1, waiting for transfers between devices, body_dense(): lax.psum_scatter(out_part.reshape(ep_count * tokens, model_width), 'ep',...  54.5 us
    reduce_scatter x2, waiting for transfers between devices, sum_all(): plane = lax.psum_scatter(part, 'ep', scatter_dimension=0, tiled=True)  52.2 us
    reduce_scatter x1, waiting for transfers between devices, body_dense(): lax.psum_scatter(ffn_plane, 'tp', scatter_dimension=0, tiled=True)  43.5 us
    reduce_scatter x1, waiting for transfers between devices, body_dense(): lax.psum_scatter(output_w_grad.astype(bf16), 'ep', scatter_dimension=1, t...  43.2 us
    all_gather x1, waiting for transfers between devices, body_dense(): branch_grad = lax.all_gather(middle_grad.astype(bf16), 'tp', tiled=True)  42 us
    unnamed x117, local copies, waits for them, and re-layouts  35.7 us
  transfers between devices with their start and end apart: 16, of which 11 were waited for; matrix products, arithmetic and copies ran while one was open for 18% of the time, Pallas kernels for 0%

profile of v3, /device:TPU:0, one launch (start us, length us, event | category | flops | bytes accessed | tf_op | source)
XLA Modules:
  0.0 898.3 jit_solution(6431826826464100929)
XLA Ops:
  11.4 5.2 all-to-all-start
  16.7 2.1 fusion
  18.8 3.8 fusion.50
  24.2 1.8 convolution_convert_fusion.4
  26.0 3.3 reshape.253
  29.3 2.5 fusion.52
  31.8 5.0 fusion.49
  36.8 1.8 subtract_convert_fusion.4
  38.8 2.1 copy.176
  41.0 3.9 fusion.51
  51.9 2.6 convolution_convert_fusion.2.part_ref
  55.5 1.9 constant_dynamic-slice_fusion.2
  57.5 1.7 maximum_maximum_fusion.w_out_ref
  59.9 1.8 copy.178
  61.7 2.0 copy.180
  63.7 1.9 copy.147
  65.6 1.9 pad.4
  67.5 2.6 copy.181
  72.0 8.3 concatenate.33.w_in_ref
  81.0 1.6 broadcast_in_dim.28.kept_ref
  82.5 195.6 %shard_map.263 = (f32[128,2048]{1,0:T(8,128)}, bf16[4,8,128,2048]{3,2,1,0:T(8,128)(2,1)}, bf16[4,8,128,2048]{3,2,1,0:T(8,128)(2,1)}, bf16[4,8,128,1024]{3,2,1,0:...) custom-call(bf16[512,2048]{1,0:T(8,128)(2,1)} %convolution_convert_f, ...), custom_call_target="tpu_custom_call" | custom-call | tf_op jit(solution)/shard_map/pallas_call | solution.py:754
  279.5 96.1 %shard_map.264 = (f32[128,2048]{1,0:T(8,128)}, f32[2048,1024]{1,0:T(8,128)}, f32[512,2048]{1,0:T(8,128)}) custom-call(bf16[4,8,128,2048]{3,2,1,0:T(8,128)(2,1)} %get-tuple-element.26.part_ref, bf16[4,8,128,2048]{3,2,1,0:T(8,128)(2,1)} %get-tuple-element.27.h_ref, bf16[4,8,128,1024]{3,2,1,0:T(8,128)(2,1)} %get-tuple-element.28.grads_ref, ...), custom_call_target="tpu_custom_call" | custom-call | tf_op jit(solution)/shard_map/pallas_call | solution.py:948
  375.7 1.9 multiply_reduce_fusion.1
  377.5 2.8 fusion.48
  381.1 2.5 slice.109
  383.7 42.0 %all-gather.6.cloned.1.call-done = bf16[512,2048]{1,0:T(8,128)(2,1)} async-done(((bf16[128,2048]{1,0:T(8,128)(2,1)}), bf16[512,2048]{1,0:T(8,128)(2,1)}) %all-gather.6.cloned.1.call-update) | async-done | bytes 2097168 | tf_op jit(solution)/shard_map/all_gather | solution.py:1127
  425.8 3.8 convolution_convert_fusion.5
  437.0 1.8 fusion.55
  441.3 3.3 add_convert_fusion
  445.1 54.5 %reduce-scatter.13.cloned.1.call-done = bf16[512,2048]{1,0:T(8,128)(2,1)} async-done(((bf16[4096,2048]{1,0:T(8,128)(2,1)}), bf16[512,2048]{1,0:T(8,128)(2,1)}) %reduce-scatter.13.cloned.1.call-update) | async-done | bytes 2097168 | tf_op jit(solution)/shard_map/reduce_scatter | solution.py:1117
  499.7 4.8 fusion.32
  504.5 34.7 %reduce-scatter.27.cloned.1.call-done = f32[256,8]{1,0:T(8,128)} async-done(((f32[2048,8]{1,0:T(8,128)}), f32[256,8]{1,0:T(8,128)}) %reduce-scatter.27.cloned.1.call-update) | async-done | bytes 8208 | tf_op jit(solution)/shard_map/reduce_scatter | solution.py:1211
  539.3 3.3 convolution_convert_fusion.3
  542.6 4.3 convolution_convert_fusion.1
  547.1 5.0 convolution_convert_fusion
  552.2 2.4 convert_multiply_fusion
  554.6 30.8 %reduce-scatter.17.cloned.1.call-done = bf16[128,2048]{1,0:T(8,128)(2,1)} async-done(((bf16[512,2048]{1,0:T(8,128)(2,1)}), bf16[128,2048]{1,0:T(8,128)(2,1)}) %reduce-scatter.17.cloned.1.call-update) | async-done | bytes 524304 | tf_op jit(solution)/shard_map/reduce_scatter | solution.py:1186
  585.4 1.7 fusion.28
  587.1 43.5 %reduce-scatter.15.cloned.1.call-done = bf16[128,2048]{1,0:T(8,128)(2,1)} async-done(((bf16[512,2048]{1,0:T(8,128)(2,1)}), bf16[128,2048]{1,0:T(8,128)(2,1)}) %reduce-scatter.15.cloned.1.call-update) | async-done | bytes 524304 | tf_op jit(solution)/shard_map/reduce_scatter | solution.py:1123
  630.6 3.7 fusion.27
  638.9 7.3 convert.73
  648.2 3.9 all-to-all-start.2
  652.3 6.2 slice_bitcast_fusion.1
  658.5 1.9 slice_bitcast_fusion.4
  660.7 9.5 %copy.157 = bf16[2,2048,88]{2,0,1:T(2,128)(2,1)} copy(bf16[2,2048,88]{2,1,0:T(8,128)(2,1)S(1)} %pad_maximum_fusion.1) | data formatting | bytes 1441792 | tf_op jit(solution)/shard_map/stack | solution.py:1109
  670.1 17.5 %reduce-scatter.21.cloned.1.call-done = f32[256,576]{0,1:T(8,128)} async-done(((f32[2048,576]{0,1:T(8,128)}), f32[256,576]{0,1:T(8,128)}) %reduce-scatter.21.cloned.1.call-update) | async-done | bytes 589840 | tf_op jit(solution)/shard_map/reduce_scatter | solution.py:1211
  687.6 2.1 copy.174
  689.8 3.6 all-to-all-start.1
  693.4 5.9 maximum_bitcast_fusion
  699.3 6.4 copy.162
  705.7 3.7 slice_bitcast_fusion.2
  709.4 19.9 %reduce-scatter.29.cloned.1.call-done = f32[64,8]{1,0:T(8,128)} async-done(((f32[256,8]{1,0:T(8,128)}), f32[64,8]{1,0:T(8,128)}) %reduce-scatter.29.cloned.1.call-update) | async-done | bytes 2064 | tf_op jit(solution)/shard_map/reduce_scatter | solution.py:1212
  732.6 1.9 convert_bitcast_fusion
  734.5 2.2 copy.158
  736.7 30.0 %reduce-scatter.23.cloned.1.call-done = bf16[64,1024]{1,0:T(8,128)(2,1)} async-done(((bf16[512,1024]{1,0:T(8,128)(2,1)}), bf16[64,1024]{1,0:T(8,128)(2,1)}) %reduce-scatter.23.cloned.1.call-update) | async-done | bytes 131088 | tf_op jit(solution)/shard_map/reduce_scatter | solution.py:1202
  766.7 1.6 convert_element_type.184
  768.3 43.2 %reduce-scatter.25.cloned.1.call-done = bf16[512,256]{1,0:T(8,128)(2,1)} async-done(((bf16[512,2048]{1,0:T(8,128)(2,1)}), bf16[512,256]{1,0:T(8,128)(2,1)}) %reduce-scatter.25.cloned.1.call-update) | async-done | bytes 262160 | tf_op jit(solution)/shard_map/reduce_scatter | solution.py:1205
  811.5 1.8 convert_element_type.186
  813.3 22.9 %all-reduce.7 = (f32[2048]{0:T(1024)S(1)}, f32[512]{0:T(512)S(1)}, f32[2048]{0:T(1024)S(1)}) all-reduce(f32[2048]{0:T(1024)S(1)} %get-tuple-element.104, f32[512]{0:T(512)S(1)} %get-tuple-element.106, f32[2048]{0:T(1024)S(1)} %get-tuple-element.108), channel_id=5, replica_groups=mesh['ep'=8,'tp'=4] {'ep'}, use_global_device_ids=true, to_apply=%region_14.15.clone | all-reduce | flops 4608 | bytes 36864
  836.5 11.7 %all-reduce.8 = (f32[256]{0:T(256)S(1)}, f32[64]{0:T(128)S(1)}, f32[256]{0:T(256)S(1)}) all-reduce(f32[256]{0:T(256)S(1)} %dynamic-slice.5, f32[64]{0:T(128)S(1)} %dynamic-slice.9, f32[256]{0:T(256)S(1)} %dynamic-slice.13), channel_id=6, replica_groups=mesh['ep'=8,'tp'=4] {'tp'}, use_global_device_ids=true, to_apply=%region_15.16.clone | all-reduce | flops 576 | bytes 4608
  849.9 11.4 %reduce-scatter.19.cloned.1.call-done = bf16[256,768]{1,0:T(8,128)(2,1)} async-done(((bf16[2048,768]{1,0:T(8,128)(2,1)}), bf16[256,768]{1,0:T(8,128)(2,1)}) %reduce-scatter.19.cloned.1.call-update) | async-done | bytes 393232 | tf_op jit(solution)/shard_map/reduce_scatter | solution.py:1199
  861.3 1.9 convert_element_type.182
  863.2 23.3 %reduce-scatter.31.cloned.1.call-done = f32[64,576]{1,0:T(8,128)} async-done(((f32[256,576]{1,0:T(8,128)}), f32[64,576]{1,0:T(8,128)}) %reduce-scatter.31.cloned.1.call-update) | async-done | bytes 147472
  886.5 3.2 copy.198
  (188 shorter events, 40.1 us)
Async XLA Ops:
  8.0 16.2 %copy-start = (bf16[512,1024]{1,0:T(8,128)(2,1)S(1)}, bf16[512,1024]{1,0:T(8,128)(2,1)}, u32[]{:S(2)}) copy-start(bf16[512,1024]{1,0:T(8,128)(2,1)} %param.21) | copy-start | bytes 3145732
  11.4 68.8 %all-to-all-start = ((bf16[8,2,256]{2,1,0:T(2,128)(2,1)}), bf16[8,2,256]{2,1,0:T(2,128)(2,1)}, u32[]{:S(2)}, u32[]{:S(2)}) async-start(bf16[8,2,256]{2,1,0:T(2,128)(2,1)} %reshape.273), calls=%async_computation | async-start | bytes 16384 | tf_op jit(solution)/shard_map/all_to_all | solution.py:1021
  16.6 409.2 %all-gather.6.cloned.1.call-start = ((), (), s32[]{:S(2)}) async-start(), calls=%async_computation.16 | async-start | bytes 2621440 | tf_op jit(solution)/shard_map/all_gather | solution.py:1127
  16.7 20.1 %copy-start.40 = (f32[32]{0:T(128)}, f32[32]{0:T(128)S(1)}, u32[]{:S(2)}) copy-start(f32[32]{0:T(128)S(1)} %multiply_exponential_fusion) | copy-start | bytes 388
  18.8 13.0 %copy-start.36 = (f32[512]{0:T(512)}, f32[512]{0:T(512)S(1)}, u32[]{:S(2)}) copy-start(f32[512]{0:T(512)S(1)} %add_rsqrt_fusion.1) | copy-start | bytes 6148
  18.8 5.4 copy-start.38
  22.6 1.0 copy-start.5
  23.6 0.6 copy-start.34
  26.0 5.8 copy-start.3
  26.0 5.8 copy-start.31
  38.6 8.5 copy-start.21
  38.6 8.8 copy-start.24
  41.0 5.5 copy-start.7
  41.0 5.5 copy-start.8
  46.5 0.8 copy-start.26
  47.4 1.3 copy-start.16
  47.4 1.3 copy-start.18
  48.7 2.4 copy-start.1
  48.7 1.4 copy-start.12
  50.1 1.0 copy-start.32
  50.1 1.8 copy-start.44
  51.1 0.8 copy-start.45
  51.9 5.6 copy-start.15
  54.5 4.7 copy-start.28
  54.5 4.7 copy-start.29
  54.5 4.7 copy-start.30
  279.5 96.1 %copy-start.27 = (f32[2048]{0:T(1024)S(1)}, f32[2048]{0:T(1024)}, u32[]{:S(2)}) copy-start(f32[2048]{0:T(1024)} %param.23) | copy-start | bytes 24580
  380.4 119.2 %reduce-scatter.13.cloned.1.call-start = ((), (), s32[]{:S(2)}) async-start(), calls=%async_computation.13 | async-start | bytes 18874368 | tf_op jit(solution)/shard_map/reduce_scatter | solution.py:1117
  380.4 0.7 copy-start.33
  380.9 158.2 %reduce-scatter.27.cloned.1.call-start = ((), (), s32[]{:S(2)}) async-start(), calls=%async_computation.23 | async-start | bytes 1179648 | tf_op jit(solution)/shard_map/reduce_scatter | solution.py:1211
  383.7 45.9 %copy-start.13 = (bf16[512,4,128]{0,2,1:T(8,128)(2,1)S(1)}, bf16[512,4,128]{0,2,1:T(8,128)(2,1)}, u32[]{:S(2)}) copy-start(bf16[512,4,128]{0,2,1:T(8,128)(2,1)} %copy.176) | copy-start | bytes 1572868
  383.7 201.7 %reduce-scatter.17.cloned.1.call-start = ((), (), s32[]{:S(2)}) async-start(), calls=%async_computation.17 | async-start | bytes 2621440 | tf_op jit(solution)/shard_map/reduce_scatter | solution.py:1186
  425.8 3.8 copy-start.2
  430.6 1.2 copy-start.25
  430.6 1.7 copy-start.17
  430.6 1.7 copy-start.19
  433.6 1.4 copy-start.9
  435.0 0.8 copy-start.41
  435.0 1.2 copy-start.22
  435.0 1.9 copy-start.42
  436.4 2.5 copy-start.20
  437.0 2.0 copy-start.6
  437.0 2.0 copy-start.35
  437.0 2.0 copy-start.39
  438.9 1.2 copy-start.11
  439.0 2.3 copy-start.43
  440.1 0.8 copy-start.23
  444.6 55.1 %copy-start.4 = (bf16[512,2048]{1,0:T(8,128)(2,1)S(1)}, bf16[512,2048]{1,0:T(8,128)(2,1)}, u32[]{:S(2)}) copy-start(bf16[512,2048]{1,0:T(8,128)(2,1)} %resid_ref.1) | copy-start | bytes 6291460
  444.6 55.1 %copy-start.37 = (f32[512]{0:T(512)S(1)}, f32[512]{0:T(512)}, u32[]{:S(2)}) copy-start(f32[512]{0:T(512)} %copy-done.36) | copy-start | bytes 6148
  444.6 186.0 %reduce-scatter.15.cloned.1.call-start = ((), (), s32[]{:S(2)}) async-start(), calls=%async_computation.14 | async-start | bytes 2621440 | tf_op jit(solution)/shard_map/reduce_scatter | solution.py:1123
  499.6 188.0 %reduce-scatter.21.cloned.1.call-start = ((), (), s32[]{:S(2)}) async-start(), calls=%async_computation.20 | async-start | bytes 5308416 | tf_op jit(solution)/shard_map/reduce_scatter | solution.py:1211
  504.5 224.8 %reduce-scatter.29.cloned.1.call-start = ((), (), s32[]{:S(2)}) async-start(), calls=%async_computation.24 | async-start | bytes 163840 | tf_op jit(solution)/shard_map/reduce_scatter | solution.py:1212
  539.2 227.5 %reduce-scatter.23.cloned.1.call-start = ((), (), s32[]{:S(2)}) async-start(), calls=%async_computation.21 | async-start | bytes 1179648 | tf_op jit(solution)/shard_map/reduce_scatter | solution.py:1202
  542.6 268.9 %reduce-scatter.25.cloned.1.call-start = ((), (), s32[]{:S(2)}) async-start(), calls=%async_computation.22 | async-start | bytes 2359296 | tf_op jit(solution)/shard_map/reduce_scatter | solution.py:1205
  547.0 314.2 %reduce-scatter.19.cloned.1.call-start = ((), (), s32[]{:S(2)}) async-start(), calls=%async_computation.19 | async-start | bytes 3538944 | tf_op jit(solution)/shard_map/reduce_scatter | solution.py:1199
  552.1 311.1 %all-gather.4.cloned.1.call-start = ((), (), s32[]{:S(2)}) async-start(), calls=%async_computation.15 | async-start | bytes 2621440 | tf_op jit(solution)/shard_map/all_gather | solution.py:1124
  587.1 48.0 %copy-start.47 = (u32[32]{0:T(128)S(1)}, u32[32]{0:T(128)}, u32[]{:S(2)}) copy-start(u32[32]{0:T(128)} %constant.79) | copy-start | bytes 388
  587.1 49.9 %copy-start.46 = (u32[32]{0:T(128)S(1)}, u32[32]{0:T(128)}, u32[]{:S(2)}) copy-start(u32[32]{0:T(128)} %constant.83) | copy-start | bytes 388
  634.4 228.8 %all-gather.8.cloned.1.call-start = ((), (), s32[]{:S(2)}) async-start(), calls=%async_computation.18 | async-start | bytes 2621440 | tf_op jit(solution)/shard_map/all_gather | solution.py:1193
  648.2 41.6 %all-to-all-start.2 = ((bf16[88,8,256]{2,0,1:T(8,128)(2,1)}), bf16[88,8,256]{2,0,1:T(8,128)(2,1)S(1)}, u32[]{:S(2)}, u32[]{:S(2)}) async-start(bf16[88,8,256]{2,0,1:T(8,128)(2,1)} %bitcast.101), calls=%async_computation.11 | async-start | bytes 720896 | tf_op jit(solution)/shard_map/all_to_all | solution.py:1113
  652.1 234.5 %reduce-scatter.31.cloned.1.call-start = ((), (), s32[]{:S(2)}) async-start(), calls=%async_computation.25 | async-start | bytes 819200
  689.8 41.8 %all-to-all-start.1 = ((bf16[2,2048,88]{2,0,1:T(2,128)(2,1)}), bf16[2,2048,88]{2,0,1:T(2,128)(2,1)S(1)}, u32[]{:S(2)}, u32[]{:S(2)}) async-start(bf16[2,2048,88]{2,0,1:T(2,128)(2,1)} %copy.157), calls=%async_computation.10 | async-start | bytes 2097152 | tf_op jit(solution)/shard_map/all_to_all | solution.py:1110
  731.6 1.0 copy-start.10
  863.2 26.5 %copy-start.14 = (bf16[512,2048]{1,0:T(8,128)(2,1)S(1)}, bf16[512,2048]{1,0:T(8,128)(2,1)}, u32[]{:S(2)}) copy-start(bf16[512,2048]{1,0:T(8,128)(2,1)} %all-gather.8.cloned.1.call-done) | copy-start | bytes 6291460
Sparse Core Ops, SparseCore 0:
  380.5 45.2 all-gather.5
  634.5 45.1 all-gather.3
  681.2 46.1 all-gather.7
Sparse Core Ops, SparseCore 1:
  384.4 115.1 reduce-scatter.12
  503.2 35.9 reduce-scatter.26
  541.9 43.4 reduce-scatter.16
  587.8 42.7 reduce-scatter.14
  634.6 52.9 reduce-scatter.20
  690.0 39.2 reduce-scatter.28
  732.3 34.3 reduce-scatter.22
  770.4 41.1 reduce-scatter.24
  815.2 46.0 reduce-scatter.18
  864.1 22.3 reduce-scatter.30

commit v4 on v3

--- a/solution.py
+++ b/solution.py
@@ -786,9 +786,9 @@
 
 
 def sum_kernel(
-    depth, part_ref, h_ref, grads_ref, gated_ref, cot_ref, out_ref, in_grad, out_grad,
+    depth, part_ref, h_ref, grads_ref, gated_ref, cot_ref, middle_ref, gain_ref, middle_grad, branch, gain_part, in_grad, out_grad,
     mine, got_pair, got_first, got_second, got_z, keep, h_tile, grads_tile, gated_tile, cot_tile,
-    mine_sem, ps, pr, fs, fr, ss, sr, zs, zr, tile_sem,
+    own_cot, mine_sem, own_sem, ps, pr, fs, fr, ss, sr, zs, zr, tile_sem,
 ):
     f32 = jnp.float32
     rows = part_ref.shape[2]
@@ -906,6 +906,8 @@
             for load in tile_loads(c + 1):
                 load.start()
 
+    own_copy = pltpu.make_async_copy(cot_ref.at[tp, ep], own_cot, own_sem)
+    own_copy.start()
     for load in tile_loads(0):
         load.start()
     for t in range(depth + 2):
@@ -920,15 +922,25 @@
     for i in range(depth - 1):
         z_copy(i).wait_recv()
 
-    def total(r, _):
+    own_copy.wait()
+
+    def total(r, gain_sum):
         at = pl.ds(pl.multiple_of(r * 16, 16), 16)
-        value = keep[at, :]
+        u = keep[at, :]
         for k in range(depth - 1):
-            value = value + got_z[k, at, :].astype(f32)
-        out_ref[at, :] = value
-        return 0
-
-    lax.fori_loop(0, rows // 16, total, 0)
+            u = u + got_z[k, at, :].astype(f32)
+        v = middle_ref[at, :]
+        inverse = lax.rsqrt(jnp.mean(v * v, axis=-1, keepdims=True) + EPSILON)
+        v_hat = v * inverse
+        gain_sum = gain_sum + (u * v_hat)[:8] + (u * v_hat)[8:]
+        s = u * gain_ref[...]
+        back = inverse * (s - v_hat * jnp.mean(s * v_hat, axis=-1, keepdims=True))
+        found = own_cot[at, :].astype(f32) + back
+        middle_grad[at, :] = found
+        branch[at, :] = found.astype(branch.dtype)
+        return gain_sum
+
+    gain_part[...] = lax.fori_loop(0, rows // 16, total, jnp.zeros((8, width), f32))
     for i in range(depth):
         for slot in range(4):
             pair_copy(i, slot).wait_send()
@@ -939,7 +951,7 @@
             z_copy(i).wait_send()
 
 
-def sum_call(part, h_all, grads, gated, cot_all, cid):
+def sum_call(part, h_all, grads, gated, cot_all, middle, gain, cid):
     f32, bf16 = jnp.float32, jnp.bfloat16
     depth, blocks, rows, width = part.shape
     hidden = gated.shape[3]
@@ -949,11 +961,13 @@
         functools.partial(sum_kernel, depth),
         out_shape=(
             jax.ShapeDtypeStruct((rows, width), f32),
+            jax.ShapeDtypeStruct((rows, width), bf16),
+            jax.ShapeDtypeStruct((8, width), f32),
             jax.ShapeDtypeStruct((width, 2 * hidden), f32),
             jax.ShapeDtypeStruct((hidden, width), f32),
         ),
-        in_specs=[anywhere] * 5,
-        out_specs=(vmem, vmem, vmem),
+        in_specs=[anywhere] * 5 + [vmem, vmem],
+        out_specs=(vmem,) * 5,
         scratch_shapes=[
             pltpu.VMEM((depth, 4, rows, width), bf16),
             pltpu.VMEM((depth, 4, rows, width), bf16),
@@ -965,11 +979,540 @@
             pltpu.VMEM((blocks, rows, 2 * hidden), bf16),
             pltpu.VMEM((blocks, rows, hidden), bf16),
             pltpu.VMEM((blocks, rows, width), bf16),
-            dma((depth, 4)), dma((depth, 4)), dma((depth, 4)), dma((depth, 2)), dma((depth, 2)),
+            pltpu.VMEM((rows, width), bf16),
+            dma((depth, 4)), dma, dma((depth, 4)), dma((depth, 4)), dma((depth, 2)), dma((depth, 2)),
             dma((depth,)), dma((depth,)), dma((depth - 1,)), dma((depth - 1,)), dma((4,)),
         ],
         compiler_params=pltpu.CompilerParams(collective_id=cid, has_side_effects=True, vmem_limit_bytes=62 << 20),
-    )(part, h_all, grads, gated, cot_all)
+    )(part, h_all, grads, gated, cot_all, middle, gain.reshape(1, width))
+
+
+def line_gather(ref, own, send_sem, recv_sem, ep, tp, depth):
+    up, down = jnp.minimum(tp + 1, depth - 1), jnp.maximum(tp - 1, 0)
+    order = line_order(tp)
+
+    def along(k, way, to):
+        chunk = order[k]
+        src = own if k == 0 else ref.at[chunk]
+        return remote(src, ref.at[chunk], send_sem.at[chunk, way], recv_sem.at[chunk], (ep, to))
+
+    def each_way(k, act):
+        @pl.when((order[k] <= tp) & (tp < depth - 1))
+        def _():
+            act(along(k, 0, up))
+
+        @pl.when((order[k] >= tp) & (tp > 0))
+        def _():
+            act(along(k, 1, down))
+
+    def pass_on(k):
+        each_way(k, lambda copy: copy.start())
+
+    def await_chunk(k):
+        along(k, 0, up).wait_recv()
+
+    def drain():
+        for k in range(depth):
+            each_way(k, lambda copy: copy.wait_send())
+
+    return pass_on, await_chunk, drain
+
+
+def add_rows(dst, a, b):
+    def body(r, _):
+        at = pl.ds(pl.multiple_of(r * 16, 16), 16)
+        dst[at, :] = (a[at, :].astype(jnp.float32) + b[at, :].astype(jnp.float32)).astype(dst.dtype)
+        return 0
+
+    lax.fori_loop(0, dst.shape[0] // 16, body, 0)
+
+
+def turn(slab, table, sign):
+    cosine, front, second = table
+    return slab * cosine + sign * (pltpu.roll(slab, 96, 1) * front + pltpu.roll(slab, 32, 1) * second)
+
+
+def tail_kernel(
+    depth, heads,
+    branch_ref, middle_grad_ref, middle_ref, part_ref, router_ref, gain_part_ref, inputs_ref,
+    w_output, w_query, w_latent, w_up, hidden_ref, qn_ref, qr_ref, kv_ref, kr_ref, attended, latent_in, compressed,
+    tables, gain_latent, gain_attn,
+    block_ref, grad_in_ref, gains_ref, w_sum_ref, latent_sum_ref, landed, w_all,
+    branch, load, held_rows, got_first, got_second, got_z, hidden_part, got_h, row_sum,
+    d_out, d_kr, q_grad, kv_grad, l_grad, u_grad, w_stage, w_pair, w_first, w_second, w_z, resid, own_grad, own_block, gains,
+    load_sem, ps, pr, fs, fr, ss, sr, zs, zr, bs, br, hs, hr, gs, gr, os, orr,
+    wps, wpr, wfs, wfr, wss, wsr, wzs, wzr, as_, ar, misc_sem, stage_sem,
+):
+    f32, bf16 = jnp.float32, jnp.bfloat16
+    ep, tp = lax.axis_index("ep"), lax.axis_index("tp")
+    pair, xn, yn = plane_partners(ep)
+    parity = lax.rem(ep, 2)
+    first = jnp.where(parity == 0, xn, yn)
+    second = jnp.where(parity == 0, yn, xn)
+    diag = xn + yn - ep
+    blocks = (first, diag, ep, second)
+    pair_slot = (3, 1, 2, 0)
+    rows, width = middle_ref.shape
+    tokens = hidden_ref.shape[0]
+    order = line_order(tp)
+    score_scale = (NOPE + ROPE) ** (-0.5)
+    greet([(pair, tp), (xn, tp), (yn, tp)] + [(ep, lax.rem(tp + k, depth)) for k in range(1, depth)])
+
+    branch_on, branch_wait, branch_drain = line_gather(branch, branch_ref, bs, br, ep, tp, depth)
+    grad_on, grad_wait, grad_drain = line_gather(grad_in_ref, own_grad, gs, gr, ep, tp, depth)
+    block_on, block_wait, block_drain = line_gather(block_ref, own_block, os, orr, ep, tp, depth)
+
+    steps = [(k + 1) % depth for k in range(depth)]
+
+    def chunk_of(i):
+        return lax.rem(tp + steps[i], depth)
+
+    def pair_copy(i, slot):
+        src = part_ref.at[blocks[slot] + pair - ep, chunk_of(i)]
+        to = pair_slot[slot]
+        return remote(src, landed.at[i, to], ps.at[i, slot], pr.at[i, to], (pair, tp))
+
+    def pair_wait(i, slot):
+        return remote(part_ref.at[0, 0], landed.at[i, slot], ps.at[i, slot], pr.at[i, slot], (pair, tp))
+
+    def loads(i, slot):
+        at = slot % 2
+        return (
+            pltpu.make_async_copy(part_ref.at[blocks[slot], chunk_of(i)], load.at[at, 0], load_sem.at[at, 0]),
+            pltpu.make_async_copy(landed.at[i, slot], load.at[at, 1], load_sem.at[at, 1]),
+        )
+
+    def first_copy(i, slot):
+        return remote(held_rows.at[i % 2, slot], got_first.at[i, slot], fs.at[i, slot], fr.at[i, slot], (first, tp))
+
+    def second_copy(i):
+        return remote(held_rows.at[i % 2, 3], got_second.at[i], ss.at[i], sr.at[i], (second, tp))
+
+    def z_copy(i):
+        k = steps[i]
+        src = held_rows.at[i % 2, 2]
+        return remote(src, got_z.at[k - 1], zs.at[k - 1], zr.at[k - 1], (ep, lax.rem(tp + k, depth)))
+
+    def start_loads(i, slot):
+        pair_wait(i, slot).wait_recv()
+        for copy in loads(i, slot):
+            copy.start()
+
+    def stage_a(i):
+        if i >= 2:
+            for slot in range(2):
+                first_copy(i - 2, slot).wait_send()
+            second_copy(i - 2).wait_send()
+            z_copy(i - 2).wait_send()
+        start_loads(i, 0)
+        for slot in range(4):
+            if slot < 3:
+                start_loads(i, slot + 1)
+            for copy in loads(i, slot):
+                copy.wait()
+            add_rows(held_rows.at[i % 2, slot], load.at[slot % 2, 0], load.at[slot % 2, 1])
+            if slot < 2:
+                first_copy(i, slot).start()
+
+    def stage_b(i):
+        first_copy(i, 1).wait_recv()
+        add_rows(held_rows.at[i % 2, 3], held_rows.at[i % 2, 3], got_first.at[i, 1])
+        second_copy(i).start()
+        first_copy(i, 0).wait_recv()
+        add_rows(held_rows.at[i % 2, 2], held_rows.at[i % 2, 2], got_first.at[i, 0])
+
+    def stage_c(i):
+        second_copy(i).wait_recv()
+        if i < depth - 1:
+            add_rows(held_rows.at[i % 2, 2], held_rows.at[i % 2, 2], got_second.at[i])
+            z_copy(i).start()
+        else:
+            add_rows(row_sum, held_rows.at[i % 2, 2], got_second.at[i])
+
+    def w_pair_copy(slot):
+        to = pair_slot[slot]
+        return remote(w_all.at[blocks[slot] + pair - ep], w_pair.at[to], wps.at[slot], wpr.at[to], (pair, tp))
+
+    def w_pair_wait(slot):
+        return remote(w_all.at[0], w_pair.at[slot], wps.at[slot], wpr.at[slot], (pair, tp))
+
+    def w_first_copy(slot):
+        return remote(w_pair.at[slot], w_first.at[slot], wfs.at[slot], wfr.at[slot], (first, tp))
+
+    def w_second_copy():
+        return remote(w_pair.at[3], w_second, wss, wsr, (second, tp))
+
+    def w_load(slot):
+        return pltpu.make_async_copy(w_all.at[blocks[slot]], w_stage.at[slot % 2], stage_sem.at[slot % 2])
+
+    def w_stage_a():
+        for slot in range(4):
+            if slot < 3:
+                w_load(slot + 1).start()
+            w_pair_wait(slot).wait_recv()
+            w_load(slot).wait()
+            add_rows(w_pair.at[slot], w_pair.at[slot], w_stage.at[slot % 2])
+            if slot < 2:
+                w_first_copy(slot).start()
+
+    def w_stage_b():
+        w_first_copy(1).wait_recv()
+        add_rows(w_pair.at[3], w_pair.at[3], w_first.at[1])
+        w_second_copy().start()
+        w_first_copy(0).wait_recv()
+        add_rows(w_pair.at[2], w_pair.at[2], w_first.at[0])
+
+    def w_stage_c():
+        w_second_copy().wait_recv()
+        add_rows(w_sum_ref, w_pair.at[2], w_second)
+
+    def h_copy(k):
+        to = lax.rem(tp + k, depth)
+        return remote(hidden_part.at[to], got_h.at[k - 1], hs.at[k - 1], hr.at[k - 1], (ep, to))
+
+    branch_on(0)
+    branch[tp] = branch_ref[...]
+    for i in range(depth):
+        for slot in (3, 1, 2, 0):
+            pair_copy(i, slot).start()
+    own_rows = pl.ds(pl.multiple_of(tp * rows, rows), rows)
+    resid_copy = pltpu.make_async_copy(inputs_ref.at[own_rows], resid, misc_sem.at[0])
+    resid_copy.start()
+
+    stage_a(0)
+    branch_wait(1)
+    branch_on(1)
+    stage_a(1)
+    branch_wait(2)
+    branch_on(2)
+    stage_b(0)
+    branch_wait(3)
+    branch_on(3)
+
+    turned, across = (((0,), (0,)), ((), ())), (((1,), (1,)), ((), ()))
+
+    def dot(a, b, dims=(((1,), (0,)), ((), ()))):
+        return lax.dot_general(a, b, dims, preferred_element_type=f32)
+
+    for c in range(depth):
+        d_out[c * rows : (c + 1) * rows, :] = dot(branch[c], w_output[...], across).astype(bf16)
+
+    lanes = lax.broadcasted_iota(jnp.int32, (1, 128), 1)
+    halves = tokens // BLOCK
+
+    def head(h, even):
+        mine = (lanes < 64) if even else (lanes >= 64)
+        at_q = pl.ds(pl.multiple_of(h * NOPE, 128), 128)
+        at_r = pl.ds(pl.multiple_of(lax.div(h, 2) * 128, 128), 128)
+        at_k = pl.ds(pl.multiple_of(h * 256, 128), 128)
+        at_v = pl.ds(pl.multiple_of(h * 256 + 128, 128), 128)
+        kv_sum = [None, None]
+        for b in reversed(range(halves)):
+            own = slice(b * BLOCK, (b + 1) * BLOCK)
+            keys = slice(0, (b + 1) * BLOCK)
+            qn, qr = qn_ref[own, at_q], qr_ref[own, at_r]
+            kn, kr = kv_ref[keys, at_k], kr_ref[0 if even else 1, keys, :]
+            scores = (dot(qn, kn, across) + dot(qr, kr, across)) * score_scale
+            exps = jnp.exp(scores - jnp.max(scores, axis=-1, keepdims=True))
+            probs = exps / jnp.sum(exps, axis=-1, keepdims=True)
+            grad = d_out[own, at_q]
+            prob_part = dot(grad, kv_ref[keys, at_v], across)
+            score_grad = (probs * (prob_part - jnp.sum(probs * prob_part, axis=-1, keepdims=True))).astype(bf16)
+            found = (dot(score_grad, qn, turned) * score_scale, dot(probs.astype(bf16), grad, turned))
+            r_grad = jnp.where(mine, dot(score_grad, qr, turned) * score_scale, 0.0)
+            for n, at in enumerate((at_k, at_v)):
+                if b < halves - 1:
+                    kv_sum[n] = kv_sum[n] + found[n]
+                else:
+                    kv_sum[n] = found[n]
+                kv_grad[own, at] = kv_sum[n][b * BLOCK :].astype(bf16)
+                if b > 0:
+                    kv_sum[n] = kv_sum[n][: b * BLOCK]
+            d_kr[keys, :] = d_kr[keys, :] + r_grad
+            q_grad[own, at_q] = (dot(score_grad, kn) * score_scale).astype(bf16)
+            yield own, at_r, dot(score_grad, kr) * score_scale
+
+    d_kr[...] = jnp.zeros_like(d_kr)
+
+    def head_pair(p, _):
+        evens = list(head(2 * p, True))
+        odds = list(head(2 * p + 1, False))
+        at = pl.ds(pl.multiple_of(heads * NOPE + p * 128, 128), 128)
+        for (own, _, even_part), (_, _, odd_part) in zip(evens, odds):
+            table = tuple(tables[n, own, :] for n in range(3))
+            q_grad[own, at] = turn(even_part + odd_part, table, -1.0).astype(bf16)
+        return 0
+
+    lax.fori_loop(0, heads // 2, head_pair, 0)
+    stage_c(0)
+    stage_b(1)
+    stage_a(2)
+
+    latent_back = dot(kv_grad[...], w_up[...], across)
+    held = compressed[...]
+    inverse = lax.rsqrt(jnp.mean(held * held, axis=-1, keepdims=True) + EPSILON)
+    normed = held * inverse
+    gain_latent_part = jnp.sum(latent_back * normed, axis=0, keepdims=True)
+    scaled = latent_back * gain_latent[...]
+    rank = held.shape[1]
+    l_grad[:, :rank] = (inverse * (scaled - normed * jnp.mean(scaled * normed, axis=-1, keepdims=True))).astype(bf16)
+    rope = d_kr[...] + pltpu.roll(d_kr[...], 64, 1)
+    rope = turn(rope, tuple(tables[n] for n in range(3)), -1.0)
+    l_grad[:, rank:] = jnp.where(lanes < 64, rope, 0.0).astype(bf16)
+
+    for n in range(0, width, 512):
+        part = dot(q_grad[...], w_query[n : n + 512, :], across) + dot(l_grad[...], w_latent[n : n + 512, :], across)
+        hidden_part[:, :, n : n + 512] = part.astype(bf16).reshape(depth, rows, 512)
+    for k in range(1, depth):
+        h_copy(k).start()
+
+    stage_c(1)
+    stage_b(2)
+    stage_a(3)
+
+    q_cols, l_cols = q_grad.shape[1], l_grad.shape[1]
+    o_rows = attended.shape[1]
+    count = w_all.shape[0]
+    w_rows = w_all.shape[1]
+    o_cols = width // count
+    u_rows = rank // count
+    u_cols = w_up.shape[1]
+    o_start = q_cols + l_cols
+    u_start = o_start + o_rows * o_cols // w_rows
+    u_wide = u_rows * u_cols // w_rows
+
+    u_grad[...] = dot(latent_in[...], kv_grad[...], turned).astype(bf16)
+
+    def w_store(b):
+        slot = lax.rem(b, 2)
+        return pltpu.make_async_copy(w_stage.at[slot], w_all.at[b], stage_sem.at[slot])
+
+    def w_block(b, _):
+        slot = lax.rem(b, 2)
+
+        @pl.when(b >= 2)
+        def _():
+            w_store(b - 2).wait()
+
+        at = pl.ds(pl.multiple_of(b * w_rows, 256), w_rows)
+        own = hidden_ref[:, at]
+        w_stage[slot, :, 0:q_cols] = dot(own, q_grad[...], turned).astype(bf16)
+        found = dot(own, l_grad[...], turned)
+        w_stage[slot, :, q_cols : q_cols + rank] = found[:, :rank].astype(bf16)
+        w_stage[slot, :, q_cols + rank : o_start] = found[:, rank:].astype(bf16) + router_ref[at, :]
+        cols = pl.ds(pl.multiple_of(b * o_cols, 256), o_cols)
+        found = dot(attended[...], branch[:, :, cols].reshape(tokens, o_cols), turned)
+        for n in range(o_rows // w_rows):
+            w_stage[slot, :, o_start + n * o_cols : o_start + (n + 1) * o_cols] = (
+                found[n * w_rows : (n + 1) * w_rows].astype(bf16)
+            )
+        u_at = pl.ds(pl.multiple_of(b * u_rows, u_rows), u_rows)
+        for n in range(u_cols // u_wide):
+            w_stage[slot, n * u_rows : (n + 1) * u_rows, u_start : u_start + u_wide] = (
+                u_grad[u_at, n * u_wide : (n + 1) * u_wide]
+            )
+        w_store(b).start()
+        return 0
+
+    lax.fori_loop(0, count, w_block, 0)
+    w_store(count - 2).wait()
+    w_store(count - 1).wait()
+    for slot in (3, 1, 2, 0):
+        w_pair_copy(slot).start()
+    w_load(0).start()
+
+    stage_b(3)
+    stage_c(2)
+    w_stage_a()
+    stage_c(3)
+
+    resid_copy.wait()
+    for k in range(1, depth):
+        h_copy(k).wait_recv()
+
+    def input_rows(r, gain_sum):
+        at = pl.ds(pl.multiple_of(r * 16, 16), 16)
+        u = hidden_part[tp, at, :].astype(f32)
+        for k in range(depth - 1):
+            u = u + got_h[k, at, :].astype(f32)
+        v = resid[at, :].astype(f32)
+        inv = lax.rsqrt(jnp.mean(v * v, axis=-1, keepdims=True) + EPSILON)
+        v_hat = v * inv
+        gain_sum = gain_sum + (u * v_hat)[:8] + (u * v_hat)[8:]
+        s = u * gain_attn[...]
+        back = inv * (s - v_hat * jnp.mean(s * v_hat, axis=-1, keepdims=True))
+        own_grad[at, :] = (middle_grad_ref[at, :] + back).astype(bf16)
+        return gain_sum
+
+    gain_sum = lax.fori_loop(0, rows // 16, input_rows, jnp.zeros((8, width), f32))
+    grad_on(0)
+    own_grad_copy = pltpu.make_async_copy(own_grad, grad_in_ref.at[tp], misc_sem.at[1])
+    own_grad_copy.start()
+    w_stage_b()
+    for i in range(depth - 1):
+        z_copy(i).wait_recv()
+
+    def block_rows(r, _):
+        at = pl.ds(pl.multiple_of(r * 16, 16), 16)
+        value = middle_ref[at, :] + row_sum[at, :]
+        for k in range(depth - 1):
+            value = value + got_z[k, at, :].astype(f32)
+        own_block[at, :] = value.astype(bf16)
+        return 0
+
+    lax.fori_loop(0, rows // 16, block_rows, 0)
+    block_on(0)
+    own_block_copy = pltpu.make_async_copy(own_block, block_ref.at[tp], misc_sem.at[2])
+    own_block_copy.start()
+
+    gains[0] = jnp.zeros_like(gains[0])
+    gains[0, 0:1, :] = jnp.sum(gain_sum, axis=0, keepdims=True)
+    gains[0, 1:2, :] = jnp.sum(gain_part_ref[...], axis=0, keepdims=True)
+    gains[0, 2:3, 0:rank] = gain_latent_part
+    flip_1 = tp + 1 - 2 * lax.rem(tp, 2)
+    flip_2 = tp + 2 - 4 * lax.div(tp, 2)
+    partners = ((pair, tp), (xn, tp), (yn, tp), (ep, flip_1), (ep, flip_2))
+
+    def gain_copy(n):
+        return remote(gains.at[2 * n], gains.at[2 * n + 1], as_.at[n], ar.at[n], partners[n])
+
+    def gain_step(n):
+        gain_copy(n).wait_recv()
+        total = gains[2 * n] + gains[2 * n + 1]
+        if n + 1 < len(partners):
+            gains[2 * n + 2] = total
+            gain_copy(n + 1).start()
+        else:
+            gains_ref[...] = total
+
+    gain_copy(0).start()
+    gain_step(0)
+    gain_step(1)
+    w_stage_c()
+    w_part = w_rows // depth
+
+    def w_z_copy(k):
+        to = lax.rem(tp + k, depth)
+        src = w_pair.at[1, pl.ds(pl.multiple_of(to * w_part, w_part), w_part), pl.ds(q_cols, l_cols)]
+        return remote(src, w_z.at[k - 1], wzs.at[k - 1], wzr.at[k - 1], (ep, to))
+
+    w_first_copy(1).wait_send()
+    w_pair[1, :, q_cols:o_start] = w_sum_ref[:, q_cols:o_start].astype(bf16)
+    for k in range(1, depth):
+        w_z_copy(k).start()
+    gain_step(2)
+    grad_wait(1)
+    grad_on(1)
+    block_wait(1)
+    block_on(1)
+    gain_step(3)
+    gain_step(4)
+    for k in range(1, depth):
+        w_z_copy(k).wait_recv()
+    own = pl.ds(pl.multiple_of(tp * w_part, w_part), w_part)
+    total = w_sum_ref[own, q_cols:o_start]
+    for k in range(depth - 1):
+        total = total + w_z[k].astype(f32)
+    latent_sum_ref[...] = total
+    for k in range(2, depth):
+        grad_wait(k)
+        grad_on(k)
+        block_wait(k)
+        block_on(k)
+
+    own_grad_copy.wait()
+    own_block_copy.wait()
+    branch_drain()
+    grad_drain()
+    block_drain()
+    for i in range(depth):
+        for slot in range(4):
+            pair_copy(i, slot).wait_send()
+        if i >= depth - 2:
+            for slot in range(2):
+                first_copy(i, slot).wait_send()
+            second_copy(i).wait_send()
+            if i < depth - 1:
+                z_copy(i).wait_send()
+    for slot in range(4):
+        w_pair_copy(slot).wait_send()
+    w_first_copy(0).wait_send()
+    w_second_copy().wait_send()
+    for k in range(1, depth):
+        h_copy(k).wait_send()
+        w_z_copy(k).wait_send()
+    for n in range(len(partners)):
+        gain_copy(n).wait_send()
+
+
+def tail_call(
+    branch, middle_grad, middle, out_part, router, gain_part, inputs, w_output, w_query, w_latent, w_up,
+    hidden, qn, qr, kv, kr, attended, latent_in, compressed, tables, gain_latent, gain_attn,
+    heads, cid,
+):
+    f32, bf16 = jnp.float32, jnp.bfloat16
+    blocks, depth, rows, width = out_part.shape
+    tokens = hidden.shape[0]
+    rank = compressed.shape[1]
+    q_cols, l_cols = w_query.shape[1], w_latent.shape[1]
+    w_rows = width // blocks
+    w_cols = q_cols + l_cols + w_output.shape[0] + rank * w_up.shape[1] // width
+    dma = pltpu.SemaphoreType.DMA
+    vmem, anywhere = pl.BlockSpec(memory_space=pltpu.VMEM), pl.BlockSpec(memory_space=pl.ANY)
+    return pl.pallas_call(
+        functools.partial(tail_kernel, depth, heads),
+        out_shape=(
+            jax.ShapeDtypeStruct((depth, rows, width), bf16),
+            jax.ShapeDtypeStruct((depth, rows, width), bf16),
+            jax.ShapeDtypeStruct((8, width), f32),
+            jax.ShapeDtypeStruct((w_rows, w_cols), f32),
+            jax.ShapeDtypeStruct((w_rows // depth, l_cols), f32),
+            jax.ShapeDtypeStruct((depth, 4, rows, width), bf16),
+            jax.ShapeDtypeStruct((blocks, w_rows, w_cols), bf16),
+        ),
+        in_specs=[vmem, vmem, vmem, anywhere, vmem, vmem, anywhere] + [vmem] * 15,
+        out_specs=(anywhere, anywhere, vmem, vmem, vmem, anywhere, anywhere),
+        scratch_shapes=[
+            pltpu.VMEM((depth, rows, width), bf16),
+            pltpu.VMEM((2, 2, rows, width), bf16),
+            pltpu.VMEM((2, 4, rows, width), bf16),
+            pltpu.VMEM((depth, 2, rows, width), bf16),
+            pltpu.VMEM((depth, rows, width), bf16),
+            pltpu.VMEM((depth - 1, rows, width), bf16),
+            pltpu.VMEM((depth, rows, width), bf16),
+            pltpu.VMEM((depth - 1, rows, width), bf16),
+            pltpu.VMEM((rows, width), f32),
+            pltpu.VMEM((tokens, heads * VDIM), bf16),
+            pltpu.VMEM((tokens, 128), f32),
+            pltpu.VMEM((tokens, q_cols), bf16),
+            pltpu.VMEM((tokens, heads * (NOPE + VDIM)), bf16),
+            pltpu.VMEM((tokens, l_cols), bf16),
+            pltpu.VMEM((rank, heads * (NOPE + VDIM)), bf16),
+            pltpu.VMEM((2, w_rows, w_cols), bf16),
+            pltpu.VMEM((4, w_rows, w_cols), bf16),
+            pltpu.VMEM((2, w_rows, w_cols), bf16),
+            pltpu.VMEM((w_rows, w_cols), bf16),
+            pltpu.VMEM((depth - 1, w_rows // depth, l_cols), bf16),
+            pltpu.VMEM((rows, width), bf16),
+            pltpu.VMEM((rows, width), bf16),
+            pltpu.VMEM((rows, width), bf16),
+            pltpu.VMEM((10, 8, width), f32),
+            dma((2, 2)),
+            dma((depth, 4)), dma((depth, 4)), dma((depth, 2)), dma((depth, 2)), dma((depth,)), dma((depth,)),
+            dma((depth - 1,)), dma((depth - 1,)),
+            dma((depth, 2)), dma((depth,)),
+            dma((depth - 1,)), dma((depth - 1,)),
+            dma((depth, 2)), dma((depth,)),
+            dma((depth, 2)), dma((depth,)),
+            dma((4,)), dma((4,)), dma((2,)), dma((2,)), dma, dma, dma((depth - 1,)), dma((depth - 1,)),
+            dma((5,)), dma((5,)), dma((3,)), dma((2,)),
+        ],
+        compiler_params=pltpu.CompilerParams(collective_id=cid, has_side_effects=True, vmem_limit_bytes=63 << 20),
+    )(
+        branch, middle_grad, middle, out_part, router, gain_part, inputs, w_output, w_query, w_latent, w_up,
+        hidden, qn, qr, kv, kr, attended, latent_in, compressed, tables,
+        gain_latent.reshape(1, rank), gain_attn.reshape(1, width),
+    )
 
 
 def padded_hidden(routed, shared):
@@ -1012,7 +1555,6 @@
     qk_width = NOPE + ROPE
     score_scale = qk_width ** (-0.5)
     rows_part = tokens // tp_count
-    row_start = tp_index * rows_part
 
     expert_range = jnp.arange(experts, dtype=jnp.int32)
     kept = jnp.any(
@@ -1053,39 +1595,52 @@
     normed_first = resid * inv_first
     hidden_attn = (normed_first * gain_attn).astype(bf16)
     cosine, sine_table = angles(tokens, ROPE)
-    query_raw = jnp.dot(hidden_attn, w_query, preferred_element_type=f32).reshape(
-        tokens, heads_here, qk_width
-    )
-    query_rot = jnp.concatenate(
+    zero = jnp.zeros_like(sine_table)
+    tables = jnp.stack(
         [
-            query_raw[..., :NOPE],
-            rotate(query_raw[..., NOPE:], cosine[:, None], sine_table[:, None]),
+            jnp.tile(cosine, (1, 4)),
+            jnp.tile(jnp.concatenate([-sine_table, zero], axis=1), (1, 2)),
+            jnp.tile(jnp.concatenate([zero, sine_table], axis=1), (1, 2)),
+        ]
+    )
+    by_head = w_query.reshape(model_width, heads_here, qk_width)
+    w_query_sorted = jnp.concatenate(
+        [
+            by_head[..., :NOPE].reshape(model_width, heads_here * NOPE),
+            by_head[..., NOPE:].reshape(model_width, heads_here * ROPE),
         ],
-        axis=-1,
+        axis=1,
+    )
+    w_latent_wide = jnp.pad(w_latent, ((0, 0), (0, 128 - ROPE)))
+    query_raw = jnp.dot(hidden_attn, w_query_sorted, preferred_element_type=f32)
+    query_nope = query_raw[:, : heads_here * NOPE].astype(bf16)
+    query_rope = rotate(
+        query_raw[:, heads_here * NOPE :].reshape(tokens, heads_here, ROPE),
+        cosine[:, None],
+        sine_table[:, None],
     ).astype(bf16)
     latent = jnp.dot(hidden_attn, w_latent, preferred_element_type=f32)
     compressed = latent[:, :KV_RANK]
     inv_latent = lax.rsqrt(jnp.mean(compressed * compressed, axis=-1, keepdims=True) + EPSILON)
-    normed_latent = compressed * inv_latent
-    latent_in = (normed_latent * gain_latent).astype(bf16)
+    latent_in = (compressed * inv_latent * gain_latent).astype(bf16)
     key_rope = rotate(latent[:, KV_RANK:], cosine, sine_table).astype(bf16)
-    key_value = (
-        jnp.dot(latent_in, w_latent_up, preferred_element_type=f32)
-        .astype(bf16)
-        .reshape(tokens, heads_here, NOPE + VDIM)
-    )
-    key_nope = key_value[..., :NOPE]
-    values = key_value[..., NOPE:]
+    key_pair = jnp.stack(
+        [jnp.pad(key_rope, ((0, 0), (0, ROPE))), jnp.pad(key_rope, ((0, 0), (ROPE, 0)))]
+    )
+    key_value = jnp.dot(latent_in, w_latent_up, preferred_element_type=f32).astype(bf16)
+    per_head = key_value.reshape(tokens, heads_here, NOPE + VDIM)
     block_ids = jnp.arange(tokens) // BLOCK
     allowed = block_ids[None, :] <= block_ids[:, None]
-    scores = attention_scores(query_rot, key_nope, key_rope, score_scale, allowed)
-    row_peak = jnp.max(scores, axis=-1, keepdims=True)
-    exp_scores = jnp.exp(scores - row_peak)
-    totals = jnp.sum(exp_scores, axis=-1, keepdims=True)
-    attn_probs = exp_scores / totals
-    log_total = row_peak + jnp.log(totals)
+    query_rot = jnp.concatenate(
+        [query_nope.reshape(tokens, heads_here, NOPE), query_rope], axis=-1
+    )
+    scores = attention_scores(query_rot, per_head[..., :NOPE], key_rope, score_scale, allowed)
+    exp_scores = jnp.exp(scores - jnp.max(scores, axis=-1, keepdims=True))
+    attn_probs = exp_scores / jnp.sum(exp_scores, axis=-1, keepdims=True)
     attended = (
-        jnp.einsum("hqk,khd->qhd", attn_probs.astype(bf16), values, preferred_element_type=f32)
+        jnp.einsum(
+            "hqk,khd->qhd", attn_probs.astype(bf16), per_head[..., NOPE:], preferred_element_type=f32
+        )
         .astype(bf16)
         .reshape(tokens, heads_here * VDIM)
     )
@@ -1095,15 +1650,20 @@
         attn_part, inputs, gain_ffn, cotangent, kept_lanes, w_in, w_out,
         ep_count, tp_count, routed, shared, experts, 0,
     )
-    ffn_grad, in_grad_w, out_grad_w = sum_call(
-        rows_grad, hidden_all, hidden_grads, gated, cot_all, 1
-    )
-    cot_rows = lax.dynamic_slice_in_dim(cotangent, row_start, rows_part, 0).astype(f32)
-    inv_second = lax.rsqrt(jnp.mean(middle * middle, axis=-1, keepdims=True) + EPSILON)
-    normed_second = middle * inv_second
+    middle_grad, branch, gain_ffn_part, in_grad_w, out_grad_w = sum_call(
+        rows_grad, hidden_all, hidden_grads, gated, cot_all, middle, gain_ffn, 1
+    )
     base = routed + shared
     in_grad_gate, in_grad_up = in_grad_w[:, :hidden], in_grad_w[:, hidden:]
-    router_grad = in_grad_gate[:, base : base + experts]
+    router_wide = jnp.pad(
+        in_grad_gate[:, base : base + experts], ((0, 0), (ROPE, 128 - ROPE - experts))
+    ).astype(bf16)
+    block_out, grad_inputs, gains, w_sum, latent_sum, _, _ = tail_call(
+        branch, middle_grad, middle, out_part, router_wide, gain_ffn_part, inputs,
+        w_output, w_query_sorted, w_latent_wide, w_latent_up, hidden_attn,
+        query_nope, query_rope.reshape(tokens, heads_here * ROPE), key_value, key_pair,
+        attended, latent_in, compressed, tables, gain_latent, gain_attn, heads_here, 2,
+    )
     grad_expert_in = jnp.stack([in_grad_gate[:, :routed], in_grad_up[:, :routed]])[None]
     grad_expert_out = out_grad_w[None, :routed]
     shared_in_part = jnp.stack([in_grad_gate[:, routed:base], in_grad_up[:, routed:base]])
@@ -1114,110 +1674,35 @@
         out_grad_w[routed:base].astype(bf16), "ep", split_axis=1, concat_axis=0, tiled=True
     ).astype(f32)
 
-    ffn_plane = lax.psum_scatter(
-        out_part.reshape(ep_count * tokens, model_width),
-        "ep",
-        scatter_dimension=0,
-        tiled=True,
-    )
-    ffn_rows = lax.psum_scatter(ffn_plane, "tp", scatter_dimension=0, tiled=True).astype(f32)
-    block_out = lax.all_gather((middle + ffn_rows).astype(bf16), "tp", tiled=True)
-    middle_grad = cot_rows + norm_back(ffn_grad, gain_ffn, normed_second, inv_second)
-    gain_ffn_grad = jnp.sum(ffn_grad * normed_second, axis=0)
-    branch_grad = lax.all_gather(middle_grad.astype(bf16), "tp", tiled=True)
-
-    output_w_grad = jnp.einsum("tf,td->fd", attended, branch_grad, preferred_element_type=f32)
-    attended_grad = (
-        jnp.einsum("td,fd->tf", branch_grad, w_output, preferred_element_type=f32)
-        .astype(bf16)
-        .reshape(tokens, heads_here, VDIM)
-    )
-    scores_again = attention_scores(query_rot, key_nope, key_rope, score_scale, allowed)
-    probs_again = jnp.exp(scores_again - log_total)
-    values_grad = jnp.einsum(
-        "hqk,qhd->khd", probs_again.astype(bf16), attended_grad, preferred_element_type=f32
-    )
-    prob_part = jnp.einsum("qhd,khd->hqk", attended_grad, values, preferred_element_type=f32)
-    score_grad = (
-        probs_again * (prob_part - jnp.sum(probs_again * prob_part, axis=-1, keepdims=True))
-    ).astype(bf16)
-    query_nope_grad = (
-        jnp.einsum("hqk,khd->qhd", score_grad, key_nope, preferred_element_type=f32) * score_scale
-    )
-    query_rope_grad = (
-        jnp.einsum("hqk,kr->qhr", score_grad, key_rope, preferred_element_type=f32) * score_scale
-    )
-    key_nope_grad = (
-        jnp.einsum("hqk,qhd->khd", score_grad, query_rot[..., :NOPE], preferred_element_type=f32)
-        * score_scale
-    )
-    key_rope_grad = (
-        jnp.einsum("hqk,qhr->kr", score_grad, query_rot[..., NOPE:], preferred_element_type=f32)
-        * score_scale
-    )
-    kv_grad = (
-        jnp.concatenate([key_nope_grad, values_grad], axis=-1)
-        .astype(bf16)
-        .reshape(tokens, heads_here * (NOPE + VDIM))
-    )
-    latent_up_grad = jnp.einsum("tr,tf->rf", latent_in, kv_grad, preferred_element_type=f32)
-    latent_in_grad = jnp.einsum("tf,rf->tr", kv_grad, w_latent_up, preferred_element_type=f32)
-    gain_latent_grad = jnp.sum(latent_in_grad * normed_latent, axis=0)
-    latent_grad_part = jnp.concatenate(
+    w_rows = model_width // ep_count
+    nope_all, rope_all = heads_here * NOPE, heads_here * qk_width
+    grad_query = jnp.concatenate(
         [
-            norm_back(latent_in_grad, gain_latent, normed_latent, inv_latent),
-            rotate(key_rope_grad, cosine, -sine_table),
+            w_sum[:, :nope_all].reshape(w_rows, heads_here, NOPE),
+            w_sum[:, nope_all:rope_all].reshape(w_rows, heads_here, ROPE),
         ],
         axis=-1,
-    ).astype(bf16)
-    query_grad = (
-        jnp.concatenate(
-            [query_nope_grad, rotate(query_rope_grad, cosine[:, None], -sine_table[:, None])],
-            axis=-1,
-        )
-        .astype(bf16)
-        .reshape(tokens, heads_here * qk_width)
-    )
-    query_w_grad = jnp.einsum("td,tf->df", hidden_attn, query_grad, preferred_element_type=f32)
-    hidden_part = (
-        jnp.einsum("tf,df->td", query_grad, w_query, preferred_element_type=f32)
-        + jnp.einsum("tf,df->td", latent_grad_part, w_latent, preferred_element_type=f32)
-    ).astype(bf16)
-    attn_in_grad = lax.psum_scatter(hidden_part, "tp", scatter_dimension=0, tiled=True).astype(f32)
-    latent_w_grad = jnp.einsum(
-        "td,tf->df", hidden_attn, latent_grad_part, preferred_element_type=f32
-    )
-    normed_rows = lax.dynamic_slice_in_dim(normed_first, row_start, rows_part, 0)
-    inv_rows = lax.dynamic_slice_in_dim(inv_first, row_start, rows_part, 0)
-    gain_attn_grad = jnp.sum(attn_in_grad * normed_rows, axis=0)
-    grad_inputs = lax.all_gather(
-        (middle_grad + norm_back(attn_in_grad, gain_attn, normed_rows, inv_rows)).astype(bf16),
-        "tp",
-        tiled=True,
-    )
-    grad_query, grad_latent_up, grad_output = (
-        lax.psum_scatter(
-            query_w_grad.astype(bf16), "ep", scatter_dimension=0, tiled=True
-        ).astype(f32),
-        lax.psum_scatter(
-            latent_up_grad.astype(bf16), "ep", scatter_dimension=0, tiled=True
-        ).astype(f32),
-        lax.psum_scatter(
-            output_w_grad.astype(bf16), "ep", scatter_dimension=1, tiled=True
-        ).astype(f32),
-    )
-
-    def sum_all(part):
-        plane = lax.psum_scatter(part, "ep", scatter_dimension=0, tiled=True)
-        return lax.psum_scatter(plane, "tp", scatter_dimension=0, tiled=True)
-
-    grad_latent, grad_gain_latent, grad_gain_attn, grad_gain_ffn, grad_router = (
-        sum_all(latent_w_grad),
-        sum_all(gain_latent_grad),
-        sum_all(gain_attn_grad),
-        sum_all(gain_ffn_grad),
-        sum_all(router_grad),
-    )
+    ).reshape(w_rows, rope_all)
+    o_start = rope_all + w_latent_wide.shape[1]
+    o_cols = model_width // ep_count
+    o_pieces = heads_here * VDIM // w_rows
+    grad_output = jnp.concatenate(
+        [w_sum[:, o_start + n * o_cols : o_start + (n + 1) * o_cols] for n in range(o_pieces)], axis=0
+    )
+    u_start = o_start + o_pieces * o_cols
+    u_rows = KV_RANK // ep_count
+    grad_latent_up = jnp.concatenate(
+        [w_sum[n * u_rows : (n + 1) * u_rows, u_start:] for n in range(w_rows // u_rows)], axis=1
+    )
+    grad_latent = latent_sum[:, : KV_RANK + ROPE]
+    grad_router = latent_sum[:, KV_RANK + ROPE : KV_RANK + ROPE + experts]
+    flat = ep_index * tp_count + tp_index
+    wide_part, rank_part = (n // (ep_count * tp_count) for n in (model_width, KV_RANK))
+    grad_gain_attn = lax.dynamic_slice_in_dim(gains[0], flat * wide_part, wide_part, 0)
+    grad_gain_ffn = lax.dynamic_slice_in_dim(gains[1], flat * wide_part, wide_part, 0)
+    grad_gain_latent = lax.dynamic_slice_in_dim(gains[2], flat * rank_part, rank_part, 0)
+    block_out = block_out.reshape(tokens, model_width)
+    grad_inputs = grad_inputs.reshape(tokens, model_width)
     return (
         block_out,
         grad_inputs,

time: 903 us -> 734 us (0.81)
  waiting for transfers between devices: 352 us -> 1.11 us
  Pallas kernels: 292 us -> 552 us
  blocking collectives: 34.6 us -> 0 us
  matrix products: 47.7 us -> 18 us
  local copies, waits for them, and re-layouts: 91 us -> 113 us
  other arithmetic: 48.6 us -> 27.6 us
  between operations: 18.8 us -> 1.54 us
    reduce_scatter x9 -> x0, waiting for transfers between devices: 285 us -> none  [the longest x1 54.5 us: body_dense(): lax.psum_scatter(out_part.reshape(ep_count * tokens, model_width), 'ep',...]
    pallas_call x0 -> x1, Pallas kernels: none -> 257 us  [tail_call(): pl.pallas_call(functools.partial(tail_kernel, depth, heads), out_shape=(j...]
    all_gather x3 -> x0, waiting for transfers between devices: 42 us -> none  [the longest x1 42 us: body_dense(): branch_grad = lax.all_gather(middle_grad.astype(bf16), 'tp', tiled=True)]
    unnamed x2 -> x0, blocking collectives: 34.6 us -> none
    dot_general x16 -> x2, matrix products: 37.5 us -> 7.32 us  [the longest x1 5.53 us: body_dense(): jnp.einsum('hqk,khd->qhd', attn_probs.astype(bf16), per_head[..., NOPE:],...]
    unnamed x14 -> x0, waiting for transfers between devices: 24.7 us -> none
    convert_element_type x6 -> x3, other arithmetic: 13.1 us -> 1.43 us  [the longest x1 0.72 us: body_dense(): query_rope = rotate(query_raw[:, heads_here * NOPE:].reshape(tokens, head...]
    slice x2 -> x13, local copies, waits for them, and re-layouts: 5.06 us -> 16.5 us  [the longest x1 3.31 us: body_dense(): by_head[..., :NOPE].reshape(model_width, heads_here * NOPE)]
  transfers between devices with their start and end apart: 16 -> 3, of which waited for: 11 -> 1; matrix products, arithmetic and copies ran while one was open for 18% -> 15% of each run, Pallas kernels for 0% -> 0%
where the time goes in v4:
time: 734 us; the launch traced here: 726 us
  Pallas kernels  552 us (75%)
  local copies, waits for them, and re-layouts  113 us (15%)
  other arithmetic  27.6 us (4%)
  matrix products  18 us (2%)
  starting transfers between devices  12.7 us (2%)
    pallas_call x1, Pallas kernels, tail_call(): pl.pallas_call(functools.partial(tail_kernel, depth, heads), out_shape=(j...  257 us
    pallas_call x1, Pallas kernels, experts_call(): pl.pallas_call(functools.partial(experts_kernel, depth, blocks, routed, s...  196 us
    pallas_call x1, Pallas kernels, sum_call(): pl.pallas_call(functools.partial(sum_kernel, depth), out_shape=(jax.Shape...  99.1 us
    unnamed x86, local copies, waits for them, and re-layouts  34.7 us
  transfers between devices with their start and end apart: 3, of which 1 were waited for; matrix products, arithmetic and copies ran while one was open for 15% of the time, Pallas kernels for 0%

profile of v4, /device:TPU:0, one launch (start us, length us, event | category | flops | bytes accessed | tf_op | source)
XLA Modules:
  0.0 725.9 jit_solution(12835015878108602256)
XLA Ops:
  4.0 5.2 all-to-all-start
  9.1 4.6 copy.170
  13.8 3.3 slice.157
  17.1 1.3 slice.158
  19.5 3.9 copy.208
  23.4 1.3 copy.172
  25.3 1.0 copy-done.5
  26.6 2.0 pad_maximum_fusion.w_query
  28.6 1.8 fusion.28
  30.4 1.8 fusion.37
  32.3 1.1 fusion.32
  33.3 1.8 fusion.15
  35.8 2.1 convolution_convert_fusion.1.kv_ref
  37.9 1.3 reshape.253
  39.2 1.2 fusion.33
  40.4 2.0 fusion.8
  44.3 1.0 fusion.5
  45.3 2.0 copy-done.2
  49.2 1.8 fusion.29
  53.7 5.5 fusion.7
  59.2 3.7 convolution_convert_fusion.part_ref
  63.0 1.1 constant_dynamic-slice_fusion.4
  64.1 2.0 constant_dynamic-slice_fusion.5
  66.2 1.5 pad_maximum_fusion.8
  67.7 1.7 maximum_maximum_fusion.w_out_ref
  69.4 0.9 pad_maximum_fusion.2.tables
  71.1 1.0 copy.210.attended
  72.1 2.1 slice.187.qn_ref
  74.2 3.1 copy.190
  77.4 1.3 copy.216
  78.6 1.0 copy.218
  79.7 1.9 copy.188
  81.6 1.9 pad.23
  83.5 2.6 copy.214
  86.1 2.6 copy.217
  89.5 1.7 pad.25.w_latent
  91.3 8.3 %concatenate.38.w_in_ref = bf16[2048,1024]{1,0:T(8,128)(2,1)} concatenate(bf16[2048,352]{1,0:T(8,128)(2,1)} %bitcast.102, bf16[2048,88]{1,0:T(8,128)(2,1)S(1)} %bitcast.107, bf16[2048,72]{1,0:T(8,128)(2,1)} %pad.23, bf16[2048,352]{1,0:T(8,128)(2,1)} %bitcast.103, bf16[2048,88]{1,0:T(8,128)(2,1)} %bitcast.108, bf16[2048,72]{1,0:T(8,128)(2,1)S(1)} %broadcast_in_dim.29), dimensions={1} | concatenate | bytes 8388608 | tf_op jit(solution)/shard_map/concatenate | solution.py:1578
  99.6 1.6 broadcast_in_dim.28.kept_ref
  101.2 195.7 %shard_map.263 = (f32[128,2048]{1,0:T(8,128)}, bf16[4,8,128,2048]{3,2,1,0:T(8,128)(2,1)}, bf16[4,8,128,2048]{3,2,1,0:T(8,128)(2,1)}, bf16[4,8,128,1024]{3,2,1,0:...) custom-call(bf16[512,2048]{1,0:T(8,128)(2,1)} %convolution_convert_f, ...), custom_call_target="tpu_custom_call" | custom-call | tf_op jit(solution)/shard_map/pallas_call | solution.py:754
  296.9 99.1 %shard_map.264 = (f32[128,2048]{1,0:T(8,128)}, bf16[128,2048]{1,0:T(8,128)(2,1)}, f32[8,2048]{1,0:T(8,128)}, f32[2048,1024]{1,0:T(8,128)}, f32[512,2048]{1,0:T(8,128)}) custom-call(bf16[4,8,128,2048]{3,2,1,0:T(8,128)(2,1)} %get-tuple-element.31.part_ref, bf16[4,8,128,2048]{3,2,1,0:T(8,128)(2,1)} %get-tuple-element.32.h_ref, ...), custom_call_target="tpu_custom_call" | custom-call | tf_op jit(solution)/shard_map/pallas_call | solution.py:960
  396.1 6.5 slice_bitcast_fusion.1
  404.1 1.2 slice_bitcast_fusion.4
  405.5 1.0 pad.24.router_ref
  406.5 257.3 %shard_map.265 = (bf16[4,128,2048]{2,1,0:T(8,128)(2,1)}, bf16[4,128,2048]{2,1,0:T(8,128)(2,1)}, f32[8,2048]{1,0:T(8,128)}, f32[256,2176]{1,0:T(8,128)}, f32[64,6...) custom-call(bf16[128,2048]{1,0:T(8,128)(2,1)} %get-tuple-element.37.branch_ref, ...), custom_call_target="tpu_custom_call" | custom-call | tf_op jit(solution)/shard_map/pallas_call | solution.py:1462
  663.8 2.0 fusion.30
  665.8 1.6 fusion.31
  667.5 1.9 slice.137
  669.6 9.5 %copy.199 = bf16[2,2048,88]{2,0,1:T(2,128)(2,1)} copy(bf16[2,2048,88]{2,1,0:T(8,128)(2,1)S(1)} %pad_maximum_fusion.1) | data formatting | bytes 1441792 | tf_op jit(solution)/shard_map/stack | solution.py:1669
  679.9 2.2 copy.211
  682.1 1.0 fusion.34
  683.0 1.1 slice.188
  685.0 3.4 all-to-all-start.2
  688.4 2.0 pad_maximum_fusion.4
  690.4 2.1 pad_maximum_fusion.3
  693.1 1.7 pad_maximum_fusion.6
  694.7 3.0 maximum_bitcast_fusion
  697.8 4.1 all-to-all-start.1
  702.5 6.4 copy.204
  708.9 1.1 copy.202
  711.6 3.7 slice_bitcast_fusion.2
  716.2 1.1 all-to-all-done.1
  718.0 2.2 copy.200
  720.2 3.3 copy.242
  723.5 1.3 copy.243
  (123 shorter events, 22.6 us)
Async XLA Ops:
  4.0 95.6 %all-to-all-start = ((bf16[8,2,256]{2,1,0:T(2,128)(2,1)}), bf16[8,2,256]{2,1,0:T(2,128)(2,1)S(1)}, u32[]{:S(2)}, u32[]{:S(2)}) async-start(bf16[8,2,256]{2,1,0:T(2,128)(2,1)} %reshape.271), calls=%async_computation | async-start | bytes 16384 | tf_op jit(solution)/shard_map/all_to_all | solution.py:1563
  13.8 5.2 copy-start
  19.5 5.2 copy-start.32
  24.7 1.6 copy-start.5
  24.7 1.9 copy-start.8
  26.6 3.8 copy-start.6
  28.6 1.8 copy-start.12
  30.4 4.9 copy-start.11
  32.3 3.4 copy-start.34
  35.8 4.6 copy-start.13
  37.9 4.4 copy-start.7
  40.4 2.0 copy-start.33
  40.4 2.2 copy-start.24
  40.4 2.3 copy-start.25
  45.3 2.0 copy-start.2
  47.3 0.8 copy-start.31
  47.3 1.9 copy-start.10
  49.2 3.5 copy-start.20
  51.0 2.7 copy-start.29
  53.7 5.5 copy-start.16
  59.2 8.5 %copy-start.17 = (bf16[1,352,2048]{2,1,0:T(8,128)(2,1)S(1)}, bf16[1,352,2048]{2,1,0:T(8,128)(2,1)}, u32[]{:S(2)}) copy-start(bf16[1,352,2048]{2,1,0:T(8,128)(2,1)} %param.28) | copy-start | bytes 4325380
  63.0 6.4 copy-start.21
  63.0 6.4 copy-start.22
  63.0 6.4 copy-start.23
  66.1 4.3 copy-start.27
  66.1 4.3 copy-start.28
  66.1 5.0 copy-start.26
  74.2 4.4 copy-start.18
  83.5 5.2 copy-start.19
  396.0 7.4 %copy-start.1 = (f32[2048,1024]{1,0:T(8,128)S(1)}, f32[2048,1024]{1,0:T(8,128)}, u32[]{:S(2)}) copy-start(f32[2048,1024]{1,0:T(8,128)} %get-tuple-element.40) | copy-start | bytes 25165828
  663.8 5.5 copy-start.15
  679.9 14.8 %copy-start.3 = (f32[1,2048,352]{2,1,0:T(8,128)S(1)}, f32[1,2048,352]{2,1,0:T(8,128)}, u32[]{:S(2)}) copy-start(f32[1,2048,352]{2,1,0:T(8,128)} %get-tuple-element.118) | copy-start | bytes 8650756
  685.0 12.8 %all-to-all-start.2 = ((bf16[88,8,256]{2,0,1:T(8,128)(2,1)}), bf16[88,8,256]{2,0,1:T(8,128)(2,1)S(1)}, u32[]{:S(2)}, u32[]{:S(2)}) async-start(bf16[88,8,256]{2,0,1:T(8,128)(2,1)} %bitcast.115), calls=%async_computation.2 | async-start | bytes 720896 | tf_op jit(solution)/shard_map/all_to_all | solution.py:1673
  688.4 6.3 copy-start.4
  697.8 19.5 %all-to-all-start.1 = ((bf16[2,2048,88]{2,0,1:T(2,128)(2,1)}), bf16[2,2048,88]{2,0,1:T(2,128)(2,1)S(1)}, u32[]{:S(2)}, u32[]{:S(2)}) async-start(bf16[2,2048,88]{2,0,1:T(2,128)(2,1)} %copy.199), calls=%async_computation.1 | async-start | bytes 2097152 | tf_op jit(solution)/shard_map/all_to_all | solution.py:1670
  702.5 6.4 copy-start.9
  720.2 3.3 copy-start.14
  723.5 1.3 copy-start.30

commit v5 on v4

--- a/solution.py
+++ b/solution.py
@@ -3,6 +3,7 @@
 
 import jax
 import jax.numpy as jnp
+import numpy as np
 from jax import lax
 from jax.experimental import pallas as pl
 from jax.experimental.pallas import tpu as pltpu
@@ -443,6 +444,102 @@
     )
 
 
+def add_rows(dst, a, b):
+    def body(r, _):
+        at = pl.ds(pl.multiple_of(r * 16, 16), 16)
+        dst[at, :] = (a[at, :].astype(jnp.float32) + b[at, :].astype(jnp.float32)).astype(dst.dtype)
+        return 0
+
+    lax.fori_loop(0, dst.shape[0] // 16, body, 0)
+
+
+def turn(slab, table, sign):
+    cosine, front, second = table
+    return slab * cosine + sign * (pltpu.roll(slab, 96, 1) * front + pltpu.roll(slab, 32, 1) * second)
+
+
+def attention_kernel(
+    heads,
+    inputs, gain_attn, w_query, w_latent, gain_latent, w_up, w_output, tables,
+    part, hidden, qn_ref, qr_ref, kv, kr_ref, attended, latent_in, compressed,
+    rope_slab,
+):
+    f32, bf16 = jnp.float32, jnp.bfloat16
+    tokens, width = inputs.shape
+    rank = compressed.shape[1]
+    across = (((1,), (1,)), ((), ()))
+    score_scale = (NOPE + ROPE) ** (-0.5)
+
+    def dot(a, b, dims=(((1,), (0,)), ((), ()))):
+        return lax.dot_general(a, b, dims, preferred_element_type=f32)
+
+    def norm_rows(r, _):
+        at = pl.ds(pl.multiple_of(r * 16, 16), 16)
+        v = inputs[at, :].astype(f32)
+        inverse = lax.rsqrt(jnp.mean(v * v, axis=-1, keepdims=True) + EPSILON)
+        hidden[at, :] = (v * inverse * gain_attn[...]).astype(bf16)
+        return 0
+
+    lax.fori_loop(0, tokens // 16, norm_rows, 0)
+    lanes = lax.broadcasted_iota(jnp.int32, (1, 128), 1)
+    table = tuple(tables[n] for n in range(3))
+    latent = dot(hidden[...], w_latent[...])
+    held = latent[:, :rank]
+    compressed[...] = held
+    inverse = lax.rsqrt(jnp.mean(held * held, axis=-1, keepdims=True) + EPSILON)
+    latent_in[...] = (held * inverse * gain_latent[...]).astype(bf16)
+    rope_slab[...] = jnp.zeros_like(rope_slab)
+    rope_slab[:, 0:ROPE] = latent[:, rank:]
+    key = turn(rope_slab[...], table, 1.0)
+    kr_ref[0] = key.astype(bf16)
+    kr_ref[1] = pltpu.roll(key, 64, 1).astype(bf16)
+    kv[...] = dot(latent_in[...], w_up[...]).astype(bf16)
+    pair = 2 * (NOPE + ROPE)
+    for p in range(heads // 2):
+        found = dot(hidden[...], w_query[:, p * pair : (p + 1) * pair])
+        slabs = [found[:, n : n + 128] for n in (0, 128, 256)]
+        qn_ref[:, 2 * p * NOPE : (2 * p + 1) * NOPE] = slabs[0].astype(bf16)
+        odd = pltpu.roll(jnp.where(lanes < 64, slabs[2], slabs[1]), 64, 1)
+        qn_ref[:, (2 * p + 1) * NOPE : (2 * p + 2) * NOPE] = odd.astype(bf16)
+        qr_ref[:, p * 128 : (p + 1) * 128] = turn(jnp.where(lanes < 64, slabs[1], slabs[2]), table, 1.0).astype(bf16)
+    for h in range(heads):
+        for b in range(tokens // BLOCK):
+            own = slice(b * BLOCK, (b + 1) * BLOCK)
+            keys = slice(0, (b + 1) * BLOCK)
+            slab = slice(h // 2 * 128, h // 2 * 128 + 128)
+            at = slice(h * 128, h * 128 + 128)
+            scores = dot(qn_ref[own, at], kv[keys, h * 256 : h * 256 + 128], across)
+            scores = (scores + dot(qr_ref[own, slab], kr_ref[h % 2, keys, :], across)) * score_scale
+            exps = jnp.exp(scores - jnp.max(scores, axis=-1, keepdims=True))
+            probs = exps / jnp.sum(exps, axis=-1, keepdims=True)
+            attended[own, at] = dot(probs.astype(bf16), kv[keys, h * 256 + 128 : h * 256 + 256]).astype(bf16)
+    for n in range(0, width, 512):
+        part[:, n : n + 512] = dot(attended[...], w_output[:, n : n + 512]).astype(bf16)
+
+
+def attention_call(inputs, gain_attn, w_query, w_latent, gain_latent, w_up, w_output, tables, heads):
+    f32, bf16 = jnp.float32, jnp.bfloat16
+    tokens, width = inputs.shape
+    rank = w_up.shape[0]
+    vmem = pl.BlockSpec(memory_space=pltpu.VMEM)
+
+    def shape(*size, kind=bf16):
+        return jax.ShapeDtypeStruct(size, kind)
+
+    return pl.pallas_call(
+        functools.partial(attention_kernel, heads),
+        out_shape=(
+            shape(tokens, width), shape(tokens, width), shape(tokens, heads * NOPE), shape(tokens, heads * ROPE),
+            shape(tokens, heads * (NOPE + VDIM)), shape(2, tokens, 128), shape(tokens, heads * VDIM),
+            shape(tokens, rank), shape(tokens, rank, kind=f32),
+        ),
+        in_specs=[vmem] * 8,
+        out_specs=(vmem,) * 9,
+        scratch_shapes=[pltpu.VMEM((tokens, 128), f32)],
+        compiler_params=pltpu.CompilerParams(vmem_limit_bytes=48 << 20),
+    )(inputs, gain_attn.reshape(1, width), w_query, w_latent, gain_latent.reshape(1, rank), w_up, w_output, tables)
+
+
 def experts_kernel(
     depth, blocks, routed, shared, experts,
     part_ref, resid_ref, gain_ref, cot_ref, kept_ref, w_in_ref, w_out_ref,
@@ -490,9 +587,12 @@
         src = cot_ref.at[pl.ds(pl.multiple_of(chunk * rows, rows), rows)]
         return remote(src, cot_all.at[chunk, ep], c_send.at[chunk, slot], c_recv.at[chunk, slot], (to, tp))
 
-    def own_cot(chunk):
+    def own_cot_in(chunk):
         src = cot_ref.at[pl.ds(pl.multiple_of(chunk * rows, rows), rows)]
-        return pltpu.make_async_copy(src, cot_all.at[chunk, ep], local_sem.at[chunk])
+        return pltpu.make_async_copy(src, out_tile.at[0, chunk], local_sem.at[chunk])
+
+    def own_cot_out(chunk):
+        return pltpu.make_async_copy(out_tile.at[0, chunk], cot_all.at[chunk, ep], local_sem.at[chunk])
 
     order = line_order(tp)
 
@@ -507,8 +607,11 @@
         c_first(order[k], 1, xn).start()
         c_first(order[k], 2, yn).start()
         c_first(order[k], 0, pair).start()
-        own_cot(order[k]).start()
+        own_cot_in(k).start()
     resid_copy.wait()
+    for k in range(depth):
+        own_cot_in(k).wait()
+        own_cot_out(k).start()
     for k in range(1, depth):
         z_copy(k).wait_recv()
 
@@ -525,6 +628,8 @@
         return 0
 
     lax.fori_loop(0, rows // 16, norm_rows, 0)
+    for k in range(depth):
+        own_cot_out(k).wait()
 
     def along(chunk, way, to):
         ref = h_all.at[chunk, ep]
@@ -553,13 +658,12 @@
         h_copy(ep, chunk, 2, yn).start()
         h_copy(ep, chunk, 0, pair).start()
 
-    def forward_chunk(chunk):
-        for copy in (h_copy, c_copy):
-            copy(xn, chunk, 1, xn).wait_recv()
-            copy(yn, chunk, 2, yn).wait_recv()
-            copy(passed, chunk, 3, onward).start()
-            copy(xn, chunk, 4, pair).start()
-            copy(yn, chunk, 5, pair).start()
+    def forward_chunk(copy, chunk):
+        copy(xn, chunk, 1, xn).wait_recv()
+        copy(yn, chunk, 2, yn).wait_recv()
+        copy(passed, chunk, 3, onward).start()
+        copy(xn, chunk, 4, pair).start()
+        copy(yn, chunk, 5, pair).start()
 
     def forward_diag(chunk):
         for copy in (h_copy, c_copy):
@@ -572,7 +676,10 @@
                 copy(block, chunk, slot, pair).wait_recv()
 
     send_chunk(0)
+    forward_chunk(c_copy, order[0])
+    forward_chunk(c_copy, order[1])
     send_chunk(1)
+    forward_chunk(h_copy, order[0])
 
     lanes = lax.broadcasted_iota(jnp.int32, (1, 128), 1)
     base = routed + shared
@@ -600,11 +707,6 @@
         k, side = lax.div(i, 2), lax.rem(i, 2)
         chunk, start, slot, load, stores = tile_copies(i)
 
-        @pl.when(side == 0)
-        def _():
-            own_cot(chunk).wait()
-            forward_chunk(chunk)
-
         @pl.when(i == 0)
         def _():
             send_chunk(2)
@@ -613,16 +715,24 @@
         def _():
             await_pair(chunk, ((0, pair), (4, twin(xn))))
 
+        @pl.when(i == 1)
+        def _():
+            forward_chunk(h_copy, order[1])
+            send_chunk(3)
+
+        @pl.when(i == 2)
+        def _():
+            forward_chunk(c_copy, order[2])
+            forward_chunk(h_copy, order[2])
+
+        @pl.when(i == 3)
+        def _():
+            forward_chunk(c_copy, order[3])
+            forward_chunk(h_copy, order[3])
+
         @pl.when(side == 1)
         def _():
             forward_diag(chunk)
-
-        @pl.when(i == 1)
-        def _():
-            send_chunk(3)
-
-        @pl.when(side == 1)
-        def _():
             await_pair(chunk, ((5, twin(yn)), (6, twin(diag))))
 
         load.start()
@@ -786,9 +896,11 @@
 
 
 def sum_kernel(
-    depth, part_ref, h_ref, grads_ref, gated_ref, cot_ref, middle_ref, gain_ref, middle_grad, branch, gain_part, in_grad, out_grad,
-    mine, got_pair, got_first, got_second, got_z, keep, h_tile, grads_tile, gated_tile, cot_tile,
-    own_cot, mine_sem, own_sem, ps, pr, fs, fr, ss, sr, zs, zr, tile_sem,
+    depth, routed, shared, experts, part_ref, layer_ref, h_ref, grads_ref, gated_ref, cot_ref, middle_ref, gain_ref,
+    middle_grad, branch, gain_part, expert_in, expert_out, s_in, s_out, router, layer_sum, landed,
+    in_grad, out_grad, e_stage, s_stage,
+    load, store, got_pair, got_first, got_second, got_z, keep, h_tile, grads_tile, gated_tile, cot_tile,
+    own_cot, load_sem, store_sem, own_sem, lps, lpr, ps, pr, fs, fr, ss, sr, zs, zr, tile_sem, e_sem, s_sem, o_sem,
 ):
     f32 = jnp.float32
     rows = part_ref.shape[2]
@@ -814,32 +926,63 @@
     def pair_wait(i, slot):
         return remote(part_ref.at[0, 0], got_pair.at[i, slot], ps.at[i, slot], pr.at[i, slot], (pair, tp))
 
-    def mine_copy(i, slot):
-        return pltpu.make_async_copy(part_ref.at[chunk_of(i), blocks[slot]], mine.at[i, slot], mine_sem.at[i, slot])
+    def own_load(i, slot):
+        return pltpu.make_async_copy(part_ref.at[chunk_of(i), blocks[slot]], load.at[slot], load_sem.at[slot])
 
     def first_copy(i, slot):
-        return remote(mine.at[i, slot], got_first.at[i, slot], fs.at[i, slot], fr.at[i, slot], (first, tp))
+        return remote(got_pair.at[i, slot], got_first.at[i, slot], fs.at[i, slot], fr.at[i, slot], (first, tp))
 
     def second_copy(i):
-        return remote(mine.at[i, 3], got_second.at[i], ss.at[i], sr.at[i], (second, tp))
+        return remote(got_pair.at[i, 3], got_second.at[i], ss.at[i], sr.at[i], (second, tp))
 
     def z_copy(i):
         k = steps[i]
-        return remote(mine.at[i, 2], got_z.at[k - 1], zs.at[k - 1], zr.at[k - 1], (ep, lax.rem(tp + k, depth)))
-
-    def add(dst, a, b):
-        def body(r, _):
-            at = pl.ds(pl.multiple_of(r * 16, 16), 16)
-            dst[at, :] = (a[at, :].astype(f32) + b[at, :].astype(f32)).astype(dst.dtype)
-            return 0
-
-        lax.fori_loop(0, rows // 16, body, 0)
+        return remote(got_pair.at[i, 2], got_z.at[k - 1], zs.at[k - 1], zr.at[k - 1], (ep, lax.rem(tp + k, depth)))
+
+    def layer_pair(i, slot):
+        src = layer_ref.at[blocks[slot] + pair - ep, chunk_of(i)]
+        to = pair_slot[slot]
+        return remote(src, landed.at[i, to], lps.at[i, slot], lpr.at[i, to], (pair, tp))
+
+    def layer_wait(i, slot):
+        return remote(layer_ref.at[0, 0], landed.at[i, slot], lps.at[i, slot], lpr.at[i, slot], (pair, tp))
+
+    def layer_loads(i, slot):
+        at = 2 * (slot % 2)
+        return (
+            pltpu.make_async_copy(layer_ref.at[blocks[slot], chunk_of(i)], load.at[at], load_sem.at[at]),
+            pltpu.make_async_copy(landed.at[i, slot], load.at[at + 1], load_sem.at[at + 1]),
+        )
+
+    def layer_store(i, slot):
+        return pltpu.make_async_copy(store.at[slot % 2], layer_sum.at[i, slot], store_sem.at[slot % 2])
+
+    def layer_stage(i):
+        def start(slot):
+            layer_wait(i, slot).wait_recv()
+            for copy in layer_loads(i, slot):
+                copy.start()
+
+        start(0)
+        for slot in range(4):
+            if slot < 3:
+                start(slot + 1)
+            for copy in layer_loads(i, slot):
+                copy.wait()
+            if slot >= 2:
+                layer_store(i, slot - 2).wait()
+            at = 2 * (slot % 2)
+            add_rows(store.at[slot % 2], load.at[at], load.at[at + 1])
+            layer_store(i, slot).start()
+        layer_store(i, 2).wait()
+        layer_store(i, 3).wait()
 
     for i in range(depth):
         for slot in (3, 1, 2, 0):
             pair_copy(i, slot).start()
-        for slot in range(4):
-            mine_copy(i, slot).start()
+    for i in range(depth):
+        for slot in (3, 1, 2, 0):
+            layer_pair(i, slot).start()
 
     def tile_loads(c):
         return [
@@ -851,35 +994,78 @@
 
     def stage_a(i):
         for slot in range(4):
-            mine_copy(i, slot).wait()
+            own_load(i, slot).start()
+        for slot in range(4):
             pair_wait(i, slot).wait_recv()
-            add(mine.at[i, slot], mine.at[i, slot], got_pair.at[i, slot])
+            own_load(i, slot).wait()
+            add_rows(got_pair.at[i, slot], got_pair.at[i, slot], load.at[slot])
             if slot < 2:
                 first_copy(i, slot).start()
 
     def stage_b(i):
         first_copy(i, 1).wait_recv()
-        add(mine.at[i, 3], mine.at[i, 3], got_first.at[i, 1])
+        add_rows(got_pair.at[i, 3], got_pair.at[i, 3], got_first.at[i, 1])
         second_copy(i).start()
         first_copy(i, 0).wait_recv()
-        add(mine.at[i, 2], mine.at[i, 2], got_first.at[i, 0])
+        add_rows(got_pair.at[i, 2], got_pair.at[i, 2], got_first.at[i, 0])
 
     def stage_c(i):
         second_copy(i).wait_recv()
         if i < depth - 1:
-            add(mine.at[i, 2], mine.at[i, 2], got_second.at[i])
+            add_rows(got_pair.at[i, 2], got_pair.at[i, 2], got_second.at[i])
             z_copy(i).start()
         else:
-            add(keep, mine.at[i, 2], got_second.at[i])
+            add_rows(keep, got_pair.at[i, 2], got_second.at[i])
 
     count = h_tile.shape[0] * rows
     width = h_tile.shape[2]
     hidden = gated_tile.shape[2]
 
+    blocks_all = h_tile.shape[0]
+    lanes = lax.broadcasted_iota(jnp.int32, (1, 128), 1)
+    slab = routed // 128 * 128
+    shift = 128 - (routed - slab)
+    router_shift = (ROPE - (routed + shared) % 128) % 128
+
+    def expert_out_copy():
+        return pltpu.make_async_copy(out_grad.at[pl.ds(0, routed)], expert_out.at[0], o_sem)
+
+    def place_copies(m):
+        side = lax.rem(m, 2)
+        at = pl.ds(pl.multiple_of(m * 512, 512), 512)
+        per = 512 // (width // blocks_all)
+        return (
+            pltpu.make_async_copy(e_stage.at[side], expert_in.at[0, :, at], e_sem.at[side]),
+            pltpu.make_async_copy(s_stage.at[side], s_in.at[pl.ds(m * per, per)], s_sem.at[side]),
+        )
+
+    def place(m, found):
+        side = lax.rem(m, 2)
+
+        @pl.when(m >= 2)
+        def _():
+            for copy in place_copies(m - 2):
+                copy.wait()
+
+        wide = width // blocks_all
+        for g in range(2):
+            e_stage[side, g] = found[:, g * hidden : g * hidden + routed]
+            first_slab = found[:, g * hidden + slab : g * hidden + slab + 128]
+            second_slab = found[:, g * hidden + slab + 128 : g * hidden + slab + 256]
+            units = jnp.where(lanes < shift, pltpu.roll(first_slab, shift, 1), pltpu.roll(second_slab, shift, 1))
+            s_stage[side, :, g] = units.astype(s_stage.dtype).reshape(512 // wide, wide, 128)
+        last_slab = pltpu.roll(found[:, (routed + shared) // 128 * 128 : (routed + shared) // 128 * 128 + 128], router_shift, 1)
+        inside = (lanes >= ROPE) & (lanes < ROPE + experts)
+        router[pl.ds(pl.multiple_of(m * 512, 512), 512), :] = jnp.where(inside, last_slab, 0.0).astype(router.dtype)
+        for copy in place_copies(m):
+            copy.start()
+
     def weights(c):
-        for load in tile_loads(c):
-            load.wait()
+        for copy in tile_loads(c):
+            copy.wait()
         turned = (((0,), (0,)), ((), ()))
+
+        last = c == depth - 1
 
         def in_part(m, _):
             at = pl.ds(pl.multiple_of(m * 512, 512), 512)
@@ -887,7 +1073,12 @@
                 h_tile[:, :, at].reshape(count, 512), grads_tile[...].reshape(count, 2 * hidden), turned,
                 preferred_element_type=f32,
             )
-            in_grad[at, :] = found if c == 0 else in_grad[at, :] + found
+            if c > 0:
+                found = in_grad[at, :] + found
+            if last:
+                place(m, found)
+            else:
+                in_grad[at, :] = found
             return 0
 
         lax.fori_loop(0, width // 512, in_part, 0)
@@ -902,14 +1093,19 @@
             return 0
 
         lax.fori_loop(0, width // 512, out_part, 0)
+        if last:
+            expert_out_copy().start()
+            wide = width // blocks_all
+            for b in range(blocks_all):
+                s_out[b] = out_grad[routed : routed + s_out.shape[1], b * wide : (b + 1) * wide].astype(s_out.dtype)
         if c + 1 < depth:
-            for load in tile_loads(c + 1):
-                load.start()
+            for copy in tile_loads(c + 1):
+                copy.start()
 
     own_copy = pltpu.make_async_copy(cot_ref.at[tp, ep], own_cot, own_sem)
     own_copy.start()
-    for load in tile_loads(0):
-        load.start()
+    for copy in tile_loads(0):
+        copy.start()
     for t in range(depth + 2):
         if t < depth:
             stage_a(t)
@@ -919,9 +1115,9 @@
             stage_c(t - 2)
         if t < depth:
             weights(t)
+            layer_stage(t)
     for i in range(depth - 1):
         z_copy(i).wait_recv()
-
     own_copy.wait()
 
     def total(r, gain_sum):
@@ -941,9 +1137,14 @@
         return gain_sum
 
     gain_part[...] = lax.fori_loop(0, rows // 16, total, jnp.zeros((8, width), f32))
+    expert_out_copy().wait()
+    for m in (width // 512 - 2, width // 512 - 1):
+        for copy in place_copies(m):
+            copy.wait()
     for i in range(depth):
         for slot in range(4):
             pair_copy(i, slot).wait_send()
+            layer_pair(i, slot).wait_send()
         for slot in range(2):
             first_copy(i, slot).wait_send()
         second_copy(i).wait_send()
@@ -951,25 +1152,35 @@
             z_copy(i).wait_send()
 
 
-def sum_call(part, h_all, grads, gated, cot_all, middle, gain, cid):
+def sum_call(part, layer, h_all, grads, gated, cot_all, middle, gain, routed, shared, experts, cid):
     f32, bf16 = jnp.float32, jnp.bfloat16
     depth, blocks, rows, width = part.shape
     hidden = gated.shape[3]
     dma = pltpu.SemaphoreType.DMA
     vmem, anywhere = pl.BlockSpec(memory_space=pltpu.VMEM), pl.BlockSpec(memory_space=pl.ANY)
     return pl.pallas_call(
-        functools.partial(sum_kernel, depth),
+        functools.partial(sum_kernel, depth, routed, shared, experts),
         out_shape=(
             jax.ShapeDtypeStruct((rows, width), f32),
             jax.ShapeDtypeStruct((rows, width), bf16),
             jax.ShapeDtypeStruct((8, width), f32),
-            jax.ShapeDtypeStruct((width, 2 * hidden), f32),
-            jax.ShapeDtypeStruct((hidden, width), f32),
+            jax.ShapeDtypeStruct((1, 2, width, routed), f32),
+            jax.ShapeDtypeStruct((1, routed, width), f32),
+            jax.ShapeDtypeStruct((blocks, 2, width // blocks, 128), bf16),
+            jax.ShapeDtypeStruct((blocks, -(-shared // 16) * 16, width // blocks), bf16),
+            jax.ShapeDtypeStruct((width, 128), bf16),
+            jax.ShapeDtypeStruct((depth, 4, rows, width), bf16),
+            jax.ShapeDtypeStruct((depth, 4, rows, width), bf16),
         ),
-        in_specs=[anywhere] * 5 + [vmem, vmem],
-        out_specs=(vmem,) * 5,
+        in_specs=[anywhere] * 6 + [vmem, vmem],
+        out_specs=(vmem,) * 3 + (anywhere,) * 3 + (vmem,) * 2 + (anywhere,) * 2,
         scratch_shapes=[
-            pltpu.VMEM((depth, 4, rows, width), bf16),
+            pltpu.VMEM((width, 2 * hidden), f32),
+            pltpu.VMEM((hidden, width), f32),
+            pltpu.VMEM((2, 2, 512, routed), f32),
+            pltpu.VMEM((2, 512 // (width // blocks), 2, width // blocks, 128), bf16),
+            pltpu.VMEM((4, rows, width), bf16),
+            pltpu.VMEM((2, rows, width), bf16),
             pltpu.VMEM((depth, 4, rows, width), bf16),
             pltpu.VMEM((depth, 2, rows, width), bf16),
             pltpu.VMEM((depth, rows, width), bf16),
@@ -980,11 +1191,11 @@
             pltpu.VMEM((blocks, rows, hidden), bf16),
             pltpu.VMEM((blocks, rows, width), bf16),
             pltpu.VMEM((rows, width), bf16),
-            dma((depth, 4)), dma, dma((depth, 4)), dma((depth, 4)), dma((depth, 2)), dma((depth, 2)),
-            dma((depth,)), dma((depth,)), dma((depth - 1,)), dma((depth - 1,)), dma((4,)),
+            dma((4,)), dma((2,)), dma, dma((depth, 4)), dma((depth, 4)), dma((depth, 4)), dma((depth, 4)), dma((depth, 2)), dma((depth, 2)),
+            dma((depth,)), dma((depth,)), dma((depth - 1,)), dma((depth - 1,)), dma((4,)), dma((2,)), dma((2,)), dma,
         ],
         compiler_params=pltpu.CompilerParams(collective_id=cid, has_side_effects=True, vmem_limit_bytes=62 << 20),
-    )(part, h_all, grads, gated, cot_all, middle, gain.reshape(1, width))
+    )(part, layer, h_all, grads, gated, cot_all, middle, gain.reshape(1, width))
 
 
 def line_gather(ref, own, send_sem, recv_sem, ep, tp, depth):
@@ -1018,30 +1229,16 @@
     return pass_on, await_chunk, drain
 
 
-def add_rows(dst, a, b):
-    def body(r, _):
-        at = pl.ds(pl.multiple_of(r * 16, 16), 16)
-        dst[at, :] = (a[at, :].astype(jnp.float32) + b[at, :].astype(jnp.float32)).astype(dst.dtype)
-        return 0
-
-    lax.fori_loop(0, dst.shape[0] // 16, body, 0)
-
-
-def turn(slab, table, sign):
-    cosine, front, second = table
-    return slab * cosine + sign * (pltpu.roll(slab, 96, 1) * front + pltpu.roll(slab, 32, 1) * second)
-
-
 def tail_kernel(
-    depth, heads,
-    branch_ref, middle_grad_ref, middle_ref, part_ref, router_ref, gain_part_ref, inputs_ref,
+    depth, heads, shared,
+    branch_ref, middle_grad_ref, middle_ref, part_ref, router_ref, gain_part_ref, inputs_ref, s_in, s_out,
     w_output, w_query, w_latent, w_up, hidden_ref, qn_ref, qr_ref, kv_ref, kr_ref, attended, latent_in, compressed,
     tables, gain_latent, gain_attn,
-    block_ref, grad_in_ref, gains_ref, w_sum_ref, latent_sum_ref, landed, w_all,
-    branch, load, held_rows, got_first, got_second, got_z, hidden_part, got_h, row_sum,
-    d_out, d_kr, q_grad, kv_grad, l_grad, u_grad, w_stage, w_pair, w_first, w_second, w_z, resid, own_grad, own_block, gains,
-    load_sem, ps, pr, fs, fr, ss, sr, zs, zr, bs, br, hs, hr, gs, gr, os, orr,
-    wps, wpr, wfs, wfr, wss, wsr, wzs, wzr, as_, ar, misc_sem, stage_sem,
+    block_ref, grad_in_ref, gains_ref, query_ref, output_ref, up_ref, latent_ref, shared_in, shared_out, w_all,
+    branch, held_rows, got_first, got_second, got_z, hidden_part, got_h, row_sum,
+    d_out, d_kr, q_grad, kv_grad, l_grad, u_grad, w_stage, w_pair, w_first, w_second, w_z, latent_part, s_in_land, s_out_land, resid, own_grad, own_block, gains,
+    load_sem, fs, fr, ss, sr, zs, zr, bs, br, hs, hr, gs, gr, os, orr,
+    wps, wpr, wfs, wfr, wss, wsr, wzs, wzr, as_, ar, misc_sem, stage_sem, sis, sir, sos, sor,
 ):
     f32, bf16 = jnp.float32, jnp.bfloat16
     ep, tp = lax.axis_index("ep"), lax.axis_index("tp")
@@ -1054,9 +1251,21 @@
     pair_slot = (3, 1, 2, 0)
     rows, width = middle_ref.shape
     tokens = hidden_ref.shape[0]
+    rank = compressed.shape[1]
+    q_cols, l_cols = q_grad.shape[1], l_grad.shape[1]
+    o_rows = attended.shape[1]
+    count = w_all.shape[0]
+    w_rows = w_all.shape[1]
+    o_cols = width // count
+    u_rows = rank // count
+    u_cols = w_up.shape[1]
+    o_start = q_cols + l_cols
+    u_start = o_start + o_rows * o_cols // w_rows
+    u_wide = u_rows * u_cols // w_rows
     order = line_order(tp)
     score_scale = (NOPE + ROPE) ** (-0.5)
-    greet([(pair, tp), (xn, tp), (yn, tp)] + [(ep, lax.rem(tp + k, depth)) for k in range(1, depth)])
+    plane = [ep + sum(((pair, xn, yn)[n] - ep) * (m >> n & 1) for n in range(3)) for m in range(8)]
+    greet([(to, tp) for to in plane[1:]] + [(ep, lax.rem(tp + k, depth)) for k in range(1, depth)])
 
     branch_on, branch_wait, branch_drain = line_gather(branch, branch_ref, bs, br, ep, tp, depth)
     grad_on, grad_wait, grad_drain = line_gather(grad_in_ref, own_grad, gs, gr, ep, tp, depth)
@@ -1067,67 +1276,36 @@
     def chunk_of(i):
         return lax.rem(tp + steps[i], depth)
 
-    def pair_copy(i, slot):
-        src = part_ref.at[blocks[slot] + pair - ep, chunk_of(i)]
-        to = pair_slot[slot]
-        return remote(src, landed.at[i, to], ps.at[i, slot], pr.at[i, to], (pair, tp))
-
-    def pair_wait(i, slot):
-        return remote(part_ref.at[0, 0], landed.at[i, slot], ps.at[i, slot], pr.at[i, slot], (pair, tp))
-
-    def loads(i, slot):
-        at = slot % 2
-        return (
-            pltpu.make_async_copy(part_ref.at[blocks[slot], chunk_of(i)], load.at[at, 0], load_sem.at[at, 0]),
-            pltpu.make_async_copy(landed.at[i, slot], load.at[at, 1], load_sem.at[at, 1]),
-        )
+    def held_load(i, slot):
+        return pltpu.make_async_copy(part_ref.at[i, slot], held_rows.at[i, slot - 2], load_sem.at[i, slot - 2])
 
     def first_copy(i, slot):
-        return remote(held_rows.at[i % 2, slot], got_first.at[i, slot], fs.at[i, slot], fr.at[i, slot], (first, tp))
+        return remote(part_ref.at[i, slot], got_first.at[i, slot], fs.at[i, slot], fr.at[i, slot], (first, tp))
 
     def second_copy(i):
-        return remote(held_rows.at[i % 2, 3], got_second.at[i], ss.at[i], sr.at[i], (second, tp))
+        return remote(held_rows.at[i, 1], got_second.at[i], ss.at[i], sr.at[i], (second, tp))
 
     def z_copy(i):
         k = steps[i]
-        src = held_rows.at[i % 2, 2]
+        src = held_rows.at[i, 0]
         return remote(src, got_z.at[k - 1], zs.at[k - 1], zr.at[k - 1], (ep, lax.rem(tp + k, depth)))
 
-    def start_loads(i, slot):
-        pair_wait(i, slot).wait_recv()
-        for copy in loads(i, slot):
-            copy.start()
-
-    def stage_a(i):
-        if i >= 2:
-            for slot in range(2):
-                first_copy(i - 2, slot).wait_send()
-            second_copy(i - 2).wait_send()
-            z_copy(i - 2).wait_send()
-        start_loads(i, 0)
-        for slot in range(4):
-            if slot < 3:
-                start_loads(i, slot + 1)
-            for copy in loads(i, slot):
-                copy.wait()
-            add_rows(held_rows.at[i % 2, slot], load.at[slot % 2, 0], load.at[slot % 2, 1])
-            if slot < 2:
-                first_copy(i, slot).start()
-
     def stage_b(i):
+        held_load(i, 3).wait()
         first_copy(i, 1).wait_recv()
-        add_rows(held_rows.at[i % 2, 3], held_rows.at[i % 2, 3], got_first.at[i, 1])
+        add_rows(held_rows.at[i, 1], held_rows.at[i, 1], got_first.at[i, 1])
         second_copy(i).start()
+        held_load(i, 2).wait()
         first_copy(i, 0).wait_recv()
-        add_rows(held_rows.at[i % 2, 2], held_rows.at[i % 2, 2], got_first.at[i, 0])
+        add_rows(held_rows.at[i, 0], held_rows.at[i, 0], got_first.at[i, 0])
 
     def stage_c(i):
         second_copy(i).wait_recv()
         if i < depth - 1:
-            add_rows(held_rows.at[i % 2, 2], held_rows.at[i % 2, 2], got_second.at[i])
+            add_rows(held_rows.at[i, 0], held_rows.at[i, 0], got_second.at[i])
             z_copy(i).start()
         else:
-            add_rows(row_sum, held_rows.at[i % 2, 2], got_second.at[i])
+            add_rows(row_sum, held_rows.at[i, 0], got_second.at[i])
 
     def w_pair_copy(slot):
         to = pair_slot[slot]
@@ -1164,7 +1342,43 @@
 
     def w_stage_c():
         w_second_copy().wait_recv()
-        add_rows(w_sum_ref, w_pair.at[2], w_second)
+
+        def total(cols, at=slice(None)):
+            return w_pair[2, at, cols].astype(f32) + w_second[at, cols].astype(f32)
+
+        query_ref[...] = total(slice(0, q_cols))
+        latent_part[...] = total(slice(q_cols, o_start))
+        for n in range(o_rows // w_rows):
+            output_ref[n * w_rows : (n + 1) * w_rows, :] = total(slice(o_start + n * o_cols, o_start + (n + 1) * o_cols))
+        for n in range(u_cols // u_wide):
+            up_ref[:, n * u_wide : (n + 1) * u_wide] = total(
+                slice(u_start, u_start + u_wide), slice(n * u_rows, (n + 1) * u_rows)
+            )
+
+    def shared_copies(m):
+        to = plane[m]
+        return (
+            remote(s_in.at[to], s_in_land.at[ep], sis.at[m], sir.at[m], (to, tp)),
+            remote(s_out.at[to], s_out_land.at[ep], sos.at[m], sor.at[m], (to, tp)),
+        )
+
+    def shared_own():
+        return (
+            pltpu.make_async_copy(s_in.at[ep], s_in_land.at[ep], sis.at[0]),
+            pltpu.make_async_copy(s_out.at[ep], s_out_land.at[ep], sos.at[0]),
+        )
+
+    def shared_place():
+        for m in range(1, 8):
+            for copy in shared_copies(m):
+                copy.wait_recv()
+        for copy in shared_own():
+            copy.wait()
+        for n in range(s_in_land.shape[0]):
+            at = slice(n * shared, (n + 1) * shared)
+            for g in range(2):
+                shared_in[g, :, at] = s_in_land[n, g].astype(f32)[:, :shared]
+            shared_out[at, :] = s_out_land[n].astype(f32)[:shared]
 
     def h_copy(k):
         to = lax.rem(tp + k, depth)
@@ -1173,19 +1387,20 @@
     branch_on(0)
     branch[tp] = branch_ref[...]
     for i in range(depth):
-        for slot in (3, 1, 2, 0):
-            pair_copy(i, slot).start()
+        first_copy(i, 1).start()
+        first_copy(i, 0).start()
+        held_load(i, 3).start()
+        held_load(i, 2).start()
     own_rows = pl.ds(pl.multiple_of(tp * rows, rows), rows)
     resid_copy = pltpu.make_async_copy(inputs_ref.at[own_rows], resid, misc_sem.at[0])
     resid_copy.start()
 
-    stage_a(0)
     branch_wait(1)
     branch_on(1)
-    stage_a(1)
+    stage_b(0)
     branch_wait(2)
     branch_on(2)
-    stage_b(0)
+    stage_c(0)
     branch_wait(3)
     branch_on(3)
 
@@ -1229,24 +1444,25 @@
                 if b > 0:
                     kv_sum[n] = kv_sum[n][: b * BLOCK]
             d_kr[keys, :] = d_kr[keys, :] + r_grad
-            q_grad[own, at_q] = (dot(score_grad, kn) * score_scale).astype(bf16)
-            yield own, at_r, dot(score_grad, kr) * score_scale
+            yield own, dot(score_grad, kn) * score_scale, dot(score_grad, kr) * score_scale
 
     d_kr[...] = jnp.zeros_like(d_kr)
 
     def head_pair(p, _):
         evens = list(head(2 * p, True))
         odds = list(head(2 * p + 1, False))
-        at = pl.ds(pl.multiple_of(heads * NOPE + p * 128, 128), 128)
-        for (own, _, even_part), (_, _, odd_part) in zip(evens, odds):
+        at = [pl.ds(pl.multiple_of(p * (2 * (NOPE + ROPE)) + n, 128), 128) for n in (0, 128, 256)]
+        for (own, even, even_rope), (_, odd, odd_rope) in zip(evens, odds):
             table = tuple(tables[n, own, :] for n in range(3))
-            q_grad[own, at] = turn(even_part + odd_part, table, -1.0).astype(bf16)
+            rope = turn(even_rope + odd_rope, table, -1.0)
+            odd = pltpu.roll(odd, 64, 1)
+            q_grad[own, at[0]] = even.astype(bf16)
+            q_grad[own, at[1]] = jnp.where(lanes < 64, rope, odd).astype(bf16)
+            q_grad[own, at[2]] = jnp.where(lanes < 64, odd, rope).astype(bf16)
         return 0
 
     lax.fori_loop(0, heads // 2, head_pair, 0)
-    stage_c(0)
     stage_b(1)
-    stage_a(2)
 
     latent_back = dot(kv_grad[...], w_up[...], across)
     held = compressed[...]
@@ -1254,32 +1470,19 @@
     normed = held * inverse
     gain_latent_part = jnp.sum(latent_back * normed, axis=0, keepdims=True)
     scaled = latent_back * gain_latent[...]
-    rank = held.shape[1]
     l_grad[:, :rank] = (inverse * (scaled - normed * jnp.mean(scaled * normed, axis=-1, keepdims=True))).astype(bf16)
     rope = d_kr[...] + pltpu.roll(d_kr[...], 64, 1)
     rope = turn(rope, tuple(tables[n] for n in range(3)), -1.0)
     l_grad[:, rank:] = jnp.where(lanes < 64, rope, 0.0).astype(bf16)
 
     for n in range(0, width, 512):
-        part = dot(q_grad[...], w_query[n : n + 512, :], across) + dot(l_grad[...], w_latent[n : n + 512, :], across)
+        part = dot(q_grad[...], w_query[n : n + 512, :], across) + dot(l_grad[:, : rank + ROPE], w_latent[n : n + 512, :], across)
         hidden_part[:, :, n : n + 512] = part.astype(bf16).reshape(depth, rows, 512)
     for k in range(1, depth):
         h_copy(k).start()
 
     stage_c(1)
     stage_b(2)
-    stage_a(3)
-
-    q_cols, l_cols = q_grad.shape[1], l_grad.shape[1]
-    o_rows = attended.shape[1]
-    count = w_all.shape[0]
-    w_rows = w_all.shape[1]
-    o_cols = width // count
-    u_rows = rank // count
-    u_cols = w_up.shape[1]
-    o_start = q_cols + l_cols
-    u_start = o_start + o_rows * o_cols // w_rows
-    u_wide = u_rows * u_cols // w_rows
 
     u_grad[...] = dot(latent_in[...], kv_grad[...], turned).astype(bf16)
 
@@ -1319,12 +1522,16 @@
     w_store(count - 1).wait()
     for slot in (3, 1, 2, 0):
         w_pair_copy(slot).start()
+    for copy in shared_own():
+        copy.start()
+    for m in range(1, 8):
+        for copy in shared_copies(m):
+            copy.start()
     w_load(0).start()
 
+    stage_c(2)
     stage_b(3)
-    stage_c(2)
     w_stage_a()
-    stage_c(3)
 
     resid_copy.wait()
     for k in range(1, depth):
@@ -1348,7 +1555,7 @@
     grad_on(0)
     own_grad_copy = pltpu.make_async_copy(own_grad, grad_in_ref.at[tp], misc_sem.at[1])
     own_grad_copy.start()
-    w_stage_b()
+    stage_c(3)
     for i in range(depth - 1):
         z_copy(i).wait_recv()
 
@@ -1364,6 +1571,7 @@
     block_on(0)
     own_block_copy = pltpu.make_async_copy(own_block, block_ref.at[tp], misc_sem.at[2])
     own_block_copy.start()
+    w_stage_b()
 
     gains[0] = jnp.zeros_like(gains[0])
     gains[0, 0:1, :] = jnp.sum(gain_sum, axis=0, keepdims=True)
@@ -1397,7 +1605,7 @@
         return remote(src, w_z.at[k - 1], wzs.at[k - 1], wzr.at[k - 1], (ep, to))
 
     w_first_copy(1).wait_send()
-    w_pair[1, :, q_cols:o_start] = w_sum_ref[:, q_cols:o_start].astype(bf16)
+    w_pair[1, :, q_cols:o_start] = latent_part[...].astype(bf16)
     for k in range(1, depth):
         w_z_copy(k).start()
     gain_step(2)
@@ -1410,10 +1618,11 @@
     for k in range(1, depth):
         w_z_copy(k).wait_recv()
     own = pl.ds(pl.multiple_of(tp * w_part, w_part), w_part)
-    total = w_sum_ref[own, q_cols:o_start]
+    total = latent_part[own, :]
     for k in range(depth - 1):
         total = total + w_z[k].astype(f32)
-    latent_sum_ref[...] = total
+    latent_ref[...] = total
+    shared_place()
     for k in range(2, depth):
         grad_wait(k)
         grad_on(k)
@@ -1426,14 +1635,11 @@
     grad_drain()
     block_drain()
     for i in range(depth):
-        for slot in range(4):
-            pair_copy(i, slot).wait_send()
-        if i >= depth - 2:
-            for slot in range(2):
-                first_copy(i, slot).wait_send()
-            second_copy(i).wait_send()
-            if i < depth - 1:
-                z_copy(i).wait_send()
+        for slot in range(2):
+            first_copy(i, slot).wait_send()
+        second_copy(i).wait_send()
+        if i < depth - 1:
+            z_copy(i).wait_send()
     for slot in range(4):
         w_pair_copy(slot).wait_send()
     w_first_copy(0).wait_send()
@@ -1443,39 +1649,45 @@
         w_z_copy(k).wait_send()
     for n in range(len(partners)):
         gain_copy(n).wait_send()
+    for m in range(1, 8):
+        for copy in shared_copies(m):
+            copy.wait_send()
 
 
 def tail_call(
-    branch, middle_grad, middle, out_part, router, gain_part, inputs, w_output, w_query, w_latent, w_up,
+    branch, middle_grad, middle, out_part, router, gain_part, inputs, s_in, s_out, w_output, w_query, w_latent, w_up,
     hidden, qn, qr, kv, kr, attended, latent_in, compressed, tables, gain_latent, gain_attn,
-    heads, cid,
+    heads, shared, cid,
 ):
     f32, bf16 = jnp.float32, jnp.bfloat16
-    blocks, depth, rows, width = out_part.shape
+    depth, _, rows, width = out_part.shape
     tokens = hidden.shape[0]
+    blocks = s_in.shape[0]
     rank = compressed.shape[1]
-    q_cols, l_cols = w_query.shape[1], w_latent.shape[1]
+    q_cols, l_cols = w_query.shape[1], rank + 128
     w_rows = width // blocks
     w_cols = q_cols + l_cols + w_output.shape[0] + rank * w_up.shape[1] // width
     dma = pltpu.SemaphoreType.DMA
     vmem, anywhere = pl.BlockSpec(memory_space=pltpu.VMEM), pl.BlockSpec(memory_space=pl.ANY)
     return pl.pallas_call(
-        functools.partial(tail_kernel, depth, heads),
+        functools.partial(tail_kernel, depth, heads, shared),
         out_shape=(
             jax.ShapeDtypeStruct((depth, rows, width), bf16),
             jax.ShapeDtypeStruct((depth, rows, width), bf16),
             jax.ShapeDtypeStruct((8, width), f32),
-            jax.ShapeDtypeStruct((w_rows, w_cols), f32),
+            jax.ShapeDtypeStruct((w_rows, q_cols), f32),
+            jax.ShapeDtypeStruct((w_output.shape[0], w_rows), f32),
+            jax.ShapeDtypeStruct((rank // blocks, w_up.shape[1]), f32),
             jax.ShapeDtypeStruct((w_rows // depth, l_cols), f32),
-            jax.ShapeDtypeStruct((depth, 4, rows, width), bf16),
+            jax.ShapeDtypeStruct((2, w_rows, blocks * shared), f32),
+            jax.ShapeDtypeStruct((blocks * shared, w_rows), f32),
             jax.ShapeDtypeStruct((blocks, w_rows, w_cols), bf16),
         ),
-        in_specs=[vmem, vmem, vmem, anywhere, vmem, vmem, anywhere] + [vmem] * 15,
-        out_specs=(anywhere, anywhere, vmem, vmem, vmem, anywhere, anywhere),
+        in_specs=[vmem, vmem, vmem, anywhere, vmem, vmem, anywhere, anywhere, anywhere] + [vmem] * 15,
+        out_specs=(anywhere, anywhere) + (vmem,) * 7 + (anywhere,),
         scratch_shapes=[
             pltpu.VMEM((depth, rows, width), bf16),
-            pltpu.VMEM((2, 2, rows, width), bf16),
-            pltpu.VMEM((2, 4, rows, width), bf16),
+            pltpu.VMEM((depth, 2, rows, width), bf16),
             pltpu.VMEM((depth, 2, rows, width), bf16),
             pltpu.VMEM((depth, rows, width), bf16),
             pltpu.VMEM((depth - 1, rows, width), bf16),
@@ -1493,26 +1705,39 @@
             pltpu.VMEM((2, w_rows, w_cols), bf16),
             pltpu.VMEM((w_rows, w_cols), bf16),
             pltpu.VMEM((depth - 1, w_rows // depth, l_cols), bf16),
+            pltpu.VMEM((w_rows, l_cols), f32),
+            pltpu.VMEM(s_in.shape, bf16),
+            pltpu.VMEM(s_out.shape, bf16),
             pltpu.VMEM((rows, width), bf16),
             pltpu.VMEM((rows, width), bf16),
             pltpu.VMEM((rows, width), bf16),
             pltpu.VMEM((10, 8, width), f32),
-            dma((2, 2)),
-            dma((depth, 4)), dma((depth, 4)), dma((depth, 2)), dma((depth, 2)), dma((depth,)), dma((depth,)),
+            dma((depth, 2)),
+            dma((depth, 2)), dma((depth, 2)), dma((depth,)), dma((depth,)),
             dma((depth - 1,)), dma((depth - 1,)),
             dma((depth, 2)), dma((depth,)),
             dma((depth - 1,)), dma((depth - 1,)),
             dma((depth, 2)), dma((depth,)),
             dma((depth, 2)), dma((depth,)),
             dma((4,)), dma((4,)), dma((2,)), dma((2,)), dma, dma, dma((depth - 1,)), dma((depth - 1,)),
-            dma((5,)), dma((5,)), dma((3,)), dma((2,)),
+            dma((5,)), dma((5,)), dma((3,)), dma((2,)), dma((8,)), dma((8,)), dma((8,)), dma((8,)),
         ],
         compiler_params=pltpu.CompilerParams(collective_id=cid, has_side_effects=True, vmem_limit_bytes=63 << 20),
     )(
-        branch, middle_grad, middle, out_part, router, gain_part, inputs, w_output, w_query, w_latent, w_up,
+        branch, middle_grad, middle, out_part, router, gain_part, inputs, s_in, s_out, w_output, w_query, w_latent, w_up,
         hidden, qn, qr, kv, kr, attended, latent_in, compressed, tables,
         gain_latent.reshape(1, rank), gain_attn.reshape(1, width),
     )
+
+
+def rope_tables(length):
+    half = ROPE // 2
+    inverse = np.exp(np.arange(half) * (-math.log(10000.0) / half))
+    angle = np.arange(length)[:, None] * inverse[None, :]
+    cosine, sine = np.cos(angle), np.sin(angle)
+    zero = np.zeros_like(sine)
+    parts = ([cosine] * 4, [-sine, zero] * 2, [zero, sine] * 2)
+    return jnp.asarray(np.stack([np.concatenate(p, axis=1) for p in parts]), jnp.float32)
 
 
 def padded_hidden(routed, shared):
@@ -1590,109 +1815,27 @@
         [w_expert_out[0], shared_out, jnp.zeros((fill, model_width), bf16)], axis=0
     )
 
-    resid = inputs.astype(f32)
-    inv_first = lax.rsqrt(jnp.mean(resid * resid, axis=-1, keepdims=True) + EPSILON)
-    normed_first = resid * inv_first
-    hidden_attn = (normed_first * gain_attn).astype(bf16)
-    cosine, sine_table = angles(tokens, ROPE)
-    zero = jnp.zeros_like(sine_table)
-    tables = jnp.stack(
-        [
-            jnp.tile(cosine, (1, 4)),
-            jnp.tile(jnp.concatenate([-sine_table, zero], axis=1), (1, 2)),
-            jnp.tile(jnp.concatenate([zero, sine_table], axis=1), (1, 2)),
-        ]
-    )
-    by_head = w_query.reshape(model_width, heads_here, qk_width)
-    w_query_sorted = jnp.concatenate(
-        [
-            by_head[..., :NOPE].reshape(model_width, heads_here * NOPE),
-            by_head[..., NOPE:].reshape(model_width, heads_here * ROPE),
-        ],
-        axis=1,
-    )
-    w_latent_wide = jnp.pad(w_latent, ((0, 0), (0, 128 - ROPE)))
-    query_raw = jnp.dot(hidden_attn, w_query_sorted, preferred_element_type=f32)
-    query_nope = query_raw[:, : heads_here * NOPE].astype(bf16)
-    query_rope = rotate(
-        query_raw[:, heads_here * NOPE :].reshape(tokens, heads_here, ROPE),
-        cosine[:, None],
-        sine_table[:, None],
-    ).astype(bf16)
-    latent = jnp.dot(hidden_attn, w_latent, preferred_element_type=f32)
-    compressed = latent[:, :KV_RANK]
-    inv_latent = lax.rsqrt(jnp.mean(compressed * compressed, axis=-1, keepdims=True) + EPSILON)
-    latent_in = (compressed * inv_latent * gain_latent).astype(bf16)
-    key_rope = rotate(latent[:, KV_RANK:], cosine, sine_table).astype(bf16)
-    key_pair = jnp.stack(
-        [jnp.pad(key_rope, ((0, 0), (0, ROPE))), jnp.pad(key_rope, ((0, 0), (ROPE, 0)))]
-    )
-    key_value = jnp.dot(latent_in, w_latent_up, preferred_element_type=f32).astype(bf16)
-    per_head = key_value.reshape(tokens, heads_here, NOPE + VDIM)
-    block_ids = jnp.arange(tokens) // BLOCK
-    allowed = block_ids[None, :] <= block_ids[:, None]
-    query_rot = jnp.concatenate(
-        [query_nope.reshape(tokens, heads_here, NOPE), query_rope], axis=-1
-    )
-    scores = attention_scores(query_rot, per_head[..., :NOPE], key_rope, score_scale, allowed)
-    exp_scores = jnp.exp(scores - jnp.max(scores, axis=-1, keepdims=True))
-    attn_probs = exp_scores / jnp.sum(exp_scores, axis=-1, keepdims=True)
-    attended = (
-        jnp.einsum(
-            "hqk,khd->qhd", attn_probs.astype(bf16), per_head[..., NOPE:], preferred_element_type=f32
+    attn_part, hidden_attn, query_nope, query_rope, key_value, key_pair, attended, latent_in, compressed = (
+        attention_call(
+            inputs, gain_attn, w_query, w_latent, gain_latent, w_latent_up, w_output, rope_tables(tokens), heads_here
         )
-        .astype(bf16)
-        .reshape(tokens, heads_here * VDIM)
-    )
-    attn_part = jnp.dot(attended, w_output, preferred_element_type=f32).astype(bf16)
-
+    )
     middle, hidden_all, cot_all, hidden_grads, gated, out_part, rows_grad = experts_call(
         attn_part, inputs, gain_ffn, cotangent, kept_lanes, w_in, w_out,
         ep_count, tp_count, routed, shared, experts, 0,
     )
-    middle_grad, branch, gain_ffn_part, in_grad_w, out_grad_w = sum_call(
-        rows_grad, hidden_all, hidden_grads, gated, cot_all, middle, gain_ffn, 1
-    )
-    base = routed + shared
-    in_grad_gate, in_grad_up = in_grad_w[:, :hidden], in_grad_w[:, hidden:]
-    router_wide = jnp.pad(
-        in_grad_gate[:, base : base + experts], ((0, 0), (ROPE, 128 - ROPE - experts))
-    ).astype(bf16)
-    block_out, grad_inputs, gains, w_sum, latent_sum, _, _ = tail_call(
-        branch, middle_grad, middle, out_part, router_wide, gain_ffn_part, inputs,
-        w_output, w_query_sorted, w_latent_wide, w_latent_up, hidden_attn,
-        query_nope, query_rope.reshape(tokens, heads_here * ROPE), key_value, key_pair,
-        attended, latent_in, compressed, tables, gain_latent, gain_attn, heads_here, 2,
-    )
-    grad_expert_in = jnp.stack([in_grad_gate[:, :routed], in_grad_up[:, :routed]])[None]
-    grad_expert_out = out_grad_w[None, :routed]
-    shared_in_part = jnp.stack([in_grad_gate[:, routed:base], in_grad_up[:, routed:base]])
-    grad_shared_in = lax.all_to_all(
-        shared_in_part.astype(bf16), "ep", split_axis=1, concat_axis=2, tiled=True
-    ).astype(f32)
-    grad_shared_out = lax.all_to_all(
-        out_grad_w[routed:base].astype(bf16), "ep", split_axis=1, concat_axis=0, tiled=True
-    ).astype(f32)
-
-    w_rows = model_width // ep_count
-    nope_all, rope_all = heads_here * NOPE, heads_here * qk_width
-    grad_query = jnp.concatenate(
-        [
-            w_sum[:, :nope_all].reshape(w_rows, heads_here, NOPE),
-            w_sum[:, nope_all:rope_all].reshape(w_rows, heads_here, ROPE),
-        ],
-        axis=-1,
-    ).reshape(w_rows, rope_all)
-    o_start = rope_all + w_latent_wide.shape[1]
-    o_cols = model_width // ep_count
-    o_pieces = heads_here * VDIM // w_rows
-    grad_output = jnp.concatenate(
-        [w_sum[:, o_start + n * o_cols : o_start + (n + 1) * o_cols] for n in range(o_pieces)], axis=0
-    )
-    u_start = o_start + o_pieces * o_cols
-    u_rows = KV_RANK // ep_count
-    grad_latent_up = jnp.concatenate(
-        [w_sum[n * u_rows : (n + 1) * u_rows, u_start:] for n in range(w_rows // u_rows)], axis=1
+    middle_grad, branch, gain_ffn_part, grad_expert_in, grad_expert_out, shared_in_part, shared_out_part, router_part, layer_sum, _ = (
+        sum_call(
+            rows_grad, out_part, hidden_all, hidden_grads, gated, cot_all, middle, gain_ffn, routed, shared, experts, 1
+        )
+    )
+    block_out, grad_inputs, gains, grad_query, grad_output, grad_latent_up, latent_sum, grad_shared_in, grad_shared_out, _ = (
+        tail_call(
+            branch, middle_grad, middle, layer_sum, router_part, gain_ffn_part, inputs, shared_in_part, shared_out_part,
+            w_output, w_query, w_latent, w_latent_up, hidden_attn,
+            query_nope, query_rope, key_value, key_pair,
+            attended, latent_in, compressed, rope_tables(tokens), gain_latent, gain_attn, heads_here, shared, 2,
+        )
     )
     grad_latent = latent_sum[:, : KV_RANK + ROPE]
     grad_router = latent_sum[:, KV_RANK + ROPE : KV_RANK + ROPE + experts]

time: 734 us -> 612 us (0.83)
  local copies, waits for them, and re-layouts: 113 us -> 54.7 us
  other arithmetic: 27.6 us -> 4.82 us
  matrix products: 18 us -> 0 us
  Pallas kernels: 552 us -> 536 us
  starting transfers between devices: 12.7 us -> 5.17 us
    another operation x9 -> x0, local copies, waits for them, and re-layouts: 20.5 us -> none  [the longest x2 10.6 us: body_dense(): jnp.stack([in_grad_gate[:, routed:base], in_grad_up[:, routed:base]])]
    dot_general x7 -> x0, matrix products: 18 us -> none  [the longest x1 5.53 us: body_dense(): jnp.einsum('hqk,khd->qhd', attn_probs.astype(bf16), per_head[..., NOPE:],...]
    slice x12 -> x0, local copies, waits for them, and re-layouts: 15.8 us -> none  [the longest x1 3.31 us: body_dense(): by_head[..., :NOPE].reshape(model_width, heads_here * NOPE)]
    pallas_call x2 -> x3, Pallas kernels: 356 us -> 346 us  [the longest x1 225 us: tail_call(): pl.pallas_call(functools.partial(tail_kernel, depth, heads, shared), out_...]
    reshape x5 -> x0, local copies, waits for them, and re-layouts: 9.68 us -> none  [the longest x1 3.93 us: body_dense(): by_head[..., :NOPE].reshape(model_width, heads_here * NOPE)]
    concatenate x5 -> x0, other arithmetic: 7.86 us -> none  [the longest x1 2.05 us: body_dense(): jnp.concatenate([w_sum[:, :nope_all].reshape(w_rows, heads_here, NOPE), w...]
    all_to_all x2 -> x0, starting transfers between devices: 7.56 us -> none  [the longest x1 4.12 us: body_dense(): lax.all_to_all(shared_in_part.astype(bf16), 'ep', split_axis=1, concat_ax...]
    unnamed x86 -> x59, local copies, waits for them, and re-layouts: 34.7 us -> 35.3 us
  transfers between devices with their start and end apart: 3 -> 1, of which waited for: 1 -> 0; matrix products, arithmetic and copies ran while one was open for 15% -> 5% of each run, Pallas kernels for 0% -> 3%
where the time goes in v5:
time: 612 us; the launch traced here: 602 us
  Pallas kernels  536 us (88%)
  local copies, waits for them, and re-layouts  54.7 us (9%)
    pallas_call x1, Pallas kernels, tail_call(): pl.pallas_call(functools.partial(tail_kernel, depth, heads, shared), out_...  225 us
    pallas_call x1, Pallas kernels, experts_call(): pl.pallas_call(functools.partial(experts_kernel, depth, blocks, routed, s...  190 us
    pallas_call x1, Pallas kernels, sum_call(): pl.pallas_call(functools.partial(sum_kernel, depth, routed, shared, exper...  102 us
    unnamed x59, local copies, waits for them, and re-layouts  35.3 us
    pallas_call x1, Pallas kernels, attention_call(): pl.pallas_call(functools.partial(attention_kernel, heads), out_shape=(sha...  19.1 us
  transfers between devices with their start and end apart: 1, of which 0 were waited for; matrix products, arithmetic and copies ran while one was open for 5% of the time, Pallas kernels for 3%

profile of v5, /device:TPU:0, one launch (start us, length us, event | category | flops | bytes accessed | tf_op | source)
XLA Modules:
  0.0 602.2 jit_solution(6540040888005121833)
XLA Ops:
  0.6 0.7 broadcast_compare_fusion
  1.4 0.7 fusion.1
  2.1 0.5 broadcast.7
  2.7 0.7 reduce
  3.4 0.6 reshape.73
  4.0 5.2 all-to-all-start
  9.1 0.9 fusion.9
  10.1 2.0 fusion.7
  12.1 0.0 copy-start.14
  12.1 0.1 pad.7.clone
  12.2 1.1 constant_dynamic-slice_fusion.4
  13.3 2.0 constant_dynamic-slice_fusion.5
  15.3 0.0 copy-done.14
  15.3 1.7 maximum_maximum_fusion.w_out_ref
  17.0 0.3 copy.75
  17.3 0.9 pad.4
  18.2 2.0 copy.85
  20.2 2.0 copy.83
  22.2 4.3 copy.70.w_latent
  26.5 1.6 copy.84
  28.1 1.6 copy.81
  29.6 0.1 broadcast_in_dim.7
  29.7 0.0 copy-start
  29.7 0.0 copy-start.1
  29.7 0.0 copy-start.9
  29.7 0.0 copy-start.10
  29.7 8.4 %concatenate.10.w_in_ref = bf16[2048,1024]{1,0:T(8,128)(2,1)} concatenate(bf16[2048,352]{1,0:T(8,128)(2,1)} %bitcast.37, bf16[2048,88]{1,0:T(8,128)(2,1)} %bitcast.39, bf16[2048,72]{1,0:T(8,128)(2,1)} %pad.4, bf16[2048,352]{1,0:T(8,128)(2,1)} %bitcast.36, bf16[2048,88]{1,0:T(8,128)(2,1)} %bitcast.38, bf16[2048,72]{1,0:T(8,128)(2,1)S(1)} %broadcast_in_dim.7), dimensions={1} | concatenate | bytes 8388608 | tf_op jit(solution)/shard_map/concatenate | solution.py:1803
  38.2 0.0 copy-done
  38.2 0.0 copy-done.1
  38.2 0.0 copy-done.9
  38.2 0.0 copy-done.10
  38.2 19.1 %shard_map.281 = (bf16[512,2048]{1,0:T(8,128)(2,1)}, bf16[512,2048]{1,0:T(8,128)(2,1)}, bf16[512,512]{1,0:T(8,128)(2,1)S(1)}, bf16[512,256]{1,0:T(8,128)(2,1)S(1...) custom-call(bf16[512,2048]{1,0:T(8,128)(2,1)} %inputs_ref.1, ...), custom_call_target="tpu_custom_call" | custom-call | tf_op jit(solution)/shard_map/pallas_call | solution.py:529
  57.3 1.0 copy-done.2
  58.3 0.8 copy-done.4
  59.1 0.8 copy-done.5
  59.9 0.8 copy-done.6
  60.7 0.7 copy-done.8
  61.4 0.0 all-to-all-done
  61.4 1.6 broadcast_in_dim.6.kept_ref
  63.0 189.8 %shard_map.282 = (f32[128,2048]{1,0:T(8,128)}, bf16[4,8,128,2048]{3,2,1,0:T(8,128)(2,1)}, bf16[4,8,128,2048]{3,2,1,0:T(8,128)(2,1)}, bf16[4,8,128,1024]{3,2,1,0:...) custom-call(bf16[512,2048]{1,0:T(8,128)(2,1)} %get-tuple-element.48., ...), custom_call_target="tpu_custom_call" | custom-call | tf_op jit(solution)/shard_map/pallas_call | solution.py:864
  252.8 0.0 copy-done.3
  252.8 0.0 copy-done.7
  252.8 102.2 %shard_map.283 = (f32[128,2048]{1,0:T(8,128)}, bf16[128,2048]{1,0:T(8,128)(2,1)}, f32[8,2048]{1,0:T(8,128)}, f32[1,2,2048,352]{3,2,1,0:T(8,128)}, f32[1,352,2048...) custom-call(bf16[4,8,128,2048]{3,2,1,0:T(8,128)(2,1)} %get-tuple-ele, ...), custom_call_target="tpu_custom_call" | custom-call | tf_op jit(solution)/shard_map/pallas_call | solution.py:1161
  355.1 225.2 %shard_map.284 = (bf16[4,128,2048]{2,1,0:T(8,128)(2,1)}, bf16[4,128,2048]{2,1,0:T(8,128)(2,1)}, f32[8,2048]{1,0:T(8,128)}, f32[256,768]{1,0:T(8,128)}, f32[512,2...) custom-call(bf16[128,2048]{1,0:T(8,128)(2,1)} %get-tuple-element.56., ...), custom_call_target="tpu_custom_call" | custom-call | tf_op jit(solution)/shard_map/pallas_call | solution.py:1672
  580.2 1.0 fusion.8
  581.2 0.8 slice.35
  582.0 0.7 copy.78
  582.7 3.0 copy.79
  585.7 6.5 %copy.80 = f32[1,2,2048,352]{2,3,1,0:T(8,128)} copy(f32[1,2,2048,352]{3,2,1,0:T(8,128)} %get-tuple-element.136) | data formatting | bytes 11534336
  592.2 0.6 fusion.5
  592.8 0.6 fusion.4
  593.4 0.0 copy-done.13
  593.4 1.3 copy.100
  594.7 0.0 copy-done.12
  594.7 1.3 copy.101
  596.0 0.3 copy-done.15
  596.3 0.9 copy.102
  597.2 0.0 copy-done.19
  597.2 0.7 copy.103
  597.8 0.7 copy.104
  598.6 0.8 copy.105
  599.3 0.0 copy-done.16
  599.3 0.9 copy.106
  600.2 1.6 copy.107
  (24 shorter events, 0.1 us)
Async XLA Ops:
  4.0 57.4 %all-to-all-start = ((bf16[8,2,256]{2,1,0:T(2,128)(2,1)}), bf16[8,2,256]{2,1,0:T(2,128)(2,1)S(1)}, u32[]{:S(2)}, u32[]{:S(2)}) async-start(bf16[8,2,256]{2,1,0:T(2,128)(2,1)} %reshape.73), calls=%async_computation | async-start | bytes 16384 | tf_op jit(solution)/shard_map/all_to_all | solution.py:1788
  12.1 3.2 copy-start.14
  29.7 8.5 %copy-start = (bf16[512,1024]{1,0:T(8,128)(2,1)S(1)}, bf16[512,1024]{1,0:T(8,128)(2,1)}, u32[]{:S(2)}) copy-start(bf16[512,1024]{1,0:T(8,128)(2,1)} %w_up.3) | copy-start | bytes 3145732
  29.7 8.5 %copy-start.1 = (f32[3,512,128]{2,1,0:T(8,128)S(1)}, f32[3,512,128]{2,1,0:T(8,128)}, u32[]{:S(2)}) copy-start(f32[3,512,128]{2,1,0:T(8,128)} %constant.36.clone.tables) | copy-start | bytes 2359300
  29.7 8.5 %copy-start.9 = (f32[2048]{0:T(1024)S(1)}, f32[2048]{0:T(1024)}, u32[]{:S(2)}) copy-start(f32[2048]{0:T(1024)} %param.19) | copy-start | bytes 24580
  29.7 8.5 %copy-start.10 = (f32[512]{0:T(512)S(1)}, f32[512]{0:T(512)}, u32[]{:S(2)}) copy-start(f32[512]{0:T(512)} %param.22) | copy-start | bytes 6148
  57.2 1.0 copy-start.2
  58.3 0.8 copy-start.4
  59.1 0.8 copy-start.5
  59.9 0.8 copy-start.6
  60.7 0.7 copy-start.8
  61.4 191.4 %copy-start.3 = (f32[512,512]{1,0:T(8,128)}, f32[512,512]{1,0:T(8,128)S(1)}, u32[]{:S(2)}) copy-start(f32[512,512]{1,0:T(8,128)S(1)} %get-tuple-element.70.compressed) | copy-start | bytes 3145732
  61.4 191.4 %copy-start.7 = (bf16[512,256]{1,0:T(8,128)(2,1)}, bf16[512,256]{1,0:T(8,128)(2,1)S(1)}, u32[]{:S(2)}) copy-start(bf16[512,256]{1,0:T(8,128)(2,1)S(1)} %get-tuple-element.65.qr_ref) | copy-start | bytes 786436
  585.7 7.7 %copy-start.13 = (bf16[4,128,2048]{2,1,0:T(8,128)(2,1)S(1)}, bf16[4,128,2048]{2,1,0:T(8,128)(2,1)}, u32[]{:S(2)}) copy-start(bf16[4,128,2048]{2,1,0:T(8,128)(2,1)} %get-tuple-element.71) | copy-start | bytes 6291460
  592.2 2.5 copy-start.12
  594.7 1.6 copy-start.15
  594.7 2.5 copy-start.19
  594.7 3.2 copy-start.18
  594.7 3.9 copy-start.17
  594.7 4.6 copy-start.16
  596.3 3.9 copy-start.11

commit v6 on v5

--- a/solution.py
+++ b/solution.py
@@ -453,35 +453,175 @@
     lax.fori_loop(0, dst.shape[0] // 16, body, 0)
 
 
+def line_sum(own_of, got, send_sem, recv_sem, ep, tp, depth):
+    far = line_order(tp)[::-1]
+    between = (tp > 0) & (tp < depth - 1)
+    near = jnp.where(tp > 0, tp - 1, tp + 1)
+
+    def copy(n, src):
+        chunk = far[n]
+        to = jnp.where(chunk > tp, tp + 1, tp - 1)
+        slot = jnp.where(chunk == tp - 1, depth, chunk)
+        return remote(src, got.at[slot], send_sem.at[n], recv_sem.at[slot], (ep, to))
+
+    def arrive(slot):
+        remote(got.at[0], got.at[slot], send_sem.at[0], recv_sem.at[slot], (ep, near)).wait_recv()
+
+    def start(n):
+        @pl.when(jnp.logical_not(between))
+        def _():
+            copy(n, own_of(n)).start()
+
+    def pass_on(n):
+        @pl.when(between)
+        def _():
+            held = got.at[far[n]]
+            arrive(far[n])
+            add_rows(held, own_of(n), held)
+            copy(n, held).start()
+
+    def clear():
+        @pl.when(tp == 0)
+        def _():
+            got[0] = jnp.zeros_like(got[0])
+
+        @pl.when(tp == depth - 1)
+        def _():
+            got[depth] = jnp.zeros_like(got[depth])
+
+    def finish():
+        @pl.when(tp > 0)
+        def _():
+            arrive(tp)
+
+        @pl.when(tp < depth - 1)
+        def _():
+            arrive(depth)
+
+    def drain():
+        for n in range(depth - 1):
+            copy(n, got.at[0]).wait_send()
+
+    return clear, start, pass_on, finish, drain
+
+
 def turn(slab, table, sign):
     cosine, front, second = table
     return slab * cosine + sign * (pltpu.roll(slab, 96, 1) * front + pltpu.roll(slab, 32, 1) * second)
 
 
-def attention_kernel(
-    heads,
-    inputs, gain_attn, w_query, w_latent, gain_latent, w_up, w_output, tables,
-    part, hidden, qn_ref, qr_ref, kv, kr_ref, attended, latent_in, compressed,
-    rope_slab,
+def experts_kernel(
+    depth, blocks, heads, routed, shared, experts,
+    inputs_ref, gain_attn, w_query, w_latent, gain_latent, w_up, w_output, tables,
+    gain_ref, cot_ref, kept_hbm, e_in, e_out, s_in, s_out,
+    middle_ref, h_out, cot_all, grads_out, gated_out, rows_out,
+    hidden_out, qn_out, qr_out, kv_out, kr_out, attended_out, latent_in_out, compressed_out, w_out_out,
+    part_ref, hidden, qn_ref, qr_ref, kv, kr_ref, attended, latent_in, compressed, rope_slab,
+    kept_ref, w_in_ref, w_out_ref, e_stage,
+    h_all, got_z, cot_tile, gu, act_grad, prob_lanes, diff_lanes, pair_lanes,
+    grads_tile, gated_tile, rows_tile,
+    weight_sem, stage_sem, save_sem, local_sem, z_send, z_recv, line_send, line_recv, h_send, h_recv, c_send, c_recv, b_send, b_recv, tile_sem, store_sem,
 ):
     f32, bf16 = jnp.float32, jnp.bfloat16
-    tokens, width = inputs.shape
+    ep, tp = lax.axis_index("ep"), lax.axis_index("tp")
+    pair, xn, yn = plane_partners(ep)
+    parity = lax.rem(ep, 2)
+    passed = jnp.where(parity == 0, xn, yn)
+    onward = jnp.where(parity == 0, yn, xn)
+    diag = xn + yn - ep
+    rows = h_all.shape[2]
+    width = h_all.shape[3]
+    hidden_units = w_out_ref.shape[0]
+    tokens = inputs_ref.shape[0]
     rank = compressed.shape[1]
+    lanes = lax.broadcasted_iota(jnp.int32, (1, 128), 1)
     across = (((1,), (1,)), ((), ()))
     score_scale = (NOPE + ROPE) ** (-0.5)
 
     def dot(a, b, dims=(((1,), (0,)), ((), ()))):
         return lax.dot_general(a, b, dims, preferred_element_type=f32)
 
-    def norm_rows(r, _):
+    half = blocks // 2
+    tile = half * rows
+    up, down = jnp.minimum(tp + 1, depth - 1), jnp.maximum(tp - 1, 0)
+
+    def twin(block):
+        return block + pair - ep
+
+    greet([(pair, tp), (xn, tp), (yn, tp)] + [(ep, lax.rem(tp + k, depth)) for k in range(1, depth)])
+
+    def part_rows(n):
+        return part_ref.at[pl.ds(pl.multiple_of(line_order(tp)[depth - 1 - n] * rows, rows), rows)]
+
+    z_clear, z_start, z_pass, z_finish, z_drain = line_sum(part_rows, got_z, z_send, z_recv, ep, tp, depth)
+    z_clear()
+    weight_loads = [
+        pltpu.make_async_copy(kept_hbm, kept_ref, weight_sem.at[0]),
+        pltpu.make_async_copy(e_out.at[0], w_out_ref.at[pl.ds(0, routed)], weight_sem.at[1]),
+        pltpu.make_async_copy(s_out, w_out_ref.at[pl.ds(routed, hidden_units - routed)], weight_sem.at[2]),
+    ]
+    for g in range(2):
+        at = pl.ds(g * hidden_units + routed // 128 * 128, s_in.shape[2])
+        weight_loads.append(pltpu.make_async_copy(s_in.at[g], w_in_ref.at[:, at], weight_sem.at[3 + g]))
+    piece = e_stage.shape[1]
+    pieces = width // piece
+
+    def e_load(n):
+        at = pl.ds(pl.multiple_of(lax.rem(n, pieces) * piece, piece), piece)
+        return pltpu.make_async_copy(e_in.at[0, lax.div(n, pieces), at], e_stage.at[lax.rem(n, 2)], stage_sem.at[lax.rem(n, 2)])
+
+    def h_copy(block, chunk, slot, to):
+        ref = h_all.at[chunk, block]
+        return remote(ref, ref, h_send.at[chunk, slot], h_recv.at[chunk, slot], (to, tp))
+
+    def c_copy(block, chunk, slot, to):
+        ref = cot_all.at[chunk, block]
+        return remote(ref, ref, c_send.at[chunk, slot], c_recv.at[chunk, slot], (to, tp))
+
+    def c_first(chunk, slot, to):
+        src = cot_ref.at[pl.ds(pl.multiple_of(chunk * rows, rows), rows)]
+        return remote(src, cot_all.at[chunk, ep], c_send.at[chunk, slot], c_recv.at[chunk, slot], (to, tp))
+
+    buddy = tp + 1 - 2 * lax.rem(tp, 2)
+    skipped, theirs = depth - 1 - tp, depth - 1 - buddy
+
+    def buddy_copy(n, chunk):
+        ref = cot_all.at[chunk, (xn, yn, diag)[n]]
+        return remote(ref, ref, b_send.at[n], b_recv.at[n], (ep, buddy))
+
+    def own_cot_in(chunk):
+        src = cot_ref.at[pl.ds(pl.multiple_of(chunk * rows, rows), rows)]
+        return pltpu.make_async_copy(src, rows_tile.at[0, chunk], local_sem.at[chunk])
+
+    def own_cot_out(chunk):
+        return pltpu.make_async_copy(rows_tile.at[0, chunk], cot_all.at[chunk, ep], local_sem.at[chunk])
+
+    order = line_order(tp)
+
+    def order_at(k):
+        return jnp.where(k == 0, order[0], jnp.where(k == 1, order[1], jnp.where(k == 2, order[2], order[3])))
+
+    for k in range(depth):
+
+        @pl.when(order[k] != skipped)
+        def _():
+            c_first(order[k], 1, xn).start()
+            c_first(order[k], 2, yn).start()
+
+        c_first(order[k], 0, pair).start()
+        own_cot_in(k).start()
+    for copy in weight_loads:
+        copy.start()
+    e_load(0).start()
+
+    def first_norm(r, _):
         at = pl.ds(pl.multiple_of(r * 16, 16), 16)
-        v = inputs[at, :].astype(f32)
+        v = inputs_ref[at, :].astype(f32)
         inverse = lax.rsqrt(jnp.mean(v * v, axis=-1, keepdims=True) + EPSILON)
         hidden[at, :] = (v * inverse * gain_attn[...]).astype(bf16)
         return 0
 
-    lax.fori_loop(0, tokens // 16, norm_rows, 0)
-    lanes = lax.broadcasted_iota(jnp.int32, (1, 128), 1)
+    lax.fori_loop(0, tokens // 16, first_norm, 0)
     table = tuple(tables[n] for n in range(3))
     latent = dot(hidden[...], w_latent[...])
     held = latent[:, :rank]
@@ -494,9 +634,9 @@
     kr_ref[0] = key.astype(bf16)
     kr_ref[1] = pltpu.roll(key, 64, 1).astype(bf16)
     kv[...] = dot(latent_in[...], w_up[...]).astype(bf16)
-    pair = 2 * (NOPE + ROPE)
+    wide = 2 * (NOPE + ROPE)
     for p in range(heads // 2):
-        found = dot(hidden[...], w_query[:, p * pair : (p + 1) * pair])
+        found = dot(hidden[...], w_query[:, p * wide : (p + 1) * wide])
         slabs = [found[:, n : n + 128] for n in (0, 128, 256)]
         qn_ref[:, 2 * p * NOPE : (2 * p + 1) * NOPE] = slabs[0].astype(bf16)
         odd = pltpu.roll(jnp.where(lanes < 64, slabs[2], slabs[1]), 64, 1)
@@ -514,114 +654,60 @@
             probs = exps / jnp.sum(exps, axis=-1, keepdims=True)
             attended[own, at] = dot(probs.astype(bf16), kv[keys, h * 256 + 128 : h * 256 + 256]).astype(bf16)
     for n in range(0, width, 512):
-        part[:, n : n + 512] = dot(attended[...], w_output[:, n : n + 512]).astype(bf16)
-
-
-def attention_call(inputs, gain_attn, w_query, w_latent, gain_latent, w_up, w_output, tables, heads):
-    f32, bf16 = jnp.float32, jnp.bfloat16
-    tokens, width = inputs.shape
-    rank = w_up.shape[0]
-    vmem = pl.BlockSpec(memory_space=pltpu.VMEM)
-
-    def shape(*size, kind=bf16):
-        return jax.ShapeDtypeStruct(size, kind)
-
-    return pl.pallas_call(
-        functools.partial(attention_kernel, heads),
-        out_shape=(
-            shape(tokens, width), shape(tokens, width), shape(tokens, heads * NOPE), shape(tokens, heads * ROPE),
-            shape(tokens, heads * (NOPE + VDIM)), shape(2, tokens, 128), shape(tokens, heads * VDIM),
-            shape(tokens, rank), shape(tokens, rank, kind=f32),
-        ),
-        in_specs=[vmem] * 8,
-        out_specs=(vmem,) * 9,
-        scratch_shapes=[pltpu.VMEM((tokens, 128), f32)],
-        compiler_params=pltpu.CompilerParams(vmem_limit_bytes=48 << 20),
-    )(inputs, gain_attn.reshape(1, width), w_query, w_latent, gain_latent.reshape(1, rank), w_up, w_output, tables)
-
-
-def experts_kernel(
-    depth, blocks, routed, shared, experts,
-    part_ref, resid_ref, gain_ref, cot_ref, kept_ref, w_in_ref, w_out_ref,
-    middle_ref, h_out, cot_all, grads_out, gated_out, out_out, rows_out,
-    h_all, got_z, resid_own, cot_tile, gu, act_grad, prob_lanes, diff_lanes, pair_lanes,
-    grads_tile, gated_tile, out_tile, rows_tile,
-    local_sem, z_send, z_recv, line_send, line_recv, h_send, h_recv, c_send, c_recv, tile_sem, store_sem,
-):
-    f32, bf16 = jnp.float32, jnp.bfloat16
-    ep, tp = lax.axis_index("ep"), lax.axis_index("tp")
-    pair, xn, yn = plane_partners(ep)
-    parity = lax.rem(ep, 2)
-    passed = jnp.where(parity == 0, xn, yn)
-    onward = jnp.where(parity == 0, yn, xn)
-    diag = xn + yn - ep
-    rows = h_all.shape[2]
-    width = h_all.shape[3]
-    hidden = w_out_ref.shape[0]
-    half = blocks // 2
-    tile = half * rows
-    up, down = jnp.minimum(tp + 1, depth - 1), jnp.maximum(tp - 1, 0)
-
-    def twin(block):
-        return block + pair - ep
-
-    greet([(pair, tp), (xn, tp), (yn, tp)] + [(ep, lax.rem(tp + k, depth)) for k in range(1, depth)])
-
-    def z_copy(k):
-        to = lax.rem(tp + k, depth)
-        start = pl.multiple_of(to * rows, rows)
-        return remote(part_ref.at[pl.ds(start, rows)], got_z.at[k - 1], z_send.at[k - 1], z_recv.at[k - 1], (ep, to))
-
-    for k in range(1, depth):
-        z_copy(k).start()
-
-    def h_copy(block, chunk, slot, to):
-        ref = h_all.at[chunk, block]
-        return remote(ref, ref, h_send.at[chunk, slot], h_recv.at[chunk, slot], (to, tp))
-
-    def c_copy(block, chunk, slot, to):
-        ref = cot_all.at[chunk, block]
-        return remote(ref, ref, c_send.at[chunk, slot], c_recv.at[chunk, slot], (to, tp))
-
-    def c_first(chunk, slot, to):
-        src = cot_ref.at[pl.ds(pl.multiple_of(chunk * rows, rows), rows)]
-        return remote(src, cot_all.at[chunk, ep], c_send.at[chunk, slot], c_recv.at[chunk, slot], (to, tp))
-
-    def own_cot_in(chunk):
-        src = cot_ref.at[pl.ds(pl.multiple_of(chunk * rows, rows), rows)]
-        return pltpu.make_async_copy(src, out_tile.at[0, chunk], local_sem.at[chunk])
-
-    def own_cot_out(chunk):
-        return pltpu.make_async_copy(out_tile.at[0, chunk], cot_all.at[chunk, ep], local_sem.at[chunk])
-
-    order = line_order(tp)
-
-    def order_at(k):
-        return jnp.where(k == 0, order[0], jnp.where(k == 1, order[1], jnp.where(k == 2, order[2], order[3])))
-
-    resid_copy = pltpu.make_async_copy(
-        resid_ref.at[pl.ds(pl.multiple_of(tp * rows, rows), rows)], resid_own, local_sem.at[depth]
-    )
-    resid_copy.start()
-    for k in range(depth):
-        c_first(order[k], 1, xn).start()
-        c_first(order[k], 2, yn).start()
-        c_first(order[k], 0, pair).start()
-        own_cot_in(k).start()
-    resid_copy.wait()
+        part_ref[:, n : n + 512] = dot(attended[...], w_output[:, n : n + 512]).astype(bf16)
+    for n in range(depth - 1):
+        z_start(n)
+    saves = [
+        pltpu.make_async_copy(src, dst, save_sem.at[n])
+        for n, (src, dst) in enumerate(
+            (
+                (hidden, hidden_out), (qn_ref, qn_out), (qr_ref, qr_out), (kv, kv_out), (kr_ref, kr_out),
+                (attended, attended_out), (latent_in, latent_in_out), (compressed, compressed_out),
+            )
+        )
+    ]
+    for copy in saves:
+        copy.start()
     for k in range(depth):
         own_cot_in(k).wait()
         own_cot_out(k).start()
-    for k in range(1, depth):
-        z_copy(k).wait_recv()
+
+    def e_place(n, _):
+        e_load(n).wait()
+
+        @pl.when(n + 1 < 2 * pieces)
+        def _():
+            e_load(n + 1).start()
+
+        at = pl.ds(pl.multiple_of(lax.rem(n, pieces) * piece, piece), piece)
+
+        @pl.when(n < pieces)
+        def _():
+            w_in_ref[at, 0:routed] = e_stage[lax.rem(n, 2)]
+
+        @pl.when(n >= pieces)
+        def _():
+            w_in_ref[at, hidden_units : hidden_units + routed] = e_stage[lax.rem(n, 2)]
+
+        return 0
+
+    for copy in weight_loads:
+        copy.wait()
+    w_out_save = pltpu.make_async_copy(w_out_ref, w_out_out, save_sem.at[8])
+    w_out_save.start()
+    lax.fori_loop(0, pieces, e_place, 0)
+    z_pass(0)
+    lax.fori_loop(pieces, 2 * pieces, e_place, 0)
+    z_pass(1)
+    z_pass(2)
+    z_finish()
 
     def norm_rows(r, _):
         here = pl.ds(pl.multiple_of(r * 16, 16), 16)
         own = pl.ds(pl.multiple_of(tp * rows + r * 16, 16), 16)
         total = part_ref[own, :].astype(f32)
-        for k in range(depth - 1):
-            total = total + got_z[k, here, :].astype(f32)
-        middle = resid_own[here, :].astype(f32) + total
+        total = total + got_z[tp, here, :].astype(f32) + got_z[depth, here, :].astype(f32)
+        middle = inputs_ref[own, :].astype(f32) + total
         inverse = lax.rsqrt(jnp.mean(middle * middle, axis=-1, keepdims=True) + EPSILON)
         middle_ref[here, :] = middle
         h_all[tp, ep, here, :] = (middle * inverse * gain_ref[...]).astype(bf16)
@@ -665,10 +751,14 @@
         copy(xn, chunk, 4, pair).start()
         copy(yn, chunk, 5, pair).start()
 
-    def forward_diag(chunk):
-        for copy in (h_copy, c_copy):
-            copy(diag, chunk, 3, onward).wait_recv()
-            copy(diag, chunk, 6, pair).start()
+    def forward_diag(copy, chunk):
+        copy(diag, chunk, 3, onward).wait_recv()
+        copy(diag, chunk, 6, pair).start()
+
+    def forward_skipped():
+        for n, (block, slot) in enumerate(((xn, 4), (yn, 5), (diag, 6))):
+            buddy_copy(n, skipped).wait_recv()
+            c_copy(block, skipped, slot, pair).start()
 
     def await_pair(chunk, slots):
         for copy in (h_copy, c_copy):
@@ -677,11 +767,12 @@
 
     send_chunk(0)
     forward_chunk(c_copy, order[0])
-    forward_chunk(c_copy, order[1])
+    forward_chunk(c_copy, theirs)
+    buddy_copy(0, theirs).start()
+    buddy_copy(1, theirs).start()
     send_chunk(1)
     forward_chunk(h_copy, order[0])
 
-    lanes = lax.broadcasted_iota(jnp.int32, (1, 128), 1)
     base = routed + shared
     slab = base // 128 * 128
     lane0 = base - slab
@@ -697,8 +788,7 @@
             pltpu.make_async_copy(h_all.at[chunk, group], h_out.at[chunk, group], store_sem.at[slot, 0]),
             pltpu.make_async_copy(grads_tile.at[slot], grads_out.at[chunk, group], store_sem.at[slot, 1]),
             pltpu.make_async_copy(gated_tile.at[slot], gated_out.at[chunk, group], store_sem.at[slot, 2]),
-            pltpu.make_async_copy(out_tile.at[slot], out_out.at[group, chunk], store_sem.at[slot, 3]),
-            pltpu.make_async_copy(rows_tile.at[slot], rows_out.at[chunk, group], store_sem.at[slot, 4]),
+            pltpu.make_async_copy(rows_tile.at[slot], rows_out.at[chunk, group], store_sem.at[slot, 3]),
         ]
         load = pltpu.make_async_copy(cot_all.at[chunk, group], cot_tile, tile_sem)
         return chunk, start, slot, load, stores
@@ -707,32 +797,33 @@
         k, side = lax.div(i, 2), lax.rem(i, 2)
         chunk, start, slot, load, stores = tile_copies(i)
 
-        @pl.when(i == 0)
+        @pl.when(side == 0)
+        def _():
+            await_pair(chunk, ((0, pair), (4, twin(xn))))
+
+        @pl.when(i == 1)
         def _():
             send_chunk(2)
-
-        @pl.when(side == 0)
-        def _():
-            await_pair(chunk, ((0, pair), (4, twin(xn))))
-
-        @pl.when(i == 1)
-        def _():
+            forward_chunk(c_copy, order[1])
             forward_chunk(h_copy, order[1])
+            forward_diag(c_copy, order[0])
+            forward_diag(c_copy, theirs)
+            buddy_copy(2, theirs).start()
+
+        @pl.when(i == 2)
+        def _():
             send_chunk(3)
-
-        @pl.when(i == 2)
-        def _():
-            forward_chunk(c_copy, order[2])
             forward_chunk(h_copy, order[2])
 
         @pl.when(i == 3)
         def _():
-            forward_chunk(c_copy, order[3])
+            forward_skipped()
             forward_chunk(h_copy, order[3])
+            forward_diag(c_copy, order[1])
 
         @pl.when(side == 1)
         def _():
-            forward_diag(chunk)
+            forward_diag(h_copy, chunk)
             await_pair(chunk, ((5, twin(yn)), (6, twin(diag))))
 
         load.start()
@@ -744,7 +835,7 @@
 
         group = pl.ds(start, half)
         stores[0].start()
-        for n in range(0, 2 * hidden, 512):
+        for n in range(0, 2 * hidden_units, 512):
             gu[:, n : n + 512] = jnp.dot(
                 h_all[chunk, group].reshape(tile, width), w_in_ref[:, n : n + 512], preferred_element_type=f32
             )
@@ -771,9 +862,9 @@
             pair_sum = jnp.zeros((strip, 128), f32)
             per = rows // strip
             block, inner = lax.div(r, per), pl.ds(pl.multiple_of(lax.rem(r, per) * strip, strip), strip)
-            for n in range(0, hidden, 128):
+            for n in range(0, hidden_units, 128):
                 gate = gu[at, n : n + 128]
-                up_val = gu[at, hidden + n : hidden + n + 128]
+                up_val = gu[at, hidden_units + n : hidden_units + n + 128]
                 grad = act_grad[at, n : n + 128]
                 if n + 128 <= routed:
                     scale = gate_here
@@ -795,7 +886,7 @@
                 grads_tile[slot, block, inner, n : n + 128] = (
                     grad * up_val * (sig * (1.0 + gate * (1.0 - sig)))
                 ).astype(bf16)
-                grads_tile[slot, block, inner, hidden + n : hidden + n + 128] = (grad * silu).astype(bf16)
+                grads_tile[slot, block, inner, hidden_units + n : hidden_units + n + 128] = (grad * silu).astype(bf16)
             pair_lanes[at, :] = pair_sum
             return 0
 
@@ -810,13 +901,9 @@
         for n in range(0, width, 512):
             rows_tile[slot, :, :, n : n + 512] = (
                 lax.dot_general(
-                    grads_tile[slot].reshape(tile, 2 * hidden), w_in_ref[n : n + 512, :], (((1,), (1,)), ((), ())),
+                    grads_tile[slot].reshape(tile, 2 * hidden_units), w_in_ref[n : n + 512, :], (((1,), (1,)), ((), ())),
                     preferred_element_type=f32,
                 ).astype(bf16).reshape(half, rows, 512)
-            )
-            out_tile[slot, :, :, n : n + 512] = (
-                jnp.dot(gated_tile[slot].reshape(tile, hidden), w_out_ref[:, n : n + 512], preferred_element_type=f32)
-                .astype(bf16).reshape(half, rows, 512)
             )
         for copy in stores[1:]:
             copy.start()
@@ -826,8 +913,10 @@
     for i in (2 * depth - 2, 2 * depth - 1):
         for copy in tile_copies(i)[4]:
             copy.wait()
-    for k in range(1, depth):
-        z_copy(k).wait_send()
+    z_drain()
+    for copy in saves:
+        copy.wait()
+    w_out_save.wait()
 
     def drain(k, _):
         chunk = order_at(k)
@@ -842,17 +931,31 @@
 
         for slot in range(7):
             h_copy(ep, chunk, slot, pair).wait_send()
+        for slot in (0, 4, 5, 6):
             c_copy(ep, chunk, slot, pair).wait_send()
+
+        @pl.when(chunk != skipped)
+        def _():
+            for slot in (1, 2, 3):
+                c_copy(ep, chunk, slot, pair).wait_send()
+
         return 0
 
     lax.fori_loop(0, depth, drain, 0)
-
-
-def experts_call(attn_part, inputs, gain, cotangent, kept, w_in, w_out, blocks, depth, routed, shared, experts, cid):
+    for n in range(3):
+        buddy_copy(n, theirs).wait_send()
+
+
+def experts_call(
+    inputs, gain_attn, w_query, w_latent, gain_latent, w_up, w_output, tables, gain, cotangent, kept, e_in, e_out, s_in, s_out,
+    blocks, depth, heads, shared, experts, cid,
+):
     f32, bf16 = jnp.float32, jnp.bfloat16
     tokens, width = inputs.shape
     rows = tokens // depth
-    hidden = w_out.shape[0]
+    routed = e_out.shape[1]
+    hidden = routed + s_out.shape[0]
+    rank = w_up.shape[0]
     half = blocks // 2
     tile = half * rows
     dma = pltpu.SemaphoreType.DMA
@@ -861,19 +964,32 @@
     def units(size):
         return jax.ShapeDtypeStruct((depth, blocks, rows, size), bf16)
 
+    kept_sizes = (
+        ((tokens, width), bf16), ((tokens, heads * NOPE), bf16), ((tokens, heads * ROPE), bf16),
+        ((tokens, heads * (NOPE + VDIM)), bf16), ((2, tokens, 128), bf16), ((tokens, heads * VDIM), bf16),
+        ((tokens, rank), bf16), ((tokens, rank), f32),
+    )
+
     return pl.pallas_call(
-        functools.partial(experts_kernel, depth, blocks, routed, shared, experts),
+        functools.partial(experts_kernel, depth, blocks, heads, routed, shared, experts),
         out_shape=(
             jax.ShapeDtypeStruct((rows, width), f32),
-            units(width), units(width), units(2 * hidden), units(hidden),
-            jax.ShapeDtypeStruct((blocks, depth, rows, width), bf16), units(width),
-        ),
-        in_specs=[vmem, anywhere, vmem, anywhere, vmem, vmem, vmem],
-        out_specs=(vmem,) + (anywhere,) * 6,
+            units(width), units(width), units(2 * hidden), units(hidden), units(width),
+        )
+        + tuple(jax.ShapeDtypeStruct(*size) for size in kept_sizes)
+        + (jax.ShapeDtypeStruct((hidden, width), bf16),),
+        in_specs=[vmem] * 9 + [anywhere] * 6,
+        out_specs=(vmem,) + (anywhere,) * 14,
         scratch_shapes=[
+            pltpu.VMEM((tokens, width), bf16),
+            *(pltpu.VMEM(*size) for size in kept_sizes),
+            pltpu.VMEM((tokens, 128), f32),
+            pltpu.VMEM((depth, blocks, rows, 128), bf16),
+            pltpu.VMEM((width, 2 * hidden), bf16),
+            pltpu.VMEM((hidden, width), bf16),
+            pltpu.VMEM((2, 256, routed), bf16),
             pltpu.VMEM((depth, blocks, rows, width), bf16),
-            pltpu.VMEM((depth - 1, rows, width), bf16),
-            pltpu.VMEM((rows, width), bf16),
+            pltpu.VMEM((depth + 1, rows, width), bf16),
             pltpu.VMEM((half, rows, width), bf16),
             pltpu.VMEM((tile, 2 * hidden), f32),
             pltpu.VMEM((tile, hidden), f32),
@@ -883,27 +999,32 @@
             pltpu.VMEM((2, half, rows, 2 * hidden), bf16),
             pltpu.VMEM((2, half, rows, hidden), bf16),
             pltpu.VMEM((2, half, rows, width), bf16),
-            pltpu.VMEM((2, half, rows, width), bf16),
-            dma((depth + 1,)),
-            dma((depth - 1,)), dma((depth - 1,)),
+            dma((5,)), dma((2,)), dma((9,)), dma((depth,)),
+            dma((depth - 1,)), dma((depth + 1,)),
             dma((depth, 2)), dma((depth,)),
             dma((depth, 7)), dma((depth, 7)),
             dma((depth, 7)), dma((depth, 7)),
-            dma, dma((2, 5)),
+            dma((3,)), dma((3,)), dma, dma((2, 4)),
         ],
-        compiler_params=pltpu.CompilerParams(collective_id=cid, has_side_effects=True, vmem_limit_bytes=60 << 20),
-    )(attn_part, inputs, gain.reshape(1, width), cotangent, kept, w_in, w_out)
+        compiler_params=pltpu.CompilerParams(collective_id=cid, has_side_effects=True, vmem_limit_bytes=63 << 20),
+    )(
+        inputs, gain_attn.reshape(1, width), w_query, w_latent, gain_latent.reshape(1, rank), w_up, w_output, tables,
+        gain.reshape(1, width), cotangent, kept, e_in, e_out, s_in, s_out,
+    )
 
 
 def sum_kernel(
-    depth, routed, shared, experts, part_ref, layer_ref, h_ref, grads_ref, gated_ref, cot_ref, middle_ref, gain_ref,
+    depth, routed, shared, experts, part_ref, h_ref, grads_ref, gated_ref, cot_ref, middle_ref, gain_ref, w_out_ref,
     middle_grad, branch, gain_part, expert_in, expert_out, s_in, s_out, router, layer_sum, landed,
     in_grad, out_grad, e_stage, s_stage,
-    load, store, got_pair, got_first, got_second, got_z, keep, h_tile, grads_tile, gated_tile, cot_tile,
+    load, store, layer, got_pair, got_first, got_second, got_z, keep, h_tile, grads_tile, gated_tile, cot_tile,
     own_cot, load_sem, store_sem, own_sem, lps, lpr, ps, pr, fs, fr, ss, sr, zs, zr, tile_sem, e_sem, s_sem, o_sem,
 ):
     f32 = jnp.float32
     rows = part_ref.shape[2]
+    count = h_tile.shape[0] * rows
+    width = h_tile.shape[2]
+    hidden = gated_tile.shape[2]
     ep, tp = lax.axis_index("ep"), lax.axis_index("tp")
     pair, xn, yn = plane_partners(ep)
     parity = lax.rem(ep, 2)
@@ -939,54 +1060,52 @@
         k = steps[i]
         return remote(got_pair.at[i, 2], got_z.at[k - 1], zs.at[k - 1], zr.at[k - 1], (ep, lax.rem(tp + k, depth)))
 
+    far = line_order(tp)[::-1]
+
     def layer_pair(i, slot):
-        src = layer_ref.at[blocks[slot] + pair - ep, chunk_of(i)]
+        src = layer.at[blocks[slot] + pair - ep]
         to = pair_slot[slot]
         return remote(src, landed.at[i, to], lps.at[i, slot], lpr.at[i, to], (pair, tp))
 
-    def layer_wait(i, slot):
-        return remote(layer_ref.at[0, 0], landed.at[i, slot], lps.at[i, slot], lpr.at[i, slot], (pair, tp))
-
-    def layer_loads(i, slot):
-        at = 2 * (slot % 2)
-        return (
-            pltpu.make_async_copy(layer_ref.at[blocks[slot], chunk_of(i)], load.at[at], load_sem.at[at]),
-            pltpu.make_async_copy(landed.at[i, slot], load.at[at + 1], load_sem.at[at + 1]),
-        )
+    def layer_load(i, slot):
+        return pltpu.make_async_copy(landed.at[i, slot], load.at[slot], load_sem.at[slot])
 
     def layer_store(i, slot):
         return pltpu.make_async_copy(store.at[slot % 2], layer_sum.at[i, slot], store_sem.at[slot % 2])
 
-    def layer_stage(i):
-        def start(slot):
-            layer_wait(i, slot).wait_recv()
-            for copy in layer_loads(i, slot):
-                copy.start()
-
-        start(0)
+    def layer_send(i):
+        def columns(m, _):
+            at = pl.ds(pl.multiple_of(m * 512, 512), 512)
+            found = jnp.dot(gated_tile[...].reshape(count, hidden), w_out_ref[:, at], preferred_element_type=f32)
+            layer[:, :, at] = found.astype(layer.dtype).reshape(layer.shape[0], rows, 512)
+            return 0
+
+        lax.fori_loop(0, width // 512, columns, 0)
+        for slot in (3, 1, 2, 0):
+            layer_pair(i, slot).start()
+
+    def layer_add(i):
         for slot in range(4):
-            if slot < 3:
-                start(slot + 1)
-            for copy in layer_loads(i, slot):
-                copy.wait()
+            layer_pair(i, pair_slot[slot]).wait_recv()
+            layer_load(i, slot).start()
+        for slot in range(4):
+            layer_load(i, slot).wait()
             if slot >= 2:
                 layer_store(i, slot - 2).wait()
-            at = 2 * (slot % 2)
-            add_rows(store.at[slot % 2], load.at[at], load.at[at + 1])
+            add_rows(store.at[slot % 2], load.at[slot], layer.at[blocks[slot]])
             layer_store(i, slot).start()
         layer_store(i, 2).wait()
         layer_store(i, 3).wait()
+        for slot in range(4):
+            layer_pair(i, slot).wait_send()
 
     for i in range(depth):
         for slot in (3, 1, 2, 0):
             pair_copy(i, slot).start()
-    for i in range(depth):
-        for slot in (3, 1, 2, 0):
-            layer_pair(i, slot).start()
 
     def tile_loads(c):
         return [
-            pltpu.make_async_copy(src.at[c], dst, tile_sem.at[n])
+            pltpu.make_async_copy(src.at[far[c]], dst, tile_sem.at[n])
             for n, (src, dst) in enumerate(
                 ((h_ref, h_tile), (grads_ref, grads_tile), (gated_ref, gated_tile), (cot_ref, cot_tile))
             )
@@ -1017,9 +1136,6 @@
         else:
             add_rows(keep, got_pair.at[i, 2], got_second.at[i])
 
-    count = h_tile.shape[0] * rows
-    width = h_tile.shape[2]
-    hidden = gated_tile.shape[2]
 
     blocks_all = h_tile.shape[0]
     lanes = lax.broadcasted_iota(jnp.int32, (1, 128), 1)
@@ -1098,6 +1214,9 @@
             wide = width // blocks_all
             for b in range(blocks_all):
                 s_out[b] = out_grad[routed : routed + s_out.shape[1], b * wide : (b + 1) * wide].astype(s_out.dtype)
+        if c > 0:
+            layer_add(c - 1)
+        layer_send(c)
         if c + 1 < depth:
             for copy in tile_loads(c + 1):
                 copy.start()
@@ -1106,16 +1225,23 @@
     own_copy.start()
     for copy in tile_loads(0):
         copy.start()
-    for t in range(depth + 2):
-        if t < depth:
-            stage_a(t)
-        if 0 <= t - 1 < depth:
-            stage_b(t - 1)
-        if 0 <= t - 2 < depth:
-            stage_c(t - 2)
-        if t < depth:
-            weights(t)
-            layer_stage(t)
+    stage_a(0)
+    stage_a(1)
+    weights(0)
+    stage_b(0)
+    stage_a(2)
+    weights(1)
+    stage_b(1)
+    stage_a(3)
+    stage_c(0)
+    weights(2)
+    stage_b(2)
+    stage_c(1)
+    stage_b(3)
+    weights(3)
+    stage_c(2)
+    stage_c(3)
+    layer_add(depth - 1)
     for i in range(depth - 1):
         z_copy(i).wait_recv()
     own_copy.wait()
@@ -1144,7 +1270,6 @@
     for i in range(depth):
         for slot in range(4):
             pair_copy(i, slot).wait_send()
-            layer_pair(i, slot).wait_send()
         for slot in range(2):
             first_copy(i, slot).wait_send()
         second_copy(i).wait_send()
@@ -1152,7 +1277,7 @@
             z_copy(i).wait_send()
 
 
-def sum_call(part, layer, h_all, grads, gated, cot_all, middle, gain, routed, shared, experts, cid):
+def sum_call(part, h_all, grads, gated, cot_all, middle, gain, w_out, routed, shared, experts, cid):
     f32, bf16 = jnp.float32, jnp.bfloat16
     depth, blocks, rows, width = part.shape
     hidden = gated.shape[3]
@@ -1172,7 +1297,7 @@
             jax.ShapeDtypeStruct((depth, 4, rows, width), bf16),
             jax.ShapeDtypeStruct((depth, 4, rows, width), bf16),
         ),
-        in_specs=[anywhere] * 6 + [vmem, vmem],
+        in_specs=[anywhere] * 5 + [vmem] * 3,
         out_specs=(vmem,) * 3 + (anywhere,) * 3 + (vmem,) * 2 + (anywhere,) * 2,
         scratch_shapes=[
             pltpu.VMEM((width, 2 * hidden), f32),
@@ -1181,6 +1306,7 @@
             pltpu.VMEM((2, 512 // (width // blocks), 2, width // blocks, 128), bf16),
             pltpu.VMEM((4, rows, width), bf16),
             pltpu.VMEM((2, rows, width), bf16),
+            pltpu.VMEM((blocks, rows, width), bf16),
             pltpu.VMEM((depth, 4, rows, width), bf16),
             pltpu.VMEM((depth, 2, rows, width), bf16),
             pltpu.VMEM((depth, rows, width), bf16),
@@ -1195,7 +1321,7 @@
             dma((depth,)), dma((depth,)), dma((depth - 1,)), dma((depth - 1,)), dma((4,)), dma((2,)), dma((2,)), dma,
         ],
         compiler_params=pltpu.CompilerParams(collective_id=cid, has_side_effects=True, vmem_limit_bytes=62 << 20),
-    )(part, layer, h_all, grads, gated, cot_all, middle, gain.reshape(1, width))
+    )(part, h_all, grads, gated, cot_all, middle, gain.reshape(1, width), w_out)
 
 
 def line_gather(ref, own, send_sem, recv_sem, ep, tp, depth):
@@ -1271,10 +1397,7 @@
     grad_on, grad_wait, grad_drain = line_gather(grad_in_ref, own_grad, gs, gr, ep, tp, depth)
     block_on, block_wait, block_drain = line_gather(block_ref, own_block, os, orr, ep, tp, depth)
 
-    steps = [(k + 1) % depth for k in range(depth)]
-
-    def chunk_of(i):
-        return lax.rem(tp + steps[i], depth)
+    middle_copy = pltpu.make_async_copy(middle_ref, row_sum, misc_sem.at[3])
 
     def held_load(i, slot):
         return pltpu.make_async_copy(part_ref.at[i, slot], held_rows.at[i, slot - 2], load_sem.at[i, slot - 2])
@@ -1285,10 +1408,13 @@
     def second_copy(i):
         return remote(held_rows.at[i, 1], got_second.at[i], ss.at[i], sr.at[i], (second, tp))
 
-    def z_copy(i):
-        k = steps[i]
-        src = held_rows.at[i, 0]
-        return remote(src, got_z.at[k - 1], zs.at[k - 1], zr.at[k - 1], (ep, lax.rem(tp + k, depth)))
+    z_clear, z_start, z_pass, z_finish, z_drain = line_sum(
+        lambda n: held_rows.at[n, 0], got_z, zs, zr, ep, tp, depth
+    )
+    far = order[::-1]
+    h_clear, h_start, h_pass, h_finish, h_drain = line_sum(
+        lambda n: hidden_part.at[far[n]], got_h, hs, hr, ep, tp, depth
+    )
 
     def stage_b(i):
         held_load(i, 3).wait()
@@ -1303,9 +1429,10 @@
         second_copy(i).wait_recv()
         if i < depth - 1:
             add_rows(held_rows.at[i, 0], held_rows.at[i, 0], got_second.at[i])
-            z_copy(i).start()
+            z_start(i)
         else:
-            add_rows(row_sum, held_rows.at[i, 0], got_second.at[i])
+            middle_copy.wait()
+            add_rows(held_rows.at[i, 0], held_rows.at[i, 0], got_second.at[i])
 
     def w_pair_copy(slot):
         to = pair_slot[slot]
@@ -1380,10 +1507,8 @@
                 shared_in[g, :, at] = s_in_land[n, g].astype(f32)[:, :shared]
             shared_out[at, :] = s_out_land[n].astype(f32)[:shared]
 
-    def h_copy(k):
-        to = lax.rem(tp + k, depth)
-        return remote(hidden_part.at[to], got_h.at[k - 1], hs.at[k - 1], hr.at[k - 1], (ep, to))
-
+    z_clear()
+    h_clear()
     branch_on(0)
     branch[tp] = branch_ref[...]
     for i in range(depth):
@@ -1394,6 +1519,7 @@
     own_rows = pl.ds(pl.multiple_of(tp * rows, rows), rows)
     resid_copy = pltpu.make_async_copy(inputs_ref.at[own_rows], resid, misc_sem.at[0])
     resid_copy.start()
+    middle_copy.start()
 
     branch_wait(1)
     branch_on(1)
@@ -1401,8 +1527,11 @@
     branch_wait(2)
     branch_on(2)
     stage_c(0)
+    stage_b(1)
     branch_wait(3)
     branch_on(3)
+    stage_c(1)
+    z_pass(0)
 
     turned, across = (((0,), (0,)), ((), ())), (((1,), (1,)), ((), ()))
 
@@ -1461,8 +1590,19 @@
             q_grad[own, at[2]] = jnp.where(lanes < 64, odd, rope).astype(bf16)
         return 0
 
-    lax.fori_loop(0, heads // 2, head_pair, 0)
-    stage_b(1)
+    def head_pairs(p, _):
+        head_pair(p, 0)
+
+        @pl.when(p == 0)
+        def _():
+            stage_b(2)
+
+        return 0
+
+    lax.fori_loop(0, heads // 2, head_pairs, 0)
+    stage_c(2)
+    z_pass(1)
+    stage_b(3)
 
     latent_back = dot(kv_grad[...], w_up[...], across)
     held = compressed[...]
@@ -1478,11 +1618,10 @@
     for n in range(0, width, 512):
         part = dot(q_grad[...], w_query[n : n + 512, :], across) + dot(l_grad[:, : rank + ROPE], w_latent[n : n + 512, :], across)
         hidden_part[:, :, n : n + 512] = part.astype(bf16).reshape(depth, rows, 512)
-    for k in range(1, depth):
-        h_copy(k).start()
-
-    stage_c(1)
-    stage_b(2)
+    for n in range(depth - 1):
+        h_start(n)
+    z_pass(2)
+    stage_c(3)
 
     u_grad[...] = dot(latent_in[...], kv_grad[...], turned).astype(bf16)
 
@@ -1529,19 +1668,33 @@
             copy.start()
     w_load(0).start()
 
-    stage_c(2)
-    stage_b(3)
+    z_finish()
+
+    def block_rows(r, _):
+        at = pl.ds(pl.multiple_of(r * 16, 16), 16)
+        value = row_sum[at, :] + held_rows[depth - 1, 0, at, :].astype(f32)
+        value = value + got_z[tp, at, :].astype(f32) + got_z[depth, at, :].astype(f32)
+        own_block[at, :] = value.astype(bf16)
+        return 0
+
+    lax.fori_loop(0, rows // 16, block_rows, 0)
+    block_on(0)
+    own_block_copy = pltpu.make_async_copy(own_block, block_ref.at[tp], misc_sem.at[2])
+    own_block_copy.start()
+    h_pass(0)
     w_stage_a()
+    h_pass(1)
+    block_wait(1)
+    block_on(1)
+    h_pass(2)
 
     resid_copy.wait()
-    for k in range(1, depth):
-        h_copy(k).wait_recv()
+    h_finish()
 
     def input_rows(r, gain_sum):
         at = pl.ds(pl.multiple_of(r * 16, 16), 16)
         u = hidden_part[tp, at, :].astype(f32)
-        for k in range(depth - 1):
-            u = u + got_h[k, at, :].astype(f32)
+        u = u + got_h[tp, at, :].astype(f32) + got_h[depth, at, :].astype(f32)
         v = resid[at, :].astype(f32)
         inv = lax.rsqrt(jnp.mean(v * v, axis=-1, keepdims=True) + EPSILON)
         v_hat = v * inv
@@ -1555,23 +1708,6 @@
     grad_on(0)
     own_grad_copy = pltpu.make_async_copy(own_grad, grad_in_ref.at[tp], misc_sem.at[1])
     own_grad_copy.start()
-    stage_c(3)
-    for i in range(depth - 1):
-        z_copy(i).wait_recv()
-
-    def block_rows(r, _):
-        at = pl.ds(pl.multiple_of(r * 16, 16), 16)
-        value = middle_ref[at, :] + row_sum[at, :]
-        for k in range(depth - 1):
-            value = value + got_z[k, at, :].astype(f32)
-        own_block[at, :] = value.astype(bf16)
-        return 0
-
-    lax.fori_loop(0, rows // 16, block_rows, 0)
-    block_on(0)
-    own_block_copy = pltpu.make_async_copy(own_block, block_ref.at[tp], misc_sem.at[2])
-    own_block_copy.start()
-    w_stage_b()
 
     gains[0] = jnp.zeros_like(gains[0])
     gains[0, 0:1, :] = jnp.sum(gain_sum, axis=0, keepdims=True)
@@ -1594,7 +1730,12 @@
             gains_ref[...] = total
 
     gain_copy(0).start()
+    block_wait(2)
+    block_on(2)
+    w_stage_b()
     gain_step(0)
+    grad_wait(1)
+    grad_on(1)
     gain_step(1)
     w_stage_c()
     w_part = w_rows // depth
@@ -1608,12 +1749,13 @@
     w_pair[1, :, q_cols:o_start] = latent_part[...].astype(bf16)
     for k in range(1, depth):
         w_z_copy(k).start()
+    grad_wait(2)
+    grad_on(2)
     gain_step(2)
-    grad_wait(1)
-    grad_on(1)
-    block_wait(1)
-    block_on(1)
+    block_wait(3)
+    block_on(3)
     gain_step(3)
+    shared_place()
     gain_step(4)
     for k in range(1, depth):
         w_z_copy(k).wait_recv()
@@ -1622,12 +1764,8 @@
     for k in range(depth - 1):
         total = total + w_z[k].astype(f32)
     latent_ref[...] = total
-    shared_place()
-    for k in range(2, depth):
-        grad_wait(k)
-        grad_on(k)
-        block_wait(k)
-        block_on(k)
+    grad_wait(3)
+    grad_on(3)
 
     own_grad_copy.wait()
     own_block_copy.wait()
@@ -1638,14 +1776,13 @@
         for slot in range(2):
             first_copy(i, slot).wait_send()
         second_copy(i).wait_send()
-        if i < depth - 1:
-            z_copy(i).wait_send()
+    z_drain()
+    h_drain()
     for slot in range(4):
         w_pair_copy(slot).wait_send()
     w_first_copy(0).wait_send()
     w_second_copy().wait_send()
     for k in range(1, depth):
-        h_copy(k).wait_send()
         w_z_copy(k).wait_send()
     for n in range(len(partners)):
         gain_copy(n).wait_send()
@@ -1683,16 +1820,16 @@
             jax.ShapeDtypeStruct((blocks * shared, w_rows), f32),
             jax.ShapeDtypeStruct((blocks, w_rows, w_cols), bf16),
         ),
-        in_specs=[vmem, vmem, vmem, anywhere, vmem, vmem, anywhere, anywhere, anywhere] + [vmem] * 15,
+        in_specs=[vmem, vmem, anywhere, anywhere, vmem, vmem, anywhere, anywhere, anywhere] + [vmem] * 15,
         out_specs=(anywhere, anywhere) + (vmem,) * 7 + (anywhere,),
         scratch_shapes=[
             pltpu.VMEM((depth, rows, width), bf16),
             pltpu.VMEM((depth, 2, rows, width), bf16),
             pltpu.VMEM((depth, 2, rows, width), bf16),
             pltpu.VMEM((depth, rows, width), bf16),
-            pltpu.VMEM((depth - 1, rows, width), bf16),
+            pltpu.VMEM((depth + 1, rows, width), bf16),
             pltpu.VMEM((depth, rows, width), bf16),
-            pltpu.VMEM((depth - 1, rows, width), bf16),
+            pltpu.VMEM((depth + 1, rows, width), bf16),
             pltpu.VMEM((rows, width), f32),
             pltpu.VMEM((tokens, heads * VDIM), bf16),
             pltpu.VMEM((tokens, 128), f32),
@@ -1714,13 +1851,13 @@
             pltpu.VMEM((10, 8, width), f32),
             dma((depth, 2)),
             dma((depth, 2)), dma((depth, 2)), dma((depth,)), dma((depth,)),
-            dma((depth - 1,)), dma((depth - 1,)),
+            dma((depth - 1,)), dma((depth + 1,)),
             dma((depth, 2)), dma((depth,)),
-            dma((depth - 1,)), dma((depth - 1,)),
+            dma((depth - 1,)), dma((depth + 1,)),
             dma((depth, 2)), dma((depth,)),
             dma((depth, 2)), dma((depth,)),
             dma((4,)), dma((4,)), dma((2,)), dma((2,)), dma, dma, dma((depth - 1,)), dma((depth - 1,)),
-            dma((5,)), dma((5,)), dma((3,)), dma((2,)), dma((8,)), dma((8,)), dma((8,)), dma((8,)),
+            dma((5,)), dma((5,)), dma((4,)), dma((2,)), dma((8,)), dma((8,)), dma((8,)), dma((8,)),
         ],
         compiler_params=pltpu.CompilerParams(collective_id=cid, has_side_effects=True, vmem_limit_bytes=63 << 20),
     )(
@@ -1796,37 +1933,30 @@
     shared = w_shared_in.shape[2] // ep_count
     hidden = padded_hidden(routed, shared)
     shared_start = ep_index * shared
+    slab = routed // 128 * 128
+    before, after = routed - slab, hidden - routed - shared
+    router_parts = jnp.concatenate(split_wide(w_router), axis=1)
+    beside = jnp.stack(
+        [
+            jnp.pad(router_parts, ((0, 0), (0, after - router_parts.shape[1]))),
+            jnp.zeros((model_width, after), bf16),
+        ]
+    )
     shared_in = lax.dynamic_slice_in_dim(w_shared_in, shared_start, shared, 2)
+    shared_in = jnp.concatenate([jnp.zeros((2, model_width, before), bf16), shared_in, beside], axis=2)
     shared_out = lax.dynamic_slice_in_dim(w_shared_out, shared_start, shared, 0)
-    router_parts = jnp.concatenate(split_wide(w_router), axis=1)
-    fill = hidden - routed - shared
-    w_in = jnp.concatenate(
-        [
-            w_expert_in[0, 0],
-            shared_in[0],
-            jnp.pad(router_parts, ((0, 0), (0, fill - router_parts.shape[1]))),
-            w_expert_in[0, 1],
-            shared_in[1],
-            jnp.zeros((model_width, fill), bf16),
-        ],
-        axis=1,
-    )
-    w_out = jnp.concatenate(
-        [w_expert_out[0], shared_out, jnp.zeros((fill, model_width), bf16)], axis=0
-    )
-
-    attn_part, hidden_attn, query_nope, query_rope, key_value, key_pair, attended, latent_in, compressed = (
-        attention_call(
-            inputs, gain_attn, w_query, w_latent, gain_latent, w_latent_up, w_output, rope_tables(tokens), heads_here
-        )
-    )
-    middle, hidden_all, cot_all, hidden_grads, gated, out_part, rows_grad = experts_call(
-        attn_part, inputs, gain_ffn, cotangent, kept_lanes, w_in, w_out,
-        ep_count, tp_count, routed, shared, experts, 0,
+    shared_out = jnp.pad(shared_out, ((0, after), (0, 0)))
+    tables = rope_tables(tokens)
+    (
+        middle, hidden_all, cot_all, hidden_grads, gated, rows_grad,
+        hidden_attn, query_nope, query_rope, key_value, key_pair, attended, latent_in, compressed, w_out,
+    ) = experts_call(
+        inputs, gain_attn, w_query, w_latent, gain_latent, w_latent_up, w_output, tables, gain_ffn, cotangent, kept_lanes,
+        w_expert_in, w_expert_out, shared_in, shared_out, ep_count, tp_count, heads_here, shared, experts, 0,
     )
     middle_grad, branch, gain_ffn_part, grad_expert_in, grad_expert_out, shared_in_part, shared_out_part, router_part, layer_sum, _ = (
         sum_call(
-            rows_grad, out_part, hidden_all, hidden_grads, gated, cot_all, middle, gain_ffn, routed, shared, experts, 1
+            rows_grad, hidden_all, hidden_grads, gated, cot_all, middle, gain_ffn, w_out, routed, shared, experts, 1
         )
     )
     block_out, grad_inputs, gains, grad_query, grad_output, grad_latent_up, latent_sum, grad_shared_in, grad_shared_out, _ = (
@@ -1834,7 +1964,7 @@
             branch, middle_grad, middle, layer_sum, router_part, gain_ffn_part, inputs, shared_in_part, shared_out_part,
             w_output, w_query, w_latent, w_latent_up, hidden_attn,
             query_nope, query_rope, key_value, key_pair,
-            attended, latent_in, compressed, rope_tables(tokens), gain_latent, gain_attn, heads_here, shared, 2,
+            attended, latent_in, compressed, tables, gain_latent, gain_attn, heads_here, shared, 2,
         )
     )
     grad_latent = latent_sum[:, : KV_RANK + ROPE]

time: 612 us -> 557 us (0.910)
  Pallas kernels: 536 us -> 500 us
  local copies, waits for them, and re-layouts: 54.7 us -> 35.6 us
    pallas_call x2 -> x1, Pallas kernels: 209 us -> 190 us  [experts_call(): pl.pallas_call(functools.partial(experts_kernel, depth, blocks, heads, ro...]
    pallas_call x1, Pallas kernels: 225 us -> 208 us  [tail_call(): pl.pallas_call(functools.partial(tail_kernel, depth, heads, shared), out_...]
    concatenate x2 -> x1, local copies, waits for them, and re-layouts: 8.5 us -> 0.01 us  [body_dense(): jnp.concatenate([jnp.zeros((2, model_width, before), bf16), shared_in, be...]
    unnamed x59 -> x35, local copies, waits for them, and re-layouts: 35.3 us -> 27.6 us
  transfers between devices with their start and end apart: 1 -> 1, of which waited for: 0 -> 0; matrix products, arithmetic and copies ran while one was open for 5% -> 3% of each run, Pallas kernels for 3% -> 0%
where the time goes in v6:
time: 557 us; the launch traced here: 548 us
  Pallas kernels  500 us (90%)
  local copies, waits for them, and re-layouts  35.6 us (6%)
    pallas_call x1, Pallas kernels, tail_call(): pl.pallas_call(functools.partial(tail_kernel, depth, heads, shared), out_...  208 us
    pallas_call x1, Pallas kernels, experts_call(): pl.pallas_call(functools.partial(experts_kernel, depth, blocks, heads, ro...  190 us
    pallas_call x1, Pallas kernels, sum_call(): pl.pallas_call(functools.partial(sum_kernel, depth, routed, shared, exper...  102 us
    unnamed x35, local copies, waits for them, and re-layouts  27.6 us
  transfers between devices with their start and end apart: 1, of which 0 were waited for; matrix products, arithmetic and copies ran while one was open for 3% of the time, Pallas kernels for 0%

profile of v6, /device:TPU:0, one launch (start us, length us, event | category | flops | bytes accessed | tf_op | source)
XLA Modules:
  0.0 547.5 jit_solution(15767560503277776222)
XLA Ops:
  0.6 0.7 broadcast_compare_fusion
  1.4 0.7 fusion.3
  2.1 0.5 broadcast.15
  2.7 0.7 reduce
  3.4 0.6 reshape.73
  4.0 5.2 all-to-all-start
  9.1 0.9 fusion.10
  10.1 0.3 copy.69
  10.4 0.1 pad_bitcast_fusion
  10.5 1.2 constant_dynamic-slice_fusion.4
  11.6 0.7 copy.76
  12.3 2.3 fusion.1.s_in
  14.6 1.0 constant_dynamic-slice_fusion.3
  15.6 0.0 copy-start
  15.6 0.9 pad.10.s_out
  16.5 4.5 copy.70.w_latent
  21.1 0.0 copy-done
  21.1 2.8 copy.71.e_in
  23.8 0.0 all-to-all-done
  23.8 1.6 broadcast_in_dim.4.kept_hbm
  25.4 190.1 %shard_map.272 = (f32[128,2048]{1,0:T(8,128)}, bf16[4,8,128,2048]{3,2,1,0:T(8,128)(2,1)}, bf16[4,8,128,2048]{3,2,1,0:T(8,128)(2,1)}, bf16[4,8,128,1024]{3,2,1,0:...) custom-call(bf16[512,2048]{1,0:T(8,128)(2,1)} %inputs_ref.3, ...), custom_call_target="tpu_custom_call" | custom-call | tf_op jit(solution)/shard_map/pallas_call | solution.py:973
  215.6 101.9 %shard_map.273 = (f32[128,2048]{1,0:T(8,128)}, bf16[128,2048]{1,0:T(8,128)(2,1)}, f32[8,2048]{1,0:T(8,128)}, f32[1,2,2048,352]{3,2,1,0:T(8,128)}, f32[1,352,2048...) custom-call(bf16[4,8,128,2048]{3,2,1,0:T(8,128)(2,1)} %get-tuple-ele, ...), custom_call_target="tpu_custom_call" | custom-call | tf_op jit(solution)/shard_map/pallas_call | solution.py:1286
  317.5 208.0 %shard_map.274 = (bf16[4,128,2048]{2,1,0:T(8,128)(2,1)}, bf16[4,128,2048]{2,1,0:T(8,128)(2,1)}, f32[8,2048]{1,0:T(8,128)}, f32[256,768]{1,0:T(8,128)}, f32[512,2...) custom-call(bf16[128,2048]{1,0:T(8,128)(2,1)} %get-tuple-element.54., ...), custom_call_target="tpu_custom_call" | custom-call | tf_op jit(solution)/shard_map/pallas_call | solution.py:1809
  525.5 1.0 fusion.9
  526.5 0.8 slice.19
  527.3 0.7 copy.73
  528.0 3.0 copy.74
  530.9 0.0 copy-start.3
  530.9 6.5 %copy.75 = f32[1,2,2048,352]{2,3,1,0:T(8,128)} copy(f32[1,2,2048,352]{3,2,1,0:T(8,128)} %get-tuple-element.134) | data formatting | bytes 11534336
  537.5 0.0 copy-start.2
  537.5 0.6 fusion.7
  538.1 0.6 fusion.6
  538.6 0.0 copy-done.3
  538.6 1.3 copy.91
  540.0 0.0 copy-done.2
  540.0 0.0 copy-start.4
  540.0 0.0 copy-start.8
  540.0 0.0 copy-start.7
  540.0 0.0 copy-start.6
  540.0 0.0 copy-start.5
  540.0 1.3 copy.92
  541.3 0.3 copy-done.4
  541.6 0.0 copy-start.1
  541.6 0.9 copy.93
  542.5 0.0 copy-done.8
  542.5 0.7 copy.94
  543.1 0.0 copy-done.7
  543.1 0.7 copy.95
  543.8 0.0 copy-done.6
  543.8 0.8 copy.96
  544.6 0.0 copy-done.5
  544.6 0.9 copy.97
  545.5 0.0 copy-done.1
  545.5 1.6 copy.98
  (7 shorter events, 0.1 us)
Async XLA Ops:
  4.0 19.8 %all-to-all-start = ((bf16[8,2,256]{2,1,0:T(2,128)(2,1)}), bf16[8,2,256]{2,1,0:T(2,128)(2,1)S(1)}, u32[]{:S(2)}, u32[]{:S(2)}) async-start(bf16[8,2,256]{2,1,0:T(2,128)(2,1)} %reshape.73), calls=%async_computation | async-start | bytes 16384 | tf_op jit(solution)/shard_map/all_to_all | solution.py:1925
  15.6 5.4 copy-start
  530.9 7.7 %copy-start.3 = (bf16[4,128,2048]{2,1,0:T(8,128)(2,1)S(1)}, bf16[4,128,2048]{2,1,0:T(8,128)(2,1)}, u32[]{:S(2)}) copy-start(bf16[4,128,2048]{2,1,0:T(8,128)(2,1)} %get-tuple-element.69) | copy-start | bytes 6291460
  537.5 2.5 copy-start.2
  540.0 1.6 copy-start.4
  540.0 2.5 copy-start.8
  540.0 3.2 copy-start.7
  540.0 3.9 copy-start.6
  540.0 4.6 copy-start.5
  541.6 3.9 copy-start.1

commit v7 on v6

--- a/solution.py
+++ b/solution.py
@@ -503,6 +503,66 @@
             copy(n, got.at[0]).wait_send()
 
     return clear, start, pass_on, finish, drain
+
+
+def line_total(own_of, pieces, up, down, up_send, up_recv, down_send, down_recv, ep, tp, depth):
+    between = (tp > 0) & (tp < depth - 1)
+    lowest, highest = tp == 0, tp == depth - 1
+    above, below = jnp.minimum(tp + 1, depth - 1), jnp.maximum(tp - 1, 0)
+
+    def up_copy(n, src):
+        return remote(src, up.at[n], up_send.at[n], up_recv.at[n], (ep, above))
+
+    def down_copy(n, src):
+        return remote(src, down.at[n], down_send.at[n], down_recv.at[n], (ep, below))
+
+    def start(n):
+        @pl.when(lowest)
+        def _():
+            up_copy(n, own_of(n)).start()
+
+        @pl.when(highest)
+        def _():
+            down_copy(n, own_of(n)).start()
+
+    def hop(k, n):
+        @pl.when(between & (tp == k))
+        def _():
+            up_copy(n, up.at[n]).wait_recv()
+            add_rows(up.at[n], up.at[n], own_of(n))
+            up_copy(n, up.at[n]).start()
+
+        @pl.when(between & (tp == depth - 1 - k))
+        def _():
+            down_copy(n, down.at[n]).wait_recv()
+            add_rows(down.at[n], down.at[n], own_of(n))
+            down_copy(n, down.at[n]).start()
+
+    def finish(n):
+        @pl.when(lowest)
+        def _():
+            up[n] = own_of(n)[...]
+            down_copy(n, down.at[n]).wait_recv()
+            add_rows(down.at[n], down.at[n], own_of(n))
+
+        @pl.when(highest)
+        def _():
+            down[n] = own_of(n)[...]
+            up_copy(n, up.at[n]).wait_recv()
+            add_rows(up.at[n], up.at[n], own_of(n))
+
+    def drain():
+        for n in range(pieces):
+
+            @pl.when(jnp.logical_not(highest))
+            def _():
+                up_copy(n, up.at[n]).wait_send()
+
+            @pl.when(jnp.logical_not(lowest))
+            def _():
+                down_copy(n, down.at[n]).wait_send()
+
+    return start, hop, finish, drain
 
 
 def turn(slab, table, sign):
@@ -1015,7 +1075,7 @@
 
 def sum_kernel(
     depth, routed, shared, experts, part_ref, h_ref, grads_ref, gated_ref, cot_ref, middle_ref, gain_ref, w_out_ref,
-    middle_grad, branch, gain_part, expert_in, expert_out, s_in, s_out, router, layer_sum, landed,
+    branch, gain_part, expert_in, expert_out, s_in, s_out, router, layer_sum, landed,
     in_grad, out_grad, e_stage, s_stage,
     load, store, layer, got_pair, got_first, got_second, got_z, keep, h_tile, grads_tile, gated_tile, cot_tile,
     own_cot, load_sem, store_sem, own_sem, lps, lpr, ps, pr, fs, fr, ss, sr, zs, zr, tile_sem, e_sem, s_sem, o_sem,
@@ -1060,8 +1120,6 @@
         k = steps[i]
         return remote(got_pair.at[i, 2], got_z.at[k - 1], zs.at[k - 1], zr.at[k - 1], (ep, lax.rem(tp + k, depth)))
 
-    far = line_order(tp)[::-1]
-
     def layer_pair(i, slot):
         src = layer.at[blocks[slot] + pair - ep]
         to = pair_slot[slot]
@@ -1105,7 +1163,7 @@
 
     def tile_loads(c):
         return [
-            pltpu.make_async_copy(src.at[far[c]], dst, tile_sem.at[n])
+            pltpu.make_async_copy(src.at[c], dst, tile_sem.at[n])
             for n, (src, dst) in enumerate(
                 ((h_ref, h_tile), (grads_ref, grads_tile), (gated_ref, gated_tile), (cot_ref, cot_tile))
             )
@@ -1258,7 +1316,6 @@
         s = u * gain_ref[...]
         back = inverse * (s - v_hat * jnp.mean(s * v_hat, axis=-1, keepdims=True))
         found = own_cot[at, :].astype(f32) + back
-        middle_grad[at, :] = found
         branch[at, :] = found.astype(branch.dtype)
         return gain_sum
 
@@ -1286,7 +1343,6 @@
     return pl.pallas_call(
         functools.partial(sum_kernel, depth, routed, shared, experts),
         out_shape=(
-            jax.ShapeDtypeStruct((rows, width), f32),
             jax.ShapeDtypeStruct((rows, width), bf16),
             jax.ShapeDtypeStruct((8, width), f32),
             jax.ShapeDtypeStruct((1, 2, width, routed), f32),
@@ -1298,7 +1354,7 @@
             jax.ShapeDtypeStruct((depth, 4, rows, width), bf16),
         ),
         in_specs=[anywhere] * 5 + [vmem] * 3,
-        out_specs=(vmem,) * 3 + (anywhere,) * 3 + (vmem,) * 2 + (anywhere,) * 2,
+        out_specs=(vmem,) * 2 + (anywhere,) * 3 + (vmem,) * 2 + (anywhere,) * 2,
         scratch_shapes=[
             pltpu.VMEM((width, 2 * hidden), f32),
             pltpu.VMEM((hidden, width), f32),
@@ -1357,14 +1413,16 @@
 
 def tail_kernel(
     depth, heads, shared,
-    branch_ref, middle_grad_ref, middle_ref, part_ref, router_ref, gain_part_ref, inputs_ref, s_in, s_out,
+    branch_ref, middle_ref, part_ref, router_in, gain_part_ref, inputs_ref, s_in, s_out,
+    w_output_in, w_query_in, w_latent_in, w_up_in, hidden_in, qn_in, qr_in, kv_in, kr_in, attended_in, latent_in_in, compressed_in,
+    tables_in, gain_latent, gain_attn,
+    block_ref, grad_in_ref, gains_ref, query_ref, output_ref, up_ref, latent_ref, shared_in, shared_out, w_all, w_first,
     w_output, w_query, w_latent, w_up, hidden_ref, qn_ref, qr_ref, kv_ref, kr_ref, attended, latent_in, compressed,
-    tables, gain_latent, gain_attn,
-    block_ref, grad_in_ref, gains_ref, query_ref, output_ref, up_ref, latent_ref, shared_in, shared_out, w_all,
-    branch, held_rows, got_first, got_second, got_z, hidden_part, got_h, row_sum,
-    d_out, d_kr, q_grad, kv_grad, l_grad, u_grad, w_stage, w_pair, w_first, w_second, w_z, latent_part, s_in_land, s_out_land, resid, own_grad, own_block, gains,
-    load_sem, fs, fr, ss, sr, zs, zr, bs, br, hs, hr, gs, gr, os, orr,
-    wps, wpr, wfs, wfr, wss, wsr, wzs, wzr, as_, ar, misc_sem, stage_sem, sis, sir, sos, sor,
+    tables, router_ref, load_in_sem,
+    branch, held_rows, got_first, got_second, z_up, z_down, hidden_part, h_up, h_down, middle,
+    d_out, d_kr, q_grad, kv_grad, l_grad, u_grad, w_stage, w_pair, w_second, w_z, latent_part, s_in_land, s_out_land, resid, grad_tile, block_tile, gains, attn_gains,
+    load_sem, fs, fr, ss, sr, zus, zur, zds, zdr, bs, br, hus, hur, hds, hdr,
+    wps, wpr, wfs, wfr, wss, wsr, wzs, wzr, as_, ar, ns, nr, misc_sem, resid_sem, grad_sem, block_sem, stage_sem, sis, sir, sos, sor,
 ):
     f32, bf16 = jnp.float32, jnp.bfloat16
     ep, tp = lax.axis_index("ep"), lax.axis_index("tp")
@@ -1375,7 +1433,7 @@
     diag = xn + yn - ep
     blocks = (first, diag, ep, second)
     pair_slot = (3, 1, 2, 0)
-    rows, width = middle_ref.shape
+    rows, width = middle.shape
     tokens = hidden_ref.shape[0]
     rank = compressed.shape[1]
     q_cols, l_cols = q_grad.shape[1], l_grad.shape[1]
@@ -1393,11 +1451,25 @@
     plane = [ep + sum(((pair, xn, yn)[n] - ep) * (m >> n & 1) for n in range(3)) for m in range(8)]
     greet([(to, tp) for to in plane[1:]] + [(ep, lax.rem(tp + k, depth)) for k in range(1, depth)])
 
+    loads = [
+        pltpu.make_async_copy(src, dst, load_in_sem.at[n])
+        for n, (src, dst) in enumerate(
+            (
+                (w_output_in, w_output),
+                (qn_in, qn_ref), (qr_in, qr_ref), (kv_in, kv_ref), (kr_in, kr_ref), (tables_in, tables),
+                (w_up_in, w_up), (compressed_in, compressed), (w_query_in, w_query), (w_latent_in, w_latent),
+                (hidden_in, hidden_ref), (attended_in, attended), (latent_in_in, latent_in), (router_in, router_ref),
+            )
+        )
+    ]
+
+    def loaded(first_load, last_load):
+        for copy in loads[first_load:last_load]:
+            copy.wait()
+
     branch_on, branch_wait, branch_drain = line_gather(branch, branch_ref, bs, br, ep, tp, depth)
-    grad_on, grad_wait, grad_drain = line_gather(grad_in_ref, own_grad, gs, gr, ep, tp, depth)
-    block_on, block_wait, block_drain = line_gather(block_ref, own_block, os, orr, ep, tp, depth)
-
-    middle_copy = pltpu.make_async_copy(middle_ref, row_sum, misc_sem.at[3])
+
+    middle_copy = pltpu.make_async_copy(middle_ref, middle, misc_sem.at[1])
 
     def held_load(i, slot):
         return pltpu.make_async_copy(part_ref.at[i, slot], held_rows.at[i, slot - 2], load_sem.at[i, slot - 2])
@@ -1408,12 +1480,14 @@
     def second_copy(i):
         return remote(held_rows.at[i, 1], got_second.at[i], ss.at[i], sr.at[i], (second, tp))
 
-    z_clear, z_start, z_pass, z_finish, z_drain = line_sum(
-        lambda n: held_rows.at[n, 0], got_z, zs, zr, ep, tp, depth
-    )
-    far = order[::-1]
-    h_clear, h_start, h_pass, h_finish, h_drain = line_sum(
-        lambda n: hidden_part.at[far[n]], got_h, hs, hr, ep, tp, depth
+    pieces, piece = h_up.shape[0], h_up.shape[1]
+    per = rows // piece
+    z_start, z_hop, z_finish, z_drain = line_total(
+        lambda n: held_rows.at[n // per, 0, pl.ds(n % per * piece, piece)],
+        pieces, z_up, z_down, zus, zur, zds, zdr, ep, tp, depth,
+    )
+    h_start, h_hop, h_finish, h_drain = line_total(
+        lambda n: hidden_part.at[n], pieces, h_up, h_down, hus, hur, hds, hdr, ep, tp, depth
     )
 
     def stage_b(i):
@@ -1427,12 +1501,15 @@
 
     def stage_c(i):
         second_copy(i).wait_recv()
-        if i < depth - 1:
-            add_rows(held_rows.at[i, 0], held_rows.at[i, 0], got_second.at[i])
-            z_start(i)
-        else:
+        add_rows(held_rows.at[i, 0], held_rows.at[i, 0], got_second.at[i])
+
+        @pl.when(tp == i)
+        def _():
             middle_copy.wait()
-            add_rows(held_rows.at[i, 0], held_rows.at[i, 0], got_second.at[i])
+            add_rows(held_rows.at[i, 0], held_rows.at[i, 0], middle)
+
+        for n in range(per * i, per * i + per):
+            z_start(n)
 
     def w_pair_copy(slot):
         to = pair_slot[slot]
@@ -1461,11 +1538,18 @@
                 w_first_copy(slot).start()
 
     def w_stage_b():
+        def load(slot):
+            return pltpu.make_async_copy(w_first.at[slot], w_stage.at[slot], stage_sem.at[slot])
+
         w_first_copy(1).wait_recv()
-        add_rows(w_pair.at[3], w_pair.at[3], w_first.at[1])
+        load(1).start()
+        w_first_copy(0).wait_recv()
+        load(0).start()
+        load(1).wait()
+        add_rows(w_pair.at[3], w_pair.at[3], w_stage.at[1])
         w_second_copy().start()
-        w_first_copy(0).wait_recv()
-        add_rows(w_pair.at[2], w_pair.at[2], w_first.at[0])
+        load(0).wait()
+        add_rows(w_pair.at[2], w_pair.at[2], w_stage.at[0])
 
     def w_stage_c():
         w_second_copy().wait_recv()
@@ -1507,8 +1591,6 @@
                 shared_in[g, :, at] = s_in_land[n, g].astype(f32)[:, :shared]
             shared_out[at, :] = s_out_land[n].astype(f32)[:shared]
 
-    z_clear()
-    h_clear()
     branch_on(0)
     branch[tp] = branch_ref[...]
     for i in range(depth):
@@ -1516,30 +1598,40 @@
         first_copy(i, 0).start()
         held_load(i, 3).start()
         held_load(i, 2).start()
-    own_rows = pl.ds(pl.multiple_of(tp * rows, rows), rows)
-    resid_copy = pltpu.make_async_copy(inputs_ref.at[own_rows], resid, misc_sem.at[0])
-    resid_copy.start()
+
+    def resid_copy(n):
+        return pltpu.make_async_copy(inputs_ref.at[pl.ds(n * piece, piece)], resid.at[n % 2], resid_sem.at[n % 2])
+
+    for copy in loads:
+        copy.start()
+    resid_copy(0).start()
+    resid_copy(1).start()
     middle_copy.start()
 
+    turned, across = (((0,), (0,)), ((), ())), (((1,), (1,)), ((), ()))
+
+    def dot(a, b, dims=(((1,), (0,)), ((), ()))):
+        return lax.dot_general(a, b, dims, preferred_element_type=f32)
+
+    def attended_grad(k):
+        at = pl.ds(pl.multiple_of(order[k] * rows, rows), rows)
+        d_out[at, :] = dot(branch[order[k]], w_output[...], across).astype(bf16)
+
+    loaded(0, 1)
+    attended_grad(0)
     branch_wait(1)
     branch_on(1)
+    attended_grad(1)
     stage_b(0)
     branch_wait(2)
     branch_on(2)
+    attended_grad(2)
     stage_c(0)
     stage_b(1)
+    loaded(1, 6)
     branch_wait(3)
     branch_on(3)
-    stage_c(1)
-    z_pass(0)
-
-    turned, across = (((0,), (0,)), ((), ())), (((1,), (1,)), ((), ()))
-
-    def dot(a, b, dims=(((1,), (0,)), ((), ()))):
-        return lax.dot_general(a, b, dims, preferred_element_type=f32)
-
-    for c in range(depth):
-        d_out[c * rows : (c + 1) * rows, :] = dot(branch[c], w_output[...], across).astype(bf16)
+    attended_grad(3)
 
     lanes = lax.broadcasted_iota(jnp.int32, (1, 128), 1)
     halves = tokens // BLOCK
@@ -1595,15 +1687,19 @@
 
         @pl.when(p == 0)
         def _():
-            stage_b(2)
+            stage_c(1)
+            for n in range(per):
+                z_hop(1, n)
 
         return 0
 
     lax.fori_loop(0, heads // 2, head_pairs, 0)
-    stage_c(2)
-    z_pass(1)
-    stage_b(3)
-
+    for n in range(per):
+        z_hop(2, n)
+        z_hop(1, per + n)
+    stage_b(2)
+
+    loaded(6, 10)
     latent_back = dot(kv_grad[...], w_up[...], across)
     held = compressed[...]
     inverse = lax.rsqrt(jnp.mean(held * held, axis=-1, keepdims=True) + EPSILON)
@@ -1617,12 +1713,48 @@
 
     for n in range(0, width, 512):
         part = dot(q_grad[...], w_query[n : n + 512, :], across) + dot(l_grad[:, : rank + ROPE], w_latent[n : n + 512, :], across)
-        hidden_part[:, :, n : n + 512] = part.astype(bf16).reshape(depth, rows, 512)
-    for n in range(depth - 1):
+        hidden_part[:, :, n : n + 512] = part.astype(bf16).reshape(pieces, piece, 512)
+    for n in range(pieces):
         h_start(n)
-    z_pass(2)
-    stage_c(3)
-
+    for n in range(per, 2 * per):
+        z_hop(2, n)
+    stage_c(2)
+    stage_b(3)
+
+    flip_1 = tp + 1 - 2 * lax.rem(tp, 2)
+    flip_2 = tp + 2 - 4 * lax.div(tp, 2)
+
+    def doubling(held, send, recv, partners):
+        def copy(n):
+            return remote(held.at[2 * n], held.at[2 * n + 1], send.at[n], recv.at[n], partners[n])
+
+        def start():
+            copy(0).start()
+
+        def step(n):
+            copy(n).wait_recv()
+            total = held[2 * n] + held[2 * n + 1]
+            if n + 1 < len(partners):
+                held[2 * n + 2] = total
+                copy(n + 1).start()
+            return total
+
+        def drain():
+            for n in range(len(partners)):
+                copy(n).wait_send()
+
+        return start, step, drain
+
+    gain_start, gain_step, gain_drain = doubling(
+        gains, as_, ar, ((pair, tp), (xn, tp), (yn, tp), (ep, flip_1), (ep, flip_2))
+    )
+    attn_start, attn_step, attn_drain = doubling(attn_gains, ns, nr, ((pair, tp), (xn, tp), (yn, tp)))
+    gains[0] = jnp.zeros_like(gains[0])
+    gains[0, 1:2, :] = jnp.sum(gain_part_ref[...], axis=0, keepdims=True)
+    gains[0, 2:3, 0:rank] = gain_latent_part
+    gain_start()
+
+    loaded(10, 14)
     u_grad[...] = dot(latent_in[...], kv_grad[...], turned).astype(bf16)
 
     def w_store(b):
@@ -1668,76 +1800,6 @@
             copy.start()
     w_load(0).start()
 
-    z_finish()
-
-    def block_rows(r, _):
-        at = pl.ds(pl.multiple_of(r * 16, 16), 16)
-        value = row_sum[at, :] + held_rows[depth - 1, 0, at, :].astype(f32)
-        value = value + got_z[tp, at, :].astype(f32) + got_z[depth, at, :].astype(f32)
-        own_block[at, :] = value.astype(bf16)
-        return 0
-
-    lax.fori_loop(0, rows // 16, block_rows, 0)
-    block_on(0)
-    own_block_copy = pltpu.make_async_copy(own_block, block_ref.at[tp], misc_sem.at[2])
-    own_block_copy.start()
-    h_pass(0)
-    w_stage_a()
-    h_pass(1)
-    block_wait(1)
-    block_on(1)
-    h_pass(2)
-
-    resid_copy.wait()
-    h_finish()
-
-    def input_rows(r, gain_sum):
-        at = pl.ds(pl.multiple_of(r * 16, 16), 16)
-        u = hidden_part[tp, at, :].astype(f32)
-        u = u + got_h[tp, at, :].astype(f32) + got_h[depth, at, :].astype(f32)
-        v = resid[at, :].astype(f32)
-        inv = lax.rsqrt(jnp.mean(v * v, axis=-1, keepdims=True) + EPSILON)
-        v_hat = v * inv
-        gain_sum = gain_sum + (u * v_hat)[:8] + (u * v_hat)[8:]
-        s = u * gain_attn[...]
-        back = inv * (s - v_hat * jnp.mean(s * v_hat, axis=-1, keepdims=True))
-        own_grad[at, :] = (middle_grad_ref[at, :] + back).astype(bf16)
-        return gain_sum
-
-    gain_sum = lax.fori_loop(0, rows // 16, input_rows, jnp.zeros((8, width), f32))
-    grad_on(0)
-    own_grad_copy = pltpu.make_async_copy(own_grad, grad_in_ref.at[tp], misc_sem.at[1])
-    own_grad_copy.start()
-
-    gains[0] = jnp.zeros_like(gains[0])
-    gains[0, 0:1, :] = jnp.sum(gain_sum, axis=0, keepdims=True)
-    gains[0, 1:2, :] = jnp.sum(gain_part_ref[...], axis=0, keepdims=True)
-    gains[0, 2:3, 0:rank] = gain_latent_part
-    flip_1 = tp + 1 - 2 * lax.rem(tp, 2)
-    flip_2 = tp + 2 - 4 * lax.div(tp, 2)
-    partners = ((pair, tp), (xn, tp), (yn, tp), (ep, flip_1), (ep, flip_2))
-
-    def gain_copy(n):
-        return remote(gains.at[2 * n], gains.at[2 * n + 1], as_.at[n], ar.at[n], partners[n])
-
-    def gain_step(n):
-        gain_copy(n).wait_recv()
-        total = gains[2 * n] + gains[2 * n + 1]
-        if n + 1 < len(partners):
-            gains[2 * n + 2] = total
-            gain_copy(n + 1).start()
-        else:
-            gains_ref[...] = total
-
-    gain_copy(0).start()
-    block_wait(2)
-    block_on(2)
-    w_stage_b()
-    gain_step(0)
-    grad_wait(1)
-    grad_on(1)
-    gain_step(1)
-    w_stage_c()
     w_part = w_rows // depth
 
     def w_z_copy(k):
@@ -1745,18 +1807,102 @@
         src = w_pair.at[1, pl.ds(pl.multiple_of(to * w_part, w_part), w_part), pl.ds(q_cols, l_cols)]
         return remote(src, w_z.at[k - 1], wzs.at[k - 1], wzr.at[k - 1], (ep, to))
 
-    w_first_copy(1).wait_send()
-    w_pair[1, :, q_cols:o_start] = latent_part[...].astype(bf16)
-    for k in range(1, depth):
-        w_z_copy(k).start()
-    grad_wait(2)
-    grad_on(2)
-    gain_step(2)
-    block_wait(3)
-    block_on(3)
-    gain_step(3)
-    shared_place()
-    gain_step(4)
+    def block_copy(n):
+        return pltpu.make_async_copy(block_tile.at[n % 2], block_ref.at[pl.ds(n * piece, piece)], block_sem.at[n % 2])
+
+    def block_rows(n):
+        z_finish(n)
+        if n >= 2:
+            block_copy(n - 2).wait()
+
+        def total(r, _):
+            at = pl.ds(pl.multiple_of(r * 16, 16), 16)
+            inside = pl.ds(pl.multiple_of(n % per * piece + r * 16, 16), 16)
+            value = z_up[n, at, :].astype(f32) + z_down[n, at, :].astype(f32) - held_rows[n // per, 0, inside, :].astype(f32)
+            block_tile[n % 2, at, :] = value.astype(bf16)
+            return 0
+
+        lax.fori_loop(0, piece // 16, total, 0)
+        block_copy(n).start()
+
+    def grad_copy(n):
+        return pltpu.make_async_copy(grad_tile.at[n % 2], grad_in_ref.at[pl.ds(n * piece, piece)], grad_sem.at[n % 2])
+
+    def grad_rows(n, gain_sum):
+        h_finish(n)
+        if n >= 2:
+            grad_copy(n - 2).wait()
+        resid_copy(n).wait()
+
+        def total(r, gain_sum):
+            at = pl.ds(pl.multiple_of(r * 16, 16), 16)
+            inside = pl.ds(pl.multiple_of(n % per * piece + r * 16, 16), 16)
+            u = h_up[n, at, :].astype(f32) + h_down[n, at, :].astype(f32) - hidden_part[n, at, :].astype(f32)
+            v = resid[n % 2, at, :].astype(f32)
+            inv = lax.rsqrt(jnp.mean(v * v, axis=-1, keepdims=True) + EPSILON)
+            v_hat = v * inv
+            gain_sum = gain_sum + (u * v_hat)[:8] + (u * v_hat)[8:]
+            s = u * gain_attn[...]
+            back = inv * (s - v_hat * jnp.mean(s * v_hat, axis=-1, keepdims=True))
+            grad_tile[n % 2, at, :] = (branch[n // per, inside, :].astype(f32) + back).astype(bf16)
+            return gain_sum
+
+        gain_sum = lax.fori_loop(0, piece // 16, total, gain_sum)
+        if n + 2 < pieces:
+            resid_copy(n + 2).start()
+        grad_copy(n).start()
+        return gain_sum
+
+    gain_sum = jnp.zeros((8, width), f32)
+    for t in range(pieces + 2):
+        if t < pieces:
+            h_hop(1, t)
+        if t >= 2:
+            h_hop(2, t - 2)
+        if t >= 4:
+            gain_sum = grad_rows(t - 4, gain_sum)
+        if t == 1:
+            gain_step(0)
+        if t == 2:
+            w_stage_a()
+        if t == 0:
+            stage_c(3)
+        if t == 3:
+            gain_step(1)
+        if t == 5:
+            block_rows(0)
+            block_rows(1)
+            gain_step(2)
+        if t == 6:
+            gain_step(3)
+        if t == 7:
+            w_stage_b()
+            block_rows(2)
+            block_rows(3)
+        if t == 8:
+            gains_ref[...] = gain_step(4)
+    for t in range(pieces // 2 + 2):
+        if t < pieces // 2:
+            z_hop(1, pieces // 2 + t)
+        if t >= 2:
+            z_hop(2, pieces // 2 + t - 2)
+        if t < 2:
+            gain_sum = grad_rows(pieces - 2 + t, gain_sum)
+        if t == 1:
+            attn_gains[0] = gain_sum
+            attn_start()
+        if t == 2:
+            w_stage_c()
+            w_first_copy(1).wait_send()
+            w_pair[1, :, q_cols:o_start] = latent_part[...].astype(bf16)
+            for k in range(1, depth):
+                w_z_copy(k).start()
+            attn_step(0)
+            shared_place()
+        if t == 4:
+            attn_step(1)
+    for n in range(pieces // 2, pieces):
+        block_rows(n)
     for k in range(1, depth):
         w_z_copy(k).wait_recv()
     own = pl.ds(pl.multiple_of(tp * w_part, w_part), w_part)
@@ -1764,14 +1910,13 @@
     for k in range(depth - 1):
         total = total + w_z[k].astype(f32)
     latent_ref[...] = total
-    grad_wait(3)
-    grad_on(3)
-
-    own_grad_copy.wait()
-    own_block_copy.wait()
+    gains_ref[0:1, :] = jnp.sum(attn_step(2), axis=0, keepdims=True)
+
+    for n in (pieces - 2, pieces - 1):
+        block_copy(n).wait()
+    for n in (pieces - 2, pieces - 1):
+        grad_copy(n).wait()
     branch_drain()
-    grad_drain()
-    block_drain()
     for i in range(depth):
         for slot in range(2):
             first_copy(i, slot).wait_send()
@@ -1784,15 +1929,15 @@
     w_second_copy().wait_send()
     for k in range(1, depth):
         w_z_copy(k).wait_send()
-    for n in range(len(partners)):
-        gain_copy(n).wait_send()
+    gain_drain()
+    attn_drain()
     for m in range(1, 8):
         for copy in shared_copies(m):
             copy.wait_send()
 
 
 def tail_call(
-    branch, middle_grad, middle, out_part, router, gain_part, inputs, s_in, s_out, w_output, w_query, w_latent, w_up,
+    branch, middle, out_part, router, gain_part, inputs, s_in, s_out, w_output, w_query, w_latent, w_up,
     hidden, qn, qr, kv, kr, attended, latent_in, compressed, tables, gain_latent, gain_attn,
     heads, shared, cid,
 ):
@@ -1802,6 +1947,7 @@
     blocks = s_in.shape[0]
     rank = compressed.shape[1]
     q_cols, l_cols = w_query.shape[1], rank + 128
+    pieces = 2 * depth
     w_rows = width // blocks
     w_cols = q_cols + l_cols + w_output.shape[0] + rank * w_up.shape[1] // width
     dma = pltpu.SemaphoreType.DMA
@@ -1809,8 +1955,8 @@
     return pl.pallas_call(
         functools.partial(tail_kernel, depth, heads, shared),
         out_shape=(
-            jax.ShapeDtypeStruct((depth, rows, width), bf16),
-            jax.ShapeDtypeStruct((depth, rows, width), bf16),
+            jax.ShapeDtypeStruct((tokens, width), bf16),
+            jax.ShapeDtypeStruct((tokens, width), bf16),
             jax.ShapeDtypeStruct((8, width), f32),
             jax.ShapeDtypeStruct((w_rows, q_cols), f32),
             jax.ShapeDtypeStruct((w_output.shape[0], w_rows), f32),
@@ -1819,17 +1965,27 @@
             jax.ShapeDtypeStruct((2, w_rows, blocks * shared), f32),
             jax.ShapeDtypeStruct((blocks * shared, w_rows), f32),
             jax.ShapeDtypeStruct((blocks, w_rows, w_cols), bf16),
+            jax.ShapeDtypeStruct((2, w_rows, w_cols), bf16),
         ),
-        in_specs=[vmem, vmem, anywhere, anywhere, vmem, vmem, anywhere, anywhere, anywhere] + [vmem] * 15,
-        out_specs=(anywhere, anywhere) + (vmem,) * 7 + (anywhere,),
+        in_specs=[vmem, anywhere, anywhere, anywhere, vmem] + [anywhere] * 16 + [vmem, vmem],
+        out_specs=(anywhere, anywhere) + (vmem,) * 7 + (anywhere, anywhere),
         scratch_shapes=[
+            *(
+                pltpu.VMEM(a.shape, a.dtype)
+                for a in (
+                    w_output, w_query, w_latent, w_up, hidden, qn, qr, kv, kr, attended, latent_in, compressed, tables, router,
+                )
+            ),
+            dma((14,)),
             pltpu.VMEM((depth, rows, width), bf16),
             pltpu.VMEM((depth, 2, rows, width), bf16),
             pltpu.VMEM((depth, 2, rows, width), bf16),
             pltpu.VMEM((depth, rows, width), bf16),
-            pltpu.VMEM((depth + 1, rows, width), bf16),
-            pltpu.VMEM((depth, rows, width), bf16),
-            pltpu.VMEM((depth + 1, rows, width), bf16),
+            pltpu.VMEM((pieces, tokens // pieces, width), bf16),
+            pltpu.VMEM((pieces, tokens // pieces, width), bf16),
+            pltpu.VMEM((pieces, tokens // pieces, width), bf16),
+            pltpu.VMEM((pieces, tokens // pieces, width), bf16),
+            pltpu.VMEM((pieces, tokens // pieces, width), bf16),
             pltpu.VMEM((rows, width), f32),
             pltpu.VMEM((tokens, heads * VDIM), bf16),
             pltpu.VMEM((tokens, 128), f32),
@@ -1839,29 +1995,27 @@
             pltpu.VMEM((rank, heads * (NOPE + VDIM)), bf16),
             pltpu.VMEM((2, w_rows, w_cols), bf16),
             pltpu.VMEM((4, w_rows, w_cols), bf16),
-            pltpu.VMEM((2, w_rows, w_cols), bf16),
             pltpu.VMEM((w_rows, w_cols), bf16),
             pltpu.VMEM((depth - 1, w_rows // depth, l_cols), bf16),
             pltpu.VMEM((w_rows, l_cols), f32),
             pltpu.VMEM(s_in.shape, bf16),
             pltpu.VMEM(s_out.shape, bf16),
-            pltpu.VMEM((rows, width), bf16),
-            pltpu.VMEM((rows, width), bf16),
-            pltpu.VMEM((rows, width), bf16),
+            pltpu.VMEM((2, tokens // pieces, width), bf16),
+            pltpu.VMEM((2, tokens // pieces, width), bf16),
+            pltpu.VMEM((2, tokens // pieces, width), bf16),
             pltpu.VMEM((10, 8, width), f32),
+            pltpu.VMEM((6, 8, width), f32),
             dma((depth, 2)),
             dma((depth, 2)), dma((depth, 2)), dma((depth,)), dma((depth,)),
-            dma((depth - 1,)), dma((depth + 1,)),
+            dma((pieces,)), dma((pieces,)), dma((pieces,)), dma((pieces,)),
             dma((depth, 2)), dma((depth,)),
-            dma((depth - 1,)), dma((depth + 1,)),
-            dma((depth, 2)), dma((depth,)),
-            dma((depth, 2)), dma((depth,)),
+            dma((pieces,)), dma((pieces,)), dma((pieces,)), dma((pieces,)),
             dma((4,)), dma((4,)), dma((2,)), dma((2,)), dma, dma, dma((depth - 1,)), dma((depth - 1,)),
-            dma((5,)), dma((5,)), dma((4,)), dma((2,)), dma((8,)), dma((8,)), dma((8,)), dma((8,)),
+            dma((5,)), dma((5,)), dma((3,)), dma((3,)), dma((2,)), dma((2,)), dma((2,)), dma((2,)), dma((2,)), dma((8,)), dma((8,)), dma((8,)), dma((8,)),
         ],
         compiler_params=pltpu.CompilerParams(collective_id=cid, has_side_effects=True, vmem_limit_bytes=63 << 20),
     )(
-        branch, middle_grad, middle, out_part, router, gain_part, inputs, s_in, s_out, w_output, w_query, w_latent, w_up,
+        branch, middle, out_part, router, gain_part, inputs, s_in, s_out, w_output, w_query, w_latent, w_up,
         hidden, qn, qr, kv, kr, attended, latent_in, compressed, tables,
         gain_latent.reshape(1, rank), gain_attn.reshape(1, width),
     )
@@ -1954,14 +2108,14 @@
         inputs, gain_attn, w_query, w_latent, gain_latent, w_latent_up, w_output, tables, gain_ffn, cotangent, kept_lanes,
         w_expert_in, w_expert_out, shared_in, shared_out, ep_count, tp_count, heads_here, shared, experts, 0,
     )
-    middle_grad, branch, gain_ffn_part, grad_expert_in, grad_expert_out, shared_in_part, shared_out_part, router_part, layer_sum, _ = (
+    branch, gain_ffn_part, grad_expert_in, grad_expert_out, shared_in_part, shared_out_part, router_part, layer_sum, _ = (
         sum_call(
             rows_grad, hidden_all, hidden_grads, gated, cot_all, middle, gain_ffn, w_out, routed, shared, experts, 1
         )
     )
-    block_out, grad_inputs, gains, grad_query, grad_output, grad_latent_up, latent_sum, grad_shared_in, grad_shared_out, _ = (
+    block_out, grad_inputs, gains, grad_query, grad_output, grad_latent_up, latent_sum, grad_shared_in, grad_shared_out, _, _ = (
         tail_call(
-            branch, middle_grad, middle, layer_sum, router_part, gain_ffn_part, inputs, shared_in_part, shared_out_part,
+            branch, middle, layer_sum, router_part, gain_ffn_part, inputs, shared_in_part, shared_out_part,
             w_output, w_query, w_latent, w_latent_up, hidden_attn,
             query_nope, query_rope, key_value, key_pair,
             attended, latent_in, compressed, tables, gain_latent, gain_attn, heads_here, shared, 2,
@@ -1974,8 +2128,6 @@
     grad_gain_attn = lax.dynamic_slice_in_dim(gains[0], flat * wide_part, wide_part, 0)
     grad_gain_ffn = lax.dynamic_slice_in_dim(gains[1], flat * wide_part, wide_part, 0)
     grad_gain_latent = lax.dynamic_slice_in_dim(gains[2], flat * rank_part, rank_part, 0)
-    block_out = block_out.reshape(tokens, model_width)
-    grad_inputs = grad_inputs.reshape(tokens, model_width)
     return (
         block_out,
         grad_inputs,

time: 557 us -> 526 us (0.944)
  Pallas kernels: 500 us -> 469 us
    pallas_call x1, Pallas kernels: 208 us -> 178 us  [tail_call(): pl.pallas_call(functools.partial(tail_kernel, depth, heads, shared), out_...]
where the time goes in v7:
time: 526 us; the launch traced here: 517 us
  Pallas kernels  469 us (89%)
  local copies, waits for them, and re-layouts  35.6 us (7%)
  other arithmetic  5.37 us (1%)
    pallas_call x1, Pallas kernels, experts_call(): pl.pallas_call(functools.partial(experts_kernel, depth, blocks, heads, ro...  190 us
    pallas_call x1, Pallas kernels, tail_call(): pl.pallas_call(functools.partial(tail_kernel, depth, heads, shared), out_...  178 us
    pallas_call x1, Pallas kernels, sum_call(): pl.pallas_call(functools.partial(sum_kernel, depth, routed, shared, exper...  101 us
    unnamed x35, local copies, waits for them, and re-layouts  27.6 us
  transfers between devices with their start and end apart: 1, of which 0 were waited for; matrix products, arithmetic and copies ran while one was open for 3% of the time, Pallas kernels for 0%

profile of v7, /device:TPU:0, one launch (start us, length us, event | category | flops | bytes accessed | tf_op | source)
XLA Modules:
  0.0 516.6 jit_solution(2004888739486296762)
XLA Ops:
  0.6 0.7 broadcast_compare_fusion
  1.4 0.7 fusion.3
  2.1 0.5 broadcast.15
  2.7 0.7 reduce
  3.4 0.6 reshape.65
  4.0 5.2 %all-to-all-start = ((bf16[8,2,256]{2,1,0:T(2,128)(2,1)}), bf16[8,2,256]{2,1,0:T(2,128)(2,1)S(1)}, u32[]{:S(2)}, u32[]{:S(2)}) async-start(bf16[8,2,256]{2,1,0:T(2,128)(2,1)} %reshape.65), calls=%async_computation | async-start | bytes 16384 | tf_op jit(solution)/shard_map/all_to_all | solution.py:2079
  9.1 0.9 fusion.10
  10.1 0.3 copy.69
  10.4 0.1 pad_bitcast_fusion
  10.5 1.2 constant_dynamic-slice_fusion.4
  11.6 0.7 copy.76
  12.3 2.3 fusion.1.s_in
  14.6 1.0 constant_dynamic-slice_fusion.3
  15.6 0.0 copy-start
  15.6 0.9 pad.10.s_out
  16.5 4.5 copy.70.w_latent.w_latent_in
  21.1 0.0 copy-done
  21.1 2.8 copy.71.e_in
  23.8 0.0 all-to-all-done
  23.8 1.6 broadcast_in_dim.4.kept_hbm
  25.4 190.1 %shard_map.272 = (f32[128,2048]{1,0:T(8,128)}, bf16[4,8,128,2048]{3,2,1,0:T(8,128)(2,1)}, bf16[4,8,128,2048]{3,2,1,0:T(8,128)(2,1)}, bf16[4,8,128,1024]{3,2,1,0:...) custom-call(bf16[512,2048]{1,0:T(8,128)(2,1)} %inputs_ref.3, ...), custom_call_target="tpu_custom_call" | custom-call | tf_op jit(solution)/shard_map/pallas_call | solution.py:1033
  215.6 101.2 %shard_map.273 = (bf16[128,2048]{1,0:T(8,128)(2,1)}, f32[8,2048]{1,0:T(8,128)}, f32[1,2,2048,352]{3,2,1,0:T(8,128)}, f32[1,352,2048]{2,1,0:T(8,128)}, bf16[8,2,2...) custom-call(bf16[4,8,128,2048]{3,2,1,0:T(8,128)(2,1)} %get-tuple-ele, ...), custom_call_target="tpu_custom_call" | custom-call | tf_op jit(solution)/shard_map/pallas_call | solution.py:1343
  316.8 177.8 %shard_map.274 = (bf16[512,2048]{1,0:T(8,128)(2,1)}, bf16[512,2048]{1,0:T(8,128)(2,1)}, f32[8,2048]{1,0:T(8,128)}, f32[256,768]{1,0:T(8,128)}, f32[512,256]{1,0:...) custom-call(bf16[128,2048]{1,0:T(8,128)(2,1)} %get-tuple-element.53., ...), custom_call_target="tpu_custom_call" | custom-call | tf_op jit(solution)/shard_map/pallas_call | solution.py:1955
  494.6 1.0 fusion.9
  495.5 0.8 slice.19
  496.4 0.7 copy.73
  497.0 3.0 copy.74
  500.0 0.0 copy-start.3
  500.0 6.5 %copy.75 = f32[1,2,2048,352]{2,3,1,0:T(8,128)} copy(f32[1,2,2048,352]{3,2,1,0:T(8,128)} %get-tuple-element.132) | data formatting | bytes 11534336
  506.5 0.0 copy-start.2
  506.5 0.6 fusion.7
  507.1 0.6 fusion.6
  507.7 0.0 copy-done.3
  507.7 1.3 copy.91
  509.0 0.0 copy-done.2
  509.0 0.0 copy-start.4
  509.0 0.0 copy-start.8
  509.0 0.0 copy-start.7
  509.0 0.0 copy-start.6
  509.0 0.0 copy-start.5
  509.0 1.3 copy.92
  510.4 0.3 copy-done.4
  510.6 0.0 copy-start.1
  510.6 0.9 copy.93
  511.5 0.0 copy-done.8
  511.5 0.7 copy.94
  512.2 0.0 copy-done.7
  512.2 0.7 copy.95
  512.9 0.0 copy-done.6
  512.9 0.8 copy.96
  513.7 0.0 copy-done.5
  513.7 0.9 copy.97
  514.5 0.0 copy-done.1
  514.5 1.6 copy.98
  (7 shorter events, 0.1 us)
Async XLA Ops:
  4.0 19.8 %all-to-all-start = ((bf16[8,2,256]{2,1,0:T(2,128)(2,1)}), bf16[8,2,256]{2,1,0:T(2,128)(2,1)S(1)}, u32[]{:S(2)}, u32[]{:S(2)}) async-start(bf16[8,2,256]{2,1,0:T(2,128)(2,1)} %reshape.65), calls=%async_computation | async-start | bytes 16384 | tf_op jit(solution)/shard_map/all_to_all | solution.py:2079
  15.6 5.4 %copy-start = (bf16[1,2,2048,352]{2,3,1,0:T(8,128)(2,1)S(1)}, bf16[1,2,2048,352]{2,3,1,0:T(8,128)(2,1)}, u32[]{:S(2)}) copy-start(bf16[1,2,2048,352]{2,3,1,0:T(8,128)(2,1)} %param.28) | copy-start | bytes 8650756
  500.0 7.7 %copy-start.3 = (bf16[512,2048]{1,0:T(8,128)(2,1)S(1)}, bf16[512,2048]{1,0:T(8,128)(2,1)}, u32[]{:S(2)}) copy-start(bf16[512,2048]{1,0:T(8,128)(2,1)} %get-tuple-element.156) | copy-start | bytes 6291460
  506.5 2.5 copy-start.2
  509.0 1.6 copy-start.4
  509.0 2.5 copy-start.8
  509.0 3.2 copy-start.7
  509.0 3.9 copy-start.6
  509.0 4.6 copy-start.5
  510.6 3.9 copy-start.1

commit v8 on v7

--- a/solution.py
+++ b/solution.py
@@ -577,10 +577,10 @@
     middle_ref, h_out, cot_all, grads_out, gated_out, rows_out,
     hidden_out, qn_out, qr_out, kv_out, kr_out, attended_out, latent_in_out, compressed_out, w_out_out,
     part_ref, hidden, qn_ref, qr_ref, kv, kr_ref, attended, latent_in, compressed, rope_slab,
-    kept_ref, w_in_ref, w_out_ref, e_stage,
+    kept_ref, w_in_ref, w_out_ref,
     h_all, got_z, cot_tile, gu, act_grad, prob_lanes, diff_lanes, pair_lanes,
     grads_tile, gated_tile, rows_tile,
-    weight_sem, stage_sem, save_sem, local_sem, z_send, z_recv, line_send, line_recv, h_send, h_recv, c_send, c_recv, b_send, b_recv, tile_sem, store_sem,
+    weight_sem, save_sem, local_sem, z_send, z_recv, line_send, line_recv, h_send, h_recv, c_send, c_recv, b_send, b_recv, tile_sem, store_sem,
 ):
     f32, bf16 = jnp.float32, jnp.bfloat16
     ep, tp = lax.axis_index("ep"), lax.axis_index("tp")
@@ -621,14 +621,9 @@
         pltpu.make_async_copy(s_out, w_out_ref.at[pl.ds(routed, hidden_units - routed)], weight_sem.at[2]),
     ]
     for g in range(2):
-        at = pl.ds(g * hidden_units + routed // 128 * 128, s_in.shape[2])
-        weight_loads.append(pltpu.make_async_copy(s_in.at[g], w_in_ref.at[:, at], weight_sem.at[3 + g]))
-    piece = e_stage.shape[1]
-    pieces = width // piece
-
-    def e_load(n):
-        at = pl.ds(pl.multiple_of(lax.rem(n, pieces) * piece, piece), piece)
-        return pltpu.make_async_copy(e_in.at[0, lax.div(n, pieces), at], e_stage.at[lax.rem(n, 2)], stage_sem.at[lax.rem(n, 2)])
+        own, beside = pl.ds(g * hidden_units, routed), pl.ds(g * hidden_units + routed, hidden_units - routed)
+        weight_loads.append(pltpu.make_async_copy(e_in.at[0, g], w_in_ref.at[own], weight_sem.at[3 + 2 * g]))
+        weight_loads.append(pltpu.make_async_copy(s_in.at[g], w_in_ref.at[beside], weight_sem.at[4 + 2 * g]))
 
     def h_copy(block, chunk, slot, to):
         ref = h_all.at[chunk, block]
@@ -672,7 +667,6 @@
         own_cot_in(k).start()
     for copy in weight_loads:
         copy.start()
-    e_load(0).start()
 
     def first_norm(r, _):
         at = pl.ds(pl.multiple_of(r * 16, 16), 16)
@@ -683,7 +677,7 @@
 
     lax.fori_loop(0, tokens // 16, first_norm, 0)
     table = tuple(tables[n] for n in range(3))
-    latent = dot(hidden[...], w_latent[...])
+    latent = dot(hidden[...], w_latent[...], across)
     held = latent[:, :rank]
     compressed[...] = held
     inverse = lax.rsqrt(jnp.mean(held * held, axis=-1, keepdims=True) + EPSILON)
@@ -732,32 +726,11 @@
         own_cot_in(k).wait()
         own_cot_out(k).start()
 
-    def e_place(n, _):
-        e_load(n).wait()
-
-        @pl.when(n + 1 < 2 * pieces)
-        def _():
-            e_load(n + 1).start()
-
-        at = pl.ds(pl.multiple_of(lax.rem(n, pieces) * piece, piece), piece)
-
-        @pl.when(n < pieces)
-        def _():
-            w_in_ref[at, 0:routed] = e_stage[lax.rem(n, 2)]
-
-        @pl.when(n >= pieces)
-        def _():
-            w_in_ref[at, hidden_units : hidden_units + routed] = e_stage[lax.rem(n, 2)]
-
-        return 0
-
     for copy in weight_loads:
         copy.wait()
     w_out_save = pltpu.make_async_copy(w_out_ref, w_out_out, save_sem.at[8])
     w_out_save.start()
-    lax.fori_loop(0, pieces, e_place, 0)
     z_pass(0)
-    lax.fori_loop(pieces, 2 * pieces, e_place, 0)
     z_pass(1)
     z_pass(2)
     z_finish()
@@ -827,11 +800,11 @@
 
     send_chunk(0)
     forward_chunk(c_copy, order[0])
+    forward_chunk(h_copy, order[0])
+    send_chunk(1)
     forward_chunk(c_copy, theirs)
     buddy_copy(0, theirs).start()
     buddy_copy(1, theirs).start()
-    send_chunk(1)
-    forward_chunk(h_copy, order[0])
 
     base = routed + shared
     slab = base // 128 * 128
@@ -863,22 +836,15 @@
 
         @pl.when(i == 1)
         def _():
-            send_chunk(2)
-            forward_chunk(c_copy, order[1])
-            forward_chunk(h_copy, order[1])
             forward_diag(c_copy, order[0])
+
+        @pl.when(i == 2)
+        def _():
             forward_diag(c_copy, theirs)
             buddy_copy(2, theirs).start()
 
-        @pl.when(i == 2)
-        def _():
-            send_chunk(3)
-            forward_chunk(h_copy, order[2])
-
         @pl.when(i == 3)
         def _():
-            forward_skipped()
-            forward_chunk(h_copy, order[3])
             forward_diag(c_copy, order[1])
 
         @pl.when(side == 1)
@@ -896,9 +862,7 @@
         group = pl.ds(start, half)
         stores[0].start()
         for n in range(0, 2 * hidden_units, 512):
-            gu[:, n : n + 512] = jnp.dot(
-                h_all[chunk, group].reshape(tile, width), w_in_ref[:, n : n + 512], preferred_element_type=f32
-            )
+            gu[:, n : n + 512] = dot(h_all[chunk, group].reshape(tile, width), w_in_ref[n : n + 512, :], across)
         piece = gu[:, slab : slab + 128]
         logits = piece + pltpu.roll(piece, 128 - experts, 1) + pltpu.roll(piece, 128 - 2 * experts, 1)
         is_logit = (lanes >= lane0) & (lanes < lane0 + experts)
@@ -910,6 +874,29 @@
         prob_here = jnp.sum(probs * here * kept, axis=-1, keepdims=True)
         prob_lanes[...] = jnp.broadcast_to(prob_here, (tile, 128))
         diff_lanes[...] = here - probs
+
+        @pl.when(i == 0)
+        def _():
+            forward_chunk(h_copy, order[1])
+            send_chunk(2)
+
+        @pl.when(i == 1)
+        def _():
+            forward_chunk(c_copy, order[1])
+            send_chunk(3)
+
+        @pl.when(i == 2)
+        def _():
+            forward_chunk(h_copy, order[2])
+
+        @pl.when(i == 3)
+        def _():
+            forward_skipped()
+
+        @pl.when(i == 4)
+        def _():
+            forward_chunk(h_copy, order[3])
+
         load.wait()
         act_grad[...] = lax.dot_general(
             cot_tile[...].reshape(tile, width), w_out_ref[...], (((1,), (1,)), ((), ())), preferred_element_type=f32
@@ -960,10 +947,7 @@
         )
         for n in range(0, width, 512):
             rows_tile[slot, :, :, n : n + 512] = (
-                lax.dot_general(
-                    grads_tile[slot].reshape(tile, 2 * hidden_units), w_in_ref[n : n + 512, :], (((1,), (1,)), ((), ())),
-                    preferred_element_type=f32,
-                ).astype(bf16).reshape(half, rows, 512)
+                dot(grads_tile[slot].reshape(tile, 2 * hidden_units), w_in_ref[:, n : n + 512]).astype(bf16).reshape(half, rows, 512)
             )
         for copy in stores[1:]:
             copy.start()
@@ -1045,9 +1029,8 @@
             *(pltpu.VMEM(*size) for size in kept_sizes),
             pltpu.VMEM((tokens, 128), f32),
             pltpu.VMEM((depth, blocks, rows, 128), bf16),
-            pltpu.VMEM((width, 2 * hidden), bf16),
+            pltpu.VMEM((2 * hidden, width), bf16),
             pltpu.VMEM((hidden, width), bf16),
-            pltpu.VMEM((2, 256, routed), bf16),
             pltpu.VMEM((depth, blocks, rows, width), bf16),
             pltpu.VMEM((depth + 1, rows, width), bf16),
             pltpu.VMEM((half, rows, width), bf16),
@@ -1059,7 +1042,7 @@
             pltpu.VMEM((2, half, rows, 2 * hidden), bf16),
             pltpu.VMEM((2, half, rows, hidden), bf16),
             pltpu.VMEM((2, half, rows, width), bf16),
-            dma((5,)), dma((2,)), dma((9,)), dma((depth,)),
+            dma((7,)), dma((9,)), dma((depth,)),
             dma((depth - 1,)), dma((depth + 1,)),
             dma((depth, 2)), dma((depth,)),
             dma((depth, 7)), dma((depth, 7)),
@@ -1076,9 +1059,9 @@
 def sum_kernel(
     depth, routed, shared, experts, part_ref, h_ref, grads_ref, gated_ref, cot_ref, middle_ref, gain_ref, w_out_ref,
     branch, gain_part, expert_in, expert_out, s_in, s_out, router, layer_sum, landed,
-    in_grad, out_grad, e_stage, s_stage,
+    in_grad, out_grad,
     load, store, layer, got_pair, got_first, got_second, got_z, keep, h_tile, grads_tile, gated_tile, cot_tile,
-    own_cot, load_sem, store_sem, own_sem, lps, lpr, ps, pr, fs, fr, ss, sr, zs, zr, tile_sem, e_sem, s_sem, o_sem,
+    own_cot, load_sem, store_sem, own_sem, lps, lpr, ps, pr, fs, fr, ss, sr, zs, zr, tile_sem, e_sem, o_sem,
 ):
     f32 = jnp.float32
     rows = part_ref.shape[2]
@@ -1196,43 +1179,11 @@
 
 
     blocks_all = h_tile.shape[0]
-    lanes = lax.broadcasted_iota(jnp.int32, (1, 128), 1)
-    slab = routed // 128 * 128
-    shift = 128 - (routed - slab)
-    router_shift = (ROPE - (routed + shared) % 128) % 128
-
     def expert_out_copy():
         return pltpu.make_async_copy(out_grad.at[pl.ds(0, routed)], expert_out.at[0], o_sem)
 
-    def place_copies(m):
-        side = lax.rem(m, 2)
-        at = pl.ds(pl.multiple_of(m * 512, 512), 512)
-        per = 512 // (width // blocks_all)
-        return (
-            pltpu.make_async_copy(e_stage.at[side], expert_in.at[0, :, at], e_sem.at[side]),
-            pltpu.make_async_copy(s_stage.at[side], s_in.at[pl.ds(m * per, per)], s_sem.at[side]),
-        )
-
-    def place(m, found):
-        side = lax.rem(m, 2)
-
-        @pl.when(m >= 2)
-        def _():
-            for copy in place_copies(m - 2):
-                copy.wait()
-
-        wide = width // blocks_all
-        for g in range(2):
-            e_stage[side, g] = found[:, g * hidden : g * hidden + routed]
-            first_slab = found[:, g * hidden + slab : g * hidden + slab + 128]
-            second_slab = found[:, g * hidden + slab + 128 : g * hidden + slab + 256]
-            units = jnp.where(lanes < shift, pltpu.roll(first_slab, shift, 1), pltpu.roll(second_slab, shift, 1))
-            s_stage[side, :, g] = units.astype(s_stage.dtype).reshape(512 // wide, wide, 128)
-        last_slab = pltpu.roll(found[:, (routed + shared) // 128 * 128 : (routed + shared) // 128 * 128 + 128], router_shift, 1)
-        inside = (lanes >= ROPE) & (lanes < ROPE + experts)
-        router[pl.ds(pl.multiple_of(m * 512, 512), 512), :] = jnp.where(inside, last_slab, 0.0).astype(router.dtype)
-        for copy in place_copies(m):
-            copy.start()
+    def expert_in_copy(g):
+        return pltpu.make_async_copy(in_grad.at[pl.ds(g * hidden, routed)], expert_in.at[0, g], e_sem.at[g])
 
     def weights(c):
         for copy in tile_loads(c):
@@ -1242,20 +1193,15 @@
         last = c == depth - 1
 
         def in_part(m, _):
-            at = pl.ds(pl.multiple_of(m * 512, 512), 512)
+            at = pl.ds(pl.multiple_of(m * 256, 256), 256)
             found = lax.dot_general(
-                h_tile[:, :, at].reshape(count, 512), grads_tile[...].reshape(count, 2 * hidden), turned,
+                grads_tile[:, :, at].reshape(count, 256), h_tile[...].reshape(count, width), turned,
                 preferred_element_type=f32,
             )
-            if c > 0:
-                found = in_grad[at, :] + found
-            if last:
-                place(m, found)
-            else:
-                in_grad[at, :] = found
+            in_grad[at, :] = found if c == 0 else in_grad[at, :] + found
             return 0
 
-        lax.fori_loop(0, width // 512, in_part, 0)
+        lax.fori_loop(0, 2 * hidden // 256, in_part, 0)
 
         def out_part(m, _):
             at = pl.ds(pl.multiple_of(m * 512, 512), 512)
@@ -1269,9 +1215,16 @@
         lax.fori_loop(0, width // 512, out_part, 0)
         if last:
             expert_out_copy().start()
+            expert_in_copy(0).start()
+            expert_in_copy(1).start()
+            router[...] = in_grad[routed + shared : routed + shared + experts, :]
             wide = width // blocks_all
             for b in range(blocks_all):
-                s_out[b] = out_grad[routed : routed + s_out.shape[1], b * wide : (b + 1) * wide].astype(s_out.dtype)
+                at = slice(b * wide, (b + 1) * wide)
+                s_out[b] = out_grad[routed : routed + s_out.shape[1], at].astype(s_out.dtype)
+                for g in range(2):
+                    top = g * hidden + routed
+                    s_in[b, g] = in_grad[top : top + s_in.shape[2], at].astype(s_in.dtype)
         if c > 0:
             layer_add(c - 1)
         layer_send(c)
@@ -1321,9 +1274,8 @@
 
     gain_part[...] = lax.fori_loop(0, rows // 16, total, jnp.zeros((8, width), f32))
     expert_out_copy().wait()
-    for m in (width // 512 - 2, width // 512 - 1):
-        for copy in place_copies(m):
-            copy.wait()
+    expert_in_copy(0).wait()
+    expert_in_copy(1).wait()
     for i in range(depth):
         for slot in range(4):
             pair_copy(i, slot).wait_send()
@@ -1345,21 +1297,19 @@
         out_shape=(
             jax.ShapeDtypeStruct((rows, width), bf16),
             jax.ShapeDtypeStruct((8, width), f32),
-            jax.ShapeDtypeStruct((1, 2, width, routed), f32),
+            jax.ShapeDtypeStruct((1, 2, routed, width), f32),
             jax.ShapeDtypeStruct((1, routed, width), f32),
-            jax.ShapeDtypeStruct((blocks, 2, width // blocks, 128), bf16),
+            jax.ShapeDtypeStruct((blocks, 2, -(-shared // 16) * 16, width // blocks), bf16),
             jax.ShapeDtypeStruct((blocks, -(-shared // 16) * 16, width // blocks), bf16),
-            jax.ShapeDtypeStruct((width, 128), bf16),
+            jax.ShapeDtypeStruct((experts, width), f32),
             jax.ShapeDtypeStruct((depth, 4, rows, width), bf16),
             jax.ShapeDtypeStruct((depth, 4, rows, width), bf16),
         ),
         in_specs=[anywhere] * 5 + [vmem] * 3,
-        out_specs=(vmem,) * 2 + (anywhere,) * 3 + (vmem,) * 2 + (anywhere,) * 2,
+        out_specs=(vmem,) * 2 + (anywhere,) * 2 + (vmem,) * 3 + (anywhere,) * 2,
         scratch_shapes=[
-            pltpu.VMEM((width, 2 * hidden), f32),
+            pltpu.VMEM((2 * hidden, width), f32),
             pltpu.VMEM((hidden, width), f32),
-            pltpu.VMEM((2, 2, 512, routed), f32),
-            pltpu.VMEM((2, 512 // (width // blocks), 2, width // blocks, 128), bf16),
             pltpu.VMEM((4, rows, width), bf16),
             pltpu.VMEM((2, rows, width), bf16),
             pltpu.VMEM((blocks, rows, width), bf16),
@@ -1374,7 +1324,7 @@
             pltpu.VMEM((blocks, rows, width), bf16),
             pltpu.VMEM((rows, width), bf16),
             dma((4,)), dma((2,)), dma, dma((depth, 4)), dma((depth, 4)), dma((depth, 4)), dma((depth, 4)), dma((depth, 2)), dma((depth, 2)),
-            dma((depth,)), dma((depth,)), dma((depth - 1,)), dma((depth - 1,)), dma((4,)), dma((2,)), dma((2,)), dma,
+            dma((depth,)), dma((depth,)), dma((depth - 1,)), dma((depth - 1,)), dma((4,)), dma((2,)), dma,
         ],
         compiler_params=pltpu.CompilerParams(collective_id=cid, has_side_effects=True, vmem_limit_bytes=62 << 20),
     )(part, h_all, grads, gated, cot_all, middle, gain.reshape(1, width), w_out)
@@ -1413,12 +1363,12 @@
 
 def tail_kernel(
     depth, heads, shared,
-    branch_ref, middle_ref, part_ref, router_in, gain_part_ref, inputs_ref, s_in, s_out,
+    branch_ref, middle_ref, part_ref, router_ref, gain_part_ref, inputs_ref, s_in, s_out,
     w_output_in, w_query_in, w_latent_in, w_up_in, hidden_in, qn_in, qr_in, kv_in, kr_in, attended_in, latent_in_in, compressed_in,
     tables_in, gain_latent, gain_attn,
     block_ref, grad_in_ref, gains_ref, query_ref, output_ref, up_ref, latent_ref, shared_in, shared_out, w_all, w_first,
     w_output, w_query, w_latent, w_up, hidden_ref, qn_ref, qr_ref, kv_ref, kr_ref, attended, latent_in, compressed,
-    tables, router_ref, load_in_sem,
+    tables, load_in_sem,
     branch, held_rows, got_first, got_second, z_up, z_down, hidden_part, h_up, h_down, middle,
     d_out, d_kr, q_grad, kv_grad, l_grad, u_grad, w_stage, w_pair, w_second, w_z, latent_part, s_in_land, s_out_land, resid, grad_tile, block_tile, gains, attn_gains,
     load_sem, fs, fr, ss, sr, zus, zur, zds, zdr, bs, br, hus, hur, hds, hdr,
@@ -1458,7 +1408,7 @@
                 (w_output_in, w_output),
                 (qn_in, qn_ref), (qr_in, qr_ref), (kv_in, kv_ref), (kr_in, kr_ref), (tables_in, tables),
                 (w_up_in, w_up), (compressed_in, compressed), (w_query_in, w_query), (w_latent_in, w_latent),
-                (hidden_in, hidden_ref), (attended_in, attended), (latent_in_in, latent_in), (router_in, router_ref),
+                (hidden_in, hidden_ref), (attended_in, attended), (latent_in_in, latent_in),
             )
         )
     ]
@@ -1588,7 +1538,7 @@
         for n in range(s_in_land.shape[0]):
             at = slice(n * shared, (n + 1) * shared)
             for g in range(2):
-                shared_in[g, :, at] = s_in_land[n, g].astype(f32)[:, :shared]
+                shared_in[g, at, :] = s_in_land[n, g].astype(f32)[:shared]
             shared_out[at, :] = s_out_land[n].astype(f32)[:shared]
 
     branch_on(0)
@@ -1712,7 +1662,7 @@
     l_grad[:, rank:] = jnp.where(lanes < 64, rope, 0.0).astype(bf16)
 
     for n in range(0, width, 512):
-        part = dot(q_grad[...], w_query[n : n + 512, :], across) + dot(l_grad[:, : rank + ROPE], w_latent[n : n + 512, :], across)
+        part = dot(q_grad[...], w_query[n : n + 512, :], across) + dot(l_grad[:, : rank + ROPE], w_latent[:, n : n + 512])
         hidden_part[:, :, n : n + 512] = part.astype(bf16).reshape(pieces, piece, 512)
     for n in range(pieces):
         h_start(n)
@@ -1752,9 +1702,10 @@
     gains[0] = jnp.zeros_like(gains[0])
     gains[0, 1:2, :] = jnp.sum(gain_part_ref[...], axis=0, keepdims=True)
     gains[0, 2:3, 0:rank] = gain_latent_part
+    gains[0, 8 : 8 + router_ref.shape[0], :] = router_ref[...]
     gain_start()
 
-    loaded(10, 14)
+    loaded(10, 13)
     u_grad[...] = dot(latent_in[...], kv_grad[...], turned).astype(bf16)
 
     def w_store(b):
@@ -1773,7 +1724,7 @@
         w_stage[slot, :, 0:q_cols] = dot(own, q_grad[...], turned).astype(bf16)
         found = dot(own, l_grad[...], turned)
         w_stage[slot, :, q_cols : q_cols + rank] = found[:, :rank].astype(bf16)
-        w_stage[slot, :, q_cols + rank : o_start] = found[:, rank:].astype(bf16) + router_ref[at, :]
+        w_stage[slot, :, q_cols + rank : o_start] = found[:, rank:].astype(bf16)
         cols = pl.ds(pl.multiple_of(b * o_cols, 256), o_cols)
         found = dot(attended[...], branch[:, :, cols].reshape(tokens, o_cols), turned)
         for n in range(o_rows // w_rows):
@@ -1957,26 +1908,26 @@
         out_shape=(
             jax.ShapeDtypeStruct((tokens, width), bf16),
             jax.ShapeDtypeStruct((tokens, width), bf16),
-            jax.ShapeDtypeStruct((8, width), f32),
+            jax.ShapeDtypeStruct((8 + router.shape[0], width), f32),
             jax.ShapeDtypeStruct((w_rows, q_cols), f32),
             jax.ShapeDtypeStruct((w_output.shape[0], w_rows), f32),
             jax.ShapeDtypeStruct((rank // blocks, w_up.shape[1]), f32),
             jax.ShapeDtypeStruct((w_rows // depth, l_cols), f32),
-            jax.ShapeDtypeStruct((2, w_rows, blocks * shared), f32),
+            jax.ShapeDtypeStruct((2, blocks * shared, w_rows), f32),
             jax.ShapeDtypeStruct((blocks * shared, w_rows), f32),
             jax.ShapeDtypeStruct((blocks, w_rows, w_cols), bf16),
             jax.ShapeDtypeStruct((2, w_rows, w_cols), bf16),
         ),
-        in_specs=[vmem, anywhere, anywhere, anywhere, vmem] + [anywhere] * 16 + [vmem, vmem],
+        in_specs=[vmem, anywhere, anywhere, vmem, vmem] + [anywhere] * 16 + [vmem, vmem],
         out_specs=(anywhere, anywhere) + (vmem,) * 7 + (anywhere, anywhere),
         scratch_shapes=[
             *(
                 pltpu.VMEM(a.shape, a.dtype)
                 for a in (
-                    w_output, w_query, w_latent, w_up, hidden, qn, qr, kv, kr, attended, latent_in, compressed, tables, router,
+                    w_output, w_query, w_latent, w_up, hidden, qn, qr, kv, kr, attended, latent_in, compressed, tables,
                 )
             ),
-            dma((14,)),
+            dma((13,)),
             pltpu.VMEM((depth, rows, width), bf16),
             pltpu.VMEM((depth, 2, rows, width), bf16),
             pltpu.VMEM((depth, 2, rows, width), bf16),
@@ -2003,7 +1954,7 @@
             pltpu.VMEM((2, tokens // pieces, width), bf16),
             pltpu.VMEM((2, tokens // pieces, width), bf16),
             pltpu.VMEM((2, tokens // pieces, width), bf16),
-            pltpu.VMEM((10, 8, width), f32),
+            pltpu.VMEM((10, 8 + router.shape[0], width), f32),
             pltpu.VMEM((6, 8, width), f32),
             dma((depth, 2)),
             dma((depth, 2)), dma((depth, 2)), dma((depth,)), dma((depth,)),
@@ -2087,17 +2038,16 @@
     shared = w_shared_in.shape[2] // ep_count
     hidden = padded_hidden(routed, shared)
     shared_start = ep_index * shared
-    slab = routed // 128 * 128
-    before, after = routed - slab, hidden - routed - shared
-    router_parts = jnp.concatenate(split_wide(w_router), axis=1)
+    after = hidden - routed - shared
+    router_parts = jnp.concatenate(split_wide(w_router), axis=1).T
     beside = jnp.stack(
         [
-            jnp.pad(router_parts, ((0, 0), (0, after - router_parts.shape[1]))),
-            jnp.zeros((model_width, after), bf16),
+            jnp.pad(router_parts, ((0, after - router_parts.shape[0]), (0, 0))),
+            jnp.zeros((after, model_width), bf16),
         ]
     )
-    shared_in = lax.dynamic_slice_in_dim(w_shared_in, shared_start, shared, 2)
-    shared_in = jnp.concatenate([jnp.zeros((2, model_width, before), bf16), shared_in, beside], axis=2)
+    shared_in = lax.dynamic_slice_in_dim(w_shared_in.swapaxes(1, 2), shared_start, shared, 1)
+    shared_in = jnp.concatenate([shared_in, beside], axis=1)
     shared_out = lax.dynamic_slice_in_dim(w_shared_out, shared_start, shared, 0)
     shared_out = jnp.pad(shared_out, ((0, after), (0, 0)))
     tables = rope_tables(tokens)
@@ -2105,8 +2055,8 @@
         middle, hidden_all, cot_all, hidden_grads, gated, rows_grad,
         hidden_attn, query_nope, query_rope, key_value, key_pair, attended, latent_in, compressed, w_out,
     ) = experts_call(
-        inputs, gain_attn, w_query, w_latent, gain_latent, w_latent_up, w_output, tables, gain_ffn, cotangent, kept_lanes,
-        w_expert_in, w_expert_out, shared_in, shared_out, ep_count, tp_count, heads_here, shared, experts, 0,
+        inputs, gain_attn, w_query, w_latent.T, gain_latent, w_latent_up, w_output, tables, gain_ffn, cotangent, kept_lanes,
+        w_expert_in.swapaxes(2, 3), w_expert_out, shared_in, shared_out, ep_count, tp_count, heads_here, shared, experts, 0,
     )
     branch, gain_ffn_part, grad_expert_in, grad_expert_out, shared_in_part, shared_out_part, router_part, layer_sum, _ = (
         sum_call(
@@ -2116,18 +2066,20 @@
     block_out, grad_inputs, gains, grad_query, grad_output, grad_latent_up, latent_sum, grad_shared_in, grad_shared_out, _, _ = (
         tail_call(
             branch, middle, layer_sum, router_part, gain_ffn_part, inputs, shared_in_part, shared_out_part,
-            w_output, w_query, w_latent, w_latent_up, hidden_attn,
+            w_output, w_query, w_latent.T, w_latent_up, hidden_attn,
             query_nope, query_rope, key_value, key_pair,
             attended, latent_in, compressed, tables, gain_latent, gain_attn, heads_here, shared, 2,
         )
     )
     grad_latent = latent_sum[:, : KV_RANK + ROPE]
-    grad_router = latent_sum[:, KV_RANK + ROPE : KV_RANK + ROPE + experts]
     flat = ep_index * tp_count + tp_index
     wide_part, rank_part = (n // (ep_count * tp_count) for n in (model_width, KV_RANK))
     grad_gain_attn = lax.dynamic_slice_in_dim(gains[0], flat * wide_part, wide_part, 0)
     grad_gain_ffn = lax.dynamic_slice_in_dim(gains[1], flat * wide_part, wide_part, 0)
     grad_gain_latent = lax.dynamic_slice_in_dim(gains[2], flat * rank_part, rank_part, 0)
+    grad_router = lax.dynamic_slice_in_dim(gains[8:], flat * wide_part, wide_part, 1).T
+    grad_expert_in = grad_expert_in.swapaxes(2, 3)
+    grad_shared_in = grad_shared_in.swapaxes(1, 2)
     return (
         block_out,
         grad_inputs,

time: 526 us -> 507 us (0.964)
  local copies, waits for them, and re-layouts: 35.6 us -> 24.7 us
    unnamed x35 -> x33, local copies, waits for them, and re-layouts: 27.6 us -> 16.3 us
    pallas_call x1, Pallas kernels: 190 us -> 180 us  [experts_call(): pl.pallas_call(functools.partial(experts_kernel, depth, blocks, heads, ro...]
  transfers between devices with their start and end apart: 1 -> 1, of which waited for: 0 -> 0; matrix products, arithmetic and copies ran while one was open for 3% -> 1% of each run, Pallas kernels for 0% -> 0%
where the time goes in v8:
time: 507 us; the launch traced here: 499 us
  Pallas kernels  464 us (92%)
  local copies, waits for them, and re-layouts  24.7 us (5%)
  starting transfers between devices  5.17 us (1%)
    pallas_call x1, Pallas kernels, tail_call(): pl.pallas_call(functools.partial(tail_kernel, depth, heads, shared), out_...  182 us
    pallas_call x1, Pallas kernels, experts_call(): pl.pallas_call(functools.partial(experts_kernel, depth, blocks, heads, ro...  180 us
    pallas_call x1, Pallas kernels, sum_call(): pl.pallas_call(functools.partial(sum_kernel, depth, routed, shared, exper...  102 us
    unnamed x33, local copies, waits for them, and re-layouts  16.3 us
  transfers between devices with their start and end apart: 1, of which 0 were waited for; matrix products, arithmetic and copies ran while one was open for 1% of the time, Pallas kernels for 0%

profile of v8, /device:TPU:0, one launch (start us, length us, event | category | flops | bytes accessed | tf_op | source)
XLA Modules:
  0.0 499.4 jit_solution(10803968844926828812)
XLA Ops:
  0.6 0.7 broadcast_compare_fusion
  1.4 0.7 fusion.3
  2.1 0.5 broadcast.13
  2.7 0.7 reduce
  3.4 0.6 reshape.65
  4.0 5.2 %all-to-all-start = ((bf16[8,2,256]{2,1,0:T(2,128)(2,1)}), bf16[8,2,256]{2,1,0:T(2,128)(2,1)S(1)}, u32[]{:S(2)}, u32[]{:S(2)}) async-start(bf16[8,2,256]{2,1,0:T(2,128)(2,1)} %reshape.65), calls=%async_computation | async-start | bytes 16384 | tf_op jit(solution)/shard_map/all_to_all | solution.py:2030
  9.1 0.9 fusion.10
  10.1 1.2 dynamic-slice_bitcast_fusion
  11.3 1.2 fusion.1.s_in
  12.5 1.0 constant_dynamic-slice_fusion.3
  13.5 0.9 pad.10.s_out
  14.4 0.0 all-to-all-done
  14.4 1.6 broadcast_in_dim.2.kept_hbm
  16.0 179.7 %shard_map.272 = (f32[128,2048]{1,0:T(8,128)}, bf16[4,8,128,2048]{3,2,1,0:T(8,128)(2,1)}, bf16[4,8,128,2048]{3,2,1,0:T(8,128)(2,1)}, bf16[4,8,128,1024]{3,2,1,0:...) custom-call(bf16[512,2048]{1,0:T(8,128)(2,1)} %inputs_ref.3, ...), custom_call_target="tpu_custom_call" | custom-call | tf_op jit(solution)/shard_map/pallas_call | solution.py:1017
  195.7 102.4 %shard_map.273 = (bf16[128,2048]{1,0:T(8,128)(2,1)}, f32[8,2048]{1,0:T(8,128)}, f32[1,2,352,2048]{3,2,1,0:T(8,128)}, f32[1,352,2048]{2,1,0:T(8,128)}, bf16[8,2,9...) custom-call(bf16[4,8,128,2048]{3,2,1,0:T(8,128)(2,1)} %get-tuple-ele, ...), custom_call_target="tpu_custom_call" | custom-call | tf_op jit(solution)/shard_map/pallas_call | solution.py:1295
  298.1 182.0 %shard_map.274 = (bf16[512,2048]{1,0:T(8,128)(2,1)}, bf16[512,2048]{1,0:T(8,128)(2,1)}, f32[16,2048]{1,0:T(8,128)}, f32[256,768]{1,0:T(8,128)}, f32[512,256]{1,0...) custom-call(bf16[128,2048]{1,0:T(8,128)(2,1)} %get-tuple-element.53., ...), custom_call_target="tpu_custom_call" | custom-call | tf_op jit(solution)/shard_map/pallas_call | solution.py:1906
  480.0 0.0 copy-start.1
  480.0 1.1 fusion.9
  481.1 0.8 slice.19
  482.0 0.7 dynamic-slice_bitcast_fusion.1
  482.6 0.6 fusion.6
  483.2 0.6 fusion.7
  483.8 0.0 copy-start.3
  483.8 0.0 slice-start
  483.8 3.3 copy.56
  487.1 0.0 copy-done.1
  487.1 0.0 copy-start.7
  487.1 0.0 copy-start.6
  487.1 0.0 copy-start.5
  487.1 0.0 slice-start.1
  487.1 1.3 copy.57
  488.5 0.0 copy-done.3
  488.5 0.0 copy-start.2
  488.5 0.9 copy.58
  489.3 0.0 copy-done.7
  489.3 0.0 copy-start.4
  489.3 0.7 copy.59
  490.0 0.0 copy-done.6
  490.0 0.7 copy.60
  490.7 0.0 copy-done.5
  490.7 0.8 copy.61
  491.5 0.0 copy-done.2
  491.5 1.1 copy.62
  492.6 0.0 copy-done.4
  492.6 0.9 copy.63
  493.5 0.0 slice-done
  493.5 0.0 slice-done.1
  493.5 0.0 copy-start
  493.5 2.9 copy.64
  496.4 1.0 copy-done
  497.4 1.6 copy.65
  (7 shorter events, 0.1 us)
Async XLA Ops:
  4.0 10.4 %all-to-all-start = ((bf16[8,2,256]{2,1,0:T(2,128)(2,1)}), bf16[8,2,256]{2,1,0:T(2,128)(2,1)S(1)}, u32[]{:S(2)}, u32[]{:S(2)}) async-start(bf16[8,2,256]{2,1,0:T(2,128)(2,1)} %reshape.65), calls=%async_computation | async-start | bytes 16384 | tf_op jit(solution)/shard_map/all_to_all | solution.py:2030
  480.0 7.1 %copy-start.1 = (bf16[512,2048]{1,0:T(8,128)(2,1)S(1)}, bf16[512,2048]{1,0:T(8,128)(2,1)}, u32[]{:S(2)}) copy-start(bf16[512,2048]{1,0:T(8,128)(2,1)} %get-tuple-element.101) | copy-start | bytes 6291460
  483.8 4.7 copy-start.3
  483.8 9.7 %slice-start = ((s8[5767168]{0:T(1024)(128)(4,1)}), s8[4194304]{0:T(1024)(128)(4,1)S(1)}, s32[]{:S(2)}) async-start(s8[5767168]{0:T(1024)(128)(4,1)} %bitcast.39), calls=%async_computation.1 | async-start | bytes 8388608
  487.1 2.2 copy-start.7
  487.1 2.9 copy-start.6
  487.1 3.6 copy-start.5
  487.1 6.4 %slice-start.1 = ((s8[5767168]{0:T(1024)(128)(4,1)}), s8[1572864]{0:T(1024)(128)(4,1)S(1)}, s32[]{:S(2)}) async-start(s8[5767168]{0:T(1024)(128)(4,1)} %bitcast.39), calls=%async_computation.2 | async-start | bytes 3145728
  488.5 3.1 copy-start.2
  489.3 3.3 copy-start.4
  493.5 3.9 copy-start

commit v9 on v8

--- a/solution.py
+++ b/solution.py
@@ -572,10 +572,11 @@
 
 def experts_kernel(
     depth, blocks, heads, routed, shared, experts,
-    inputs_ref, gain_attn, w_query, w_latent, gain_latent, w_up, w_output, tables,
+    inputs_in, gain_attn, w_query_in, w_latent_in, gain_latent, w_up_in, w_output_in, tables_in,
     gain_ref, cot_ref, kept_hbm, e_in, e_out, s_in, s_out,
     middle_ref, h_out, cot_all, grads_out, gated_out, rows_out,
     hidden_out, qn_out, qr_out, kv_out, kr_out, attended_out, latent_in_out, compressed_out, w_out_out,
+    inputs_ref, w_query, w_latent, w_up, w_output, tables, in_sem,
     part_ref, hidden, qn_ref, qr_ref, kv, kr_ref, attended, latent_in, compressed, rope_slab,
     kept_ref, w_in_ref, w_out_ref,
     h_all, got_z, cot_tile, gu, act_grad, prob_lanes, diff_lanes, pair_lanes,
@@ -608,6 +609,17 @@
     def twin(block):
         return block + pair - ep
 
+    loads = [
+        pltpu.make_async_copy(src, dst, in_sem.at[n])
+        for n, (src, dst) in enumerate(
+            (
+                (inputs_in, inputs_ref), (w_latent_in, w_latent), (tables_in, tables), (w_up_in, w_up),
+                (w_query_in, w_query), (w_output_in, w_output),
+            )
+        )
+    ]
+    for copy in loads:
+        copy.start()
     greet([(pair, tp), (xn, tp), (yn, tp)] + [(ep, lax.rem(tp + k, depth)) for k in range(1, depth)])
 
     def part_rows(n):
@@ -675,7 +687,10 @@
         hidden[at, :] = (v * inverse * gain_attn[...]).astype(bf16)
         return 0
 
+    loads[0].wait()
     lax.fori_loop(0, tokens // 16, first_norm, 0)
+    for copy in loads[1:]:
+        copy.wait()
     table = tuple(tables[n] for n in range(3))
     latent = dot(hidden[...], w_latent[...], across)
     held = latent[:, :rank]
@@ -1022,9 +1037,11 @@
         )
         + tuple(jax.ShapeDtypeStruct(*size) for size in kept_sizes)
         + (jax.ShapeDtypeStruct((hidden, width), bf16),),
-        in_specs=[vmem] * 9 + [anywhere] * 6,
+        in_specs=[anywhere, vmem, anywhere, anywhere, vmem, anywhere, anywhere, anywhere, vmem] + [anywhere] * 6,
         out_specs=(vmem,) + (anywhere,) * 14,
         scratch_shapes=[
+            *(pltpu.VMEM(a.shape, a.dtype) for a in (inputs, w_query, w_latent, w_up, w_output, tables)),
+            dma((6,)),
             pltpu.VMEM((tokens, width), bf16),
             *(pltpu.VMEM(*size) for size in kept_sizes),
             pltpu.VMEM((tokens, 128), f32),

time: 507 us -> 503 us (level)
  no operation moved by 1% of the time
where the time goes in v9:
time: 503 us; the launch traced here: 496 us
  Pallas kernels  461 us (92%)
  local copies, waits for them, and re-layouts  24.7 us (5%)
  starting transfers between devices  5.17 us (1%)
    pallas_call x1, Pallas kernels, tail_call(): pl.pallas_call(functools.partial(tail_kernel, depth, heads, shared), out_...  182 us
    pallas_call x1, Pallas kernels, experts_call(): pl.pallas_call(functools.partial(experts_kernel, depth, blocks, heads, ro...  177 us
    pallas_call x1, Pallas kernels, sum_call(): pl.pallas_call(functools.partial(sum_kernel, depth, routed, shared, exper...  102 us
    unnamed x33, local copies, waits for them, and re-layouts  16.3 us
  transfers between devices with their start and end apart: 1, of which 0 were waited for; matrix products, arithmetic and copies ran while one was open for 1% of the time, Pallas kernels for 0%

profile of v9, /device:TPU:0, one launch (start us, length us, event | category | flops | bytes accessed | tf_op | source)
XLA Modules:
  0.0 495.9 jit_solution(3271798927697051278)
XLA Ops:
  0.6 0.7 broadcast_compare_fusion
  1.4 0.7 fusion.3
  2.1 0.5 broadcast.13
  2.7 0.7 reduce
  3.4 0.6 reshape.65
  4.0 5.2 %all-to-all-start = ((bf16[8,2,256]{2,1,0:T(2,128)(2,1)}), bf16[8,2,256]{2,1,0:T(2,128)(2,1)S(1)}, u32[]{:S(2)}, u32[]{:S(2)}) async-start(bf16[8,2,256]{2,1,0:T(2,128)(2,1)} %reshape.65), calls=%async_computation | async-start | bytes 16384 | tf_op jit(solution)/shard_map/all_to_all | solution.py:2047
  9.1 0.9 fusion.10
  10.1 1.2 dynamic-slice_bitcast_fusion
  11.3 1.2 fusion.1.s_in
  12.5 1.0 constant_dynamic-slice_fusion.3
  13.5 0.9 pad.10.s_out
  14.4 0.0 all-to-all-done
  14.4 1.6 broadcast_in_dim.2.kept_hbm
  16.0 176.8 %shard_map.272 = (f32[128,2048]{1,0:T(8,128)}, bf16[4,8,128,2048]{3,2,1,0:T(8,128)(2,1)}, bf16[4,8,128,2048]{3,2,1,0:T(8,128)(2,1)}, bf16[4,8,128,1024]{3,2,1,0:...) custom-call(bf16[512,2048]{1,0:T(8,128)(2,1)} %inputs_ref.1, ...), custom_call_target="tpu_custom_call" | custom-call | tf_op jit(solution)/shard_map/pallas_call | solution.py:1032
  192.8 101.7 %shard_map.273 = (bf16[128,2048]{1,0:T(8,128)(2,1)}, f32[8,2048]{1,0:T(8,128)}, f32[1,2,352,2048]{3,2,1,0:T(8,128)}, f32[1,352,2048]{2,1,0:T(8,128)}, bf16[8,2,9...) custom-call(bf16[4,8,128,2048]{3,2,1,0:T(8,128)(2,1)} %get-tuple-ele, ...), custom_call_target="tpu_custom_call" | custom-call | tf_op jit(solution)/shard_map/pallas_call | solution.py:1312
  294.5 182.1 %shard_map.274 = (bf16[512,2048]{1,0:T(8,128)(2,1)}, bf16[512,2048]{1,0:T(8,128)(2,1)}, f32[16,2048]{1,0:T(8,128)}, f32[256,768]{1,0:T(8,128)}, f32[512,256]{1,0...) custom-call(bf16[128,2048]{1,0:T(8,128)(2,1)} %get-tuple-element.53., ...), custom_call_target="tpu_custom_call" | custom-call | tf_op jit(solution)/shard_map/pallas_call | solution.py:1923
  476.6 0.0 copy-start.1
  476.6 1.1 fusion.9
  477.7 0.8 slice.19
  478.5 0.7 dynamic-slice_bitcast_fusion.1
  479.2 0.6 fusion.6
  479.8 0.6 fusion.7
  480.3 0.0 copy-start.3
  480.3 0.0 slice-start
  480.3 3.3 copy.56
  483.7 0.0 copy-done.1
  483.7 0.0 copy-start.7
  483.7 0.0 copy-start.6
  483.7 0.0 copy-start.5
  483.7 0.0 slice-start.1
  483.7 1.3 copy.57
  485.0 0.0 copy-done.3
  485.0 0.0 copy-start.2
  485.0 0.9 copy.58
  485.9 0.0 copy-done.7
  485.9 0.0 copy-start.4
  485.9 0.7 copy.59
  486.6 0.0 copy-done.6
  486.6 0.7 copy.60
  487.3 0.0 copy-done.5
  487.3 0.8 copy.61
  488.1 0.0 copy-done.2
  488.1 1.1 copy.62
  489.2 0.0 copy-done.4
  489.2 0.9 copy.63
  490.0 0.0 slice-done
  490.0 0.0 slice-done.1
  490.0 0.0 copy-start
  490.0 2.9 copy.64
  493.0 1.0 copy-done
  493.9 1.6 copy.65
  (7 shorter events, 0.1 us)
Async XLA Ops:
  4.0 10.4 %all-to-all-start = ((bf16[8,2,256]{2,1,0:T(2,128)(2,1)}), bf16[8,2,256]{2,1,0:T(2,128)(2,1)S(1)}, u32[]{:S(2)}, u32[]{:S(2)}) async-start(bf16[8,2,256]{2,1,0:T(2,128)(2,1)} %reshape.65), calls=%async_computation | async-start | bytes 16384 | tf_op jit(solution)/shard_map/all_to_all | solution.py:2047
  476.6 7.1 %copy-start.1 = (bf16[512,2048]{1,0:T(8,128)(2,1)S(1)}, bf16[512,2048]{1,0:T(8,128)(2,1)}, u32[]{:S(2)}) copy-start(bf16[512,2048]{1,0:T(8,128)(2,1)} %get-tuple-element.101) | copy-start | bytes 6291460
  480.3 4.7 copy-start.3
  480.3 9.7 %slice-start = ((s8[5767168]{0:T(1024)(128)(4,1)}), s8[4194304]{0:T(1024)(128)(4,1)S(1)}, s32[]{:S(2)}) async-start(s8[5767168]{0:T(1024)(128)(4,1)} %bitcast.39), calls=%async_computation.1 | async-start | bytes 8388608
  483.7 2.2 copy-start.7
  483.7 2.9 copy-start.6
  483.7 3.6 copy-start.5
  483.7 6.4 %slice-start.1 = ((s8[5767168]{0:T(1024)(128)(4,1)}), s8[1572864]{0:T(1024)(128)(4,1)S(1)}, s32[]{:S(2)}) async-start(s8[5767168]{0:T(1024)(128)(4,1)} %bitcast.39), calls=%async_computation.2 | async-start | bytes 3145728
  485.0 3.1 copy-start.2
  485.9 3.3 copy-start.4
  490.0 3.9 copy-start
